TPU v7x, 32 devices: a whole 2x2x4 slice. The times are simulated.
32 devices in a mesh: dp: 4 (over y, x), seq: 8 (over z, core).
Axes of the slice: x: 2, y: 2, z: 4, core: 2. Of those that a mesh axis runs over, the one named last changes fastest.
Arguments:
- qkv: bfloat16 [3, 4, 2, 512, 4096], P(None, 'dp', None, 'seq'), may hold values from -4 to 4
- master: float32 [4, 4096], P(None, 'dp'), may hold values from -0.9 to 5.2
- moment_one: float32 [4, 4096], P(None, 'dp'), may hold values from -3 to 3
- moment_two: float32 [4, 4096], P(None, 'dp'), may hold values from 0.25 to 4
- grads: float32 [4, 4096], P(None, 'dp'), may hold values from -8 to 8
Outputs:
- attended: bfloat16 [4, 2, 512, 4096], P('dp', None, 'seq')
- updated: float32 [4, 4096], P(None, 'dp')
- first_moment: float32 [4, 4096], P(None, 'dp')
- second_moment: float32 [4, 4096], P(None, 'dp')
All inputs are finite; a program needn't handle non-finite values.
Results may differ from a plain program's by a relative error of at most 0.0011.
The roundings to bfloat16 on the way count: a program that leaves them out, or rounds other values in their place, can miss the bound.
Values may be sent and summed in bfloat16 or wider, within the bound.
No kernel may reach another device: no remote copies, remote signals or barrier semaphores. Data moves between devices by JAX's collectives and lax.ppermute only.
A program may use at most 64 MiB of HBM per device.

v0:
```python
import jax
import jax.numpy as jnp
from jax import lax
from jax.sharding import PartitionSpec as P

HEADS = 32
HD = 128
OPT_STEP = 10


BETA_ONE = 0.9
BETA_TWO = 0.95
RATE = 0.02
DECAY = 0.1
EPSILON = 1e-08


def from_root(array, axis, root):
    mine = lax.axis_index(axis) == root
    return lax.psum(jnp.where(mine, array, jnp.zeros_like(array)), axis)


def adamw(master, moment_one, moment_two, grads):
    first_moment = BETA_ONE * moment_one + (1.0 - BETA_ONE) * grads
    second_moment = BETA_TWO * moment_two + (1.0 - BETA_TWO) * grads * grads
    first_hat = first_moment / (1.0 - BETA_ONE**OPT_STEP)
    second_hat = second_moment / (1.0 - BETA_TWO**OPT_STEP)
    updated = master - RATE * (first_hat / (jnp.sqrt(second_hat) + EPSILON) + DECAY * master)
    return (updated, first_moment, second_moment)


def normalize(values, gain_row, bias_row):
    row_count = values.shape[0]
    head_count = values.shape[1] // HD
    grouped = values.astype(jnp.float32).reshape(row_count, head_count, HD)
    centre = jnp.mean(grouped, axis=-1, keepdims=True)
    spread = jnp.mean((grouped - centre) ** 2, axis=-1, keepdims=True)
    scaled = (grouped - centre) / jnp.sqrt(spread + 1e-06)
    scaled = scaled * gain_row.reshape(head_count, HD) + bias_row.reshape(head_count, HD)
    return scaled.reshape(row_count, head_count * HD).astype(jnp.bfloat16)


def normalize_block(values, gain_row, bias_row):
    flat = values.reshape(-1, values.shape[-1])
    return normalize(flat, gain_row, bias_row).reshape(values.shape)


def attend(queries, key_rows, value_rows):
    sample_count = queries.shape[0]
    patches = queries.shape[1]
    head_count = queries.shape[2] // HD
    query_heads = queries.reshape(sample_count, patches, head_count, HD)
    key_heads = key_rows.reshape(sample_count, patches, head_count, HD)
    value_heads = value_rows.reshape(sample_count, patches, head_count, HD)
    block_rows = min(512, patches)
    block_count = patches // block_rows
    scale_value = HD ** (-0.5)

    def one_block(position):
        sample_id = position // block_count
        start_row = position % block_count * block_rows
        sample_queries = lax.dynamic_index_in_dim(query_heads, sample_id, 0, keepdims=False)
        sample_keys = lax.dynamic_index_in_dim(key_heads, sample_id, 0, keepdims=False)
        sample_values = lax.dynamic_index_in_dim(value_heads, sample_id, 0, keepdims=False)
        block_queries = lax.dynamic_slice_in_dim(sample_queries, start_row, block_rows, 0)
        scores = (
            jnp.einsum(
                "qhd,khd->hqk", block_queries, sample_keys, preferred_element_type=jnp.float32
            )
            * scale_value
        )
        probs = jax.nn.softmax(scores, axis=-1).astype(jnp.bfloat16)
        block_out = jnp.einsum(
            "hqk,khd->qhd", probs, sample_values, preferred_element_type=jnp.float32
        )
        return block_out.astype(jnp.bfloat16)

    outputs = lax.map(one_block, jnp.arange(sample_count * block_count, dtype=jnp.int32))
    return outputs.reshape(sample_count, patches, head_count * HD)


def shards(qkv, master, moment_one, moment_two, grads):
    updated, first_moment, second_moment = adamw(master, moment_one, moment_two, grads)
    layer_bf = updated.astype(jnp.bfloat16)
    groups = lax.axis_size("seq")
    width = HEADS // groups * HD
    shard_cols = layer_bf.shape[1]
    first_col = lax.axis_index("seq") * width
    owner_index = first_col // shard_cols
    own_layer = from_root(layer_bf, "dp", owner_index).astype(jnp.float32)
    own_part = lax.dynamic_slice_in_dim(own_layer, first_col % shard_cols, width, 1)
    arrived = lax.all_to_all(qkv, "seq", split_axis=4, concat_axis=3, tiled=True)
    queries = normalize_block(arrived[0, 0], own_part[0], own_part[1])
    key_rows = normalize_block(arrived[1, 0], own_part[2], own_part[3])
    head_out = attend(queries, key_rows, arrived[2, 0])[None]
    attended = lax.all_to_all(head_out, "seq", split_axis=2, concat_axis=3, tiled=True)
    return (attended, updated, first_moment, second_moment)


def solution(mesh):
    placed = (
        P(None, "dp", None, "seq", None),
        P(None, "dp"),
        P(None, "dp"),
        P(None, "dp"),
        P(None, "dp"),
    )
    return jax.shard_map(
        shards,
        mesh=mesh,
        in_specs=placed,
        out_specs=(P("dp", None, "seq", None), P(None, "dp"), P(None, "dp"), P(None, "dp")),
        check_vma=False,
    )
```

profile of v0, /device:TPU:0, one launch (start us, length us, event | category | flops | bytes accessed | tf_op | source)
XLA Modules:
  0.0 234.5 jit_solution(12014299362431774412)
XLA Ops:
  0.6 11.8 %copy.71 = bf16[3,1,2,64,4096]{3,0,2,1,4:T(4,128)(2,1)} copy(bf16[3,1,2,64,4096]{4,3,2,1,0:T(8,128)(2,1)} %param.7) | data formatting | bytes 6291456 | tf_op args[0]
  12.4 9.8 %reshape.136 = bf16[8,2,98304]{2,1,0:T(2,128)(2,1)} reshape(bf16[4096,1,2,3,64]{4,3,2,1,0:T(4,128)(2,1)} %bitcast.55) | data formatting | bytes 6291456
  22.2 6.5 %all-to-all-start = ((bf16[8,2,98304]{2,1,0:T(2,128)(2,1)}), bf16[8,2,98304]{2,1,0:T(2,128)(2,1)S(1)}, u32[]{:S(2)}, u32[]{:S(2)}) async-start(bf16[8,2,98304]{2,1,0:T(2,128)(2,1)} %reshape.136), calls=%async_computation | async-start | bytes 6291456 | tf_op jit(solution)/shard_map/all_to_all | solution.py:92
  29.4 10.0 %psum.7 = bf16[4,1024]{1,0:T(4,128)(2,1)S(1)} all-reduce(bf16[4,1024]{1,0:T(4,128)(2,1)S(1)} %get-tuple-element.126), channel_id=1, replica_groups=mesh['dp'=4,'seq'=8] {'dp'}, use_global_device_ids=true, to_apply=%region_2.3 | all-reduce | flops 4096 | bytes 16384 | tf_op jit(solution)/shard_map/psum | solution.py:20
  39.4 60.8 %all-to-all-done = bf16[8,2,98304]{2,1,0:T(2,128)(2,1)S(1)} async-done(((bf16[8,2,98304]{2,1,0:T(2,128)(2,1)}), bf16[8,2,98304]{2,1,0:T(2,128)(2,1)S(1)}, u32[]{:S(2)}, u32[]{:S(2)}) %all-to-all-start) | async-done | bytes 3145760 | tf_op jit(solution)/shard_map/all_to_all | solution.py:92
  100.2 7.0 %reshape.137 = bf16[4096,1,2,3,64]{4,3,2,1,0:T(4,128)(2,1)} reshape(bf16[8,2,98304]{2,1,0:T(2,128)(2,1)S(1)} %all-to-all-done) | data formatting | bytes 6291456
  107.2 10.6 %copy.72 = bf16[3,1,2,64,8,512]{5,3,4,2,1,0:T(8,128)(2,1)S(1)} copy(bf16[3,1,2,64,8,512]{3,0,2,5,4,1:T(4,128)(2,1)} %bitcast.54) | data formatting | bytes 6291456 | tf_op jit(solution)/shard_map/all_to_all | solution.py:92
  117.9 2.6 %slice_convert_fusion = (f32[1,1,2,8,64,512]{5,4,3,2,1,0:T(8,128)}, f32[1,1,2,8,64,512]{5,4,3,2,1,0:T(8,128)}, bf16[1,1,2,8,64,512]{5,4,3,2,1,0:T(8,128)(2,1)}) fusion(bf16[3,1,2,8,64,512]{5,4,3,2,1,0:T(8,128)(2,1)S(1)} %bitcast.56), kind=kLoop, calls=%fused_computation.24 | loop fusion | flops 1048576 | bytes 8388608 | tf_op jit(solution)/shard_map/convert_element_type | solution.py:35
  120.5 1.9 reshape.133
  122.4 1.1 reduce_sum.48
  123.6 14.4 %multiply_reduce_fusion.2 = f32[1024,4]{1,0:T(8,128)S(1)} fusion(f32[1024,4,128]{2,1,0:T(4,128)S(1)} %reshape.133, f32[1024,4]{1,0:T(8,128)S(1)} %broadcast_multiply_fusion.1), kind=kLoop, calls=%fused_computation.23 | loop fusion | flops 1568768 | bytes 2129920 | tf_op jit(solution)/shard_map/reduce_sum | solution.py:37
  138.3 1.9 reshape.135
  140.2 1.9 reduce_sum.50
  142.2 1.1 broadcast_multiply_fusion
  143.2 15.2 %multiply_reduce_fusion.1 = f32[1024,4]{1,0:T(8,128)} fusion(f32[1024,4,128]{2,1,0:T(4,128)S(1)} %reshape.135, f32[1024,4]{1,0:T(8,128)S(1)} %broadcast_multiply_fusion), kind=kLoop, calls=%fused_computation.21 | loop fusion | flops 1568768 | bytes 2129920 | tf_op jit(solution)/shard_map/reduce_sum | solution.py:37
  158.7 3.1 %reshape.132 = f32[2,512,4,128]{3,2,1,0:T(4,128)} reshape(f32[1,1,2,8,64,512]{5,4,3,2,1,0:T(8,128)} %get-tuple-element.133) | data formatting | bytes 4194304 | tf_op jit(solution)/shard_map/convert_element_type | solution.py:35
  161.8 1.7 reshape.134
  163.8 1.1 copy.77
  165.2 1.1 copy.82
  166.3 1.0 copy.74
  167.3 1.0 copy.79
  168.4 1.1 reshape_squeeze.2
  169.5 7.8 %add_convert_fusion = (bf16[2,512,4,128]{3,2,1,0:T(4,128)(2,1)S(1)}, bf16[2,512,4,128]{3,2,1,0:T(4,128)(2,1)S(1)}) fusion(f32[2,512,4,128]{3,2,1,0:T(4,128)} %reshape.134, f32[4,128]{1,0:T(4,128)S(1)} %bitcast.67, f32[4,128]{1,0:T(4,128)S(1)} %bitcast.64, f32[2,512,4]{2,1,0:T(8,128)} %copy.82, f32[2,512,4]{2,1,0:T(8,128)} %copy.79, ...), kind=kLoop, calls=%fused_computation.20 | loop fusion | flops 5242880 | bytes 6365184 | tf_op jit(solution)/shard_map/convert_element_type | solution.py:40
  177.2 24.4 %while.12 = (s32[]{:T(128)}, bf16[2,512,4,128]{1,3,2,0:T(8,128)(2,1)}, s32[2]{0:T(128)S(1)}, bf16[2,512,4,128]{3,2,1,0:T(4,128)(2,1)}, bf16[2,512,4,128]{3,2,1,0...) while((s32[]{:T(128)}, ...), condition=%wide.region_8.9_spmd, body=%wide.region_5.8_spmd.sunk | while | flops 546573312 | bytes 44057288 | solution.py:78
  181.1 1.1 fusion.31
  182.2 0.8 copy-done
  183.6 5.9 %fusion.32 = bf16[2,512,4,128]{1,3,2,0:T(8,128)(2,1)} fusion(bf16[2,512,4,128]{1,3,2,0:T(8,128)(2,1)} %get-tuple-element.192, s32[]{:T(128)} %get-tuple-element.191, f32[4,512]{1,0:T(4,128)S(1)} %fusion.31, bf16[1,512,4,128]{1,3,2,0:T(8,128)(2,1)S(1)} %copy.108, f32[4,512,512]{1,2,0:T(8,128)} %copy-done), kind=kOutput, calls=%fused_computation.9.clone.1 | convolution fusion | flops 273943040 | bytes 9445888 | tf_op jit(solution)/shard_map/while/body/eval_jaxpr/hqk,khd->qhd/dot_general | solution.py:73
  193.3 1.1 fusion.31
  195.8 5.9 %fusion.32 = bf16[2,512,4,128]{1,3,2,0:T(8,128)(2,1)} fusion(bf16[2,512,4,128]{1,3,2,0:T(8,128)(2,1)} %get-tuple-element.192, s32[]{:T(128)} %get-tuple-element.191, f32[4,512]{1,0:T(4,128)S(1)} %fusion.31, bf16[1,512,4,128]{1,3,2,0:T(8,128)(2,1)S(1)} %copy.108, f32[4,512,512]{1,2,0:T(8,128)} %copy-done), kind=kOutput, calls=%fused_computation.9.clone.1 | convolution fusion | flops 273943040 | bytes 9445888 | tf_op jit(solution)/shard_map/while/body/eval_jaxpr/hqk,khd->qhd/dot_general | solution.py:73
  201.7 2.5 %copy.90 = bf16[1,2,512,512]{3,1,0,2:T(2,128)(2,1)S(1)} copy(bf16[1,2,512,512]{2,3,1,0:T(8,128)(2,1)} %bitcast.58) | data formatting | bytes 2097152 | tf_op jit(solution)/shard_map/broadcast_in_dim;reshape | solution.py:95
  204.2 29.0 %all_to_all.33 = bf16[1,2,512,512]{3,1,0,2:T(2,128)(2,1)S(1)} all-to-all(bf16[1,2,512,512]{3,1,0,2:T(2,128)(2,1)S(1)} %copy.90), channel_id=1, replica_groups=mesh['dp'=4,'seq'=8] {'seq'}, dimensions={2} | all-to-all | bytes 2097152 | tf_op jit(solution)/shard_map/all_to_all | solution.py:96
  233.4 1.1 copy.94
  (44 shorter events, 7.5 us)
Async XLA Ops:
  22.2 6.5 %copy-start.5 = (f32[4,1024]{1,0:T(4,128)S(1)}, f32[4,1024]{1,0:T(4,128)}, u32[]{:S(2)}) copy-start(f32[4,1024]{1,0:T(4,128)} %param.8) | copy-start | bytes 49156
  22.2 6.5 %copy-start.6 = (f32[4,1024]{1,0:T(4,128)S(1)}, f32[4,1024]{1,0:T(4,128)}, u32[]{:S(2)}) copy-start(f32[4,1024]{1,0:T(4,128)} %param.11) | copy-start | bytes 49156
  22.2 6.5 %copy-start.7 = (f32[4,1024]{1,0:T(4,128)S(1)}, f32[4,1024]{1,0:T(4,128)}, u32[]{:S(2)}) copy-start(f32[4,1024]{1,0:T(4,128)} %param.9) | copy-start | bytes 49156
  22.2 6.5 %copy-start.8 = (f32[4,1024]{1,0:T(4,128)S(1)}, f32[4,1024]{1,0:T(4,128)}, u32[]{:S(2)}) copy-start(f32[4,1024]{1,0:T(4,128)} %param.10) | copy-start | bytes 49156
  22.2 78.0 %all-to-all-start = ((bf16[8,2,98304]{2,1,0:T(2,128)(2,1)}), bf16[8,2,98304]{2,1,0:T(2,128)(2,1)S(1)}, u32[]{:S(2)}, u32[]{:S(2)}) async-start(bf16[8,2,98304]{2,1,0:T(2,128)(2,1)} %reshape.136), calls=%async_computation | async-start | bytes 6291456 | tf_op jit(solution)/shard_map/all_to_all | solution.py:92
  158.6 3.1 %copy-start.1 = (f32[1,1,2,8,64,512]{5,4,3,2,1,0:T(8,128)S(1)}, f32[1,1,2,8,64,512]{5,4,3,2,1,0:T(8,128)}, u32[]{:S(2)}) copy-start(f32[1,1,2,8,64,512]{5,4,3,2,1,0:T(8,128)} %get-tuple-element.132) | copy-start | bytes 6291460
  163.5 1.4 copy-start.4
  163.6 4.7 %copy-start.3 = (bf16[1,1,2,8,64,512]{5,4,3,2,1,0:T(8,128)(2,1)S(1)}, bf16[1,1,2,8,64,512]{5,4,3,2,1,0:T(8,128)(2,1)}, u32[]{:S(2)}) copy-start(bf16[1,1,2,8,64,512]{5,4,3,2,1,0:T(8,128)(2,1)} %get-tuple-element.134) | copy-start | bytes 3145732
  181.1 1.9 copy-start
  181.1 2.0 copy-start.2
  193.3 1.9 copy-start
  193.3 2.0 copy-start.2
where the time goes:
time: 236 us; the launch traced here: 234 us
  local copies, waits for them, and re-layouts  62.7 us (27%)
  waiting for transfers between devices  60.8 us (26%)
  other arithmetic  47.4 us (20%)
  blocking collectives  39.1 us (17%)
  matrix products  13.1 us (6%)
  starting transfers between devices  6.47 us (3%)
  loops' own time  4.24 us (2%)
    all_to_all x1, waiting for transfers between devices, shards(): lax.all_to_all(qkv, 'seq', split_axis=4, concat_axis=3, tiled=True)  60.8 us
    reduce_sum x2, other arithmetic, normalize(): spread = jnp.mean((grouped - centre) ** 2, axis=-1, keepdims=True)  29.7 us
    unnamed x21, local copies, waits for them, and re-layouts  29.4 us
    all_to_all x1, blocking collectives, shards(): lax.all_to_all(head_out, 'seq', split_axis=2, concat_axis=3, tiled=True)  29 us
    dot_general x2, matrix products, one_block(): jnp.einsum('hqk,khd->qhd', probs, sample_values, preferred_element_type=j...  11.7 us
    all_to_all x1, local copies, waits for them, and re-layouts, shards(): lax.all_to_all(qkv, 'seq', split_axis=4, concat_axis=3, tiled=True)  10.6 us
    psum x1, blocking collectives, from_root(): return lax.psum(jnp.where(mine, array, jnp.zeros_like(array)), axis)  10 us
    convert_element_type x4, local copies, waits for them, and re-layouts, normalize(): grouped = values.astype(jnp.float32).reshape(row_count, head_count, HD)  8.69 us
  transfers between devices with their start and end apart: 1, of which 1 were waited for; matrix products, arithmetic and copies ran while one was open for 0% of the time, Pallas kernels for 0%

commit v1 on v0

v1 whole, which is shorter than its diff:
```python
import functools

import jax
import jax.numpy as jnp
from jax import lax
from jax.experimental import pallas as pl
from jax.experimental.pallas import tpu as pltpu
from jax.sharding import PartitionSpec as P

HEADS = 32
HD = 128
OPT_STEP = 10

BETA_ONE = 0.9
BETA_TWO = 0.95
RATE = 0.02
DECAY = 0.1
EPSILON = 1e-08

LOG2E = 1.4426950408889634
ANY = pl.BlockSpec(memory_space=pl.ANY)
VMEM = pl.BlockSpec(memory_space=pltpu.VMEM)


def adamw(master, moment_one, moment_two, grads):
    first_moment = BETA_ONE * moment_one + (1.0 - BETA_ONE) * grads
    second_moment = BETA_TWO * moment_two + (1.0 - BETA_TWO) * grads * grads
    first_hat = first_moment / (1.0 - BETA_ONE**OPT_STEP)
    second_hat = second_moment / (1.0 - BETA_TWO**OPT_STEP)
    updated = master - RATE * (first_hat / (jnp.sqrt(second_hat) + EPSILON) + DECAY * master)
    return (updated, first_moment, second_moment)


def own_columns(layer, dp_count, seq_count, width):
    shard_cols = layer.shape[1]
    assert shard_cols % width == 0
    rounds = []
    for owner in range(dp_count):
        wanted = [
            (dp, seq)
            for seq in range(seq_count)
            if seq * width // shard_cols == owner
            for dp in range(dp_count)
            if dp != owner
        ]
        for place, (dp, seq) in enumerate(wanted):
            turn, source = divmod(place, seq_count)
            while len(rounds) <= turn:
                rounds.append([])
            rounds[turn].append((owner * seq_count + source, dp * seq_count + seq))
    first_col = lax.axis_index("seq") * width
    mine = lax.axis_index("dp") == first_col // shard_cols
    found = jnp.where(mine, layer, jnp.zeros_like(layer))
    for pairs in rounds:
        found = found + lax.ppermute(layer, ("dp", "seq"), pairs)
    return lax.dynamic_slice_in_dim(found, first_col % shard_cols, width, 1)


def pack_kernel(sample, count, width, source, *rest):
    outs, sems = rest[:count], rest[count]
    me = lax.axis_index("seq")
    copies = []
    for slot in range(count):
        first = pl.multiple_of(lax.bitwise_xor(me, slot) * width, width)
        copies.append(
            pltpu.make_async_copy(
                source.at[:, 0, sample, :, pl.ds(first, width)], outs[slot], sems.at[slot]
            )
        )
    for copy in copies:
        copy.start()
    for copy in copies:
        copy.wait()


def pack(qkv, sample, count, width):
    rows = qkv.shape[3]
    shape = jax.ShapeDtypeStruct((3, rows, width), qkv.dtype)
    return pl.pallas_call(
        functools.partial(pack_kernel, sample, count, width),
        out_shape=[shape] * count,
        in_specs=[ANY],
        out_specs=[ANY] * count,
        scratch_shapes=[pltpu.SemaphoreType.DMA((count,))],
        name="pack",
    )(qkv)


def normed(rows, gain, bias):
    grouped = rows.astype(jnp.float32)
    centred = grouped - jnp.mean(grouped, axis=-1, keepdims=True)
    spread = jnp.mean(centred * centred, axis=-1, keepdims=True)
    return (centred * lax.rsqrt(spread + 1e-06) * gain + bias).astype(jnp.bfloat16)


def attend_kernel(count, block, layer, *rest):
    arrived, outs = rest[:count], rest[count : 2 * count]
    rows, width = outs[0].shape
    per_block = max(1, block // rows)
    for head in range(width // HD):
        cols = slice(head * HD, (head + 1) * HD)
        gains = layer[:, cols].astype(jnp.float32)
        keys = jnp.concatenate([normed(a[1, :, cols], gains[2:3], gains[3:4]) for a in arrived])
        values = jnp.concatenate([a[2, :, cols] for a in arrived])
        for first in range(0, count, per_block):
            slots = range(first, first + per_block)
            queries = jnp.concatenate(
                [normed(arrived[slot][0, :, cols], gains[0:1], gains[1:2]) for slot in slots]
            )
            scores = lax.dot_general(
                queries, keys, (((1,), (1,)), ((), ())), preferred_element_type=jnp.float32
            )
            top = jnp.max(scores, axis=-1, keepdims=True)
            raised = jnp.exp2((scores - top) * (HD**-0.5 * LOG2E))
            total = jnp.sum(raised, axis=-1, keepdims=True)
            probs = (raised * (1.0 / total)).astype(jnp.bfloat16)
            result = jnp.dot(probs, values, preferred_element_type=jnp.float32)
            result = result.astype(jnp.bfloat16)
            for place, slot in enumerate(slots):
                outs[slot][:, cols] = result[place * rows : (place + 1) * rows]


def attend(layer, arrived):
    count = len(arrived)
    _, rows, width = arrived[0].shape
    patches = count * rows
    return pl.pallas_call(
        functools.partial(attend_kernel, count, 256),
        out_shape=[jax.ShapeDtypeStruct((rows, width), jnp.bfloat16)] * count,
        in_specs=[VMEM] * (1 + count),
        out_specs=[VMEM] * count,
        compiler_params=pltpu.CompilerParams(vmem_limit_bytes=32 * 1024 * 1024),
        cost_estimate=pl.CostEstimate(
            flops=4 * patches * patches * width,
            bytes_accessed=8 * patches * width,
            transcendentals=patches * patches * (width // HD),
        ),
        name="attend",
    )(layer, *arrived)


def unpack_kernel(samples, count, width, *rest):
    parts, out, sems = rest[: samples * count], rest[samples * count], rest[samples * count + 1]
    me = lax.axis_index("seq")
    copies = []
    for sample in range(samples):
        for slot in range(count):
            first = pl.multiple_of(lax.bitwise_xor(me, slot) * width, width)
            place = sample * count + slot
            copies.append(
                pltpu.make_async_copy(
                    parts[place], out.at[0, sample, :, pl.ds(first, width)], sems.at[place]
                )
            )
    for copy in copies:
        copy.start()
    for copy in copies:
        copy.wait()


def unpack(parts, samples, count):
    rows, width = parts[0].shape
    return pl.pallas_call(
        functools.partial(unpack_kernel, samples, count, width),
        out_shape=jax.ShapeDtypeStruct((1, samples, rows, width * count), parts[0].dtype),
        in_specs=[ANY] * len(parts),
        out_specs=ANY,
        scratch_shapes=[pltpu.SemaphoreType.DMA((len(parts),))],
        name="unpack",
    )(*parts)


def exchange(parts, order):
    count = len(parts)
    landed = list(parts)
    for slot in order:
        pairs = [(place, place ^ slot) for place in range(count)]
        landed[slot] = lax.ppermute(parts[slot], "seq", pairs)
    return landed


def shards(dp_count, seq_count, qkv, master, moment_one, moment_two, grads):
    samples = qkv.shape[2]
    width = qkv.shape[4] // seq_count
    order = list(range(seq_count - 1, 0, -1))
    landed = [exchange(pack(qkv, sample, seq_count, width), order) for sample in range(samples)]
    updated, first_moment, second_moment = adamw(master, moment_one, moment_two, grads)
    layer = own_columns(updated.astype(jnp.bfloat16), dp_count, seq_count, width)
    parts = []
    for sample in range(samples):
        parts += exchange(attend(layer, landed[sample]), order)
    attended = unpack(parts, samples, seq_count)
    return (attended, updated, first_moment, second_moment)


def solution(mesh):
    placed = (
        P(None, "dp", None, "seq", None),
        P(None, "dp"),
        P(None, "dp"),
        P(None, "dp"),
        P(None, "dp"),
    )
    return jax.shard_map(
        functools.partial(shards, mesh.shape["dp"], mesh.shape["seq"]),
        mesh=mesh,
        in_specs=placed,
        out_specs=(P("dp", None, "seq", None), P(None, "dp"), P(None, "dp"), P(None, "dp")),
        check_vma=False,
    )
```

time: 236 us -> 231 us (0.979)
  Pallas kernels: 0 us -> 138 us
  local copies, waits for them, and re-layouts: 62.7 us -> 2.81 us
  other arithmetic: 47.4 us -> 0.66 us
  starting transfers between devices: 6.47 us -> 52.6 us
  blocking collectives: 39.1 us -> 0 us
  waiting for transfers between devices: 60.8 us -> 34.6 us
  matrix products: 13.1 us -> 0 us
  loops' own time: 4.24 us -> 0 us
    pallas_call x0 -> x5, Pallas kernels: none -> 138 us  [the longest x2 97.7 us: pack(): pl.pallas_call(functools.partial(pack_kernel, sample, count, width), out_...]
    all_to_all x1 -> x0, waiting for transfers between devices: 60.8 us -> none  [shards(): lax.all_to_all(qkv, 'seq', split_axis=4, concat_axis=3, tiled=True)]
    ppermute x0 -> x29, starting transfers between devices: none -> 52.6 us  [the longest x28 49.2 us: exchange(): landed[slot] = lax.ppermute(parts[slot], 'seq', pairs)]
    ppermute x0 -> x29, waiting for transfers between devices: none -> 34.6 us  [the longest x28 34.6 us: exchange(): landed[slot] = lax.ppermute(parts[slot], 'seq', pairs)]
    reduce_sum x4 -> x0, other arithmetic: 32.8 us -> none  [the longest x2 29.7 us: normalize(): spread = jnp.mean((grouped - centre) ** 2, axis=-1, keepdims=True)]
    all_to_all x1 -> x0, blocking collectives: 29 us -> none  [shards(): lax.all_to_all(head_out, 'seq', split_axis=2, concat_axis=3, tiled=True)]
    unnamed x21 -> x50, local copies, waits for them, and re-layouts: 29.4 us -> 2.81 us
    dot_general x4 -> x0, matrix products: 13.1 us -> none  [the longest x2 11.7 us: one_block(): jnp.einsum('hqk,khd->qhd', probs, sample_values, preferred_element_type=j...]
  transfers between devices with their start and end apart: 1 -> 29, of which waited for: 1 -> 7; matrix products, arithmetic and copies ran while one was open for 0% -> 0% of each run, Pallas kernels for 0% -> 25%
where the time goes in v1:
time: 231 us; the launch traced here: 230 us
  Pallas kernels  138 us (60%)
  starting transfers between devices  52.6 us (23%)
  waiting for transfers between devices  34.6 us (15%)
  local copies, waits for them, and re-layouts  2.81 us (1%)
    pallas_call x2, Pallas kernels, pack(): pl.pallas_call(functools.partial(pack_kernel, sample, count, width), out_...  97.7 us
    ppermute x28, starting transfers between devices, exchange(): landed[slot] = lax.ppermute(parts[slot], 'seq', pairs)  49.2 us
    ppermute x28, waiting for transfers between devices, exchange(): landed[slot] = lax.ppermute(parts[slot], 'seq', pairs)  34.6 us
    pallas_call x1, Pallas kernels, unpack(): pl.pallas_call(functools.partial(unpack_kernel, samples, count, width), o...  33 us
    pallas_call x2, Pallas kernels, attend(): pl.pallas_call(functools.partial(attend_kernel, count, 256), out_shape=[j...  7.83 us
  transfers between devices with their start and end apart: 29, of which 7 were waited for; matrix products, arithmetic and copies ran while one was open for 0% of the time, Pallas kernels for 25%

profile of v1, /device:TPU:0, one launch (start us, length us, event | category | flops | bytes accessed | tf_op | source)
XLA Modules:
  0.0 230.2 jit_solution(2235380880096369262)
XLA Ops:
  0.7 48.8 %pack.3 = (bf16[3,64,512]{2,1,0:T(8,128)(2,1)}, bf16[3,64,512]{2,1,0:T(8,128)(2,1)}, bf16[3,64,512]{2,1,0:T(8,128)(2,1)}, bf16[3,64,512]{2,1,0:T(8,128)(2,1)}, b...) custom-call(bf16[3,1,2,64,4096]{4,3,2,1,0:T(8,128)(2,1)} %source.3), custom_call_target="tpu_custom_call" | custom-call | tf_op jit(solution)/shard_map/pack/pallas_call | solution.py:79
  50.1 2.6 %collective-permute-start.16 = (bf16[3,64,512]{2,1,0:T(8,128)(2,1)}, bf16[3,64,512]{2,1,0:T(8,128)(2,1)S(1)}, u32[]{:S(2)}, u32[]{:S(2)}) collective-permute-start(bf16[3,64,512]{2,1,0:T(8,128)(2,1)} %get-tuple-element.54), channel_id=1, source_target_pairs={{0,2},{1,3},{2,0},{3,1},{4,6},{5,7},{6,4},{7,5},{8,10},{9,11},{10,... | collective-permute-start | bytes 589832 | tf_op jit(solution)/shard_map/ppermute | solution.py:178
  52.8 2.7 %collective-permute-start.18 = (bf16[3,64,512]{2,1,0:T(8,128)(2,1)}, bf16[3,64,512]{2,1,0:T(8,128)(2,1)S(1)}, u32[]{:S(2)}, u32[]{:S(2)}) collective-permute-start(bf16[3,64,512]{2,1,0:T(8,128)(2,1)} %get-tuple-element.56), channel_id=1, source_target_pairs={{0,4},{1,5},{2,6},{3,7},{4,0},{5,1},{6,2},{7,3},{8,12},{9,13},{10,... | collective-permute-start | bytes 589832 | tf_op jit(solution)/shard_map/ppermute | solution.py:178
  55.5 0.6 fusion.1
  56.2 3.4 %collective-permute-start = (bf16[4,1024]{1,0:T(4,128)(2,1)S(1)}, bf16[4,1024]{1,0:T(4,128)(2,1)S(1)}, u32[]{:S(2)}, u32[]{:S(2)}) collective-permute-start(bf16[4,1024]{1,0:T(4,128)(2,1)S(1)} %get-tuple-element.68), channel_id=1, source_target_pairs={{0,8},{1,16},{2,24},{3,9},{4,17},{5,25},{8,2},{9,18},{10,26},{11,3... | collective-permute-start | bytes 24584 | tf_op jit(solution)/shard_map/ppermute | solution.py:55
  59.6 48.8 %pack.2 = (bf16[3,64,512]{2,1,0:T(8,128)(2,1)}, bf16[3,64,512]{2,1,0:T(8,128)(2,1)}, bf16[3,64,512]{2,1,0:T(8,128)(2,1)}, bf16[3,64,512]{2,1,0:T(8,128)(2,1)}, b...) custom-call(bf16[3,1,2,64,4096]{4,3,2,1,0:T(8,128)(2,1)} %source.3), custom_call_target="tpu_custom_call" | custom-call | tf_op jit(solution)/shard_map/pack/pallas_call | solution.py:79
  108.4 2.8 %collective-permute-start.19 = (bf16[3,64,512]{2,1,0:T(8,128)(2,1)S(1)}, bf16[3,64,512]{2,1,0:T(8,128)(2,1)S(1)}, u32[]{:S(2)}, u32[]{:S(2)}) collective-permute-start(bf16[3,64,512]{2,1,0:T(8,128)(2,1)S(1)} %copy-done.24), channel_id=1, source_target_pairs={{0,5},{1,4},{2,7},{3,6},{4,1},{5,0},{6,3},{7,2},{8,13},{9,12},{10,... | collective-permute-start | bytes 589832 | tf_op jit(solution)/shard_map/ppermute | solution.py:178
  111.7 2.1 collective-permute-start.21
  113.8 1.3 collective-permute-start.1
  115.2 14.0 %collective-permute-done.19.rest_5_ = bf16[3,64,512]{2,1,0:T(8,128)(2,1)S(1)} collective-permute-done((bf16[3,64,512]{2,1,0:T(8,128)(2,1)S(1)}, bf16[3,64,512]{2,1,0:T(8,128)(2,1)S(1)}, u32[]{:S(2)}, u32[]{:S(2)}) %collective-permute-start.19) | collective-permute-done | bytes 196640 | tf_op jit(solution)/shard_map/ppermute | solution.py:178
  129.2 5.9 %collective-permute-start.4 = (bf16[3,64,512]{2,1,0:T(8,128)(2,1)}, bf16[3,64,512]{2,1,0:T(8,128)(2,1)S(1)}, u32[]{:S(2)}, u32[]{:S(2)}) collective-permute-start(bf16[3,64,512]{2,1,0:T(8,128)(2,1)} %get-tuple-element.40), channel_id=1, source_target_pairs={{0,4},{1,5},{2,6},{3,7},{4,0},{5,1},{6,2},{7,3},{8,12},{9,13},{10,... | collective-permute-start | bytes 589832 | tf_op jit(solution)/shard_map/ppermute | solution.py:178
  135.1 6.7 %collective-permute-start.5 = (bf16[3,64,512]{2,1,0:T(8,128)(2,1)}, bf16[3,64,512]{2,1,0:T(8,128)(2,1)S(1)}, u32[]{:S(2)}, u32[]{:S(2)}) collective-permute-start(bf16[3,64,512]{2,1,0:T(8,128)(2,1)} %get-tuple-element.41), channel_id=1, source_target_pairs={{0,5},{1,4},{2,7},{3,6},{4,1},{5,0},{6,3},{7,2},{8,13},{9,12},{10,... | collective-permute-start | bytes 589832 | tf_op jit(solution)/shard_map/ppermute | solution.py:178
  141.8 2.8 %collective-permute-start.6 = (bf16[3,64,512]{2,1,0:T(8,128)(2,1)}, bf16[3,64,512]{2,1,0:T(8,128)(2,1)S(1)}, u32[]{:S(2)}, u32[]{:S(2)}) collective-permute-start(bf16[3,64,512]{2,1,0:T(8,128)(2,1)} %get-tuple-element.42), channel_id=1, source_target_pairs={{0,6},{1,7},{2,4},{3,5},{4,2},{5,3},{6,0},{7,1},{8,14},{9,15},{10,... | collective-permute-start | bytes 589832 | tf_op jit(solution)/shard_map/ppermute | solution.py:178
  144.9 3.9 %attend.3 = (bf16[64,512]{1,0:T(8,128)(2,1)S(1)}, bf16[64,512]{1,0:T(8,128)(2,1)S(1)}, bf16[64,512]{1,0:T(8,128)(2,1)S(1)}, bf16[64,512]{1,0:T(8,128)(2,1)S(1)},...) custom-call(bf16[4,512]{1,0:T(4,128)(2,1)S(1)} %dynamic-slice_add_fu, ...), custom_call_target="tpu_custom_call" | custom-call | flops 536870912 | bytes 2097152 | tf_op jit(solution)/shard_map/attend/pallas_call | solution.py:127
  148.9 0.6 copy-done
  149.5 0.9 collective-permute-start.22
  150.4 8.7 %collective-permute-done.4.rest_4_ = bf16[3,64,512]{2,1,0:T(8,128)(2,1)S(1)} collective-permute-done((bf16[3,64,512]{2,1,0:T(8,128)(2,1)}, bf16[3,64,512]{2,1,0:T(8,128)(2,1)S(1)}, u32[]{:S(2)}, u32[]{:S(2)}) %collective-permute-start.4) | collective-permute-done | bytes 196640 | tf_op jit(solution)/shard_map/ppermute | solution.py:178
  159.1 3.8 %collective-permute-done.5.rest_5_ = bf16[3,64,512]{2,1,0:T(8,128)(2,1)S(1)} collective-permute-done((bf16[3,64,512]{2,1,0:T(8,128)(2,1)}, bf16[3,64,512]{2,1,0:T(8,128)(2,1)S(1)}, u32[]{:S(2)}, u32[]{:S(2)}) %collective-permute-start.5) | collective-permute-done | bytes 196640 | tf_op jit(solution)/shard_map/ppermute | solution.py:178
  162.9 4.6 %collective-permute-start.25 = (bf16[64,512]{1,0:T(8,128)(2,1)S(1)}, bf16[64,512]{1,0:T(8,128)(2,1)S(1)}, u32[]{:S(2)}, u32[]{:S(2)}) collective-permute-start(bf16[64,512]{1,0:T(8,128)(2,1)S(1)} %get-tuple-element.64), channel_id=1, source_target_pairs={{0,4},{1,5},{2,6},{3,7},{4,0},{5,1},{6,2},{7,3},{8,12},{9,13},{10,... | collective-permute-start | bytes 196616 | tf_op jit(solution)/shard_map/ppermute | solution.py:178
  167.5 5.0 %collective-permute-start.26 = (bf16[64,512]{1,0:T(8,128)(2,1)S(1)}, bf16[64,512]{1,0:T(8,128)(2,1)S(1)}, u32[]{:S(2)}, u32[]{:S(2)}) collective-permute-start(bf16[64,512]{1,0:T(8,128)(2,1)S(1)} %get-tuple-element.65), channel_id=1, source_target_pairs={{0,5},{1,4},{2,7},{3,6},{4,1},{5,0},{6,3},{7,2},{8,13},{9,12},{10,... | collective-permute-start | bytes 196616 | tf_op jit(solution)/shard_map/ppermute | solution.py:178
  172.6 0.9 copy-done.2
  173.5 3.9 %attend.2 = (bf16[64,512]{1,0:T(8,128)(2,1)S(1)}, bf16[64,512]{1,0:T(8,128)(2,1)S(1)}, bf16[64,512]{1,0:T(8,128)(2,1)S(1)}, bf16[64,512]{1,0:T(8,128)(2,1)S(1)},...) custom-call(bf16[4,512]{1,0:T(4,128)(2,1)S(1)} %dynamic-slice_add_fu, ...), custom_call_target="tpu_custom_call" | custom-call | flops 536870912 | bytes 2097152 | tf_op jit(solution)/shard_map/attend/pallas_call | solution.py:127
  178.0 3.0 %collective-permute-start.27 = (bf16[64,512]{1,0:T(8,128)(2,1)S(1)}, bf16[64,512]{1,0:T(8,128)(2,1)S(1)}, u32[]{:S(2)}, u32[]{:S(2)}) collective-permute-start(bf16[64,512]{1,0:T(8,128)(2,1)S(1)} %get-tuple-element.66), channel_id=1, source_target_pairs={{0,6},{1,7},{2,4},{3,5},{4,2},{5,3},{6,0},{7,1},{8,14},{9,15},{10,... | collective-permute-start | bytes 196616 | tf_op jit(solution)/shard_map/ppermute | solution.py:178
  181.0 0.9 collective-permute-start.8
  182.0 1.4 collective-permute-start.10
  183.4 0.8 collective-permute-done.27.rest_14_
  184.2 1.4 collective-permute-start.11
  185.6 1.1 collective-permute-done.28.rest_15_
  186.8 2.6 %collective-permute-start.13 = (bf16[64,512]{1,0:T(8,128)(2,1)S(1)}, bf16[64,512]{1,0:T(8,128)(2,1)S(1)}, u32[]{:S(2)}, u32[]{:S(2)}) collective-permute-start(bf16[64,512]{1,0:T(8,128)(2,1)S(1)} %get-tuple-element.50), channel_id=1, source_target_pairs={{0,6},{1,7},{2,4},{3,5},{4,2},{5,3},{6,0},{7,1},{8,14},{9,15},{10,... | collective-permute-start | bytes 196616 | tf_op jit(solution)/shard_map/ppermute | solution.py:178
  189.5 0.9 collective-permute-start.14
  190.4 6.0 %collective-permute-done.12.rest_5_ = bf16[64,512]{1,0:T(8,128)(2,1)S(1)} collective-permute-done((bf16[64,512]{1,0:T(8,128)(2,1)S(1)}, bf16[64,512]{1,0:T(8,128)(2,1)S(1)}, u32[]{:S(2)}, u32[]{:S(2)}) %collective-permute-start.12) | collective-permute-done | bytes 65568 | tf_op jit(solution)/shard_map/ppermute | solution.py:178
  197.2 33.0 %unpack.1 = bf16[1,2,64,4096]{3,2,1,0:T(8,128)(2,1)} custom-call(bf16[64,512]{1,0:T(8,128)(2,1)} %copy-done.1, bf16[64,512]{1,0:T(8,128)(2,1)} %copy-done.11, bf16[64,512]{1,0:T(8,128)(2,1)} %copy-done.12, bf16[64,512]{1,0:T(8,128)(2,1)} %copy-done.13, bf16[64,512]{1,0:T(8,128)(2,1)} %copy-done.14, bf16[64,512]{1,0:T(8,128)(2,1)} %copy-done.15, ...), custom_call_target="tpu_custom_call" | custom-call | tf_op jit(solution)/shard_map/unpack/pallas_call | solution.py:163
  (83 shorter events, 2.9 us)
Async XLA Ops:
  49.5 61.7 %copy-start.23 = (bf16[3,64,512]{2,1,0:T(8,128)(2,1)S(1)}, bf16[3,64,512]{2,1,0:T(8,128)(2,1)}, u32[]{:S(2)}) copy-start(bf16[3,64,512]{2,1,0:T(8,128)(2,1)} %get-tuple-element.58) | copy-start | bytes 589828
  49.5 62.2 %copy-start.22 = (bf16[3,64,512]{2,1,0:T(8,128)(2,1)S(1)}, bf16[3,64,512]{2,1,0:T(8,128)(2,1)}, u32[]{:S(2)}) copy-start(bf16[3,64,512]{2,1,0:T(8,128)(2,1)} %get-tuple-element.59) | copy-start | bytes 589828
  49.5 95.4 %copy-start.3 = (bf16[3,64,512]{2,1,0:T(8,128)(2,1)S(1)}, bf16[3,64,512]{2,1,0:T(8,128)(2,1)}, u32[]{:S(2)}) copy-start(bf16[3,64,512]{2,1,0:T(8,128)(2,1)} %get-tuple-element.52.rest_0_) | copy-start | bytes 589828
  49.5 61.7 %collective-permute-start.15 = (bf16[3,64,512]{2,1,0:T(8,128)(2,1)}, bf16[3,64,512]{2,1,0:T(8,128)(2,1)S(1)}, u32[]{:S(2)}, u32[]{:S(2)}) collective-permute-start(bf16[3,64,512]{2,1,0:T(8,128)(2,1)} %get-tuple-element.53), channel_id=1, source_target_pairs={{0,1},{1,0},{2,3},{3,2},{4,5},{5,4},{6,7},{7,6},{8,9},{9,8},{10,11... | collective-permute-start | bytes 589832 | tf_op jit(solution)/shard_map/ppermute | solution.py:178
  50.1 61.7 %collective-permute-start.16 = (bf16[3,64,512]{2,1,0:T(8,128)(2,1)}, bf16[3,64,512]{2,1,0:T(8,128)(2,1)S(1)}, u32[]{:S(2)}, u32[]{:S(2)}) collective-permute-start(bf16[3,64,512]{2,1,0:T(8,128)(2,1)} %get-tuple-element.54), channel_id=1, source_target_pairs={{0,2},{1,3},{2,0},{3,1},{4,6},{5,7},{6,4},{7,5},{8,10},{9,11},{10,... | collective-permute-start | bytes 589832 | tf_op jit(solution)/shard_map/ppermute | solution.py:178
  52.7 61.1 %collective-permute-start.17 = (bf16[3,64,512]{2,1,0:T(8,128)(2,1)}, bf16[3,64,512]{2,1,0:T(8,128)(2,1)S(1)}, u32[]{:S(2)}, u32[]{:S(2)}) collective-permute-start(bf16[3,64,512]{2,1,0:T(8,128)(2,1)} %get-tuple-element.55), channel_id=1, source_target_pairs={{0,3},{1,2},{2,1},{3,0},{4,7},{5,6},{6,5},{7,4},{8,11},{9,10},{10,... | collective-permute-start | bytes 589832 | tf_op jit(solution)/shard_map/ppermute | solution.py:178
  52.8 62.4 %collective-permute-start.18 = (bf16[3,64,512]{2,1,0:T(8,128)(2,1)}, bf16[3,64,512]{2,1,0:T(8,128)(2,1)S(1)}, u32[]{:S(2)}, u32[]{:S(2)}) collective-permute-start(bf16[3,64,512]{2,1,0:T(8,128)(2,1)} %get-tuple-element.56), channel_id=1, source_target_pairs={{0,4},{1,5},{2,6},{3,7},{4,0},{5,1},{6,2},{7,3},{8,12},{9,13},{10,... | collective-permute-start | bytes 589832 | tf_op jit(solution)/shard_map/ppermute | solution.py:178
  56.2 52.2 %collective-permute-start = (bf16[4,1024]{1,0:T(4,128)(2,1)S(1)}, bf16[4,1024]{1,0:T(4,128)(2,1)S(1)}, u32[]{:S(2)}, u32[]{:S(2)}) collective-permute-start(bf16[4,1024]{1,0:T(4,128)(2,1)S(1)} %get-tuple-element.68), channel_id=1, source_target_pairs={{0,8},{1,16},{2,24},{3,9},{4,17},{5,25},{8,2},{9,18},{10,26},{11,3... | collective-permute-start | bytes 24584 | tf_op jit(solution)/shard_map/ppermute | solution.py:55
  108.4 20.7 %collective-permute-start.19 = (bf16[3,64,512]{2,1,0:T(8,128)(2,1)S(1)}, bf16[3,64,512]{2,1,0:T(8,128)(2,1)S(1)}, u32[]{:S(2)}, u32[]{:S(2)}) collective-permute-start(bf16[3,64,512]{2,1,0:T(8,128)(2,1)S(1)} %copy-done.24), channel_id=1, source_target_pairs={{0,5},{1,4},{2,7},{3,6},{4,1},{5,0},{6,3},{7,2},{8,13},{9,12},{10,... | collective-permute-start | bytes 589832 | tf_op jit(solution)/shard_map/ppermute | solution.py:178
  111.2 17.9 %collective-permute-start.20 = (bf16[3,64,512]{2,1,0:T(8,128)(2,1)S(1)}, bf16[3,64,512]{2,1,0:T(8,128)(2,1)S(1)}, u32[]{:S(2)}, u32[]{:S(2)}) collective-permute-start(bf16[3,64,512]{2,1,0:T(8,128)(2,1)S(1)} %copy-done.23), channel_id=1, source_target_pairs={{0,6},{1,7},{2,4},{3,5},{4,2},{5,3},{6,0},{7,1},{8,14},{9,15},{10,... | collective-permute-start | bytes 589832 | tf_op jit(solution)/shard_map/ppermute | solution.py:178
  111.7 23.4 %collective-permute-start.21 = (bf16[3,64,512]{2,1,0:T(8,128)(2,1)S(1)}, bf16[3,64,512]{2,1,0:T(8,128)(2,1)S(1)}, u32[]{:S(2)}, u32[]{:S(2)}) collective-permute-start(bf16[3,64,512]{2,1,0:T(8,128)(2,1)S(1)} %copy-done.22), channel_id=1, source_target_pairs={{0,7},{1,6},{2,5},{3,4},{4,3},{5,2},{6,1},{7,0},{8,15},{9,14},{10,... | collective-permute-start | bytes 589832 | tf_op jit(solution)/shard_map/ppermute | solution.py:178
  113.8 28.0 %collective-permute-start.1 = (bf16[3,64,512]{2,1,0:T(8,128)(2,1)}, bf16[3,64,512]{2,1,0:T(8,128)(2,1)S(1)}, u32[]{:S(2)}, u32[]{:S(2)}) collective-permute-start(bf16[3,64,512]{2,1,0:T(8,128)(2,1)} %get-tuple-element.37), channel_id=1, source_target_pairs={{0,1},{1,0},{2,3},{3,2},{4,5},{5,4},{6,7},{7,6},{8,9},{9,8},{10,11... | collective-permute-start | bytes 589832 | tf_op jit(solution)/shard_map/ppermute | solution.py:178
  115.2 29.4 %collective-permute-start.2 = (bf16[3,64,512]{2,1,0:T(8,128)(2,1)}, bf16[3,64,512]{2,1,0:T(8,128)(2,1)S(1)}, u32[]{:S(2)}, u32[]{:S(2)}) collective-permute-start(bf16[3,64,512]{2,1,0:T(8,128)(2,1)} %get-tuple-element.38), channel_id=1, source_target_pairs={{0,2},{1,3},{2,0},{3,1},{4,6},{5,7},{6,4},{7,5},{8,10},{9,11},{10,... | collective-permute-start | bytes 589832 | tf_op jit(solution)/shard_map/ppermute | solution.py:178
  129.2 20.3 %collective-permute-start.3 = (bf16[3,64,512]{2,1,0:T(8,128)(2,1)}, bf16[3,64,512]{2,1,0:T(8,128)(2,1)S(1)}, u32[]{:S(2)}, u32[]{:S(2)}) collective-permute-start(bf16[3,64,512]{2,1,0:T(8,128)(2,1)} %get-tuple-element.39), channel_id=1, source_target_pairs={{0,3},{1,2},{2,1},{3,0},{4,7},{5,6},{6,5},{7,4},{8,11},{9,10},{10,... | collective-permute-start | bytes 589832 | tf_op jit(solution)/shard_map/ppermute | solution.py:178
  129.2 29.9 %collective-permute-start.4 = (bf16[3,64,512]{2,1,0:T(8,128)(2,1)}, bf16[3,64,512]{2,1,0:T(8,128)(2,1)S(1)}, u32[]{:S(2)}, u32[]{:S(2)}) collective-permute-start(bf16[3,64,512]{2,1,0:T(8,128)(2,1)} %get-tuple-element.40), channel_id=1, source_target_pairs={{0,4},{1,5},{2,6},{3,7},{4,0},{5,1},{6,2},{7,3},{8,12},{9,13},{10,... | collective-permute-start | bytes 589832 | tf_op jit(solution)/shard_map/ppermute | solution.py:178
  135.1 27.8 %collective-permute-start.5 = (bf16[3,64,512]{2,1,0:T(8,128)(2,1)}, bf16[3,64,512]{2,1,0:T(8,128)(2,1)S(1)}, u32[]{:S(2)}, u32[]{:S(2)}) collective-permute-start(bf16[3,64,512]{2,1,0:T(8,128)(2,1)} %get-tuple-element.41), channel_id=1, source_target_pairs={{0,5},{1,4},{2,7},{3,6},{4,1},{5,0},{6,3},{7,2},{8,13},{9,12},{10,... | collective-permute-start | bytes 589832 | tf_op jit(solution)/shard_map/ppermute | solution.py:178
  141.8 21.1 %collective-permute-start.6 = (bf16[3,64,512]{2,1,0:T(8,128)(2,1)}, bf16[3,64,512]{2,1,0:T(8,128)(2,1)S(1)}, u32[]{:S(2)}, u32[]{:S(2)}) collective-permute-start(bf16[3,64,512]{2,1,0:T(8,128)(2,1)} %get-tuple-element.42), channel_id=1, source_target_pairs={{0,6},{1,7},{2,4},{3,5},{4,2},{5,3},{6,0},{7,1},{8,14},{9,15},{10,... | collective-permute-start | bytes 589832 | tf_op jit(solution)/shard_map/ppermute | solution.py:178
  144.6 22.9 %collective-permute-start.7 = (bf16[3,64,512]{2,1,0:T(8,128)(2,1)}, bf16[3,64,512]{2,1,0:T(8,128)(2,1)S(1)}, u32[]{:S(2)}, u32[]{:S(2)}) collective-permute-start(bf16[3,64,512]{2,1,0:T(8,128)(2,1)} %get-tuple-element.43), channel_id=1, source_target_pairs={{0,7},{1,6},{2,5},{3,4},{4,3},{5,2},{6,1},{7,0},{8,15},{9,14},{10,... | collective-permute-start | bytes 589832 | tf_op jit(solution)/shard_map/ppermute | solution.py:178
  149.5 28.5 %collective-permute-start.22 = (bf16[64,512]{1,0:T(8,128)(2,1)S(1)}, bf16[64,512]{1,0:T(8,128)(2,1)S(1)}, u32[]{:S(2)}, u32[]{:S(2)}) collective-permute-start(bf16[64,512]{1,0:T(8,128)(2,1)S(1)} %get-tuple-element.61), channel_id=1, source_target_pairs={{0,1},{1,0},{2,3},{3,2},{4,5},{5,4},{6,7},{7,6},{8,9},{9,8},{10,11... | collective-permute-start | bytes 196616 | tf_op jit(solution)/shard_map/ppermute | solution.py:178
  159.1 21.9 %collective-permute-start.23 = (bf16[64,512]{1,0:T(8,128)(2,1)S(1)}, bf16[64,512]{1,0:T(8,128)(2,1)S(1)}, u32[]{:S(2)}, u32[]{:S(2)}) collective-permute-start(bf16[64,512]{1,0:T(8,128)(2,1)S(1)} %get-tuple-element.62), channel_id=1, source_target_pairs={{0,2},{1,3},{2,0},{3,1},{4,6},{5,7},{6,4},{7,5},{8,10},{9,11},{10,... | collective-permute-start | bytes 196616 | tf_op jit(solution)/shard_map/ppermute | solution.py:178
  162.9 18.1 %collective-permute-start.24 = (bf16[64,512]{1,0:T(8,128)(2,1)S(1)}, bf16[64,512]{1,0:T(8,128)(2,1)S(1)}, u32[]{:S(2)}, u32[]{:S(2)}) collective-permute-start(bf16[64,512]{1,0:T(8,128)(2,1)S(1)} %get-tuple-element.63), channel_id=1, source_target_pairs={{0,3},{1,2},{2,1},{3,0},{4,7},{5,6},{6,5},{7,4},{8,11},{9,10},{10,... | collective-permute-start | bytes 196616 | tf_op jit(solution)/shard_map/ppermute | solution.py:178
  162.9 19.1 %collective-permute-start.25 = (bf16[64,512]{1,0:T(8,128)(2,1)S(1)}, bf16[64,512]{1,0:T(8,128)(2,1)S(1)}, u32[]{:S(2)}, u32[]{:S(2)}) collective-permute-start(bf16[64,512]{1,0:T(8,128)(2,1)S(1)} %get-tuple-element.64), channel_id=1, source_target_pairs={{0,4},{1,5},{2,6},{3,7},{4,0},{5,1},{6,2},{7,3},{8,12},{9,13},{10,... | collective-permute-start | bytes 196616 | tf_op jit(solution)/shard_map/ppermute | solution.py:178
  167.5 14.5 %collective-permute-start.26 = (bf16[64,512]{1,0:T(8,128)(2,1)S(1)}, bf16[64,512]{1,0:T(8,128)(2,1)S(1)}, u32[]{:S(2)}, u32[]{:S(2)}) collective-permute-start(bf16[64,512]{1,0:T(8,128)(2,1)S(1)} %get-tuple-element.65), channel_id=1, source_target_pairs={{0,5},{1,4},{2,7},{3,6},{4,1},{5,0},{6,3},{7,2},{8,13},{9,12},{10,... | collective-permute-start | bytes 196616 | tf_op jit(solution)/shard_map/ppermute | solution.py:178
  178.0 6.2 %collective-permute-start.27 = (bf16[64,512]{1,0:T(8,128)(2,1)S(1)}, bf16[64,512]{1,0:T(8,128)(2,1)S(1)}, u32[]{:S(2)}, u32[]{:S(2)}) collective-permute-start(bf16[64,512]{1,0:T(8,128)(2,1)S(1)} %get-tuple-element.66), channel_id=1, source_target_pairs={{0,6},{1,7},{2,4},{3,5},{4,2},{5,3},{6,0},{7,1},{8,14},{9,15},{10,... | collective-permute-start | bytes 196616 | tf_op jit(solution)/shard_map/ppermute | solution.py:178
  181.0 5.7 %collective-permute-start.28 = (bf16[64,512]{1,0:T(8,128)(2,1)S(1)}, bf16[64,512]{1,0:T(8,128)(2,1)S(1)}, u32[]{:S(2)}, u32[]{:S(2)}) collective-permute-start(bf16[64,512]{1,0:T(8,128)(2,1)S(1)} %get-tuple-element.67), channel_id=1, source_target_pairs={{0,7},{1,6},{2,5},{3,4},{4,3},{5,2},{6,1},{7,0},{8,15},{9,14},{10,... | collective-permute-start | bytes 196616 | tf_op jit(solution)/shard_map/ppermute | solution.py:178
  181.0 5.7 %collective-permute-start.8 = (bf16[64,512]{1,0:T(8,128)(2,1)S(1)}, bf16[64,512]{1,0:T(8,128)(2,1)S(1)}, u32[]{:S(2)}, u32[]{:S(2)}) collective-permute-start(bf16[64,512]{1,0:T(8,128)(2,1)S(1)} %get-tuple-element.45), channel_id=1, source_target_pairs={{0,1},{1,0},{2,3},{3,2},{4,5},{5,4},{6,7},{7,6},{8,9},{9,8},{10,11... | collective-permute-start | bytes 196616 | tf_op jit(solution)/shard_map/ppermute | solution.py:178
  182.0 7.5 %collective-permute-start.9 = (bf16[64,512]{1,0:T(8,128)(2,1)S(1)}, bf16[64,512]{1,0:T(8,128)(2,1)S(1)}, u32[]{:S(2)}, u32[]{:S(2)}) collective-permute-start(bf16[64,512]{1,0:T(8,128)(2,1)S(1)} %get-tuple-element.46), channel_id=1, source_target_pairs={{0,2},{1,3},{2,0},{3,1},{4,6},{5,7},{6,4},{7,5},{8,10},{9,11},{10,... | collective-permute-start | bytes 196616 | tf_op jit(solution)/shard_map/ppermute | solution.py:178
  182.0 8.4 %collective-permute-start.10 = (bf16[64,512]{1,0:T(8,128)(2,1)S(1)}, bf16[64,512]{1,0:T(8,128)(2,1)S(1)}, u32[]{:S(2)}, u32[]{:S(2)}) collective-permute-start(bf16[64,512]{1,0:T(8,128)(2,1)S(1)} %get-tuple-element.47), channel_id=1, source_target_pairs={{0,3},{1,2},{2,1},{3,0},{4,7},{5,6},{6,5},{7,4},{8,11},{9,10},{10,... | collective-permute-start | bytes 196616 | tf_op jit(solution)/shard_map/ppermute | solution.py:178
  184.2 6.2 %collective-permute-start.11 = (bf16[64,512]{1,0:T(8,128)(2,1)S(1)}, bf16[64,512]{1,0:T(8,128)(2,1)S(1)}, u32[]{:S(2)}, u32[]{:S(2)}) collective-permute-start(bf16[64,512]{1,0:T(8,128)(2,1)S(1)} %get-tuple-element.48), channel_id=1, source_target_pairs={{0,4},{1,5},{2,6},{3,7},{4,0},{5,1},{6,2},{7,3},{8,12},{9,13},{10,... | collective-permute-start | bytes 196616 | tf_op jit(solution)/shard_map/ppermute | solution.py:178
  186.7 9.7 %collective-permute-start.12 = (bf16[64,512]{1,0:T(8,128)(2,1)S(1)}, bf16[64,512]{1,0:T(8,128)(2,1)S(1)}, u32[]{:S(2)}, u32[]{:S(2)}) collective-permute-start(bf16[64,512]{1,0:T(8,128)(2,1)S(1)} %get-tuple-element.49), channel_id=1, source_target_pairs={{0,5},{1,4},{2,7},{3,6},{4,1},{5,0},{6,3},{7,2},{8,13},{9,12},{10,... | collective-permute-start | bytes 196616 | tf_op jit(solution)/shard_map/ppermute | solution.py:178
  186.8 9.7 %collective-permute-start.13 = (bf16[64,512]{1,0:T(8,128)(2,1)S(1)}, bf16[64,512]{1,0:T(8,128)(2,1)S(1)}, u32[]{:S(2)}, u32[]{:S(2)}) collective-permute-start(bf16[64,512]{1,0:T(8,128)(2,1)S(1)} %get-tuple-element.50), channel_id=1, source_target_pairs={{0,6},{1,7},{2,4},{3,5},{4,2},{5,3},{6,0},{7,1},{8,14},{9,15},{10,... | collective-permute-start | bytes 196616 | tf_op jit(solution)/shard_map/ppermute | solution.py:178
  189.5 7.0 %collective-permute-start.14 = (bf16[64,512]{1,0:T(8,128)(2,1)S(1)}, bf16[64,512]{1,0:T(8,128)(2,1)S(1)}, u32[]{:S(2)}, u32[]{:S(2)}) collective-permute-start(bf16[64,512]{1,0:T(8,128)(2,1)S(1)} %get-tuple-element.51), channel_id=1, source_target_pairs={{0,7},{1,6},{2,5},{3,4},{4,3},{5,2},{6,1},{7,0},{8,15},{9,14},{10,... | collective-permute-start | bytes 196616 | tf_op jit(solution)/shard_map/ppermute | solution.py:178
  (22 other events, 412.5 us)

commit v2 on v1

--- a/solution.py
+++ b/solution.py
@@ -80,7 +80,7 @@
         functools.partial(pack_kernel, sample, count, width),
         out_shape=[shape] * count,
         in_specs=[ANY],
-        out_specs=[ANY] * count,
+        out_specs=[VMEM] * count,
         scratch_shapes=[pltpu.SemaphoreType.DMA((count,))],
         name="pack",
     )(qkv)
@@ -163,7 +163,7 @@
     return pl.pallas_call(
         functools.partial(unpack_kernel, samples, count, width),
         out_shape=jax.ShapeDtypeStruct((1, samples, rows, width * count), parts[0].dtype),
-        in_specs=[ANY] * len(parts),
+        in_specs=[VMEM] * len(parts),
         out_specs=ANY,
         scratch_shapes=[pltpu.SemaphoreType.DMA((len(parts),))],
         name="unpack",

time: 231 us -> 114 us (0.49)
  Pallas kernels: 138 us -> 15.6 us
  starting transfers between devices: 52.6 us -> 73.7 us
  waiting for transfers between devices: 34.6 us -> 17.9 us
    pallas_call x2, Pallas kernels: 97.7 us -> 5.42 us  [pack(): pl.pallas_call(functools.partial(pack_kernel, sample, count, width), out_...]
    pallas_call x1, Pallas kernels: 33 us -> 2.32 us  [unpack(): pl.pallas_call(functools.partial(unpack_kernel, samples, count, width), o...]
    ppermute x28, starting transfers between devices: 49.2 us -> 70.3 us  [exchange(): landed[slot] = lax.ppermute(parts[slot], 'seq', pairs)]
    ppermute x28, waiting for transfers between devices: 34.6 us -> 17.9 us  [exchange(): landed[slot] = lax.ppermute(parts[slot], 'seq', pairs)]
  transfers between devices with their start and end apart: 29 -> 29, of which waited for: 7 -> 6; matrix products, arithmetic and copies ran while one was open for 0% -> 1% of each run, Pallas kernels for 25% -> 9%
where the time goes in v2:
time: 114 us; the launch traced here: 112 us
  starting transfers between devices  73.7 us (65%)
  waiting for transfers between devices  17.9 us (16%)
  Pallas kernels  15.6 us (14%)
  local copies, waits for them, and re-layouts  2.81 us (2%)
    ppermute x28, starting transfers between devices, exchange(): landed[slot] = lax.ppermute(parts[slot], 'seq', pairs)  70.3 us
    ppermute x28, waiting for transfers between devices, exchange(): landed[slot] = lax.ppermute(parts[slot], 'seq', pairs)  17.9 us
    pallas_call x2, Pallas kernels, attend(): pl.pallas_call(functools.partial(attend_kernel, count, 256), out_shape=[j...  7.83 us
    pallas_call x2, Pallas kernels, pack(): pl.pallas_call(functools.partial(pack_kernel, sample, count, width), out_...  5.42 us
    ppermute x1, starting transfers between devices, own_columns(): found = found + lax.ppermute(layer, ('dp', 'seq'), pairs)  3.38 us
    unnamed x50, local copies, waits for them, and re-layouts  2.81 us
    pallas_call x1, Pallas kernels, unpack(): pl.pallas_call(functools.partial(unpack_kernel, samples, count, width), o...  2.32 us
  transfers between devices with their start and end apart: 29, of which 6 were waited for; matrix products, arithmetic and copies ran while one was open for 1% of the time, Pallas kernels for 9%

profile of v2, /device:TPU:0, one launch (start us, length us, event | category | flops | bytes accessed | tf_op | source)
XLA Modules:
  0.0 111.6 jit_solution(15327668643790746626)
XLA Ops:
  0.7 2.7 %pack.3 = (bf16[3,64,512]{2,1,0:T(8,128)(2,1)}, bf16[3,64,512]{2,1,0:T(8,128)(2,1)}, bf16[3,64,512]{2,1,0:T(8,128)(2,1)}, bf16[3,64,512]{2,1,0:T(8,128)(2,1)}, b...) custom-call(bf16[3,1,2,64,4096]{4,3,2,1,0:T(8,128)(2,1)} %source.3), custom_call_target="tpu_custom_call" | custom-call | tf_op jit(solution)/shard_map/pack/pallas_call | solution.py:79
  4.0 2.6 %collective-permute-start.16 = (bf16[3,64,512]{2,1,0:T(8,128)(2,1)}, bf16[3,64,512]{2,1,0:T(8,128)(2,1)S(1)}, u32[]{:S(2)}, u32[]{:S(2)}) collective-permute-start(bf16[3,64,512]{2,1,0:T(8,128)(2,1)} %get-tuple-element.54), channel_id=1, source_target_pairs={{0,2},{1,3},{2,0},{3,1},{4,6},{5,7},{6,4},{7,5},{8,10},{9,11},{10,... | collective-permute-start | bytes 589832 | tf_op jit(solution)/shard_map/ppermute | solution.py:178
  6.7 2.7 %collective-permute-start.18 = (bf16[3,64,512]{2,1,0:T(8,128)(2,1)}, bf16[3,64,512]{2,1,0:T(8,128)(2,1)S(1)}, u32[]{:S(2)}, u32[]{:S(2)}) collective-permute-start(bf16[3,64,512]{2,1,0:T(8,128)(2,1)} %get-tuple-element.56), channel_id=1, source_target_pairs={{0,4},{1,5},{2,6},{3,7},{4,0},{5,1},{6,2},{7,3},{8,12},{9,13},{10,... | collective-permute-start | bytes 589832 | tf_op jit(solution)/shard_map/ppermute | solution.py:178
  9.5 0.6 fusion.1
  10.1 3.4 %collective-permute-start = (bf16[4,1024]{1,0:T(4,128)(2,1)S(1)}, bf16[4,1024]{1,0:T(4,128)(2,1)S(1)}, u32[]{:S(2)}, u32[]{:S(2)}) collective-permute-start(bf16[4,1024]{1,0:T(4,128)(2,1)S(1)} %get-tuple-element.68), channel_id=1, source_target_pairs={{0,8},{1,16},{2,24},{3,9},{4,17},{5,25},{8,2},{9,18},{10,26},{11,3... | collective-permute-start | bytes 24584 | tf_op jit(solution)/shard_map/ppermute | solution.py:55
  13.5 2.7 %pack.2 = (bf16[3,64,512]{2,1,0:T(8,128)(2,1)}, bf16[3,64,512]{2,1,0:T(8,128)(2,1)}, bf16[3,64,512]{2,1,0:T(8,128)(2,1)}, bf16[3,64,512]{2,1,0:T(8,128)(2,1)}, b...) custom-call(bf16[3,1,2,64,4096]{4,3,2,1,0:T(8,128)(2,1)} %source.3), custom_call_target="tpu_custom_call" | custom-call | tf_op jit(solution)/shard_map/pack/pallas_call | solution.py:79
  16.2 2.8 %collective-permute-start.19 = (bf16[3,64,512]{2,1,0:T(8,128)(2,1)S(1)}, bf16[3,64,512]{2,1,0:T(8,128)(2,1)S(1)}, u32[]{:S(2)}, u32[]{:S(2)}) collective-permute-start(bf16[3,64,512]{2,1,0:T(8,128)(2,1)S(1)} %copy-done.24), channel_id=1, source_target_pairs={{0,5},{1,4},{2,7},{3,6},{4,1},{5,0},{6,3},{7,2},{8,13},{9,12},{10,... | collective-permute-start | bytes 589832 | tf_op jit(solution)/shard_map/ppermute | solution.py:178
  19.0 7.7 %collective-permute-start.20 = (bf16[3,64,512]{2,1,0:T(8,128)(2,1)S(1)}, bf16[3,64,512]{2,1,0:T(8,128)(2,1)S(1)}, u32[]{:S(2)}, u32[]{:S(2)}) collective-permute-start(bf16[3,64,512]{2,1,0:T(8,128)(2,1)S(1)} %copy-done.23), channel_id=1, source_target_pairs={{0,6},{1,7},{2,4},{3,5},{4,2},{5,3},{6,0},{7,1},{8,14},{9,15},{10,... | collective-permute-start | bytes 589832 | tf_op jit(solution)/shard_map/ppermute | solution.py:178
  26.7 1.2 %collective-permute-start.21 = (bf16[3,64,512]{2,1,0:T(8,128)(2,1)S(1)}, bf16[3,64,512]{2,1,0:T(8,128)(2,1)S(1)}, u32[]{:S(2)}, u32[]{:S(2)}) collective-permute-start(bf16[3,64,512]{2,1,0:T(8,128)(2,1)S(1)} %copy-done.22), channel_id=1, source_target_pairs={{0,7},{1,6},{2,5},{3,4},{4,3},{5,2},{6,1},{7,0},{8,15},{9,14},{10,... | collective-permute-start | bytes 589832 | tf_op jit(solution)/shard_map/ppermute | solution.py:178
  27.9 0.8 collective-permute-start.2
  28.7 12.6 %collective-permute-start.3 = (bf16[3,64,512]{2,1,0:T(8,128)(2,1)}, bf16[3,64,512]{2,1,0:T(8,128)(2,1)S(1)}, u32[]{:S(2)}, u32[]{:S(2)}) collective-permute-start(bf16[3,64,512]{2,1,0:T(8,128)(2,1)} %get-tuple-element.39), channel_id=1, source_target_pairs={{0,3},{1,2},{2,1},{3,0},{4,7},{5,6},{6,5},{7,4},{8,11},{9,10},{10,... | collective-permute-start | bytes 589832 | tf_op jit(solution)/shard_map/ppermute | solution.py:178
  41.3 4.6 %collective-permute-start.4 = (bf16[3,64,512]{2,1,0:T(8,128)(2,1)}, bf16[3,64,512]{2,1,0:T(8,128)(2,1)S(1)}, u32[]{:S(2)}, u32[]{:S(2)}) collective-permute-start(bf16[3,64,512]{2,1,0:T(8,128)(2,1)} %get-tuple-element.40), channel_id=1, source_target_pairs={{0,4},{1,5},{2,6},{3,7},{4,0},{5,1},{6,2},{7,3},{8,12},{9,13},{10,... | collective-permute-start | bytes 589832 | tf_op jit(solution)/shard_map/ppermute | solution.py:178
  45.9 1.6 %collective-permute-start.5 = (bf16[3,64,512]{2,1,0:T(8,128)(2,1)}, bf16[3,64,512]{2,1,0:T(8,128)(2,1)S(1)}, u32[]{:S(2)}, u32[]{:S(2)}) collective-permute-start(bf16[3,64,512]{2,1,0:T(8,128)(2,1)} %get-tuple-element.41), channel_id=1, source_target_pairs={{0,5},{1,4},{2,7},{3,6},{4,1},{5,0},{6,3},{7,2},{8,13},{9,12},{10,... | collective-permute-start | bytes 589832 | tf_op jit(solution)/shard_map/ppermute | solution.py:178
  47.5 11.3 %collective-permute-start.6 = (bf16[3,64,512]{2,1,0:T(8,128)(2,1)}, bf16[3,64,512]{2,1,0:T(8,128)(2,1)S(1)}, u32[]{:S(2)}, u32[]{:S(2)}) collective-permute-start(bf16[3,64,512]{2,1,0:T(8,128)(2,1)} %get-tuple-element.42), channel_id=1, source_target_pairs={{0,6},{1,7},{2,4},{3,5},{4,2},{5,3},{6,0},{7,1},{8,14},{9,15},{10,... | collective-permute-start | bytes 589832 | tf_op jit(solution)/shard_map/ppermute | solution.py:178
  59.3 3.9 %attend.3 = (bf16[64,512]{1,0:T(8,128)(2,1)S(1)}, bf16[64,512]{1,0:T(8,128)(2,1)S(1)}, bf16[64,512]{1,0:T(8,128)(2,1)S(1)}, bf16[64,512]{1,0:T(8,128)(2,1)S(1)},...) custom-call(bf16[4,512]{1,0:T(4,128)(2,1)S(1)} %dynamic-slice_add_fu, ...), custom_call_target="tpu_custom_call" | custom-call | flops 536870912 | bytes 2097152 | tf_op jit(solution)/shard_map/attend/pallas_call | solution.py:127
  63.2 0.6 copy-done
  63.9 5.6 %collective-permute-done.4.rest_4_ = bf16[3,64,512]{2,1,0:T(8,128)(2,1)S(1)} collective-permute-done((bf16[3,64,512]{2,1,0:T(8,128)(2,1)}, bf16[3,64,512]{2,1,0:T(8,128)(2,1)S(1)}, u32[]{:S(2)}, u32[]{:S(2)}) %collective-permute-start.4) | collective-permute-done | bytes 196640 | tf_op jit(solution)/shard_map/ppermute | solution.py:178
  69.5 4.5 %collective-permute-done.5.rest_5_ = bf16[3,64,512]{2,1,0:T(8,128)(2,1)S(1)} collective-permute-done((bf16[3,64,512]{2,1,0:T(8,128)(2,1)}, bf16[3,64,512]{2,1,0:T(8,128)(2,1)S(1)}, u32[]{:S(2)}, u32[]{:S(2)}) %collective-permute-start.5) | collective-permute-done | bytes 196640 | tf_op jit(solution)/shard_map/ppermute | solution.py:178
  74.0 5.7 %collective-permute-start.25 = (bf16[64,512]{1,0:T(8,128)(2,1)S(1)}, bf16[64,512]{1,0:T(8,128)(2,1)S(1)}, u32[]{:S(2)}, u32[]{:S(2)}) collective-permute-start(bf16[64,512]{1,0:T(8,128)(2,1)S(1)} %get-tuple-element.64), channel_id=1, source_target_pairs={{0,4},{1,5},{2,6},{3,7},{4,0},{5,1},{6,2},{7,3},{8,12},{9,13},{10,... | collective-permute-start | bytes 196616 | tf_op jit(solution)/shard_map/ppermute | solution.py:178
  79.7 5.0 %collective-permute-start.26 = (bf16[64,512]{1,0:T(8,128)(2,1)S(1)}, bf16[64,512]{1,0:T(8,128)(2,1)S(1)}, u32[]{:S(2)}, u32[]{:S(2)}) collective-permute-start(bf16[64,512]{1,0:T(8,128)(2,1)S(1)} %get-tuple-element.65), channel_id=1, source_target_pairs={{0,5},{1,4},{2,7},{3,6},{4,1},{5,0},{6,3},{7,2},{8,13},{9,12},{10,... | collective-permute-start | bytes 196616 | tf_op jit(solution)/shard_map/ppermute | solution.py:178
  84.8 0.9 copy-done.2
  85.7 3.9 %attend.2 = (bf16[64,512]{1,0:T(8,128)(2,1)S(1)}, bf16[64,512]{1,0:T(8,128)(2,1)S(1)}, bf16[64,512]{1,0:T(8,128)(2,1)S(1)}, bf16[64,512]{1,0:T(8,128)(2,1)S(1)},...) custom-call(bf16[4,512]{1,0:T(4,128)(2,1)S(1)} %dynamic-slice_add_fu, ...), custom_call_target="tpu_custom_call" | custom-call | flops 536870912 | bytes 2097152 | tf_op jit(solution)/shard_map/attend/pallas_call | solution.py:127
  90.2 2.8 %collective-permute-start.27 = (bf16[64,512]{1,0:T(8,128)(2,1)S(1)}, bf16[64,512]{1,0:T(8,128)(2,1)S(1)}, u32[]{:S(2)}, u32[]{:S(2)}) collective-permute-start(bf16[64,512]{1,0:T(8,128)(2,1)S(1)} %get-tuple-element.66), channel_id=1, source_target_pairs={{0,6},{1,7},{2,4},{3,5},{4,2},{5,3},{6,0},{7,1},{8,14},{9,15},{10,... | collective-permute-start | bytes 196616 | tf_op jit(solution)/shard_map/ppermute | solution.py:178
  93.1 1.1 collective-permute-start.8
  94.2 1.4 %collective-permute-start.10 = (bf16[64,512]{1,0:T(8,128)(2,1)S(1)}, bf16[64,512]{1,0:T(8,128)(2,1)S(1)}, u32[]{:S(2)}, u32[]{:S(2)}) collective-permute-start(bf16[64,512]{1,0:T(8,128)(2,1)S(1)} %get-tuple-element.47), channel_id=1, source_target_pairs={{0,3},{1,2},{2,1},{3,0},{4,7},{5,6},{6,5},{7,4},{8,11},{9,10},{10,... | collective-permute-start | bytes 196616 | tf_op jit(solution)/shard_map/ppermute | solution.py:178
  95.6 0.8 collective-permute-done.27.rest_14_
  96.4 1.3 %collective-permute-start.11 = (bf16[64,512]{1,0:T(8,128)(2,1)S(1)}, bf16[64,512]{1,0:T(8,128)(2,1)S(1)}, u32[]{:S(2)}, u32[]{:S(2)}) collective-permute-start(bf16[64,512]{1,0:T(8,128)(2,1)S(1)} %get-tuple-element.48), channel_id=1, source_target_pairs={{0,4},{1,5},{2,6},{3,7},{4,0},{5,1},{6,2},{7,3},{8,12},{9,13},{10,... | collective-permute-start | bytes 196616 | tf_op jit(solution)/shard_map/ppermute | solution.py:178
  97.7 1.0 collective-permute-done.28.rest_15_
  98.7 2.7 %collective-permute-start.13 = (bf16[64,512]{1,0:T(8,128)(2,1)S(1)}, bf16[64,512]{1,0:T(8,128)(2,1)S(1)}, u32[]{:S(2)}, u32[]{:S(2)}) collective-permute-start(bf16[64,512]{1,0:T(8,128)(2,1)S(1)} %get-tuple-element.50), channel_id=1, source_target_pairs={{0,6},{1,7},{2,4},{3,5},{4,2},{5,3},{6,0},{7,1},{8,14},{9,15},{10,... | collective-permute-start | bytes 196616 | tf_op jit(solution)/shard_map/ppermute | solution.py:178
  101.4 1.2 %collective-permute-start.14 = (bf16[64,512]{1,0:T(8,128)(2,1)S(1)}, bf16[64,512]{1,0:T(8,128)(2,1)S(1)}, u32[]{:S(2)}, u32[]{:S(2)}) collective-permute-start(bf16[64,512]{1,0:T(8,128)(2,1)S(1)} %get-tuple-element.51), channel_id=1, source_target_pairs={{0,7},{1,6},{2,5},{3,4},{4,3},{5,2},{6,1},{7,0},{8,15},{9,14},{10,... | collective-permute-start | bytes 196616 | tf_op jit(solution)/shard_map/ppermute | solution.py:178
  103.0 5.6 %collective-permute-done.12.rest_5_ = bf16[64,512]{1,0:T(8,128)(2,1)S(1)} collective-permute-done((bf16[64,512]{1,0:T(8,128)(2,1)S(1)}, bf16[64,512]{1,0:T(8,128)(2,1)S(1)}, u32[]{:S(2)}, u32[]{:S(2)}) %collective-permute-start.12) | collective-permute-done | bytes 65568 | tf_op jit(solution)/shard_map/ppermute | solution.py:178
  109.3 2.3 %unpack.1 = bf16[1,2,64,4096]{3,2,1,0:T(8,128)(2,1)} custom-call(bf16[64,512]{1,0:T(8,128)(2,1)} %copy-done.1, bf16[64,512]{1,0:T(8,128)(2,1)} %copy-done.11, bf16[64,512]{1,0:T(8,128)(2,1)} %copy-done.12, bf16[64,512]{1,0:T(8,128)(2,1)} %copy-done.13, bf16[64,512]{1,0:T(8,128)(2,1)} %copy-done.14, bf16[64,512]{1,0:T(8,128)(2,1)} %copy-done.15, ...), custom_call_target="tpu_custom_call" | custom-call | tf_op jit(solution)/shard_map/unpack/pallas_call | solution.py:163
  (83 shorter events, 2.7 us)
Async XLA Ops:
  3.4 23.2 %copy-start.22 = (bf16[3,64,512]{2,1,0:T(8,128)(2,1)S(1)}, bf16[3,64,512]{2,1,0:T(8,128)(2,1)}, u32[]{:S(2)}) copy-start(bf16[3,64,512]{2,1,0:T(8,128)(2,1)} %get-tuple-element.59) | copy-start | bytes 589828
  3.5 55.8 %copy-start.3 = (bf16[3,64,512]{2,1,0:T(8,128)(2,1)S(1)}, bf16[3,64,512]{2,1,0:T(8,128)(2,1)}, u32[]{:S(2)}) copy-start(bf16[3,64,512]{2,1,0:T(8,128)(2,1)} %get-tuple-element.52.rest_0_) | copy-start | bytes 589828
  3.5 15.5 %collective-permute-start.15 = (bf16[3,64,512]{2,1,0:T(8,128)(2,1)}, bf16[3,64,512]{2,1,0:T(8,128)(2,1)S(1)}, u32[]{:S(2)}, u32[]{:S(2)}) collective-permute-start(bf16[3,64,512]{2,1,0:T(8,128)(2,1)} %get-tuple-element.53), channel_id=1, source_target_pairs={{0,1},{1,0},{2,3},{3,2},{4,5},{5,4},{6,7},{7,6},{8,9},{9,8},{10,11... | collective-permute-start | bytes 589832 | tf_op jit(solution)/shard_map/ppermute | solution.py:178
  4.0 22.7 %collective-permute-start.16 = (bf16[3,64,512]{2,1,0:T(8,128)(2,1)}, bf16[3,64,512]{2,1,0:T(8,128)(2,1)S(1)}, u32[]{:S(2)}, u32[]{:S(2)}) collective-permute-start(bf16[3,64,512]{2,1,0:T(8,128)(2,1)} %get-tuple-element.54), channel_id=1, source_target_pairs={{0,2},{1,3},{2,0},{3,1},{4,6},{5,7},{6,4},{7,5},{8,10},{9,11},{10,... | collective-permute-start | bytes 589832 | tf_op jit(solution)/shard_map/ppermute | solution.py:178
  6.6 21.3 %collective-permute-start.17 = (bf16[3,64,512]{2,1,0:T(8,128)(2,1)}, bf16[3,64,512]{2,1,0:T(8,128)(2,1)S(1)}, u32[]{:S(2)}, u32[]{:S(2)}) collective-permute-start(bf16[3,64,512]{2,1,0:T(8,128)(2,1)} %get-tuple-element.55), channel_id=1, source_target_pairs={{0,3},{1,2},{2,1},{3,0},{4,7},{5,6},{6,5},{7,4},{8,11},{9,10},{10,... | collective-permute-start | bytes 589832 | tf_op jit(solution)/shard_map/ppermute | solution.py:178
  6.7 21.2 %collective-permute-start.18 = (bf16[3,64,512]{2,1,0:T(8,128)(2,1)}, bf16[3,64,512]{2,1,0:T(8,128)(2,1)S(1)}, u32[]{:S(2)}, u32[]{:S(2)}) collective-permute-start(bf16[3,64,512]{2,1,0:T(8,128)(2,1)} %get-tuple-element.56), channel_id=1, source_target_pairs={{0,4},{1,5},{2,6},{3,7},{4,0},{5,1},{6,2},{7,3},{8,12},{9,13},{10,... | collective-permute-start | bytes 589832 | tf_op jit(solution)/shard_map/ppermute | solution.py:178
  10.1 6.1 %collective-permute-start = (bf16[4,1024]{1,0:T(4,128)(2,1)S(1)}, bf16[4,1024]{1,0:T(4,128)(2,1)S(1)}, u32[]{:S(2)}, u32[]{:S(2)}) collective-permute-start(bf16[4,1024]{1,0:T(4,128)(2,1)S(1)} %get-tuple-element.68), channel_id=1, source_target_pairs={{0,8},{1,16},{2,24},{3,9},{4,17},{5,25},{8,2},{9,18},{10,26},{11,3... | collective-permute-start | bytes 24584 | tf_op jit(solution)/shard_map/ppermute | solution.py:55
  16.2 12.5 %collective-permute-start.19 = (bf16[3,64,512]{2,1,0:T(8,128)(2,1)S(1)}, bf16[3,64,512]{2,1,0:T(8,128)(2,1)S(1)}, u32[]{:S(2)}, u32[]{:S(2)}) collective-permute-start(bf16[3,64,512]{2,1,0:T(8,128)(2,1)S(1)} %copy-done.24), channel_id=1, source_target_pairs={{0,5},{1,4},{2,7},{3,6},{4,1},{5,0},{6,3},{7,2},{8,13},{9,12},{10,... | collective-permute-start | bytes 589832 | tf_op jit(solution)/shard_map/ppermute | solution.py:178
  19.0 22.3 %collective-permute-start.20 = (bf16[3,64,512]{2,1,0:T(8,128)(2,1)S(1)}, bf16[3,64,512]{2,1,0:T(8,128)(2,1)S(1)}, u32[]{:S(2)}, u32[]{:S(2)}) collective-permute-start(bf16[3,64,512]{2,1,0:T(8,128)(2,1)S(1)} %copy-done.23), channel_id=1, source_target_pairs={{0,6},{1,7},{2,4},{3,5},{4,2},{5,3},{6,0},{7,1},{8,14},{9,15},{10,... | collective-permute-start | bytes 589832 | tf_op jit(solution)/shard_map/ppermute | solution.py:178
  26.7 19.2 %collective-permute-start.21 = (bf16[3,64,512]{2,1,0:T(8,128)(2,1)S(1)}, bf16[3,64,512]{2,1,0:T(8,128)(2,1)S(1)}, u32[]{:S(2)}, u32[]{:S(2)}) collective-permute-start(bf16[3,64,512]{2,1,0:T(8,128)(2,1)S(1)} %copy-done.22), channel_id=1, source_target_pairs={{0,7},{1,6},{2,5},{3,4},{4,3},{5,2},{6,1},{7,0},{8,15},{9,14},{10,... | collective-permute-start | bytes 589832 | tf_op jit(solution)/shard_map/ppermute | solution.py:178
  27.9 19.6 %collective-permute-start.1 = (bf16[3,64,512]{2,1,0:T(8,128)(2,1)}, bf16[3,64,512]{2,1,0:T(8,128)(2,1)S(1)}, u32[]{:S(2)}, u32[]{:S(2)}) collective-permute-start(bf16[3,64,512]{2,1,0:T(8,128)(2,1)} %get-tuple-element.37), channel_id=1, source_target_pairs={{0,1},{1,0},{2,3},{3,2},{4,5},{5,4},{6,7},{7,6},{8,9},{9,8},{10,11... | collective-permute-start | bytes 589832 | tf_op jit(solution)/shard_map/ppermute | solution.py:178
  27.9 30.9 %collective-permute-start.2 = (bf16[3,64,512]{2,1,0:T(8,128)(2,1)}, bf16[3,64,512]{2,1,0:T(8,128)(2,1)S(1)}, u32[]{:S(2)}, u32[]{:S(2)}) collective-permute-start(bf16[3,64,512]{2,1,0:T(8,128)(2,1)} %get-tuple-element.38), channel_id=1, source_target_pairs={{0,2},{1,3},{2,0},{3,1},{4,6},{5,7},{6,4},{7,5},{8,10},{9,11},{10,... | collective-permute-start | bytes 589832 | tf_op jit(solution)/shard_map/ppermute | solution.py:178
  28.7 35.1 %collective-permute-start.3 = (bf16[3,64,512]{2,1,0:T(8,128)(2,1)}, bf16[3,64,512]{2,1,0:T(8,128)(2,1)S(1)}, u32[]{:S(2)}, u32[]{:S(2)}) collective-permute-start(bf16[3,64,512]{2,1,0:T(8,128)(2,1)} %get-tuple-element.39), channel_id=1, source_target_pairs={{0,3},{1,2},{2,1},{3,0},{4,7},{5,6},{6,5},{7,4},{8,11},{9,10},{10,... | collective-permute-start | bytes 589832 | tf_op jit(solution)/shard_map/ppermute | solution.py:178
  41.3 28.2 %collective-permute-start.4 = (bf16[3,64,512]{2,1,0:T(8,128)(2,1)}, bf16[3,64,512]{2,1,0:T(8,128)(2,1)S(1)}, u32[]{:S(2)}, u32[]{:S(2)}) collective-permute-start(bf16[3,64,512]{2,1,0:T(8,128)(2,1)} %get-tuple-element.40), channel_id=1, source_target_pairs={{0,4},{1,5},{2,6},{3,7},{4,0},{5,1},{6,2},{7,3},{8,12},{9,13},{10,... | collective-permute-start | bytes 589832 | tf_op jit(solution)/shard_map/ppermute | solution.py:178
  45.9 28.1 %collective-permute-start.5 = (bf16[3,64,512]{2,1,0:T(8,128)(2,1)}, bf16[3,64,512]{2,1,0:T(8,128)(2,1)S(1)}, u32[]{:S(2)}, u32[]{:S(2)}) collective-permute-start(bf16[3,64,512]{2,1,0:T(8,128)(2,1)} %get-tuple-element.41), channel_id=1, source_target_pairs={{0,5},{1,4},{2,7},{3,6},{4,1},{5,0},{6,3},{7,2},{8,13},{9,12},{10,... | collective-permute-start | bytes 589832 | tf_op jit(solution)/shard_map/ppermute | solution.py:178
  47.5 26.5 %collective-permute-start.6 = (bf16[3,64,512]{2,1,0:T(8,128)(2,1)}, bf16[3,64,512]{2,1,0:T(8,128)(2,1)S(1)}, u32[]{:S(2)}, u32[]{:S(2)}) collective-permute-start(bf16[3,64,512]{2,1,0:T(8,128)(2,1)} %get-tuple-element.42), channel_id=1, source_target_pairs={{0,6},{1,7},{2,4},{3,5},{4,2},{5,3},{6,0},{7,1},{8,14},{9,15},{10,... | collective-permute-start | bytes 589832 | tf_op jit(solution)/shard_map/ppermute | solution.py:178
  58.8 20.9 %collective-permute-start.7 = (bf16[3,64,512]{2,1,0:T(8,128)(2,1)}, bf16[3,64,512]{2,1,0:T(8,128)(2,1)S(1)}, u32[]{:S(2)}, u32[]{:S(2)}) collective-permute-start(bf16[3,64,512]{2,1,0:T(8,128)(2,1)} %get-tuple-element.43), channel_id=1, source_target_pairs={{0,7},{1,6},{2,5},{3,4},{4,3},{5,2},{6,1},{7,0},{8,15},{9,14},{10,... | collective-permute-start | bytes 589832 | tf_op jit(solution)/shard_map/ppermute | solution.py:178
  63.9 26.4 %collective-permute-start.22 = (bf16[64,512]{1,0:T(8,128)(2,1)S(1)}, bf16[64,512]{1,0:T(8,128)(2,1)S(1)}, u32[]{:S(2)}, u32[]{:S(2)}) collective-permute-start(bf16[64,512]{1,0:T(8,128)(2,1)S(1)} %get-tuple-element.61), channel_id=1, source_target_pairs={{0,1},{1,0},{2,3},{3,2},{4,5},{5,4},{6,7},{7,6},{8,9},{9,8},{10,11... | collective-permute-start | bytes 196616 | tf_op jit(solution)/shard_map/ppermute | solution.py:178
  69.5 23.6 %collective-permute-start.23 = (bf16[64,512]{1,0:T(8,128)(2,1)S(1)}, bf16[64,512]{1,0:T(8,128)(2,1)S(1)}, u32[]{:S(2)}, u32[]{:S(2)}) collective-permute-start(bf16[64,512]{1,0:T(8,128)(2,1)S(1)} %get-tuple-element.62), channel_id=1, source_target_pairs={{0,2},{1,3},{2,0},{3,1},{4,6},{5,7},{6,4},{7,5},{8,10},{9,11},{10,... | collective-permute-start | bytes 196616 | tf_op jit(solution)/shard_map/ppermute | solution.py:178
  74.0 19.1 %collective-permute-start.24 = (bf16[64,512]{1,0:T(8,128)(2,1)S(1)}, bf16[64,512]{1,0:T(8,128)(2,1)S(1)}, u32[]{:S(2)}, u32[]{:S(2)}) collective-permute-start(bf16[64,512]{1,0:T(8,128)(2,1)S(1)} %get-tuple-element.63), channel_id=1, source_target_pairs={{0,3},{1,2},{2,1},{3,0},{4,7},{5,6},{6,5},{7,4},{8,11},{9,10},{10,... | collective-permute-start | bytes 196616 | tf_op jit(solution)/shard_map/ppermute | solution.py:178
  74.0 20.2 %collective-permute-start.25 = (bf16[64,512]{1,0:T(8,128)(2,1)S(1)}, bf16[64,512]{1,0:T(8,128)(2,1)S(1)}, u32[]{:S(2)}, u32[]{:S(2)}) collective-permute-start(bf16[64,512]{1,0:T(8,128)(2,1)S(1)} %get-tuple-element.64), channel_id=1, source_target_pairs={{0,4},{1,5},{2,6},{3,7},{4,0},{5,1},{6,2},{7,3},{8,12},{9,13},{10,... | collective-permute-start | bytes 196616 | tf_op jit(solution)/shard_map/ppermute | solution.py:178
  79.7 14.5 %collective-permute-start.26 = (bf16[64,512]{1,0:T(8,128)(2,1)S(1)}, bf16[64,512]{1,0:T(8,128)(2,1)S(1)}, u32[]{:S(2)}, u32[]{:S(2)}) collective-permute-start(bf16[64,512]{1,0:T(8,128)(2,1)S(1)} %get-tuple-element.65), channel_id=1, source_target_pairs={{0,5},{1,4},{2,7},{3,6},{4,1},{5,0},{6,3},{7,2},{8,13},{9,12},{10,... | collective-permute-start | bytes 196616 | tf_op jit(solution)/shard_map/ppermute | solution.py:178
  90.2 18.4 %copy-start.4 = (bf16[64,512]{1,0:T(8,128)(2,1)}, bf16[64,512]{1,0:T(8,128)(2,1)S(1)}, u32[]{:S(2)}) copy-start(bf16[64,512]{1,0:T(8,128)(2,1)S(1)} %collective-permute-done.22.rest_9_) | copy-start | bytes 196612
  90.2 6.2 %collective-permute-start.27 = (bf16[64,512]{1,0:T(8,128)(2,1)S(1)}, bf16[64,512]{1,0:T(8,128)(2,1)S(1)}, u32[]{:S(2)}, u32[]{:S(2)}) collective-permute-start(bf16[64,512]{1,0:T(8,128)(2,1)S(1)} %get-tuple-element.66), channel_id=1, source_target_pairs={{0,6},{1,7},{2,4},{3,5},{4,2},{5,3},{6,0},{7,1},{8,14},{9,15},{10,... | collective-permute-start | bytes 196616 | tf_op jit(solution)/shard_map/ppermute | solution.py:178
  93.1 5.6 %collective-permute-start.28 = (bf16[64,512]{1,0:T(8,128)(2,1)S(1)}, bf16[64,512]{1,0:T(8,128)(2,1)S(1)}, u32[]{:S(2)}, u32[]{:S(2)}) collective-permute-start(bf16[64,512]{1,0:T(8,128)(2,1)S(1)} %get-tuple-element.67), channel_id=1, source_target_pairs={{0,7},{1,6},{2,5},{3,4},{4,3},{5,2},{6,1},{7,0},{8,15},{9,14},{10,... | collective-permute-start | bytes 196616 | tf_op jit(solution)/shard_map/ppermute | solution.py:178
  93.1 5.6 %collective-permute-start.8 = (bf16[64,512]{1,0:T(8,128)(2,1)S(1)}, bf16[64,512]{1,0:T(8,128)(2,1)S(1)}, u32[]{:S(2)}, u32[]{:S(2)}) collective-permute-start(bf16[64,512]{1,0:T(8,128)(2,1)S(1)} %get-tuple-element.45), channel_id=1, source_target_pairs={{0,1},{1,0},{2,3},{3,2},{4,5},{5,4},{6,7},{7,6},{8,9},{9,8},{10,11... | collective-permute-start | bytes 196616 | tf_op jit(solution)/shard_map/ppermute | solution.py:178
  94.2 7.3 %collective-permute-start.9 = (bf16[64,512]{1,0:T(8,128)(2,1)S(1)}, bf16[64,512]{1,0:T(8,128)(2,1)S(1)}, u32[]{:S(2)}, u32[]{:S(2)}) collective-permute-start(bf16[64,512]{1,0:T(8,128)(2,1)S(1)} %get-tuple-element.46), channel_id=1, source_target_pairs={{0,2},{1,3},{2,0},{3,1},{4,6},{5,7},{6,4},{7,5},{8,10},{9,11},{10,... | collective-permute-start | bytes 196616 | tf_op jit(solution)/shard_map/ppermute | solution.py:178
  94.2 8.4 %collective-permute-start.10 = (bf16[64,512]{1,0:T(8,128)(2,1)S(1)}, bf16[64,512]{1,0:T(8,128)(2,1)S(1)}, u32[]{:S(2)}, u32[]{:S(2)}) collective-permute-start(bf16[64,512]{1,0:T(8,128)(2,1)S(1)} %get-tuple-element.47), channel_id=1, source_target_pairs={{0,3},{1,2},{2,1},{3,0},{4,7},{5,6},{6,5},{7,4},{8,11},{9,10},{10,... | collective-permute-start | bytes 196616 | tf_op jit(solution)/shard_map/ppermute | solution.py:178
  96.4 6.6 %collective-permute-start.11 = (bf16[64,512]{1,0:T(8,128)(2,1)S(1)}, bf16[64,512]{1,0:T(8,128)(2,1)S(1)}, u32[]{:S(2)}, u32[]{:S(2)}) collective-permute-start(bf16[64,512]{1,0:T(8,128)(2,1)S(1)} %get-tuple-element.48), channel_id=1, source_target_pairs={{0,4},{1,5},{2,6},{3,7},{4,0},{5,1},{6,2},{7,3},{8,12},{9,13},{10,... | collective-permute-start | bytes 196616 | tf_op jit(solution)/shard_map/ppermute | solution.py:178
  98.7 9.9 %collective-permute-start.12 = (bf16[64,512]{1,0:T(8,128)(2,1)S(1)}, bf16[64,512]{1,0:T(8,128)(2,1)S(1)}, u32[]{:S(2)}, u32[]{:S(2)}) collective-permute-start(bf16[64,512]{1,0:T(8,128)(2,1)S(1)} %get-tuple-element.49), channel_id=1, source_target_pairs={{0,5},{1,4},{2,7},{3,6},{4,1},{5,0},{6,3},{7,2},{8,13},{9,12},{10,... | collective-permute-start | bytes 196616 | tf_op jit(solution)/shard_map/ppermute | solution.py:178
  98.7 9.9 %collective-permute-start.13 = (bf16[64,512]{1,0:T(8,128)(2,1)S(1)}, bf16[64,512]{1,0:T(8,128)(2,1)S(1)}, u32[]{:S(2)}, u32[]{:S(2)}) collective-permute-start(bf16[64,512]{1,0:T(8,128)(2,1)S(1)} %get-tuple-element.50), channel_id=1, source_target_pairs={{0,6},{1,7},{2,4},{3,5},{4,2},{5,3},{6,0},{7,1},{8,14},{9,15},{10,... | collective-permute-start | bytes 196616 | tf_op jit(solution)/shard_map/ppermute | solution.py:178
  101.4 7.2 %collective-permute-start.14 = (bf16[64,512]{1,0:T(8,128)(2,1)S(1)}, bf16[64,512]{1,0:T(8,128)(2,1)S(1)}, u32[]{:S(2)}, u32[]{:S(2)}) collective-permute-start(bf16[64,512]{1,0:T(8,128)(2,1)S(1)} %get-tuple-element.51), channel_id=1, source_target_pairs={{0,7},{1,6},{2,5},{3,4},{4,3},{5,2},{6,1},{7,0},{8,15},{9,14},{10,... | collective-permute-start | bytes 196616 | tf_op jit(solution)/shard_map/ppermute | solution.py:178
  (22 other events, 179.1 us)

commit v3 on v2

--- a/solution.py
+++ b/solution.py
@@ -56,15 +56,15 @@
     return lax.dynamic_slice_in_dim(found, first_col % shard_cols, width, 1)
 
 
-def pack_kernel(sample, count, width, source, *rest):
-    outs, sems = rest[:count], rest[count]
+def pack_kernel(sample, slots, width, source, *rest):
+    outs, sems = rest[:-1], rest[-1]
     me = lax.axis_index("seq")
     copies = []
-    for slot in range(count):
+    for place, slot in enumerate(slots):
         first = pl.multiple_of(lax.bitwise_xor(me, slot) * width, width)
         copies.append(
             pltpu.make_async_copy(
-                source.at[:, 0, sample, :, pl.ds(first, width)], outs[slot], sems.at[slot]
+                source.at[:, 0, sample, :, pl.ds(first, width)], outs[place], sems.at[place]
             )
         )
     for copy in copies:
@@ -73,11 +73,12 @@
         copy.wait()
 
 
-def pack(qkv, sample, count, width):
+def pack(qkv, sample, slots, width):
     rows = qkv.shape[3]
+    count = len(slots)
     shape = jax.ShapeDtypeStruct((3, rows, width), qkv.dtype)
     return pl.pallas_call(
-        functools.partial(pack_kernel, sample, count, width),
+        functools.partial(pack_kernel, sample, slots, width),
         out_shape=[shape] * count,
         in_specs=[ANY],
         out_specs=[VMEM] * count,
@@ -139,14 +140,14 @@
     )(layer, *arrived)
 
 
-def unpack_kernel(samples, count, width, *rest):
-    parts, out, sems = rest[: samples * count], rest[samples * count], rest[samples * count + 1]
+def unpack_kernel(samples, slots, width, *rest):
+    parts, out, sems = rest[:-2], rest[-2], rest[-1]
     me = lax.axis_index("seq")
     copies = []
     for sample in range(samples):
-        for slot in range(count):
+        for slot in slots:
             first = pl.multiple_of(lax.bitwise_xor(me, slot) * width, width)
-            place = sample * count + slot
+            place = len(copies)
             copies.append(
                 pltpu.make_async_copy(
                     parts[place], out.at[0, sample, :, pl.ds(first, width)], sems.at[place]
@@ -158,11 +159,11 @@
         copy.wait()
 
 
-def unpack(parts, samples, count):
+def unpack(parts, samples, slots):
     rows, width = parts[0].shape
     return pl.pallas_call(
-        functools.partial(unpack_kernel, samples, count, width),
-        out_shape=jax.ShapeDtypeStruct((1, samples, rows, width * count), parts[0].dtype),
+        functools.partial(unpack_kernel, samples, slots, width),
+        out_shape=jax.ShapeDtypeStruct((1, samples, rows, width * len(slots)), parts[0].dtype),
         in_specs=[VMEM] * len(parts),
         out_specs=ANY,
         scratch_shapes=[pltpu.SemaphoreType.DMA((len(parts),))],
@@ -170,26 +171,28 @@
     )(*parts)
 
 
-def exchange(parts, order):
-    count = len(parts)
-    landed = list(parts)
-    for slot in order:
-        pairs = [(place, place ^ slot) for place in range(count)]
-        landed[slot] = lax.ppermute(parts[slot], "seq", pairs)
+def exchange(parts, slots):
+    landed = []
+    for part, slot in zip(parts, slots, strict=True):
+        pairs = [(place, place ^ slot) for place in range(len(slots))]
+        landed.append(lax.ppermute(part, "seq", pairs) if slot else part)
     return landed
 
 
 def shards(dp_count, seq_count, qkv, master, moment_one, moment_two, grads):
     samples = qkv.shape[2]
     width = qkv.shape[4] // seq_count
-    order = list(range(seq_count - 1, 0, -1))
-    landed = [exchange(pack(qkv, sample, seq_count, width), order) for sample in range(samples)]
+    half = seq_count // 2
+    far, near = list(range(half, seq_count)), list(range(1, half))
+    slots_in = slots_out = [slot for pair in zip(far, near + [0]) for slot in pair]
+    landed = [exchange(pack(qkv, sample, slots_in, width), slots_in) for sample in range(samples)]
     updated, first_moment, second_moment = adamw(master, moment_one, moment_two, grads)
     layer = own_columns(updated.astype(jnp.bfloat16), dp_count, seq_count, width)
-    parts = []
+    outs = []
     for sample in range(samples):
-        parts += exchange(attend(layer, landed[sample]), order)
-    attended = unpack(parts, samples, seq_count)
+        result = attend(layer, landed[sample])
+        outs += exchange([result[slots_in.index(slot)] for slot in slots_out], slots_out)
+    attended = unpack(outs, samples, slots_out)
     return (attended, updated, first_moment, second_moment)
 
 

time: 114 us -> 110 us (0.965); the launches traced: 112 us -> 110 us
  starting transfers between devices: 73.7 us -> 69.7 us
  waiting for transfers between devices: 17.9 us -> 20.2 us
    ppermute x28, starting transfers between devices: 70.3 us -> 66.4 us  [exchange(): landed.append(lax.ppermute(part, 'seq', pairs) if slot else part)]
    ppermute x28, waiting for transfers between devices: 17.9 us -> 20.2 us  [exchange(): landed.append(lax.ppermute(part, 'seq', pairs) if slot else part)]
  transfers between devices with their start and end apart: 29 -> 29, of which waited for: 6 -> 6; matrix products, arithmetic and copies ran while one was open for 1% -> 1% of each run, Pallas kernels for 9% -> 10%
where the time goes in v3:
time: 110 us
  starting transfers between devices  69.7 us (63%)
  waiting for transfers between devices  20.2 us (18%)
  Pallas kernels  15.5 us (14%)
  local copies, waits for them, and re-layouts  2.78 us (3%)
    ppermute x28, starting transfers between devices, exchange(): landed.append(lax.ppermute(part, 'seq', pairs) if slot else part)  66.4 us
    ppermute x28, waiting for transfers between devices, exchange(): landed.append(lax.ppermute(part, 'seq', pairs) if slot else part)  20.2 us
    pallas_call x2, Pallas kernels, attend(): pl.pallas_call(functools.partial(attend_kernel, count, 256), out_shape=[j...  7.83 us
    pallas_call x2, Pallas kernels, pack(): pl.pallas_call(functools.partial(pack_kernel, sample, slots, width), out_...  5.39 us
    ppermute x1, starting transfers between devices, own_columns(): found = found + lax.ppermute(layer, ('dp', 'seq'), pairs)  3.38 us
    unnamed x50, local copies, waits for them, and re-layouts  2.78 us
    pallas_call x1, Pallas kernels, unpack(): pl.pallas_call(functools.partial(unpack_kernel, samples, slots, width), o...  2.32 us
  transfers between devices with their start and end apart: 29, of which 6 were waited for; matrix products, arithmetic and copies ran while one was open for 1% of the time, Pallas kernels for 10%

profile of v3, /device:TPU:0, one launch (start us, length us, event | category | flops | bytes accessed | tf_op | source)
XLA Modules:
  0.0 109.9 jit_solution(6705141382289160359)
XLA Ops:
  0.7 2.7 %pack.3 = (bf16[3,64,512]{2,1,0:T(8,128)(2,1)}, bf16[3,64,512]{2,1,0:T(8,128)(2,1)}, bf16[3,64,512]{2,1,0:T(8,128)(2,1)}, bf16[3,64,512]{2,1,0:T(8,128)(2,1)}, b...) custom-call(bf16[3,1,2,64,4096]{4,3,2,1,0:T(8,128)(2,1)} %source.3), custom_call_target="tpu_custom_call" | custom-call | tf_op jit(solution)/shard_map/pack/pallas_call | solution.py:80
  3.4 4.1 %collective-permute-start.15 = (bf16[3,64,512]{2,1,0:T(8,128)(2,1)}, bf16[3,64,512]{2,1,0:T(8,128)(2,1)S(1)}, u32[]{:S(2)}, u32[]{:S(2)}) collective-permute-start(bf16[3,64,512]{2,1,0:T(8,128)(2,1)} %get-tuple-element.52), channel_id=1, source_target_pairs={{0,4},{1,5},{2,6},{3,7},{4,0},{5,1},{6,2},{7,3},{8,12},{9,13},{10,... | collective-permute-start | bytes 589832 | tf_op jit(solution)/shard_map/ppermute | solution.py:178
  7.7 1.8 %collective-permute-start.18 = (bf16[3,64,512]{2,1,0:T(8,128)(2,1)}, bf16[3,64,512]{2,1,0:T(8,128)(2,1)S(1)}, u32[]{:S(2)}, u32[]{:S(2)}) collective-permute-start(bf16[3,64,512]{2,1,0:T(8,128)(2,1)} %get-tuple-element.55), channel_id=1, source_target_pairs={{0,2},{1,3},{2,0},{3,1},{4,6},{5,7},{6,4},{7,5},{8,10},{9,11},{10,... | collective-permute-start | bytes 589832 | tf_op jit(solution)/shard_map/ppermute | solution.py:178
  9.6 0.6 fusion.1
  10.2 3.4 %collective-permute-start = (bf16[4,1024]{1,0:T(4,128)(2,1)S(1)}, bf16[4,1024]{1,0:T(4,128)(2,1)S(1)}, u32[]{:S(2)}, u32[]{:S(2)}) collective-permute-start(bf16[4,1024]{1,0:T(4,128)(2,1)S(1)} %get-tuple-element.68), channel_id=1, source_target_pairs={{0,8},{1,16},{2,24},{3,9},{4,17},{5,25},{8,2},{9,18},{10,26},{11,3... | collective-permute-start | bytes 24584 | tf_op jit(solution)/shard_map/ppermute | solution.py:55
  13.6 2.7 %pack.2 = (bf16[3,64,512]{2,1,0:T(8,128)(2,1)}, bf16[3,64,512]{2,1,0:T(8,128)(2,1)}, bf16[3,64,512]{2,1,0:T(8,128)(2,1)}, bf16[3,64,512]{2,1,0:T(8,128)(2,1)}, b...) custom-call(bf16[3,1,2,64,4096]{4,3,2,1,0:T(8,128)(2,1)} %source.3), custom_call_target="tpu_custom_call" | custom-call | tf_op jit(solution)/shard_map/pack/pallas_call | solution.py:80
  16.3 10.5 %collective-permute-start.19 = (bf16[3,64,512]{2,1,0:T(8,128)(2,1)S(1)}, bf16[3,64,512]{2,1,0:T(8,128)(2,1)S(1)}, u32[]{:S(2)}, u32[]{:S(2)}) collective-permute-start(bf16[3,64,512]{2,1,0:T(8,128)(2,1)S(1)} %copy-done.24), channel_id=1, source_target_pairs={{0,6},{1,7},{2,4},{3,5},{4,2},{5,3},{6,0},{7,1},{8,14},{9,15},{10,... | collective-permute-start | bytes 589832 | tf_op jit(solution)/shard_map/ppermute | solution.py:178
  26.8 2.0 %collective-permute-start.20 = (bf16[3,64,512]{2,1,0:T(8,128)(2,1)S(1)}, bf16[3,64,512]{2,1,0:T(8,128)(2,1)S(1)}, u32[]{:S(2)}, u32[]{:S(2)}) collective-permute-start(bf16[3,64,512]{2,1,0:T(8,128)(2,1)S(1)} %copy-done.23), channel_id=1, source_target_pairs={{0,3},{1,2},{2,1},{3,0},{4,7},{5,6},{6,5},{7,4},{8,11},{9,10},{10,... | collective-permute-start | bytes 589832 | tf_op jit(solution)/shard_map/ppermute | solution.py:178
  28.9 5.9 %collective-permute-start.21 = (bf16[3,64,512]{2,1,0:T(8,128)(2,1)S(1)}, bf16[3,64,512]{2,1,0:T(8,128)(2,1)S(1)}, u32[]{:S(2)}, u32[]{:S(2)}) collective-permute-start(bf16[3,64,512]{2,1,0:T(8,128)(2,1)S(1)} %copy-done.22), channel_id=1, source_target_pairs={{0,7},{1,6},{2,5},{3,4},{4,3},{5,2},{6,1},{7,0},{8,15},{9,14},{10,... | collective-permute-start | bytes 589832 | tf_op jit(solution)/shard_map/ppermute | solution.py:178
  35.3 2.3 %collective-permute-start.2 = (bf16[3,64,512]{2,1,0:T(8,128)(2,1)}, bf16[3,64,512]{2,1,0:T(8,128)(2,1)S(1)}, u32[]{:S(2)}, u32[]{:S(2)}) collective-permute-start(bf16[3,64,512]{2,1,0:T(8,128)(2,1)} %get-tuple-element.37), channel_id=1, source_target_pairs={{0,1},{1,0},{2,3},{3,2},{4,5},{5,4},{6,7},{7,6},{8,9},{9,8},{10,11... | collective-permute-start | bytes 589832 | tf_op jit(solution)/shard_map/ppermute | solution.py:178
  37.8 7.5 %collective-permute-start.4 = (bf16[3,64,512]{2,1,0:T(8,128)(2,1)}, bf16[3,64,512]{2,1,0:T(8,128)(2,1)S(1)}, u32[]{:S(2)}, u32[]{:S(2)}) collective-permute-start(bf16[3,64,512]{2,1,0:T(8,128)(2,1)} %get-tuple-element.39), channel_id=1, source_target_pairs={{0,2},{1,3},{2,0},{3,1},{4,6},{5,7},{6,4},{7,5},{8,10},{9,11},{10,... | collective-permute-start | bytes 589832 | tf_op jit(solution)/shard_map/ppermute | solution.py:178
  45.3 6.1 %collective-permute-start.5 = (bf16[3,64,512]{2,1,0:T(8,128)(2,1)}, bf16[3,64,512]{2,1,0:T(8,128)(2,1)S(1)}, u32[]{:S(2)}, u32[]{:S(2)}) collective-permute-start(bf16[3,64,512]{2,1,0:T(8,128)(2,1)} %get-tuple-element.40), channel_id=1, source_target_pairs={{0,6},{1,7},{2,4},{3,5},{4,2},{5,3},{6,0},{7,1},{8,14},{9,15},{10,... | collective-permute-start | bytes 589832 | tf_op jit(solution)/shard_map/ppermute | solution.py:178
  51.4 10.9 %collective-permute-done.1.rest_0_ = bf16[3,64,512]{2,1,0:T(8,128)(2,1)S(1)} collective-permute-done((bf16[3,64,512]{2,1,0:T(8,128)(2,1)}, bf16[3,64,512]{2,1,0:T(8,128)(2,1)S(1)}, u32[]{:S(2)}, u32[]{:S(2)}) %collective-permute-start.1) | collective-permute-done | bytes 196640 | tf_op jit(solution)/shard_map/ppermute | solution.py:178
  62.3 0.9 collective-permute-start.6
  63.2 2.7 %collective-permute-start.7 = (bf16[3,64,512]{2,1,0:T(8,128)(2,1)}, bf16[3,64,512]{2,1,0:T(8,128)(2,1)S(1)}, u32[]{:S(2)}, u32[]{:S(2)}) collective-permute-start(bf16[3,64,512]{2,1,0:T(8,128)(2,1)} %get-tuple-element.42), channel_id=1, source_target_pairs={{0,7},{1,6},{2,5},{3,4},{4,3},{5,2},{6,1},{7,0},{8,15},{9,14},{10,... | collective-permute-start | bytes 589832 | tf_op jit(solution)/shard_map/ppermute | solution.py:178
  65.9 3.9 %attend.3 = (bf16[64,512]{1,0:T(8,128)(2,1)S(1)}, bf16[64,512]{1,0:T(8,128)(2,1)S(1)}, bf16[64,512]{1,0:T(8,128)(2,1)S(1)}, bf16[64,512]{1,0:T(8,128)(2,1)S(1)},...) custom-call(bf16[4,512]{1,0:T(4,128)(2,1)S(1)} %dynamic-slice_add_fu, ...), custom_call_target="tpu_custom_call" | custom-call | flops 536870912 | bytes 2097152 | tf_op jit(solution)/shard_map/attend/pallas_call | solution.py:128
  69.9 0.6 copy-done
  71.1 0.8 collective-permute-start.23
  71.9 7.2 %collective-permute-start.24 = (bf16[64,512]{1,0:T(8,128)(2,1)S(1)}, bf16[64,512]{1,0:T(8,128)(2,1)S(1)}, u32[]{:S(2)}, u32[]{:S(2)}) collective-permute-start(bf16[64,512]{1,0:T(8,128)(2,1)S(1)} %get-tuple-element.62), channel_id=1, source_target_pairs={{0,5},{1,4},{2,7},{3,6},{4,1},{5,0},{6,3},{7,2},{8,13},{9,12},{10,... | collective-permute-start | bytes 196616 | tf_op jit(solution)/shard_map/ppermute | solution.py:178
  79.1 2.4 %collective-permute-start.26 = (bf16[64,512]{1,0:T(8,128)(2,1)S(1)}, bf16[64,512]{1,0:T(8,128)(2,1)S(1)}, u32[]{:S(2)}, u32[]{:S(2)}) collective-permute-start(bf16[64,512]{1,0:T(8,128)(2,1)S(1)} %get-tuple-element.64), channel_id=1, source_target_pairs={{0,6},{1,7},{2,4},{3,5},{4,2},{5,3},{6,0},{7,1},{8,14},{9,15},{10,... | collective-permute-start | bytes 196616 | tf_op jit(solution)/shard_map/ppermute | solution.py:178
  81.5 0.9 copy-done.2
  82.4 3.9 %attend.2 = (bf16[64,512]{1,0:T(8,128)(2,1)S(1)}, bf16[64,512]{1,0:T(8,128)(2,1)S(1)}, bf16[64,512]{1,0:T(8,128)(2,1)S(1)}, bf16[64,512]{1,0:T(8,128)(2,1)S(1)},...) custom-call(bf16[4,512]{1,0:T(4,128)(2,1)S(1)} %dynamic-slice_add_fu, ...), custom_call_target="tpu_custom_call" | custom-call | flops 536870912 | bytes 2097152 | tf_op jit(solution)/shard_map/attend/pallas_call | solution.py:128
  87.0 3.9 %collective-permute-start.27 = (bf16[64,512]{1,0:T(8,128)(2,1)S(1)}, bf16[64,512]{1,0:T(8,128)(2,1)S(1)}, u32[]{:S(2)}, u32[]{:S(2)}) collective-permute-start(bf16[64,512]{1,0:T(8,128)(2,1)S(1)} %get-tuple-element.65), channel_id=1, source_target_pairs={{0,3},{1,2},{2,1},{3,0},{4,7},{5,6},{6,5},{7,4},{8,11},{9,10},{10,... | collective-permute-start | bytes 196616 | tf_op jit(solution)/shard_map/ppermute | solution.py:178
  90.8 1.6 %collective-permute-start.28 = (bf16[64,512]{1,0:T(8,128)(2,1)S(1)}, bf16[64,512]{1,0:T(8,128)(2,1)S(1)}, u32[]{:S(2)}, u32[]{:S(2)}) collective-permute-start(bf16[64,512]{1,0:T(8,128)(2,1)S(1)} %get-tuple-element.66), channel_id=1, source_target_pairs={{0,7},{1,6},{2,5},{3,4},{4,3},{5,2},{6,1},{7,0},{8,15},{9,14},{10,... | collective-permute-start | bytes 196616 | tf_op jit(solution)/shard_map/ppermute | solution.py:178
  92.6 2.9 %collective-permute-start.10 = (bf16[64,512]{1,0:T(8,128)(2,1)S(1)}, bf16[64,512]{1,0:T(8,128)(2,1)S(1)}, u32[]{:S(2)}, u32[]{:S(2)}) collective-permute-start(bf16[64,512]{1,0:T(8,128)(2,1)S(1)} %get-tuple-element.46), channel_id=1, source_target_pairs={{0,5},{1,4},{2,7},{3,6},{4,1},{5,0},{6,3},{7,2},{8,13},{9,12},{10,... | collective-permute-start | bytes 196616 | tf_op jit(solution)/shard_map/ppermute | solution.py:178
  95.6 1.5 %collective-permute-done.28.rest_14_ = bf16[64,512]{1,0:T(8,128)(2,1)S(1)} collective-permute-done((bf16[64,512]{1,0:T(8,128)(2,1)S(1)}, bf16[64,512]{1,0:T(8,128)(2,1)S(1)}, u32[]{:S(2)}, u32[]{:S(2)}) %collective-permute-start.28) | collective-permute-done | bytes 65568 | tf_op jit(solution)/shard_map/ppermute | solution.py:178
  97.6 3.1 %collective-permute-done.8.rest_0_ = bf16[64,512]{1,0:T(8,128)(2,1)S(1)} collective-permute-done((bf16[64,512]{1,0:T(8,128)(2,1)S(1)}, bf16[64,512]{1,0:T(8,128)(2,1)S(1)}, u32[]{:S(2)}, u32[]{:S(2)}) %collective-permute-start.8) | collective-permute-done | bytes 65568 | tf_op jit(solution)/shard_map/ppermute | solution.py:178
  100.7 1.6 %collective-permute-start.14 = (bf16[64,512]{1,0:T(8,128)(2,1)S(1)}, bf16[64,512]{1,0:T(8,128)(2,1)S(1)}, u32[]{:S(2)}, u32[]{:S(2)}) collective-permute-start(bf16[64,512]{1,0:T(8,128)(2,1)S(1)} %get-tuple-element.50), channel_id=1, source_target_pairs={{0,7},{1,6},{2,5},{3,4},{4,3},{5,2},{6,1},{7,0},{8,15},{9,14},{10,... | collective-permute-start | bytes 196616 | tf_op jit(solution)/shard_map/ppermute | solution.py:178
  102.3 1.0 collective-permute-done.10.rest_2_
  103.3 1.7 %collective-permute-done.13.rest_5_ = bf16[64,512]{1,0:T(8,128)(2,1)S(1)} collective-permute-done((bf16[64,512]{1,0:T(8,128)(2,1)S(1)}, bf16[64,512]{1,0:T(8,128)(2,1)S(1)}, u32[]{:S(2)}, u32[]{:S(2)}) %collective-permute-start.13) | collective-permute-done | bytes 65568 | tf_op jit(solution)/shard_map/ppermute | solution.py:178
  105.0 2.0 %collective-permute-done.14.rest_6_ = bf16[64,512]{1,0:T(8,128)(2,1)S(1)} collective-permute-done((bf16[64,512]{1,0:T(8,128)(2,1)S(1)}, bf16[64,512]{1,0:T(8,128)(2,1)S(1)}, u32[]{:S(2)}, u32[]{:S(2)}) %collective-permute-start.14) | collective-permute-done | bytes 65568 | tf_op jit(solution)/shard_map/ppermute | solution.py:178
  107.6 2.3 %unpack.1 = bf16[1,2,64,4096]{3,2,1,0:T(8,128)(2,1)} custom-call(bf16[64,512]{1,0:T(8,128)(2,1)} %copy-done.11, bf16[64,512]{1,0:T(8,128)(2,1)} %copy-done.12, bf16[64,512]{1,0:T(8,128)(2,1)} %copy-done.13, bf16[64,512]{1,0:T(8,128)(2,1)} %copy-done.14, bf16[64,512]{1,0:T(8,128)(2,1)} %copy-done.15, bf16[64,512]{1,0:T(8,128)(2,1)} %copy-done.16, ...), custom_call_target="tpu_custom_call" | custom-call | tf_op jit(solution)/shard_map/unpack/pallas_call | solution.py:164
  (83 shorter events, 3.4 us)
Async XLA Ops:
  3.4 23.4 %copy-start.23 = (bf16[3,64,512]{2,1,0:T(8,128)(2,1)S(1)}, bf16[3,64,512]{2,1,0:T(8,128)(2,1)}, u32[]{:S(2)}) copy-start(bf16[3,64,512]{2,1,0:T(8,128)(2,1)} %get-tuple-element.57) | copy-start | bytes 589828
  3.4 25.4 %copy-start.22 = (bf16[3,64,512]{2,1,0:T(8,128)(2,1)S(1)}, bf16[3,64,512]{2,1,0:T(8,128)(2,1)}, u32[]{:S(2)}) copy-start(bf16[3,64,512]{2,1,0:T(8,128)(2,1)} %get-tuple-element.58) | copy-start | bytes 589828
  3.4 62.5 %copy-start.3 = (bf16[3,64,512]{2,1,0:T(8,128)(2,1)S(1)}, bf16[3,64,512]{2,1,0:T(8,128)(2,1)}, u32[]{:S(2)}) copy-start(bf16[3,64,512]{2,1,0:T(8,128)(2,1)} %get-tuple-element.59.rest_7_) | copy-start | bytes 589828
  3.4 23.4 %collective-permute-start.15 = (bf16[3,64,512]{2,1,0:T(8,128)(2,1)}, bf16[3,64,512]{2,1,0:T(8,128)(2,1)S(1)}, u32[]{:S(2)}, u32[]{:S(2)}) collective-permute-start(bf16[3,64,512]{2,1,0:T(8,128)(2,1)} %get-tuple-element.52), channel_id=1, source_target_pairs={{0,4},{1,5},{2,6},{3,7},{4,0},{5,1},{6,2},{7,3},{8,12},{9,13},{10,... | collective-permute-start | bytes 589832 | tf_op jit(solution)/shard_map/ppermute | solution.py:178
  7.5 21.3 %collective-permute-start.16 = (bf16[3,64,512]{2,1,0:T(8,128)(2,1)}, bf16[3,64,512]{2,1,0:T(8,128)(2,1)S(1)}, u32[]{:S(2)}, u32[]{:S(2)}) collective-permute-start(bf16[3,64,512]{2,1,0:T(8,128)(2,1)} %get-tuple-element.53), channel_id=1, source_target_pairs={{0,1},{1,0},{2,3},{3,2},{4,5},{5,4},{6,7},{7,6},{8,9},{9,8},{10,11... | collective-permute-start | bytes 589832 | tf_op jit(solution)/shard_map/ppermute | solution.py:178
  7.5 27.3 %collective-permute-start.17 = (bf16[3,64,512]{2,1,0:T(8,128)(2,1)}, bf16[3,64,512]{2,1,0:T(8,128)(2,1)S(1)}, u32[]{:S(2)}, u32[]{:S(2)}) collective-permute-start(bf16[3,64,512]{2,1,0:T(8,128)(2,1)} %get-tuple-element.54), channel_id=1, source_target_pairs={{0,5},{1,4},{2,7},{3,6},{4,1},{5,0},{6,3},{7,2},{8,13},{9,12},{10,... | collective-permute-start | bytes 589832 | tf_op jit(solution)/shard_map/ppermute | solution.py:178
  7.7 27.6 %collective-permute-start.18 = (bf16[3,64,512]{2,1,0:T(8,128)(2,1)}, bf16[3,64,512]{2,1,0:T(8,128)(2,1)S(1)}, u32[]{:S(2)}, u32[]{:S(2)}) collective-permute-start(bf16[3,64,512]{2,1,0:T(8,128)(2,1)} %get-tuple-element.55), channel_id=1, source_target_pairs={{0,2},{1,3},{2,0},{3,1},{4,6},{5,7},{6,4},{7,5},{8,10},{9,11},{10,... | collective-permute-start | bytes 589832 | tf_op jit(solution)/shard_map/ppermute | solution.py:178
  10.2 6.1 %collective-permute-start = (bf16[4,1024]{1,0:T(4,128)(2,1)S(1)}, bf16[4,1024]{1,0:T(4,128)(2,1)S(1)}, u32[]{:S(2)}, u32[]{:S(2)}) collective-permute-start(bf16[4,1024]{1,0:T(4,128)(2,1)S(1)} %get-tuple-element.68), channel_id=1, source_target_pairs={{0,8},{1,16},{2,24},{3,9},{4,17},{5,25},{8,2},{9,18},{10,26},{11,3... | collective-permute-start | bytes 24584 | tf_op jit(solution)/shard_map/ppermute | solution.py:55
  16.3 21.3 %collective-permute-start.19 = (bf16[3,64,512]{2,1,0:T(8,128)(2,1)S(1)}, bf16[3,64,512]{2,1,0:T(8,128)(2,1)S(1)}, u32[]{:S(2)}, u32[]{:S(2)}) collective-permute-start(bf16[3,64,512]{2,1,0:T(8,128)(2,1)S(1)} %copy-done.24), channel_id=1, source_target_pairs={{0,6},{1,7},{2,4},{3,5},{4,2},{5,3},{6,0},{7,1},{8,14},{9,15},{10,... | collective-permute-start | bytes 589832 | tf_op jit(solution)/shard_map/ppermute | solution.py:178
  26.8 11.0 %collective-permute-start.20 = (bf16[3,64,512]{2,1,0:T(8,128)(2,1)S(1)}, bf16[3,64,512]{2,1,0:T(8,128)(2,1)S(1)}, u32[]{:S(2)}, u32[]{:S(2)}) collective-permute-start(bf16[3,64,512]{2,1,0:T(8,128)(2,1)S(1)} %copy-done.23), channel_id=1, source_target_pairs={{0,3},{1,2},{2,1},{3,0},{4,7},{5,6},{6,5},{7,4},{8,11},{9,10},{10,... | collective-permute-start | bytes 589832 | tf_op jit(solution)/shard_map/ppermute | solution.py:178
  28.9 16.5 %collective-permute-start.21 = (bf16[3,64,512]{2,1,0:T(8,128)(2,1)S(1)}, bf16[3,64,512]{2,1,0:T(8,128)(2,1)S(1)}, u32[]{:S(2)}, u32[]{:S(2)}) collective-permute-start(bf16[3,64,512]{2,1,0:T(8,128)(2,1)S(1)} %copy-done.22), channel_id=1, source_target_pairs={{0,7},{1,6},{2,5},{3,4},{4,3},{5,2},{6,1},{7,0},{8,15},{9,14},{10,... | collective-permute-start | bytes 589832 | tf_op jit(solution)/shard_map/ppermute | solution.py:178
  34.8 27.5 %collective-permute-start.1 = (bf16[3,64,512]{2,1,0:T(8,128)(2,1)}, bf16[3,64,512]{2,1,0:T(8,128)(2,1)S(1)}, u32[]{:S(2)}, u32[]{:S(2)}) collective-permute-start(bf16[3,64,512]{2,1,0:T(8,128)(2,1)} %get-tuple-element.36), channel_id=1, source_target_pairs={{0,4},{1,5},{2,6},{3,7},{4,0},{5,1},{6,2},{7,3},{8,12},{9,13},{10,... | collective-permute-start | bytes 589832 | tf_op jit(solution)/shard_map/ppermute | solution.py:178
  35.3 27.9 %collective-permute-start.2 = (bf16[3,64,512]{2,1,0:T(8,128)(2,1)}, bf16[3,64,512]{2,1,0:T(8,128)(2,1)S(1)}, u32[]{:S(2)}, u32[]{:S(2)}) collective-permute-start(bf16[3,64,512]{2,1,0:T(8,128)(2,1)} %get-tuple-element.37), channel_id=1, source_target_pairs={{0,1},{1,0},{2,3},{3,2},{4,5},{5,4},{6,7},{7,6},{8,9},{9,8},{10,11... | collective-permute-start | bytes 589832 | tf_op jit(solution)/shard_map/ppermute | solution.py:178
  37.7 32.8 %collective-permute-start.3 = (bf16[3,64,512]{2,1,0:T(8,128)(2,1)}, bf16[3,64,512]{2,1,0:T(8,128)(2,1)S(1)}, u32[]{:S(2)}, u32[]{:S(2)}) collective-permute-start(bf16[3,64,512]{2,1,0:T(8,128)(2,1)} %get-tuple-element.38), channel_id=1, source_target_pairs={{0,5},{1,4},{2,7},{3,6},{4,1},{5,0},{6,3},{7,2},{8,13},{9,12},{10,... | collective-permute-start | bytes 589832 | tf_op jit(solution)/shard_map/ppermute | solution.py:178
  37.8 33.2 %collective-permute-start.4 = (bf16[3,64,512]{2,1,0:T(8,128)(2,1)}, bf16[3,64,512]{2,1,0:T(8,128)(2,1)S(1)}, u32[]{:S(2)}, u32[]{:S(2)}) collective-permute-start(bf16[3,64,512]{2,1,0:T(8,128)(2,1)} %get-tuple-element.39), channel_id=1, source_target_pairs={{0,2},{1,3},{2,0},{3,1},{4,6},{5,7},{6,4},{7,5},{8,10},{9,11},{10,... | collective-permute-start | bytes 589832 | tf_op jit(solution)/shard_map/ppermute | solution.py:178
  45.3 26.5 %collective-permute-start.5 = (bf16[3,64,512]{2,1,0:T(8,128)(2,1)}, bf16[3,64,512]{2,1,0:T(8,128)(2,1)S(1)}, u32[]{:S(2)}, u32[]{:S(2)}) collective-permute-start(bf16[3,64,512]{2,1,0:T(8,128)(2,1)} %get-tuple-element.40), channel_id=1, source_target_pairs={{0,6},{1,7},{2,4},{3,5},{4,2},{5,3},{6,0},{7,1},{8,14},{9,15},{10,... | collective-permute-start | bytes 589832 | tf_op jit(solution)/shard_map/ppermute | solution.py:178
  62.3 16.7 %collective-permute-start.6 = (bf16[3,64,512]{2,1,0:T(8,128)(2,1)}, bf16[3,64,512]{2,1,0:T(8,128)(2,1)S(1)}, u32[]{:S(2)}, u32[]{:S(2)}) collective-permute-start(bf16[3,64,512]{2,1,0:T(8,128)(2,1)} %get-tuple-element.41), channel_id=1, source_target_pairs={{0,3},{1,2},{2,1},{3,0},{4,7},{5,6},{6,5},{7,4},{8,11},{9,10},{10,... | collective-permute-start | bytes 589832 | tf_op jit(solution)/shard_map/ppermute | solution.py:178
  63.2 15.9 %collective-permute-start.7 = (bf16[3,64,512]{2,1,0:T(8,128)(2,1)}, bf16[3,64,512]{2,1,0:T(8,128)(2,1)S(1)}, u32[]{:S(2)}, u32[]{:S(2)}) collective-permute-start(bf16[3,64,512]{2,1,0:T(8,128)(2,1)} %get-tuple-element.42), channel_id=1, source_target_pairs={{0,7},{1,6},{2,5},{3,4},{4,3},{5,2},{6,1},{7,0},{8,15},{9,14},{10,... | collective-permute-start | bytes 589832 | tf_op jit(solution)/shard_map/ppermute | solution.py:178
  70.5 16.5 %collective-permute-start.22 = (bf16[64,512]{1,0:T(8,128)(2,1)S(1)}, bf16[64,512]{1,0:T(8,128)(2,1)S(1)}, u32[]{:S(2)}, u32[]{:S(2)}) collective-permute-start(bf16[64,512]{1,0:T(8,128)(2,1)S(1)} %get-tuple-element.60), channel_id=1, source_target_pairs={{0,4},{1,5},{2,6},{3,7},{4,0},{5,1},{6,2},{7,3},{8,12},{9,13},{10,... | collective-permute-start | bytes 196616 | tf_op jit(solution)/shard_map/ppermute | solution.py:178
  71.1 19.8 %collective-permute-start.23 = (bf16[64,512]{1,0:T(8,128)(2,1)S(1)}, bf16[64,512]{1,0:T(8,128)(2,1)S(1)}, u32[]{:S(2)}, u32[]{:S(2)}) collective-permute-start(bf16[64,512]{1,0:T(8,128)(2,1)S(1)} %get-tuple-element.61), channel_id=1, source_target_pairs={{0,1},{1,0},{2,3},{3,2},{4,5},{5,4},{6,7},{7,6},{8,9},{9,8},{10,11... | collective-permute-start | bytes 196616 | tf_op jit(solution)/shard_map/ppermute | solution.py:178
  71.9 20.6 %collective-permute-start.24 = (bf16[64,512]{1,0:T(8,128)(2,1)S(1)}, bf16[64,512]{1,0:T(8,128)(2,1)S(1)}, u32[]{:S(2)}, u32[]{:S(2)}) collective-permute-start(bf16[64,512]{1,0:T(8,128)(2,1)S(1)} %get-tuple-element.62), channel_id=1, source_target_pairs={{0,5},{1,4},{2,7},{3,6},{4,1},{5,0},{6,3},{7,2},{8,13},{9,12},{10,... | collective-permute-start | bytes 196616 | tf_op jit(solution)/shard_map/ppermute | solution.py:178
  79.1 13.4 %collective-permute-start.25 = (bf16[64,512]{1,0:T(8,128)(2,1)S(1)}, bf16[64,512]{1,0:T(8,128)(2,1)S(1)}, u32[]{:S(2)}, u32[]{:S(2)}) collective-permute-start(bf16[64,512]{1,0:T(8,128)(2,1)S(1)} %get-tuple-element.63), channel_id=1, source_target_pairs={{0,2},{1,3},{2,0},{3,1},{4,6},{5,7},{6,4},{7,5},{8,10},{9,11},{10,... | collective-permute-start | bytes 196616 | tf_op jit(solution)/shard_map/ppermute | solution.py:178
  79.1 13.5 %collective-permute-start.26 = (bf16[64,512]{1,0:T(8,128)(2,1)S(1)}, bf16[64,512]{1,0:T(8,128)(2,1)S(1)}, u32[]{:S(2)}, u32[]{:S(2)}) collective-permute-start(bf16[64,512]{1,0:T(8,128)(2,1)S(1)} %get-tuple-element.64), channel_id=1, source_target_pairs={{0,6},{1,7},{2,4},{3,5},{4,2},{5,3},{6,0},{7,1},{8,14},{9,15},{10,... | collective-permute-start | bytes 196616 | tf_op jit(solution)/shard_map/ppermute | solution.py:178
  87.0 8.6 %collective-permute-start.27 = (bf16[64,512]{1,0:T(8,128)(2,1)S(1)}, bf16[64,512]{1,0:T(8,128)(2,1)S(1)}, u32[]{:S(2)}, u32[]{:S(2)}) collective-permute-start(bf16[64,512]{1,0:T(8,128)(2,1)S(1)} %get-tuple-element.65), channel_id=1, source_target_pairs={{0,3},{1,2},{2,1},{3,0},{4,7},{5,6},{6,5},{7,4},{8,11},{9,10},{10,... | collective-permute-start | bytes 196616 | tf_op jit(solution)/shard_map/ppermute | solution.py:178
  90.8 6.2 %collective-permute-start.28 = (bf16[64,512]{1,0:T(8,128)(2,1)S(1)}, bf16[64,512]{1,0:T(8,128)(2,1)S(1)}, u32[]{:S(2)}, u32[]{:S(2)}) collective-permute-start(bf16[64,512]{1,0:T(8,128)(2,1)S(1)} %get-tuple-element.66), channel_id=1, source_target_pairs={{0,7},{1,6},{2,5},{3,4},{4,3},{5,2},{6,1},{7,0},{8,15},{9,14},{10,... | collective-permute-start | bytes 196616 | tf_op jit(solution)/shard_map/ppermute | solution.py:178
  92.5 8.2 %collective-permute-start.8 = (bf16[64,512]{1,0:T(8,128)(2,1)S(1)}, bf16[64,512]{1,0:T(8,128)(2,1)S(1)}, u32[]{:S(2)}, u32[]{:S(2)}) collective-permute-start(bf16[64,512]{1,0:T(8,128)(2,1)S(1)} %get-tuple-element.44), channel_id=1, source_target_pairs={{0,4},{1,5},{2,6},{3,7},{4,0},{5,1},{6,2},{7,3},{8,12},{9,13},{10,... | collective-permute-start | bytes 196616 | tf_op jit(solution)/shard_map/ppermute | solution.py:178
  92.5 8.2 %collective-permute-start.9 = (bf16[64,512]{1,0:T(8,128)(2,1)S(1)}, bf16[64,512]{1,0:T(8,128)(2,1)S(1)}, u32[]{:S(2)}, u32[]{:S(2)}) collective-permute-start(bf16[64,512]{1,0:T(8,128)(2,1)S(1)} %get-tuple-element.45), channel_id=1, source_target_pairs={{0,1},{1,0},{2,3},{3,2},{4,5},{5,4},{6,7},{7,6},{8,9},{9,8},{10,11... | collective-permute-start | bytes 196616 | tf_op jit(solution)/shard_map/ppermute | solution.py:178
  92.6 10.7 %collective-permute-start.10 = (bf16[64,512]{1,0:T(8,128)(2,1)S(1)}, bf16[64,512]{1,0:T(8,128)(2,1)S(1)}, u32[]{:S(2)}, u32[]{:S(2)}) collective-permute-start(bf16[64,512]{1,0:T(8,128)(2,1)S(1)} %get-tuple-element.46), channel_id=1, source_target_pairs={{0,5},{1,4},{2,7},{3,6},{4,1},{5,0},{6,3},{7,2},{8,13},{9,12},{10,... | collective-permute-start | bytes 196616 | tf_op jit(solution)/shard_map/ppermute | solution.py:178
  95.6 7.7 %collective-permute-start.11 = (bf16[64,512]{1,0:T(8,128)(2,1)S(1)}, bf16[64,512]{1,0:T(8,128)(2,1)S(1)}, u32[]{:S(2)}, u32[]{:S(2)}) collective-permute-start(bf16[64,512]{1,0:T(8,128)(2,1)S(1)} %get-tuple-element.47), channel_id=1, source_target_pairs={{0,2},{1,3},{2,0},{3,1},{4,6},{5,7},{6,4},{7,5},{8,10},{9,11},{10,... | collective-permute-start | bytes 196616 | tf_op jit(solution)/shard_map/ppermute | solution.py:178
  97.1 6.2 %collective-permute-start.12 = (bf16[64,512]{1,0:T(8,128)(2,1)S(1)}, bf16[64,512]{1,0:T(8,128)(2,1)S(1)}, u32[]{:S(2)}, u32[]{:S(2)}) collective-permute-start(bf16[64,512]{1,0:T(8,128)(2,1)S(1)} %get-tuple-element.48), channel_id=1, source_target_pairs={{0,6},{1,7},{2,4},{3,5},{4,2},{5,3},{6,0},{7,1},{8,14},{9,15},{10,... | collective-permute-start | bytes 196616 | tf_op jit(solution)/shard_map/ppermute | solution.py:178
  100.7 4.3 %collective-permute-start.13 = (bf16[64,512]{1,0:T(8,128)(2,1)S(1)}, bf16[64,512]{1,0:T(8,128)(2,1)S(1)}, u32[]{:S(2)}, u32[]{:S(2)}) collective-permute-start(bf16[64,512]{1,0:T(8,128)(2,1)S(1)} %get-tuple-element.49), channel_id=1, source_target_pairs={{0,3},{1,2},{2,1},{3,0},{4,7},{5,6},{6,5},{7,4},{8,11},{9,10},{10,... | collective-permute-start | bytes 196616 | tf_op jit(solution)/shard_map/ppermute | solution.py:178
  100.7 6.3 %collective-permute-start.14 = (bf16[64,512]{1,0:T(8,128)(2,1)S(1)}, bf16[64,512]{1,0:T(8,128)(2,1)S(1)}, u32[]{:S(2)}, u32[]{:S(2)}) collective-permute-start(bf16[64,512]{1,0:T(8,128)(2,1)S(1)} %get-tuple-element.50), channel_id=1, source_target_pairs={{0,7},{1,6},{2,5},{3,4},{4,3},{5,2},{6,1},{7,0},{8,15},{9,14},{10,... | collective-permute-start | bytes 196616 | tf_op jit(solution)/shard_map/ppermute | solution.py:178
  (22 other events, 178.0 us)

commit v4 on v3

--- a/solution.py
+++ b/solution.py
@@ -83,6 +83,7 @@
         in_specs=[ANY],
         out_specs=[VMEM] * count,
         scratch_shapes=[pltpu.SemaphoreType.DMA((count,))],
+        compiler_params=pltpu.CompilerParams(vmem_limit_bytes=4 * 1024 * 1024),
         name="pack",
     )(qkv)
 
@@ -94,19 +95,35 @@
     return (centred * lax.rsqrt(spread + 1e-06) * gain + bias).astype(jnp.bfloat16)
 
 
-def attend_kernel(count, block, layer, *rest):
-    arrived, outs = rest[:count], rest[count : 2 * count]
-    rows, width = outs[0].shape
+def attend_kernel(sample, slots, block, layer, qkv, *rest):
+    count = len(slots)
+    half = count // 2
+    landed, rest = dict(zip(slots[:-1], rest[: count - 1], strict=True)), rest[count - 1 :]
+    given, rest = (rest[:half], rest[half:]) if sample else ([], rest)
+    outs = rest[:count]
+    held, sem = rest[count:]
+    _, rows, width = held.shape
+    own = pl.multiple_of(lax.axis_index("seq") * width, width)
+    copy = pltpu.make_async_copy(qkv.at[:, 0, sample, :, pl.ds(own, width)], held, sem)
+    copy.start()
+    for before, out in zip(given, outs):
+        out[:sample] = before[...]
+    landed[0] = held
     per_block = max(1, block // rows)
     for head in range(width // HD):
         cols = slice(head * HD, (head + 1) * HD)
         gains = layer[:, cols].astype(jnp.float32)
-        keys = jnp.concatenate([normed(a[1, :, cols], gains[2:3], gains[3:4]) for a in arrived])
-        values = jnp.concatenate([a[2, :, cols] for a in arrived])
+        others = [
+            normed(landed[slot][1, :, cols], gains[2:3], gains[3:4]) for slot in range(1, count)
+        ]
+        if head == 0:
+            copy.wait()
+        keys = jnp.concatenate([normed(held[1, :, cols], gains[2:3], gains[3:4])] + others)
+        values = jnp.concatenate([landed[slot][2, :, cols] for slot in range(count)])
         for first in range(0, count, per_block):
-            slots = range(first, first + per_block)
+            here = range(first, min(first + per_block, count))
             queries = jnp.concatenate(
-                [normed(arrived[slot][0, :, cols], gains[0:1], gains[1:2]) for slot in slots]
+                [normed(landed[slot][0, :, cols], gains[0:1], gains[1:2]) for slot in here]
             )
             scores = lax.dot_general(
                 queries, keys, (((1,), (1,)), ((), ())), preferred_element_type=jnp.float32
@@ -117,56 +134,55 @@
             probs = (raised * (1.0 / total)).astype(jnp.bfloat16)
             result = jnp.dot(probs, values, preferred_element_type=jnp.float32)
             result = result.astype(jnp.bfloat16)
-            for place, slot in enumerate(slots):
-                outs[slot][:, cols] = result[place * rows : (place + 1) * rows]
-
-
-def attend(layer, arrived):
-    count = len(arrived)
+            for place, slot in enumerate(here):
+                there = sample if slot < half else 0
+                outs[slot][there, :, cols] = result[place * rows : (place + 1) * rows]
+
+
+def attend(sample, slots, layer, qkv, arrived, given):
+    count = len(slots)
+    half = count // 2
     _, rows, width = arrived[0].shape
     patches = count * rows
     return pl.pallas_call(
-        functools.partial(attend_kernel, count, 256),
-        out_shape=[jax.ShapeDtypeStruct((rows, width), jnp.bfloat16)] * count,
-        in_specs=[VMEM] * (1 + count),
+        functools.partial(attend_kernel, sample, slots, 512),
+        out_shape=[jax.ShapeDtypeStruct((sample + 1, rows, width), jnp.bfloat16)] * half
+        + [jax.ShapeDtypeStruct((1, rows, width), jnp.bfloat16)] * half,
+        in_specs=[VMEM, ANY] + [VMEM] * (count - 1 + len(given)),
         out_specs=[VMEM] * count,
-        compiler_params=pltpu.CompilerParams(vmem_limit_bytes=32 * 1024 * 1024),
+        scratch_shapes=[pltpu.VMEM((3, rows, width), jnp.bfloat16), pltpu.SemaphoreType.DMA(())],
+        compiler_params=pltpu.CompilerParams(vmem_limit_bytes=16 * 1024 * 1024),
         cost_estimate=pl.CostEstimate(
             flops=4 * patches * patches * width,
             bytes_accessed=8 * patches * width,
             transcendentals=patches * patches * (width // HD),
         ),
         name="attend",
-    )(layer, *arrived)
-
-
-def unpack_kernel(samples, slots, width, *rest):
+    )(layer, qkv, *arrived, *given)
+
+
+def unpack_kernel(places, width, *rest):
     parts, out, sems = rest[:-2], rest[-2], rest[-1]
     me = lax.axis_index("seq")
     copies = []
-    for sample in range(samples):
-        for slot in slots:
-            first = pl.multiple_of(lax.bitwise_xor(me, slot) * width, width)
-            place = len(copies)
-            copies.append(
-                pltpu.make_async_copy(
-                    parts[place], out.at[0, sample, :, pl.ds(first, width)], sems.at[place]
-                )
-            )
+    for place, (sample, samples, slot) in enumerate(places):
+        first = pl.multiple_of(lax.bitwise_xor(me, slot) * width, width)
+        there = out.at[0, pl.ds(sample, samples), :, pl.ds(first, width)]
+        copies.append(pltpu.make_async_copy(parts[place], there, sems.at[place]))
     for copy in copies:
         copy.start()
     for copy in copies:
         copy.wait()
 
 
-def unpack(parts, samples, slots):
-    rows, width = parts[0].shape
+def unpack(parts, places, shape):
     return pl.pallas_call(
-        functools.partial(unpack_kernel, samples, slots, width),
-        out_shape=jax.ShapeDtypeStruct((1, samples, rows, width * len(slots)), parts[0].dtype),
+        functools.partial(unpack_kernel, places, parts[0].shape[2]),
+        out_shape=jax.ShapeDtypeStruct(shape, parts[0].dtype),
         in_specs=[VMEM] * len(parts),
         out_specs=ANY,
         scratch_shapes=[pltpu.SemaphoreType.DMA((len(parts),))],
+        compiler_params=pltpu.CompilerParams(vmem_limit_bytes=4 * 1024 * 1024),
         name="unpack",
     )(*parts)
 
@@ -174,9 +190,13 @@
 def exchange(parts, slots):
     landed = []
     for part, slot in zip(parts, slots, strict=True):
-        pairs = [(place, place ^ slot) for place in range(len(slots))]
+        pairs = [(place, place ^ slot) for place in range(lax.axis_size("seq"))]
         landed.append(lax.ppermute(part, "seq", pairs) if slot else part)
     return landed
+
+
+def mixed(one, other):
+    return [slot for pair in zip(one, other, strict=True) for slot in pair]
 
 
 def shards(dp_count, seq_count, qkv, master, moment_one, moment_two, grads):
@@ -184,15 +204,24 @@
     width = qkv.shape[4] // seq_count
     half = seq_count // 2
     far, near = list(range(half, seq_count)), list(range(1, half))
-    slots_in = slots_out = [slot for pair in zip(far, near + [0]) for slot in pair]
-    landed = [exchange(pack(qkv, sample, slots_in, width), slots_in) for sample in range(samples)]
+    turned = far[half // 2 :] + far[: half // 2]
+    slots_in = [mixed(far if sample else turned, near + [0]) for sample in range(samples)]
+    landed = [
+        exchange(pack(qkv, sample, slots_in[sample][:-1], width), slots_in[sample][:-1])
+        for sample in range(samples)
+    ]
     updated, first_moment, second_moment = adamw(master, moment_one, moment_two, grads)
     layer = own_columns(updated.astype(jnp.bfloat16), dp_count, seq_count, width)
-    outs = []
+    outs, near_out = {}, []
     for sample in range(samples):
-        result = attend(layer, landed[sample])
-        outs += exchange([result[slots_in.index(slot)] for slot in slots_out], slots_out)
-    attended = unpack(outs, samples, slots_out)
+        result = attend(sample, slots_in[sample], layer, qkv, landed[sample], near_out)
+        near_out = result[:half]
+        outs.update({(sample, 1, slot): result[slot] for slot in far})
+    outs.update({(0, samples, slot): part for slot, part in enumerate(near_out)})
+    places = [(sample, 1, slot) for sample in range(samples) for slot in far]
+    places += [(0, samples, slot) for slot in near[1:] + near[:1] + [0]]
+    parts = exchange([outs[place] for place in places], [place[2] for place in places])
+    attended = unpack(parts, places, (1, *qkv.shape[2:]))
     return (attended, updated, first_moment, second_moment)
 
 

time: 110 us -> 105 us (0.955)
  starting transfers between devices: 69.7 us -> 58.8 us
  local copies, waits for them, and re-layouts: 2.78 us -> 11.3 us
  Pallas kernels: 15.5 us -> 9.98 us
  waiting for transfers between devices: 20.2 us -> 22.5 us
    ppermute x28 -> x25, starting transfers between devices: 66.4 us -> 55.3 us  [exchange(): landed.append(lax.ppermute(part, 'seq', pairs) if slot else part)]
    unnamed x50 -> x32, local copies, waits for them, and re-layouts: 2.78 us -> 11.3 us
    pallas_call x2, Pallas kernels: 5.39 us -> 1.52 us  [pack(): pl.pallas_call(functools.partial(pack_kernel, sample, slots, width), out_...]
    ppermute x28 -> x25, waiting for transfers between devices: 20.2 us -> 22.4 us  [exchange(): landed.append(lax.ppermute(part, 'seq', pairs) if slot else part)]
    pallas_call x3, Pallas kernels: 10.2 us -> 8.46 us  [the longest x2 7.39 us: attend(): pl.pallas_call(functools.partial(attend_kernel, sample, slots, 512), out_...]
  transfers between devices with their start and end apart: 29 -> 26, of which waited for: 6 -> 7; matrix products, arithmetic and copies ran while one was open for 1% -> 1% of each run, Pallas kernels for 10% -> 8%
where the time goes in v4:
time: 105 us
  starting transfers between devices  58.8 us (56%)
  waiting for transfers between devices  22.5 us (21%)
  local copies, waits for them, and re-layouts  11.3 us (11%)
  Pallas kernels  9.98 us (10%)
  other arithmetic  1.42 us (1%)
    ppermute x25, starting transfers between devices, exchange(): landed.append(lax.ppermute(part, 'seq', pairs) if slot else part)  55.3 us
    ppermute x25, waiting for transfers between devices, exchange(): landed.append(lax.ppermute(part, 'seq', pairs) if slot else part)  22.4 us
    unnamed x32, local copies, waits for them, and re-layouts  11.3 us
    pallas_call x2, Pallas kernels, attend(): pl.pallas_call(functools.partial(attend_kernel, sample, slots, 512), out_...  7.39 us
    ppermute x1, starting transfers between devices, own_columns(): found = found + lax.ppermute(layer, ('dp', 'seq'), pairs)  3.51 us
  transfers between devices with their start and end apart: 26, of which 7 were waited for; matrix products, arithmetic and copies ran while one was open for 1% of the time, Pallas kernels for 8%

profile of v4, /device:TPU:0, one launch (start us, length us, event | category | flops | bytes accessed | tf_op | source)
XLA Modules:
  0.0 104.8 jit_solution(1220101658364141130)
XLA Ops:
  0.6 1.9 %copy-done = bf16[3,1,2,64,4096]{4,3,2,1,0:T(8,128)(2,1)S(1)} copy-done((bf16[3,1,2,64,4096]{4,3,2,1,0:T(8,128)(2,1)S(1)}, bf16[3,1,2,64,4096]{4,3,2,1,0:T(8,128)(2,1)}, u32[]{:S(2)}) %copy-start) | copy-done | bytes 3145752
  2.8 5.1 %collective-permute-start.1 = (bf16[3,64,512]{2,1,0:T(8,128)(2,1)S(1)}, bf16[3,64,512]{2,1,0:T(8,128)(2,1)S(1)}, u32[]{:S(2)}, u32[]{:S(2)}) collective-permute-start(bf16[3,64,512]{2,1,0:T(8,128)(2,1)S(1)} %get-tuple-element.34), channel_id=1, source_target_pairs={{0,6},{1,7},{2,4},{3,5},{4,2},{5,3},{6,0},{7,1},{8,14},{9,15},{10,... | collective-permute-start | bytes 589832 | tf_op jit(solution)/shard_map/ppermute | solution.py:194
  8.1 1.4 %fusion.1 = (bf16[4,1024]{1,0:T(4,128)(2,1)S(1)}, f32[4,1024]{1,0:T(4,128)}, f32[4,1024]{1,0:T(4,128)}, f32[4,1024]{1,0:T(4,128)}) fusion(f32[4,1024]{1,0:T(4,128)} %param.6, f32[4,1024]{1,0:T(4,128)} %param.9, f32[4,1024]{1,0:T(4,128)} %param.7, f32[4,1024]{1,0:T(4,128)} %param.8), kind=kLoop, calls=%fused_computation.6 | loop fusion | flops 65536 | bytes 122880 | tf_op jit(solution)/shard_map/convert_element_type | solution.py:214
  9.5 3.5 %collective-permute-start = (bf16[4,1024]{1,0:T(4,128)(2,1)S(1)}, bf16[4,1024]{1,0:T(4,128)(2,1)S(1)}, u32[]{:S(2)}, u32[]{:S(2)}) collective-permute-start(bf16[4,1024]{1,0:T(4,128)(2,1)S(1)} %get-tuple-element.64), channel_id=1, source_target_pairs={{0,8},{1,16},{2,24},{3,9},{4,17},{5,25},{8,2},{9,18},{10,26},{11,3... | collective-permute-start | bytes 24584 | tf_op jit(solution)/shard_map/ppermute | solution.py:55
  13.1 1.3 %pack.3 = (bf16[3,64,512]{2,1,0:T(8,128)(2,1)S(1)}, bf16[3,64,512]{2,1,0:T(8,128)(2,1)S(1)}, bf16[3,64,512]{2,1,0:T(8,128)(2,1)}, bf16[3,64,512]{2,1,0:T(8,128)(...) custom-call(bf16[3,1,2,64,4096]{4,3,2,1,0:T(8,128)(2,1)S(1)} %copy-done.1), custom_call_target="tpu_custom_call" | custom-call | tf_op jit(solution)/shard_map/pack/pallas_call | solution.py:80
  14.4 10.8 %collective-permute-start.5 = (bf16[3,64,512]{2,1,0:T(8,128)(2,1)S(1)}, bf16[3,64,512]{2,1,0:T(8,128)(2,1)S(1)}, u32[]{:S(2)}, u32[]{:S(2)}) collective-permute-start(bf16[3,64,512]{2,1,0:T(8,128)(2,1)S(1)} %get-tuple-element.38), channel_id=1, source_target_pairs={{0,4},{1,5},{2,6},{3,7},{4,0},{5,1},{6,2},{7,3},{8,12},{9,13},{10,... | collective-permute-start | bytes 589832 | tf_op jit(solution)/shard_map/ppermute | solution.py:194
  25.2 2.7 %collective-permute-start.6 = (bf16[3,64,512]{2,1,0:T(8,128)(2,1)S(1)}, bf16[3,64,512]{2,1,0:T(8,128)(2,1)S(1)}, u32[]{:S(2)}, u32[]{:S(2)}) collective-permute-start(bf16[3,64,512]{2,1,0:T(8,128)(2,1)S(1)} %get-tuple-element.39), channel_id=1, source_target_pairs={{0,3},{1,2},{2,1},{3,0},{4,7},{5,6},{6,5},{7,4},{8,11},{9,10},{10,... | collective-permute-start | bytes 589832 | tf_op jit(solution)/shard_map/ppermute | solution.py:194
  28.6 2.6 %collective-permute-start.12 = (bf16[3,64,512]{2,1,0:T(8,128)(2,1)S(1)}, bf16[3,64,512]{2,1,0:T(8,128)(2,1)S(1)}, u32[]{:S(2)}, u32[]{:S(2)}) collective-permute-start(bf16[3,64,512]{2,1,0:T(8,128)(2,1)S(1)} %get-tuple-element.45), channel_id=1, source_target_pairs={{0,4},{1,5},{2,6},{3,7},{4,0},{5,1},{6,2},{7,3},{8,12},{9,13},{10,... | collective-permute-start | bytes 589832 | tf_op jit(solution)/shard_map/ppermute | solution.py:194
  32.0 1.3 %collective-permute-done.5.rest_4_ = bf16[3,64,512]{2,1,0:T(8,128)(2,1)S(1)} collective-permute-done((bf16[3,64,512]{2,1,0:T(8,128)(2,1)S(1)}, bf16[3,64,512]{2,1,0:T(8,128)(2,1)S(1)}, u32[]{:S(2)}, u32[]{:S(2)}) %collective-permute-start.5) | collective-permute-done | bytes 196640 | tf_op jit(solution)/shard_map/ppermute | solution.py:194
  34.0 3.1 %collective-permute-start.14 = (bf16[3,64,512]{2,1,0:T(8,128)(2,1)}, bf16[3,64,512]{2,1,0:T(8,128)(2,1)}, u32[]{:S(2)}, u32[]{:S(2)}) collective-permute-start(bf16[3,64,512]{2,1,0:T(8,128)(2,1)} %get-tuple-element.47), channel_id=1, source_target_pairs={{0,5},{1,4},{2,7},{3,6},{4,1},{5,0},{6,3},{7,2},{8,13},{9,12},{10,... | collective-permute-start | bytes 589832 | tf_op jit(solution)/shard_map/ppermute | solution.py:194
  37.8 4.5 %collective-permute-start.15 = (bf16[3,64,512]{2,1,0:T(8,128)(2,1)}, bf16[3,64,512]{2,1,0:T(8,128)(2,1)}, u32[]{:S(2)}, u32[]{:S(2)}) collective-permute-start(bf16[3,64,512]{2,1,0:T(8,128)(2,1)} %get-tuple-element.48), channel_id=1, source_target_pairs={{0,2},{1,3},{2,0},{3,1},{4,6},{5,7},{6,4},{7,5},{8,10},{9,11},{10,... | collective-permute-start | bytes 589832 | tf_op jit(solution)/shard_map/ppermute | solution.py:194
  42.2 11.8 %collective-permute-done.7.rest_6_ = bf16[3,64,512]{2,1,0:T(8,128)(2,1)S(1)} collective-permute-done((bf16[3,64,512]{2,1,0:T(8,128)(2,1)S(1)}, bf16[3,64,512]{2,1,0:T(8,128)(2,1)S(1)}, u32[]{:S(2)}, u32[]{:S(2)}) %collective-permute-start.7) | collective-permute-done | bytes 196640 | tf_op jit(solution)/shard_map/ppermute | solution.py:194
  54.8 0.9 collective-permute-start.16
  56.4 5.5 %collective-permute-start.17 = (bf16[3,64,512]{2,1,0:T(8,128)(2,1)}, bf16[3,64,512]{2,1,0:T(8,128)(2,1)}, u32[]{:S(2)}, u32[]{:S(2)}) collective-permute-start(bf16[3,64,512]{2,1,0:T(8,128)(2,1)} %get-tuple-element.50), channel_id=1, source_target_pairs={{0,3},{1,2},{2,1},{3,0},{4,7},{5,6},{6,5},{7,4},{8,11},{9,10},{10,... | collective-permute-start | bytes 589832 | tf_op jit(solution)/shard_map/ppermute | solution.py:194
  62.6 2.8 %collective-permute-start.18 = (bf16[3,64,512]{2,1,0:T(8,128)(2,1)}, bf16[3,64,512]{2,1,0:T(8,128)(2,1)}, u32[]{:S(2)}, u32[]{:S(2)}) collective-permute-start(bf16[3,64,512]{2,1,0:T(8,128)(2,1)} %get-tuple-element.51), channel_id=1, source_target_pairs={{0,7},{1,6},{2,5},{3,4},{4,3},{5,2},{6,1},{7,0},{8,15},{9,14},{10,... | collective-permute-start | bytes 589832 | tf_op jit(solution)/shard_map/ppermute | solution.py:194
  65.4 0.9 copy-done.3
  66.4 0.9 copy-done.7
  67.3 0.9 copy-done.11
  68.2 0.9 copy-done.13
  69.1 0.9 copy-done.15
  70.1 3.1 %attend.2 = (bf16[1,64,512]{2,1,0:T(8,128)(2,1)S(1)}, bf16[1,64,512]{2,1,0:T(8,128)(2,1)S(1)}, bf16[1,64,512]{2,1,0:T(8,128)(2,1)S(1)}, bf16[1,64,512]{2,1,0:T(8...) custom-call(bf16[4,512]{1,0:T(4,128)(2,1)S(1)} %dynamic-slice_add_fu, ...), custom_call_target="tpu_custom_call" | custom-call | flops 536870912 | bytes 2097152 | tf_op jit(solution)/shard_map/attend/pallas_call | solution.py:147
  73.8 2.1 %collective-permute-start.9 = (bf16[1,64,512]{2,1,0:T(8,128)(2,1)S(1)}, bf16[1,64,512]{2,1,0:T(8,128)(2,1)S(1)}, u32[]{:S(2)}, u32[]{:S(2)}) collective-permute-start(bf16[1,64,512]{2,1,0:T(8,128)(2,1)S(1)} %get-tuple-element.42), channel_id=1, source_target_pairs={{0,5},{1,4},{2,7},{3,6},{4,1},{5,0},{6,3},{7,2},{8,13},{9,12},{10,... | collective-permute-start | bytes 196616 | tf_op jit(solution)/shard_map/ppermute | solution.py:194
  75.9 0.9 collective-permute-start.10
  76.8 2.6 %collective-permute-start.11 = (bf16[1,64,512]{2,1,0:T(8,128)(2,1)S(1)}, bf16[1,64,512]{2,1,0:T(8,128)(2,1)S(1)}, u32[]{:S(2)}, u32[]{:S(2)}) collective-permute-start(bf16[1,64,512]{2,1,0:T(8,128)(2,1)S(1)} %get-tuple-element.44), channel_id=1, source_target_pairs={{0,7},{1,6},{2,5},{3,4},{4,3},{5,2},{6,1},{7,0},{8,15},{9,14},{10,... | collective-permute-start | bytes 196616 | tf_op jit(solution)/shard_map/ppermute | solution.py:194
  79.4 4.3 %attend.3 = (bf16[2,64,512]{2,1,0:T(8,128)(2,1)S(1)}, bf16[2,64,512]{2,1,0:T(8,128)(2,1)S(1)}, bf16[2,64,512]{2,1,0:T(8,128)(2,1)S(1)}, bf16[2,64,512]{2,1,0:T(8...) custom-call(bf16[4,512]{1,0:T(4,128)(2,1)S(1)} %dynamic-slice_add_fu, ...), custom_call_target="tpu_custom_call" | custom-call | flops 536870912 | bytes 2097152 | tf_op jit(solution)/shard_map/attend/pallas_call | solution.py:147
  83.8 6.6 %collective-permute-start.19 = (bf16[1,64,512]{2,1,0:T(8,128)(2,1)S(1)}, bf16[1,64,512]{2,1,0:T(8,128)(2,1)S(1)}, u32[]{:S(2)}, u32[]{:S(2)}) collective-permute-start(bf16[1,64,512]{2,1,0:T(8,128)(2,1)S(1)} %get-tuple-element.56), channel_id=1, source_target_pairs={{0,4},{1,5},{2,6},{3,7},{4,0},{5,1},{6,2},{7,3},{8,12},{9,13},{10,... | collective-permute-start | bytes 196616 | tf_op jit(solution)/shard_map/ppermute | solution.py:194
  90.7 1.2 %collective-permute-start.24 = (bf16[2,64,512]{2,1,0:T(8,128)(2,1)S(1)}, bf16[2,64,512]{2,1,0:T(8,128)(2,1)S(1)}, u32[]{:S(2)}, u32[]{:S(2)}) collective-permute-start(bf16[2,64,512]{2,1,0:T(8,128)(2,1)S(1)} %get-tuple-element.61), channel_id=1, source_target_pairs={{0,3},{1,2},{2,1},{3,0},{4,7},{5,6},{6,5},{7,4},{8,11},{9,10},{10,... | collective-permute-start | bytes 393224 | tf_op jit(solution)/shard_map/ppermute | solution.py:194
  92.6 3.2 %collective-permute-done.19.rest_4_ = bf16[1,64,512]{2,1,0:T(8,128)(2,1)S(1)} collective-permute-done((bf16[1,64,512]{2,1,0:T(8,128)(2,1)S(1)}, bf16[1,64,512]{2,1,0:T(8,128)(2,1)S(1)}, u32[]{:S(2)}, u32[]{:S(2)}) %collective-permute-start.19) | collective-permute-done | bytes 65568 | tf_op jit(solution)/shard_map/ppermute | solution.py:194
  95.8 1.2 %collective-permute-done.20.rest_5_ = bf16[1,64,512]{2,1,0:T(8,128)(2,1)S(1)} collective-permute-done((bf16[1,64,512]{2,1,0:T(8,128)(2,1)S(1)}, bf16[1,64,512]{2,1,0:T(8,128)(2,1)S(1)}, u32[]{:S(2)}, u32[]{:S(2)}) %collective-permute-start.20) | collective-permute-done | bytes 65568 | tf_op jit(solution)/shard_map/ppermute | solution.py:194
  96.9 1.8 %collective-permute-start.22 = (bf16[1,64,512]{2,1,0:T(8,128)(2,1)S(1)}, bf16[1,64,512]{2,1,0:T(8,128)(2,1)S(1)}, u32[]{:S(2)}, u32[]{:S(2)}) collective-permute-start(bf16[1,64,512]{2,1,0:T(8,128)(2,1)S(1)} %get-tuple-element.59), channel_id=1, source_target_pairs={{0,7},{1,6},{2,5},{3,4},{4,3},{5,2},{6,1},{7,0},{8,15},{9,14},{10,... | collective-permute-start | bytes 196616 | tf_op jit(solution)/shard_map/ppermute | solution.py:194
  98.8 4.1 %collective-permute-done.21.rest_6_ = bf16[1,64,512]{2,1,0:T(8,128)(2,1)S(1)} collective-permute-done((bf16[1,64,512]{2,1,0:T(8,128)(2,1)S(1)}, bf16[1,64,512]{2,1,0:T(8,128)(2,1)S(1)}, u32[]{:S(2)}, u32[]{:S(2)}) %collective-permute-start.21) | collective-permute-done | bytes 65568 | tf_op jit(solution)/shard_map/ppermute | solution.py:194
  103.7 1.1 %unpack.1 = bf16[1,2,64,4096]{3,2,1,0:T(8,128)(2,1)} custom-call(bf16[1,64,512]{2,1,0:T(8,128)(2,1)S(1)} %collective-permute-done.8.rest_0_, bf16[1,64,512]{2,1,0:T(8,128)(2,1)S(1)} %collective-permute-done.9.rest_1_, bf16[1,64,512]{2,1,0:T(8,128)(2,1)S(1)} %collective-permute-done.10.rest_2_, bf16[1,64,512]{2,1,0:T(8,128)(2,1)S(1)} %collective-permute-done.11.rest_3_, ...), custom_call_target="tpu_custom_call" | custom-call | tf_op jit(solution)/shard_map/unpack/pallas_call | solution.py:179
  (59 shorter events, 8.0 us)
Async XLA Ops:
  0.6 1.9 %copy-start = (bf16[3,1,2,64,4096]{4,3,2,1,0:T(8,128)(2,1)S(1)}, bf16[3,1,2,64,4096]{4,3,2,1,0:T(8,128)(2,1)}, u32[]{:S(2)}) copy-start(bf16[3,1,2,64,4096]{4,3,2,1,0:T(8,128)(2,1)} %qkv.3) | copy-start | bytes 9437188
  2.5 10.5 %copy-start.1 = (bf16[3,1,2,64,4096]{4,3,2,1,0:T(8,128)(2,1)S(1)}, bf16[3,1,2,64,4096]{4,3,2,1,0:T(8,128)(2,1)}, u32[]{:S(2)}) copy-start(bf16[3,1,2,64,4096]{4,3,2,1,0:T(8,128)(2,1)} %qkv.3) | copy-start | bytes 9437188
  2.8 22.4 %collective-permute-start.1 = (bf16[3,64,512]{2,1,0:T(8,128)(2,1)S(1)}, bf16[3,64,512]{2,1,0:T(8,128)(2,1)S(1)}, u32[]{:S(2)}, u32[]{:S(2)}) collective-permute-start(bf16[3,64,512]{2,1,0:T(8,128)(2,1)S(1)} %get-tuple-element.34), channel_id=1, source_target_pairs={{0,6},{1,7},{2,4},{3,5},{4,2},{5,3},{6,0},{7,1},{8,14},{9,15},{10,... | collective-permute-start | bytes 589832 | tf_op jit(solution)/shard_map/ppermute | solution.py:194
  7.9 20.0 %collective-permute-start.2 = (bf16[3,64,512]{2,1,0:T(8,128)(2,1)S(1)}, bf16[3,64,512]{2,1,0:T(8,128)(2,1)S(1)}, u32[]{:S(2)}, u32[]{:S(2)}) collective-permute-start(bf16[3,64,512]{2,1,0:T(8,128)(2,1)S(1)} %get-tuple-element.35), channel_id=1, source_target_pairs={{0,1},{1,0},{2,3},{3,2},{4,5},{5,4},{6,7},{7,6},{8,9},{9,8},{10,11... | collective-permute-start | bytes 589832 | tf_op jit(solution)/shard_map/ppermute | solution.py:194
  7.9 20.0 %collective-permute-start.3 = (bf16[3,64,512]{2,1,0:T(8,128)(2,1)S(1)}, bf16[3,64,512]{2,1,0:T(8,128)(2,1)S(1)}, u32[]{:S(2)}, u32[]{:S(2)}) collective-permute-start(bf16[3,64,512]{2,1,0:T(8,128)(2,1)S(1)} %get-tuple-element.36), channel_id=1, source_target_pairs={{0,7},{1,6},{2,5},{3,4},{4,3},{5,2},{6,1},{7,0},{8,15},{9,14},{10,... | collective-permute-start | bytes 589832 | tf_op jit(solution)/shard_map/ppermute | solution.py:194
  8.1 23.2 %collective-permute-start.4 = (bf16[3,64,512]{2,1,0:T(8,128)(2,1)S(1)}, bf16[3,64,512]{2,1,0:T(8,128)(2,1)S(1)}, u32[]{:S(2)}, u32[]{:S(2)}) collective-permute-start(bf16[3,64,512]{2,1,0:T(8,128)(2,1)S(1)} %get-tuple-element.37), channel_id=1, source_target_pairs={{0,2},{1,3},{2,0},{3,1},{4,6},{5,7},{6,4},{7,5},{8,10},{9,11},{10,... | collective-permute-start | bytes 589832 | tf_op jit(solution)/shard_map/ppermute | solution.py:194
  9.5 4.9 %collective-permute-start = (bf16[4,1024]{1,0:T(4,128)(2,1)S(1)}, bf16[4,1024]{1,0:T(4,128)(2,1)S(1)}, u32[]{:S(2)}, u32[]{:S(2)}) collective-permute-start(bf16[4,1024]{1,0:T(4,128)(2,1)S(1)} %get-tuple-element.64), channel_id=1, source_target_pairs={{0,8},{1,16},{2,24},{3,9},{4,17},{5,25},{8,2},{9,18},{10,26},{11,3... | collective-permute-start | bytes 24584 | tf_op jit(solution)/shard_map/ppermute | solution.py:55
  14.4 18.9 %collective-permute-start.5 = (bf16[3,64,512]{2,1,0:T(8,128)(2,1)S(1)}, bf16[3,64,512]{2,1,0:T(8,128)(2,1)S(1)}, u32[]{:S(2)}, u32[]{:S(2)}) collective-permute-start(bf16[3,64,512]{2,1,0:T(8,128)(2,1)S(1)} %get-tuple-element.38), channel_id=1, source_target_pairs={{0,4},{1,5},{2,6},{3,7},{4,0},{5,1},{6,2},{7,3},{8,12},{9,13},{10,... | collective-permute-start | bytes 589832 | tf_op jit(solution)/shard_map/ppermute | solution.py:194
  25.2 11.9 %collective-permute-start.6 = (bf16[3,64,512]{2,1,0:T(8,128)(2,1)S(1)}, bf16[3,64,512]{2,1,0:T(8,128)(2,1)S(1)}, u32[]{:S(2)}, u32[]{:S(2)}) collective-permute-start(bf16[3,64,512]{2,1,0:T(8,128)(2,1)S(1)} %get-tuple-element.39), channel_id=1, source_target_pairs={{0,3},{1,2},{2,1},{3,0},{4,7},{5,6},{6,5},{7,4},{8,11},{9,10},{10,... | collective-permute-start | bytes 589832 | tf_op jit(solution)/shard_map/ppermute | solution.py:194
  27.9 26.2 %collective-permute-start.7 = (bf16[3,64,512]{2,1,0:T(8,128)(2,1)S(1)}, bf16[3,64,512]{2,1,0:T(8,128)(2,1)S(1)}, u32[]{:S(2)}, u32[]{:S(2)}) collective-permute-start(bf16[3,64,512]{2,1,0:T(8,128)(2,1)S(1)} %get-tuple-element.40), channel_id=1, source_target_pairs={{0,5},{1,4},{2,7},{3,6},{4,1},{5,0},{6,3},{7,2},{8,13},{9,12},{10,... | collective-permute-start | bytes 589832 | tf_op jit(solution)/shard_map/ppermute | solution.py:194
  28.6 27.1 %collective-permute-start.12 = (bf16[3,64,512]{2,1,0:T(8,128)(2,1)S(1)}, bf16[3,64,512]{2,1,0:T(8,128)(2,1)S(1)}, u32[]{:S(2)}, u32[]{:S(2)}) collective-permute-start(bf16[3,64,512]{2,1,0:T(8,128)(2,1)S(1)} %get-tuple-element.45), channel_id=1, source_target_pairs={{0,4},{1,5},{2,6},{3,7},{4,0},{5,1},{6,2},{7,3},{8,12},{9,13},{10,... | collective-permute-start | bytes 589832 | tf_op jit(solution)/shard_map/ppermute | solution.py:194
  32.0 30.0 %collective-permute-start.13 = (bf16[3,64,512]{2,1,0:T(8,128)(2,1)S(1)}, bf16[3,64,512]{2,1,0:T(8,128)(2,1)S(1)}, u32[]{:S(2)}, u32[]{:S(2)}) collective-permute-start(bf16[3,64,512]{2,1,0:T(8,128)(2,1)S(1)} %get-tuple-element.46), channel_id=1, source_target_pairs={{0,1},{1,0},{2,3},{3,2},{4,5},{5,4},{6,7},{7,6},{8,9},{9,8},{10,11... | collective-permute-start | bytes 589832 | tf_op jit(solution)/shard_map/ppermute | solution.py:194
  34.0 39.2 %collective-permute-start.14 = (bf16[3,64,512]{2,1,0:T(8,128)(2,1)}, bf16[3,64,512]{2,1,0:T(8,128)(2,1)}, u32[]{:S(2)}, u32[]{:S(2)}) collective-permute-start(bf16[3,64,512]{2,1,0:T(8,128)(2,1)} %get-tuple-element.47), channel_id=1, source_target_pairs={{0,5},{1,4},{2,7},{3,6},{4,1},{5,0},{6,3},{7,2},{8,13},{9,12},{10,... | collective-permute-start | bytes 589832 | tf_op jit(solution)/shard_map/ppermute | solution.py:194
  37.8 36.0 %collective-permute-start.15 = (bf16[3,64,512]{2,1,0:T(8,128)(2,1)}, bf16[3,64,512]{2,1,0:T(8,128)(2,1)}, u32[]{:S(2)}, u32[]{:S(2)}) collective-permute-start(bf16[3,64,512]{2,1,0:T(8,128)(2,1)} %get-tuple-element.48), channel_id=1, source_target_pairs={{0,2},{1,3},{2,0},{3,1},{4,6},{5,7},{6,4},{7,5},{8,10},{9,11},{10,... | collective-permute-start | bytes 589832 | tf_op jit(solution)/shard_map/ppermute | solution.py:194
  54.8 21.2 %collective-permute-start.16 = (bf16[3,64,512]{2,1,0:T(8,128)(2,1)}, bf16[3,64,512]{2,1,0:T(8,128)(2,1)}, u32[]{:S(2)}, u32[]{:S(2)}) collective-permute-start(bf16[3,64,512]{2,1,0:T(8,128)(2,1)} %get-tuple-element.49), channel_id=1, source_target_pairs={{0,6},{1,7},{2,4},{3,5},{4,2},{5,3},{6,0},{7,1},{8,14},{9,15},{10,... | collective-permute-start | bytes 589832 | tf_op jit(solution)/shard_map/ppermute | solution.py:194
  56.4 20.4 %collective-permute-start.17 = (bf16[3,64,512]{2,1,0:T(8,128)(2,1)}, bf16[3,64,512]{2,1,0:T(8,128)(2,1)}, u32[]{:S(2)}, u32[]{:S(2)}) collective-permute-start(bf16[3,64,512]{2,1,0:T(8,128)(2,1)} %get-tuple-element.50), channel_id=1, source_target_pairs={{0,3},{1,2},{2,1},{3,0},{4,7},{5,6},{6,5},{7,4},{8,11},{9,10},{10,... | collective-permute-start | bytes 589832 | tf_op jit(solution)/shard_map/ppermute | solution.py:194
  62.6 16.8 %collective-permute-start.18 = (bf16[3,64,512]{2,1,0:T(8,128)(2,1)}, bf16[3,64,512]{2,1,0:T(8,128)(2,1)}, u32[]{:S(2)}, u32[]{:S(2)}) collective-permute-start(bf16[3,64,512]{2,1,0:T(8,128)(2,1)} %get-tuple-element.51), channel_id=1, source_target_pairs={{0,7},{1,6},{2,5},{3,4},{4,3},{5,2},{6,1},{7,0},{8,15},{9,14},{10,... | collective-permute-start | bytes 589832 | tf_op jit(solution)/shard_map/ppermute | solution.py:194
  65.4 0.9 copy-start.3
  66.4 0.9 copy-start.7
  70.1 9.4 %copy-start.5 = (bf16[3,64,512]{2,1,0:T(8,128)(2,1)S(1)}, bf16[3,64,512]{2,1,0:T(8,128)(2,1)}, u32[]{:S(2)}) copy-start(bf16[3,64,512]{2,1,0:T(8,128)(2,1)} %copy-done.4) | copy-start | bytes 589828
  70.1 9.4 %copy-start.9 = (bf16[3,64,512]{2,1,0:T(8,128)(2,1)S(1)}, bf16[3,64,512]{2,1,0:T(8,128)(2,1)}, u32[]{:S(2)}) copy-start(bf16[3,64,512]{2,1,0:T(8,128)(2,1)} %copy-done.8) | copy-start | bytes 589828
  73.1 17.2 %collective-permute-start.8 = (bf16[1,64,512]{2,1,0:T(8,128)(2,1)S(1)}, bf16[1,64,512]{2,1,0:T(8,128)(2,1)S(1)}, u32[]{:S(2)}, u32[]{:S(2)}) collective-permute-start(bf16[1,64,512]{2,1,0:T(8,128)(2,1)S(1)} %get-tuple-element.41), channel_id=1, source_target_pairs={{0,4},{1,5},{2,6},{3,7},{4,0},{5,1},{6,2},{7,3},{8,12},{9,13},{10,... | collective-permute-start | bytes 196616 | tf_op jit(solution)/shard_map/ppermute | solution.py:194
  73.8 16.6 %collective-permute-start.9 = (bf16[1,64,512]{2,1,0:T(8,128)(2,1)S(1)}, bf16[1,64,512]{2,1,0:T(8,128)(2,1)S(1)}, u32[]{:S(2)}, u32[]{:S(2)}) collective-permute-start(bf16[1,64,512]{2,1,0:T(8,128)(2,1)S(1)} %get-tuple-element.42), channel_id=1, source_target_pairs={{0,5},{1,4},{2,7},{3,6},{4,1},{5,0},{6,3},{7,2},{8,13},{9,12},{10,... | collective-permute-start | bytes 196616 | tf_op jit(solution)/shard_map/ppermute | solution.py:194
  75.9 14.8 %collective-permute-start.10 = (bf16[1,64,512]{2,1,0:T(8,128)(2,1)S(1)}, bf16[1,64,512]{2,1,0:T(8,128)(2,1)S(1)}, u32[]{:S(2)}, u32[]{:S(2)}) collective-permute-start(bf16[1,64,512]{2,1,0:T(8,128)(2,1)S(1)} %get-tuple-element.43), channel_id=1, source_target_pairs={{0,6},{1,7},{2,4},{3,5},{4,2},{5,3},{6,0},{7,1},{8,14},{9,15},{10,... | collective-permute-start | bytes 196616 | tf_op jit(solution)/shard_map/ppermute | solution.py:194
  76.8 15.1 %collective-permute-start.11 = (bf16[1,64,512]{2,1,0:T(8,128)(2,1)S(1)}, bf16[1,64,512]{2,1,0:T(8,128)(2,1)S(1)}, u32[]{:S(2)}, u32[]{:S(2)}) collective-permute-start(bf16[1,64,512]{2,1,0:T(8,128)(2,1)S(1)} %get-tuple-element.44), channel_id=1, source_target_pairs={{0,7},{1,6},{2,5},{3,4},{4,3},{5,2},{6,1},{7,0},{8,15},{9,14},{10,... | collective-permute-start | bytes 196616 | tf_op jit(solution)/shard_map/ppermute | solution.py:194
  83.8 12.0 %collective-permute-start.19 = (bf16[1,64,512]{2,1,0:T(8,128)(2,1)S(1)}, bf16[1,64,512]{2,1,0:T(8,128)(2,1)S(1)}, u32[]{:S(2)}, u32[]{:S(2)}) collective-permute-start(bf16[1,64,512]{2,1,0:T(8,128)(2,1)S(1)} %get-tuple-element.56), channel_id=1, source_target_pairs={{0,4},{1,5},{2,6},{3,7},{4,0},{5,1},{6,2},{7,3},{8,12},{9,13},{10,... | collective-permute-start | bytes 196616 | tf_op jit(solution)/shard_map/ppermute | solution.py:194
  90.4 6.6 %collective-permute-start.20 = (bf16[1,64,512]{2,1,0:T(8,128)(2,1)S(1)}, bf16[1,64,512]{2,1,0:T(8,128)(2,1)S(1)}, u32[]{:S(2)}, u32[]{:S(2)}) collective-permute-start(bf16[1,64,512]{2,1,0:T(8,128)(2,1)S(1)} %get-tuple-element.57), channel_id=1, source_target_pairs={{0,5},{1,4},{2,7},{3,6},{4,1},{5,0},{6,3},{7,2},{8,13},{9,12},{10,... | collective-permute-start | bytes 196616 | tf_op jit(solution)/shard_map/ppermute | solution.py:194
  90.4 13.3 %collective-permute-start.23 = (bf16[2,64,512]{2,1,0:T(8,128)(2,1)S(1)}, bf16[2,64,512]{2,1,0:T(8,128)(2,1)S(1)}, u32[]{:S(2)}, u32[]{:S(2)}) collective-permute-start(bf16[2,64,512]{2,1,0:T(8,128)(2,1)S(1)} %get-tuple-element.60), channel_id=1, source_target_pairs={{0,2},{1,3},{2,0},{3,1},{4,6},{5,7},{6,4},{7,5},{8,10},{9,11},{10,... | collective-permute-start | bytes 393224 | tf_op jit(solution)/shard_map/ppermute | solution.py:194
  90.7 13.0 %collective-permute-start.24 = (bf16[2,64,512]{2,1,0:T(8,128)(2,1)S(1)}, bf16[2,64,512]{2,1,0:T(8,128)(2,1)S(1)}, u32[]{:S(2)}, u32[]{:S(2)}) collective-permute-start(bf16[2,64,512]{2,1,0:T(8,128)(2,1)S(1)} %get-tuple-element.61), channel_id=1, source_target_pairs={{0,3},{1,2},{2,1},{3,0},{4,7},{5,6},{6,5},{7,4},{8,11},{9,10},{10,... | collective-permute-start | bytes 393224 | tf_op jit(solution)/shard_map/ppermute | solution.py:194
  92.0 11.8 %collective-permute-start.25 = (bf16[2,64,512]{2,1,0:T(8,128)(2,1)S(1)}, bf16[2,64,512]{2,1,0:T(8,128)(2,1)S(1)}, u32[]{:S(2)}, u32[]{:S(2)}) collective-permute-start(bf16[2,64,512]{2,1,0:T(8,128)(2,1)S(1)} %get-tuple-element.62), channel_id=1, source_target_pairs={{0,1},{1,0},{2,3},{3,2},{4,5},{5,4},{6,7},{7,6},{8,9},{9,8},{10,11... | collective-permute-start | bytes 393224 | tf_op jit(solution)/shard_map/ppermute | solution.py:194
  95.8 7.1 %collective-permute-start.21 = (bf16[1,64,512]{2,1,0:T(8,128)(2,1)S(1)}, bf16[1,64,512]{2,1,0:T(8,128)(2,1)S(1)}, u32[]{:S(2)}, u32[]{:S(2)}) collective-permute-start(bf16[1,64,512]{2,1,0:T(8,128)(2,1)S(1)} %get-tuple-element.58), channel_id=1, source_target_pairs={{0,6},{1,7},{2,4},{3,5},{4,2},{5,3},{6,0},{7,1},{8,14},{9,15},{10,... | collective-permute-start | bytes 196616 | tf_op jit(solution)/shard_map/ppermute | solution.py:194
  96.9 6.8 %collective-permute-start.22 = (bf16[1,64,512]{2,1,0:T(8,128)(2,1)S(1)}, bf16[1,64,512]{2,1,0:T(8,128)(2,1)S(1)}, u32[]{:S(2)}, u32[]{:S(2)}) collective-permute-start(bf16[1,64,512]{2,1,0:T(8,128)(2,1)S(1)} %get-tuple-element.59), channel_id=1, source_target_pairs={{0,7},{1,6},{2,5},{3,4},{4,3},{5,2},{6,1},{7,0},{8,15},{9,14},{10,... | collective-permute-start | bytes 196616 | tf_op jit(solution)/shard_map/ppermute | solution.py:194
  (10 other events, 7.5 us)

commit v5 on v4

v5 whole, which is shorter than its diff:
```python
import functools

import jax
import jax.numpy as jnp
from jax import lax
from jax.experimental import pallas as pl
from jax.experimental.pallas import tpu as pltpu
from jax.sharding import PartitionSpec as P

HEADS = 32
HD = 128
OPT_STEP = 10

BETA_ONE = 0.9
BETA_TWO = 0.95
RATE = 0.02
DECAY = 0.1
EPSILON = 1e-08

LOG2E = 1.4426950408889634
ANY = pl.BlockSpec(memory_space=pl.ANY)
HBM = pl.BlockSpec(memory_space=pltpu.HBM)
VMEM = pl.BlockSpec(memory_space=pltpu.VMEM)


def adamw(master, moment_one, moment_two, grads):
    first_moment = BETA_ONE * moment_one + (1.0 - BETA_ONE) * grads
    second_moment = BETA_TWO * moment_two + (1.0 - BETA_TWO) * grads * grads
    first_hat = first_moment / (1.0 - BETA_ONE**OPT_STEP)
    second_hat = second_moment / (1.0 - BETA_TWO**OPT_STEP)
    updated = master - RATE * (first_hat / (jnp.sqrt(second_hat) + EPSILON) + DECAY * master)
    return (updated, first_moment, second_moment)


def own_columns(layer, dp_count, seq_count, width):
    shard_cols = layer.shape[1]
    assert shard_cols % width == 0
    rounds = []
    for owner in range(dp_count):
        wanted = [
            (dp, seq)
            for seq in range(seq_count)
            if seq * width // shard_cols == owner
            for dp in range(dp_count)
            if dp != owner
        ]
        for place, (dp, seq) in enumerate(wanted):
            turn, source = divmod(place, seq_count)
            while len(rounds) <= turn:
                rounds.append([])
            rounds[turn].append((owner * seq_count + source, dp * seq_count + seq))
    first_col = lax.axis_index("seq") * width
    mine = lax.axis_index("dp") == first_col // shard_cols
    found = jnp.where(mine, layer, jnp.zeros_like(layer))
    for pairs in rounds:
        found = found + lax.ppermute(layer, ("dp", "seq"), pairs)
    return lax.dynamic_slice_in_dim(found, first_col % shard_cols, width, 1)


def spans(chunk):
    runs = []
    for place, (sample, head) in enumerate(chunk):
        if runs and runs[-1][0] == sample and runs[-1][1] + runs[-1][2] == head:
            runs[-1][2] += 1
        else:
            runs.append([sample, head, 1, place])
    return [
        (sample, first * HD, slice(place * HD, (place + count) * HD), count * HD)
        for sample, first, count, place in runs
    ]


def pack_kernel(chunk, slots, width, source, *rest):
    outs, sems = rest[:-1], rest[-1]
    me = lax.axis_index("seq")
    copies = []
    for out, slot in zip(outs, slots, strict=True):
        for sample, first, cols, size in spans(chunk):
            start = pl.multiple_of(lax.bitwise_xor(me, slot) * width + first, HD)
            part = source.at[:, 0, sample, :, pl.ds(start, size)]
            copies.append(pltpu.make_async_copy(part, out.at[:, :, cols], sems.at[len(copies)]))
    for copy in copies:
        copy.start()
    for copy in copies:
        copy.wait()


def pack(qkv, chunk, slots, width):
    shape = jax.ShapeDtypeStruct((3, qkv.shape[3], len(chunk) * HD), qkv.dtype)
    count = len(slots) * len(spans(chunk))
    return pl.pallas_call(
        functools.partial(pack_kernel, chunk, slots, width),
        out_shape=[shape] * len(slots),
        in_specs=[HBM],
        out_specs=[VMEM] * len(slots),
        scratch_shapes=[pltpu.SemaphoreType.DMA((count,))],
        compiler_params=pltpu.CompilerParams(vmem_limit_bytes=62 * 1024 * 1024),
        name="pack",
    )(qkv)


def normed(rows, gain, bias):
    grouped = rows.astype(jnp.float32)
    centred = grouped - jnp.mean(grouped, axis=-1, keepdims=True)
    spread = jnp.mean(centred * centred, axis=-1, keepdims=True)
    return (centred * lax.rsqrt(spread + 1e-06) * gain + bias).astype(jnp.bfloat16)


def attend_kernel(chunk, slots, width, fetch, layer, qkv, *rest):
    count = len(slots)
    half = count // 2
    landed, rest = dict(zip(slots[:-1], rest[: count - 1], strict=True)), rest[count - 1 :]
    held, sems = rest[-2:]
    outs = rest[-2 - count : -2]
    given = rest[: -2 - count]
    rows = held.shape[2]
    copies = []
    own = lax.axis_index("seq") * width
    for sample, first, cols, size in spans(chunk):
        start = pl.multiple_of(own + first, HD)
        part = qkv.at[:, 0, sample, :, pl.ds(start, size)]
        copies.append(pltpu.make_async_copy(part, held.at[0, :, :, cols], sems.at[len(copies)]))
    if fetch:
        for slot in range(1, count):
            copies.append(pltpu.make_async_copy(landed[slot], held.at[slot], sems.at[len(copies)]))
            landed[slot] = held.at[slot]
    landed[0] = held.at[0]
    for copy in copies:
        copy.start()
    done = 0
    for out, before in zip(outs, given):
        done = before.shape[1]
        out[:, :done] = before[...]
    if fetch:
        for copy in copies:
            copy.wait()
    for place, (_, head) in enumerate(chunk):
        cols = slice(place * HD, (place + 1) * HD)
        gains = layer[:, head * HD : (head + 1) * HD].astype(jnp.float32)
        others = [
            normed(landed[slot][1, :, cols], gains[2:3], gains[3:4]) for slot in range(1, count)
        ]
        if place == 0 and not fetch:
            for copy in copies:
                copy.wait()
        keys = jnp.concatenate([normed(landed[0][1, :, cols], gains[2:3], gains[3:4])] + others)
        values = jnp.concatenate([landed[slot][2, :, cols] for slot in range(count)])
        per_block = max(1, 512 // rows)
        for first in range(0, count, per_block):
            here = range(first, min(first + per_block, count))
            queries = jnp.concatenate(
                [normed(landed[slot][0, :, cols], gains[0:1], gains[1:2]) for slot in here]
            )
            scores = lax.dot_general(
                queries, keys, (((1,), (1,)), ((), ())), preferred_element_type=jnp.float32
            )
            top = jnp.max(scores, axis=-1, keepdims=True)
            raised = jnp.exp2((scores - top) * (HD**-0.5 * LOG2E))
            total = jnp.sum(raised, axis=-1, keepdims=True)
            probs = (raised * (1.0 / total)).astype(jnp.bfloat16)
            result = jnp.dot(probs, values, preferred_element_type=jnp.float32)
            result = result.astype(jnp.bfloat16)
            for turn, slot in enumerate(here):
                part = result[turn * rows : (turn + 1) * rows]
                if slot < half:
                    outs[slot][:, done + place * HD : done + (place + 1) * HD] = part
                else:
                    outs[slot][:, cols] = part


def attend(chunk, slots, width, fetch, layer, qkv, arrived, given):
    count = len(slots)
    half = count // 2
    _, rows, cols = arrived[0].shape
    patches = count * rows
    before = given[0].shape[1] if given else 0
    outs = pl.pallas_call(
        functools.partial(attend_kernel, chunk, slots, width, fetch),
        out_shape=[jax.ShapeDtypeStruct((rows, before + cols), jnp.bfloat16)] * half
        + [jax.ShapeDtypeStruct((rows, cols), jnp.bfloat16)] * half,
        in_specs=[VMEM, HBM]
        + [ANY if fetch else VMEM] * (count - 1)
        + [VMEM] * len(given),
        out_specs=[VMEM] * count,
        scratch_shapes=[
            pltpu.VMEM((count if fetch else 1, 3, rows, cols), jnp.bfloat16),
            pltpu.SemaphoreType.DMA((len(spans(chunk)) + count,)),
        ],
        compiler_params=pltpu.CompilerParams(vmem_limit_bytes=16 * 1024 * 1024),
        cost_estimate=pl.CostEstimate(
            flops=4 * patches * patches * cols,
            bytes_accessed=8 * patches * cols,
            transcendentals=patches * patches * len(chunk),
        ),
        name="attend",
    )(layer, qkv, *arrived, *given)
    return list(outs[:half]), list(outs[half:])


def unpack_kernel(places, width, *rest):
    parts, out, sems = rest[: len(places)], rest[-2], rest[-1]
    me = lax.axis_index("seq")
    copies = []
    for part, (chunk, slot) in zip(parts, places, strict=True):
        for sample, first, cols, size in spans(chunk):
            start = pl.multiple_of(lax.bitwise_xor(me, slot) * width + first, HD)
            there = out.at[0, sample, :, pl.ds(start, size)]
            copies.append(pltpu.make_async_copy(part.at[:, cols], there, sems.at[len(copies)]))
    for copy in copies:
        copy.start()
    for copy in copies:
        copy.wait()


def unpack(parts, places, width, shape):
    return pl.pallas_call(
        functools.partial(unpack_kernel, places, width),
        out_shape=jax.ShapeDtypeStruct(shape, parts[0].dtype),
        in_specs=[VMEM] * len(parts),
        out_specs=ANY,
        scratch_shapes=[
            pltpu.SemaphoreType.DMA((sum(len(spans(chunk)) for chunk, _ in places),))
        ],
        compiler_params=pltpu.CompilerParams(vmem_limit_bytes=4 * 1024 * 1024),
        name="unpack",
    )(*parts)


def swap(part, slot):
    if slot == 0:
        return part
    return lax.ppermute(part, "seq", [(place, place ^ slot) for place in range(lax.axis_size("seq"))])


def mixed(one, other):
    return [slot for pair in zip(one, other, strict=True) for slot in pair]


def shards(dp_count, seq_count, qkv, master, moment_one, moment_two, grads):
    width = qkv.shape[4] // seq_count
    half = seq_count // 2
    far, near = list(range(half, seq_count)), list(range(1, half))
    turned = far[half // 2 :] + far[: half // 2]
    pairs = [(sample, head) for sample in range(qkv.shape[2]) for head in range(width // HD)]
    cut = len(pairs) - max(1, len(pairs) // 2)
    chunks = [pairs[:cut], pairs[cut:]]
    orders = [
        [turned[0], near[0], turned[1]] + mixed(turned[2:], near[1:]) + [0],
        mixed(far, near + [0]),
    ]
    landed = []
    for chunk, slots in zip(chunks, orders, strict=True):
        parts = []
        for some in [slots[:1], slots[1:-1]] if chunk is chunks[0] else [slots[:-1]]:
            parts += pack(qkv, chunk, some, width)
        landed.append([swap(part, slot) for part, slot in zip(parts, slots[:-1], strict=True)])
    updated, first_moment, second_moment = adamw(master, moment_one, moment_two, grads)
    layer = own_columns(updated.astype(jnp.bfloat16), dp_count, seq_count, width)
    parts, places, near_out = [], [], []
    for turn, (chunk, slots) in enumerate(zip(chunks, orders, strict=True)):
        near_out, far_out = attend(
            chunk, slots, width, turn == 0, layer, qkv, landed[turn], near_out
        )
        parts += [swap(out, slot) for out, slot in zip(far_out, far, strict=True)]
        places += [(chunk, slot) for slot in far]
    for slot in near[1:] + near[:1] + [0]:
        parts.append(swap(near_out[slot], slot))
        places.append((pairs, slot))
    attended = unpack(parts, places, width, (1, *qkv.shape[2:]))
    return (attended, updated, first_moment, second_moment)


def solution(mesh):
    placed = (
        P(None, "dp", None, "seq", None),
        P(None, "dp"),
        P(None, "dp"),
        P(None, "dp"),
        P(None, "dp"),
    )
    return jax.shard_map(
        functools.partial(shards, mesh.shape["dp"], mesh.shape["seq"]),
        mesh=mesh,
        in_specs=placed,
        out_specs=(P("dp", None, "seq", None), P(None, "dp"), P(None, "dp"), P(None, "dp")),
        check_vma=False,
    )
```

time: 105 us -> 102 us (0.971)
  starting transfers between devices: 58.8 us -> 78.1 us
  waiting for transfers between devices: 22.5 us -> 4.9 us
  local copies, waits for them, and re-layouts: 11.3 us -> 1.91 us
  Pallas kernels: 9.98 us -> 15.6 us
    ppermute x25, starting transfers between devices: 55.3 us -> 74.8 us  [swap(): lax.ppermute(part, 'seq', [(place, place ^ slot) for place in range(lax.a...]
    ppermute x25, waiting for transfers between devices: 22.4 us -> 4.9 us  [swap(): lax.ppermute(part, 'seq', [(place, place ^ slot) for place in range(lax.a...]
    unnamed x32 -> x16, local copies, waits for them, and re-layouts: 11.3 us -> 1.91 us
    pallas_call x5 -> x6, Pallas kernels: 9.98 us -> 15.6 us  [the longest x2 7.85 us: attend(): pl.pallas_call(functools.partial(attend_kernel, chunk, slots, width, fetc...]
  transfers between devices with their start and end apart: 26 -> 26, of which waited for: 7 -> 2; matrix products, arithmetic and copies ran while one was open for 1% -> 1% of each run, Pallas kernels for 8% -> 13%
where the time goes in v5:
time: 102 us
  starting transfers between devices  78.1 us (77%)
  Pallas kernels  15.6 us (15%)
  waiting for transfers between devices  4.9 us (5%)
  local copies, waits for them, and re-layouts  1.91 us (2%)
    ppermute x25, starting transfers between devices, swap(): lax.ppermute(part, 'seq', [(place, place ^ slot) for place in range(lax.a...  74.8 us
    pallas_call x2, Pallas kernels, attend(): pl.pallas_call(functools.partial(attend_kernel, chunk, slots, width, fetc...  7.85 us
    pallas_call x3, Pallas kernels, pack(): pl.pallas_call(functools.partial(pack_kernel, chunk, slots, width), out_s...  6.67 us
    ppermute x25, waiting for transfers between devices, swap(): lax.ppermute(part, 'seq', [(place, place ^ slot) for place in range(lax.a...  4.9 us
    ppermute x1, starting transfers between devices, own_columns(): found = found + lax.ppermute(layer, ('dp', 'seq'), pairs)  3.38 us
  transfers between devices with their start and end apart: 26, of which 2 were waited for; matrix products, arithmetic and copies ran while one was open for 1% of the time, Pallas kernels for 13%

profile of v5, /device:TPU:0, one launch (start us, length us, event | category | flops | bytes accessed | tf_op | source)
XLA Modules:
  0.0 102.1 jit_solution(2722531855146683941)
XLA Ops:
  0.7 1.6 %pack.3 = bf16[3,64,512]{2,1,0:T(8,128)(2,1)} custom-call(bf16[3,1,2,64,4096]{4,3,2,1,0:T(8,128)(2,1)} %qkv.3), custom_call_target="tpu_custom_call" | custom-call | tf_op jit(solution)/shard_map/pack/pallas_call | solution.py:91
  2.3 5.1 %collective-permute-start.1 = (bf16[3,64,512]{2,1,0:T(8,128)(2,1)}, bf16[3,64,512]{2,1,0:T(8,128)(2,1)S(1)}, u32[]{:S(2)}, u32[]{:S(2)}) collective-permute-start(bf16[3,64,512]{2,1,0:T(8,128)(2,1)} %pack.3), channel_id=1, source_target_pairs={{0,6},{1,7},{2,4},{3,5},{4,2},{5,3},{6,0},{7,1},{8,14},{9,15},{10,... | collective-permute-start | bytes 589832 | tf_op jit(solution)/shard_map/ppermute | solution.py:232
  7.4 2.4 %pack.4 = (bf16[3,64,512]{2,1,0:T(8,128)(2,1)}, bf16[3,64,512]{2,1,0:T(8,128)(2,1)}, bf16[3,64,512]{2,1,0:T(8,128)(2,1)}, bf16[3,64,512]{2,1,0:T(8,128)(2,1)}, b...) custom-call(bf16[3,1,2,64,4096]{4,3,2,1,0:T(8,128)(2,1)} %qkv.3), custom_call_target="tpu_custom_call" | custom-call | tf_op jit(solution)/shard_map/pack/pallas_call | solution.py:91
  10.1 1.0 collective-permute-start.4
  11.1 0.6 fusion.1
  11.8 3.4 %collective-permute-start = (bf16[4,1024]{1,0:T(4,128)(2,1)S(1)}, bf16[4,1024]{1,0:T(4,128)(2,1)S(1)}, u32[]{:S(2)}, u32[]{:S(2)}) collective-permute-start(bf16[4,1024]{1,0:T(4,128)(2,1)S(1)} %get-tuple-element.62), channel_id=1, source_target_pairs={{0,8},{1,16},{2,24},{3,9},{4,17},{5,25},{8,2},{9,18},{10,26},{11,3... | collective-permute-start | bytes 24584 | tf_op jit(solution)/shard_map/ppermute | solution.py:56
  15.2 2.6 %pack.5 = (bf16[3,64,512]{2,1,0:T(8,128)(2,1)}, bf16[3,64,512]{2,1,0:T(8,128)(2,1)}, bf16[3,64,512]{2,1,0:T(8,128)(2,1)}, bf16[3,64,512]{2,1,0:T(8,128)(2,1)}, b...) custom-call(bf16[3,1,2,64,4096]{4,3,2,1,0:T(8,128)(2,1)} %qkv.3), custom_call_target="tpu_custom_call" | custom-call | tf_op jit(solution)/shard_map/pack/pallas_call | solution.py:91
  17.8 6.1 %collective-permute-start.5 = (bf16[3,64,512]{2,1,0:T(8,128)(2,1)S(1)}, bf16[3,64,512]{2,1,0:T(8,128)(2,1)S(1)}, u32[]{:S(2)}, u32[]{:S(2)}) collective-permute-start(bf16[3,64,512]{2,1,0:T(8,128)(2,1)S(1)} %copy-done.7), channel_id=1, source_target_pairs={{0,2},{1,3},{2,0},{3,1},{4,6},{5,7},{6,4},{7,5},{8,10},{9,11},{10,... | collective-permute-start | bytes 589832 | tf_op jit(solution)/shard_map/ppermute | solution.py:232
  23.9 12.2 %collective-permute-start.6 = (bf16[3,64,512]{2,1,0:T(8,128)(2,1)S(1)}, bf16[3,64,512]{2,1,0:T(8,128)(2,1)S(1)}, u32[]{:S(2)}, u32[]{:S(2)}) collective-permute-start(bf16[3,64,512]{2,1,0:T(8,128)(2,1)S(1)} %copy-done.6), channel_id=1, source_target_pairs={{0,5},{1,4},{2,7},{3,6},{4,1},{5,0},{6,3},{7,2},{8,13},{9,12},{10,... | collective-permute-start | bytes 589832 | tf_op jit(solution)/shard_map/ppermute | solution.py:232
  36.1 0.4 collective-permute-start.12
  36.6 7.1 %collective-permute-start.14 = (bf16[3,64,512]{2,1,0:T(8,128)(2,1)}, bf16[3,64,512]{2,1,0:T(8,128)(2,1)S(1)}, u32[]{:S(2)}, u32[]{:S(2)}) collective-permute-start(bf16[3,64,512]{2,1,0:T(8,128)(2,1)} %get-tuple-element.45), channel_id=1, source_target_pairs={{0,5},{1,4},{2,7},{3,6},{4,1},{5,0},{6,3},{7,2},{8,13},{9,12},{10,... | collective-permute-start | bytes 589832 | tf_op jit(solution)/shard_map/ppermute | solution.py:232
  43.7 2.5 %collective-permute-start.15 = (bf16[3,64,512]{2,1,0:T(8,128)(2,1)}, bf16[3,64,512]{2,1,0:T(8,128)(2,1)S(1)}, u32[]{:S(2)}, u32[]{:S(2)}) collective-permute-start(bf16[3,64,512]{2,1,0:T(8,128)(2,1)} %get-tuple-element.46), channel_id=1, source_target_pairs={{0,2},{1,3},{2,0},{3,1},{4,6},{5,7},{6,4},{7,5},{8,10},{9,11},{10,... | collective-permute-start | bytes 589832 | tf_op jit(solution)/shard_map/ppermute | solution.py:232
  46.2 6.0 %collective-permute-start.16 = (bf16[3,64,512]{2,1,0:T(8,128)(2,1)}, bf16[3,64,512]{2,1,0:T(8,128)(2,1)S(1)}, u32[]{:S(2)}, u32[]{:S(2)}) collective-permute-start(bf16[3,64,512]{2,1,0:T(8,128)(2,1)} %get-tuple-element.47), channel_id=1, source_target_pairs={{0,6},{1,7},{2,4},{3,5},{4,2},{5,3},{6,0},{7,1},{8,14},{9,15},{10,... | collective-permute-start | bytes 589832 | tf_op jit(solution)/shard_map/ppermute | solution.py:232
  52.3 1.8 %collective-permute-start.17 = (bf16[3,64,512]{2,1,0:T(8,128)(2,1)}, bf16[3,64,512]{2,1,0:T(8,128)(2,1)S(1)}, u32[]{:S(2)}, u32[]{:S(2)}) collective-permute-start(bf16[3,64,512]{2,1,0:T(8,128)(2,1)} %get-tuple-element.48), channel_id=1, source_target_pairs={{0,3},{1,2},{2,1},{3,0},{4,7},{5,6},{6,5},{7,4},{8,11},{9,10},{10,... | collective-permute-start | bytes 589832 | tf_op jit(solution)/shard_map/ppermute | solution.py:232
  54.0 2.6 %collective-permute-start.18 = (bf16[3,64,512]{2,1,0:T(8,128)(2,1)}, bf16[3,64,512]{2,1,0:T(8,128)(2,1)S(1)}, u32[]{:S(2)}, u32[]{:S(2)}) collective-permute-start(bf16[3,64,512]{2,1,0:T(8,128)(2,1)} %get-tuple-element.49), channel_id=1, source_target_pairs={{0,7},{1,6},{2,5},{3,4},{4,3},{5,2},{6,1},{7,0},{8,15},{9,14},{10,... | collective-permute-start | bytes 589832 | tf_op jit(solution)/shard_map/ppermute | solution.py:232
  56.7 1.9 %copy-done = bf16[3,1,2,64,4096]{4,3,2,1,0:T(8,128)(2,1)S(1)} copy-done((bf16[3,1,2,64,4096]{4,3,2,1,0:T(8,128)(2,1)S(1)}, bf16[3,1,2,64,4096]{4,3,2,1,0:T(8,128)(2,1)}, u32[]{:S(2)}) %copy-start) | copy-done | bytes 3145752
  58.6 4.7 %attend.2 = (bf16[64,512]{1,0:T(8,128)(2,1)S(1)}, bf16[64,512]{1,0:T(8,128)(2,1)S(1)}, bf16[64,512]{1,0:T(8,128)(2,1)S(1)}, bf16[64,512]{1,0:T(8,128)(2,1)S(1)},...) custom-call(bf16[4,512]{1,0:T(4,128)(2,1)S(1)} %dynamic-slice_add_fu, ...), custom_call_target="tpu_custom_call" | custom-call | flops 536870912 | bytes 2097152 | tf_op jit(solution)/shard_map/attend/pallas_call | solution.py:177
  63.3 0.6 collective-permute-start.8
  64.0 6.1 %collective-permute-start.9 = (bf16[64,512]{1,0:T(8,128)(2,1)S(1)}, bf16[64,512]{1,0:T(8,128)(2,1)S(1)}, u32[]{:S(2)}, u32[]{:S(2)}) collective-permute-start(bf16[64,512]{1,0:T(8,128)(2,1)S(1)} %get-tuple-element.40), channel_id=1, source_target_pairs={{0,5},{1,4},{2,7},{3,6},{4,1},{5,0},{6,3},{7,2},{8,13},{9,12},{10,... | collective-permute-start | bytes 196616 | tf_op jit(solution)/shard_map/ppermute | solution.py:232
  70.0 1.0 %collective-permute-start.10 = (bf16[64,512]{1,0:T(8,128)(2,1)S(1)}, bf16[64,512]{1,0:T(8,128)(2,1)S(1)}, u32[]{:S(2)}, u32[]{:S(2)}) collective-permute-start(bf16[64,512]{1,0:T(8,128)(2,1)S(1)} %get-tuple-element.41), channel_id=1, source_target_pairs={{0,6},{1,7},{2,4},{3,5},{4,2},{5,3},{6,0},{7,1},{8,14},{9,15},{10,... | collective-permute-start | bytes 196616 | tf_op jit(solution)/shard_map/ppermute | solution.py:232
  71.1 3.9 %collective-permute-start.11 = (bf16[64,512]{1,0:T(8,128)(2,1)S(1)}, bf16[64,512]{1,0:T(8,128)(2,1)S(1)}, u32[]{:S(2)}, u32[]{:S(2)}) collective-permute-start(bf16[64,512]{1,0:T(8,128)(2,1)S(1)} %get-tuple-element.42), channel_id=1, source_target_pairs={{0,7},{1,6},{2,5},{3,4},{4,3},{5,2},{6,1},{7,0},{8,15},{9,14},{10,... | collective-permute-start | bytes 196616 | tf_op jit(solution)/shard_map/ppermute | solution.py:232
  75.0 3.1 %attend.3 = (bf16[64,1024]{1,0:T(8,128)(2,1)S(1)}, bf16[64,1024]{1,0:T(8,128)(2,1)S(1)}, bf16[64,1024]{1,0:T(8,128)(2,1)S(1)}, bf16[64,1024]{1,0:T(8,128)(2,1)S(...) custom-call(bf16[4,512]{1,0:T(4,128)(2,1)S(1)} %dynamic-slice_add_fu, ...), custom_call_target="tpu_custom_call" | custom-call | flops 536870912 | bytes 2097152 | tf_op jit(solution)/shard_map/attend/pallas_call | solution.py:177
  78.1 8.5 %collective-permute-start.19 = (bf16[64,512]{1,0:T(8,128)(2,1)S(1)}, bf16[64,512]{1,0:T(8,128)(2,1)S(1)}, u32[]{:S(2)}, u32[]{:S(2)}) collective-permute-start(bf16[64,512]{1,0:T(8,128)(2,1)S(1)} %get-tuple-element.54), channel_id=1, source_target_pairs={{0,4},{1,5},{2,6},{3,7},{4,0},{5,1},{6,2},{7,3},{8,12},{9,13},{10,... | collective-permute-start | bytes 196616 | tf_op jit(solution)/shard_map/ppermute | solution.py:232
  86.6 1.3 %collective-permute-start.20 = (bf16[64,512]{1,0:T(8,128)(2,1)S(1)}, bf16[64,512]{1,0:T(8,128)(2,1)S(1)}, u32[]{:S(2)}, u32[]{:S(2)}) collective-permute-start(bf16[64,512]{1,0:T(8,128)(2,1)S(1)} %get-tuple-element.55), channel_id=1, source_target_pairs={{0,5},{1,4},{2,7},{3,6},{4,1},{5,0},{6,3},{7,2},{8,13},{9,12},{10,... | collective-permute-start | bytes 196616 | tf_op jit(solution)/shard_map/ppermute | solution.py:232
  87.9 1.1 %collective-permute-start.23 = (bf16[64,1024]{1,0:T(8,128)(2,1)S(1)}, bf16[64,1024]{1,0:T(8,128)(2,1)S(1)}, u32[]{:S(2)}, u32[]{:S(2)}) collective-permute-start(bf16[64,1024]{1,0:T(8,128)(2,1)S(1)} %get-tuple-element.58), channel_id=1, source_target_pairs={{0,2},{1,3},{2,0},{3,1},{4,6},{5,7},{6,4},{7,5},{8,10},{9,11},{10,... | collective-permute-start | bytes 393224 | tf_op jit(solution)/shard_map/ppermute | solution.py:232
  89.0 0.3 collective-permute-start.24
  89.3 0.7 collective-permute-start.25
  90.0 5.2 %collective-permute-start.21 = (bf16[64,512]{1,0:T(8,128)(2,1)S(1)}, bf16[64,512]{1,0:T(8,128)(2,1)S(1)}, u32[]{:S(2)}, u32[]{:S(2)}) collective-permute-start(bf16[64,512]{1,0:T(8,128)(2,1)S(1)} %get-tuple-element.56), channel_id=1, source_target_pairs={{0,6},{1,7},{2,4},{3,5},{4,2},{5,3},{6,0},{7,1},{8,14},{9,15},{10,... | collective-permute-start | bytes 196616 | tf_op jit(solution)/shard_map/ppermute | solution.py:232
  95.2 0.9 collective-permute-start.22
  96.1 3.4 %collective-permute-done.21.rest_6_ = bf16[64,512]{1,0:T(8,128)(2,1)S(1)} collective-permute-done((bf16[64,512]{1,0:T(8,128)(2,1)S(1)}, bf16[64,512]{1,0:T(8,128)(2,1)S(1)}, u32[]{:S(2)}, u32[]{:S(2)}) %collective-permute-start.21) | collective-permute-done | bytes 65568 | tf_op jit(solution)/shard_map/ppermute | solution.py:232
  99.5 1.4 %collective-permute-done.22.rest_7_ = bf16[64,512]{1,0:T(8,128)(2,1)S(1)} collective-permute-done((bf16[64,512]{1,0:T(8,128)(2,1)S(1)}, bf16[64,512]{1,0:T(8,128)(2,1)S(1)}, u32[]{:S(2)}, u32[]{:S(2)}) %collective-permute-start.22) | collective-permute-done | bytes 65568 | tf_op jit(solution)/shard_map/ppermute | solution.py:232
  101.0 1.1 %unpack.1 = bf16[1,2,64,4096]{3,2,1,0:T(8,128)(2,1)} custom-call(bf16[64,512]{1,0:T(8,128)(2,1)S(1)} %collective-permute-done.8.rest_0_, bf16[64,512]{1,0:T(8,128)(2,1)S(1)} %collective-permute-done.9.rest_1_, bf16[64,512]{1,0:T(8,128)(2,1)S(1)} %collective-permute-done.10.rest_2_, bf16[64,512]{1,0:T(8,128)(2,1)S(1)} %collective-permute-done.11.rest_3_, ...), custom_call_target="tpu_custom_call" | custom-call | tf_op jit(solution)/shard_map/unpack/pallas_call | solution.py:216
  (44 shorter events, 0.4 us)
Async XLA Ops:
  0.6 10.5 %copy-start.2 = (f32[4,1024]{1,0:T(4,128)S(1)}, f32[4,1024]{1,0:T(4,128)}, u32[]{:S(2)}) copy-start(f32[4,1024]{1,0:T(4,128)} %param.9) | copy-start | bytes 49156
  0.6 10.5 %copy-start.4 = (f32[4,1024]{1,0:T(4,128)S(1)}, f32[4,1024]{1,0:T(4,128)}, u32[]{:S(2)}) copy-start(f32[4,1024]{1,0:T(4,128)} %param.8) | copy-start | bytes 49156
  0.7 10.5 %copy-start.3 = (f32[4,1024]{1,0:T(4,128)S(1)}, f32[4,1024]{1,0:T(4,128)}, u32[]{:S(2)}) copy-start(f32[4,1024]{1,0:T(4,128)} %param.7) | copy-start | bytes 49156
  0.7 10.5 %copy-start.1 = (f32[4,1024]{1,0:T(4,128)S(1)}, f32[4,1024]{1,0:T(4,128)}, u32[]{:S(2)}) copy-start(f32[4,1024]{1,0:T(4,128)} %param.6) | copy-start | bytes 49156
  2.3 21.5 %collective-permute-start.1 = (bf16[3,64,512]{2,1,0:T(8,128)(2,1)}, bf16[3,64,512]{2,1,0:T(8,128)(2,1)S(1)}, u32[]{:S(2)}, u32[]{:S(2)}) collective-permute-start(bf16[3,64,512]{2,1,0:T(8,128)(2,1)} %pack.3), channel_id=1, source_target_pairs={{0,6},{1,7},{2,4},{3,5},{4,2},{5,3},{6,0},{7,1},{8,14},{9,15},{10,... | collective-permute-start | bytes 589832 | tf_op jit(solution)/shard_map/ppermute | solution.py:232
  9.9 14.0 %copy-start.6 = (bf16[3,64,512]{2,1,0:T(8,128)(2,1)S(1)}, bf16[3,64,512]{2,1,0:T(8,128)(2,1)}, u32[]{:S(2)}) copy-start(bf16[3,64,512]{2,1,0:T(8,128)(2,1)} %get-tuple-element.37) | copy-start | bytes 589828
  9.9 26.1 %copy-start.5 = (bf16[3,64,512]{2,1,0:T(8,128)(2,1)S(1)}, bf16[3,64,512]{2,1,0:T(8,128)(2,1)}, u32[]{:S(2)}) copy-start(bf16[3,64,512]{2,1,0:T(8,128)(2,1)} %get-tuple-element.38) | copy-start | bytes 589828
  9.9 26.1 %collective-permute-start.2 = (bf16[3,64,512]{2,1,0:T(8,128)(2,1)}, bf16[3,64,512]{2,1,0:T(8,128)(2,1)S(1)}, u32[]{:S(2)}, u32[]{:S(2)}) collective-permute-start(bf16[3,64,512]{2,1,0:T(8,128)(2,1)} %get-tuple-element.33), channel_id=1, source_target_pairs={{0,1},{1,0},{2,3},{3,2},{4,5},{5,4},{6,7},{7,6},{8,9},{9,8},{10,11... | collective-permute-start | bytes 589832 | tf_op jit(solution)/shard_map/ppermute | solution.py:232
  10.0 26.1 %collective-permute-start.3 = (bf16[3,64,512]{2,1,0:T(8,128)(2,1)}, bf16[3,64,512]{2,1,0:T(8,128)(2,1)S(1)}, u32[]{:S(2)}, u32[]{:S(2)}) collective-permute-start(bf16[3,64,512]{2,1,0:T(8,128)(2,1)} %get-tuple-element.34), channel_id=1, source_target_pairs={{0,7},{1,6},{2,5},{3,4},{4,3},{5,2},{6,1},{7,0},{8,15},{9,14},{10,... | collective-permute-start | bytes 589832 | tf_op jit(solution)/shard_map/ppermute | solution.py:232
  10.1 26.4 %collective-permute-start.4 = (bf16[3,64,512]{2,1,0:T(8,128)(2,1)}, bf16[3,64,512]{2,1,0:T(8,128)(2,1)S(1)}, u32[]{:S(2)}, u32[]{:S(2)}) collective-permute-start(bf16[3,64,512]{2,1,0:T(8,128)(2,1)} %get-tuple-element.35), channel_id=1, source_target_pairs={{0,4},{1,5},{2,6},{3,7},{4,0},{5,1},{6,2},{7,3},{8,12},{9,13},{10,... | collective-permute-start | bytes 589832 | tf_op jit(solution)/shard_map/ppermute | solution.py:232
  11.8 6.0 %collective-permute-start = (bf16[4,1024]{1,0:T(4,128)(2,1)S(1)}, bf16[4,1024]{1,0:T(4,128)(2,1)S(1)}, u32[]{:S(2)}, u32[]{:S(2)}) collective-permute-start(bf16[4,1024]{1,0:T(4,128)(2,1)S(1)} %get-tuple-element.62), channel_id=1, source_target_pairs={{0,8},{1,16},{2,24},{3,9},{4,17},{5,25},{8,2},{9,18},{10,26},{11,3... | collective-permute-start | bytes 24584 | tf_op jit(solution)/shard_map/ppermute | solution.py:56
  17.8 18.8 %collective-permute-start.5 = (bf16[3,64,512]{2,1,0:T(8,128)(2,1)S(1)}, bf16[3,64,512]{2,1,0:T(8,128)(2,1)S(1)}, u32[]{:S(2)}, u32[]{:S(2)}) collective-permute-start(bf16[3,64,512]{2,1,0:T(8,128)(2,1)S(1)} %copy-done.7), channel_id=1, source_target_pairs={{0,2},{1,3},{2,0},{3,1},{4,6},{5,7},{6,4},{7,5},{8,10},{9,11},{10,... | collective-permute-start | bytes 589832 | tf_op jit(solution)/shard_map/ppermute | solution.py:232
  23.9 19.8 %collective-permute-start.6 = (bf16[3,64,512]{2,1,0:T(8,128)(2,1)S(1)}, bf16[3,64,512]{2,1,0:T(8,128)(2,1)S(1)}, u32[]{:S(2)}, u32[]{:S(2)}) collective-permute-start(bf16[3,64,512]{2,1,0:T(8,128)(2,1)S(1)} %copy-done.6), channel_id=1, source_target_pairs={{0,5},{1,4},{2,7},{3,6},{4,1},{5,0},{6,3},{7,2},{8,13},{9,12},{10,... | collective-permute-start | bytes 589832 | tf_op jit(solution)/shard_map/ppermute | solution.py:232
  36.0 10.2 %collective-permute-start.7 = (bf16[3,64,512]{2,1,0:T(8,128)(2,1)S(1)}, bf16[3,64,512]{2,1,0:T(8,128)(2,1)S(1)}, u32[]{:S(2)}, u32[]{:S(2)}) collective-permute-start(bf16[3,64,512]{2,1,0:T(8,128)(2,1)S(1)} %copy-done.5), channel_id=1, source_target_pairs={{0,3},{1,2},{2,1},{3,0},{4,7},{5,6},{6,5},{7,4},{8,11},{9,10},{10,... | collective-permute-start | bytes 589832 | tf_op jit(solution)/shard_map/ppermute | solution.py:232
  36.1 16.2 %collective-permute-start.12 = (bf16[3,64,512]{2,1,0:T(8,128)(2,1)}, bf16[3,64,512]{2,1,0:T(8,128)(2,1)S(1)}, u32[]{:S(2)}, u32[]{:S(2)}) collective-permute-start(bf16[3,64,512]{2,1,0:T(8,128)(2,1)} %get-tuple-element.43), channel_id=1, source_target_pairs={{0,4},{1,5},{2,6},{3,7},{4,0},{5,1},{6,2},{7,3},{8,12},{9,13},{10,... | collective-permute-start | bytes 589832 | tf_op jit(solution)/shard_map/ppermute | solution.py:232
  36.5 17.5 %collective-permute-start.13 = (bf16[3,64,512]{2,1,0:T(8,128)(2,1)}, bf16[3,64,512]{2,1,0:T(8,128)(2,1)S(1)}, u32[]{:S(2)}, u32[]{:S(2)}) collective-permute-start(bf16[3,64,512]{2,1,0:T(8,128)(2,1)} %get-tuple-element.44), channel_id=1, source_target_pairs={{0,1},{1,0},{2,3},{3,2},{4,5},{5,4},{6,7},{7,6},{8,9},{9,8},{10,11... | collective-permute-start | bytes 589832 | tf_op jit(solution)/shard_map/ppermute | solution.py:232
  36.6 26.7 %collective-permute-start.14 = (bf16[3,64,512]{2,1,0:T(8,128)(2,1)}, bf16[3,64,512]{2,1,0:T(8,128)(2,1)S(1)}, u32[]{:S(2)}, u32[]{:S(2)}) collective-permute-start(bf16[3,64,512]{2,1,0:T(8,128)(2,1)} %get-tuple-element.45), channel_id=1, source_target_pairs={{0,5},{1,4},{2,7},{3,6},{4,1},{5,0},{6,3},{7,2},{8,13},{9,12},{10,... | collective-permute-start | bytes 589832 | tf_op jit(solution)/shard_map/ppermute | solution.py:232
  43.7 20.3 %collective-permute-start.15 = (bf16[3,64,512]{2,1,0:T(8,128)(2,1)}, bf16[3,64,512]{2,1,0:T(8,128)(2,1)S(1)}, u32[]{:S(2)}, u32[]{:S(2)}) collective-permute-start(bf16[3,64,512]{2,1,0:T(8,128)(2,1)} %get-tuple-element.46), channel_id=1, source_target_pairs={{0,2},{1,3},{2,0},{3,1},{4,6},{5,7},{6,4},{7,5},{8,10},{9,11},{10,... | collective-permute-start | bytes 589832 | tf_op jit(solution)/shard_map/ppermute | solution.py:232
  46.2 23.8 %collective-permute-start.16 = (bf16[3,64,512]{2,1,0:T(8,128)(2,1)}, bf16[3,64,512]{2,1,0:T(8,128)(2,1)S(1)}, u32[]{:S(2)}, u32[]{:S(2)}) collective-permute-start(bf16[3,64,512]{2,1,0:T(8,128)(2,1)} %get-tuple-element.47), channel_id=1, source_target_pairs={{0,6},{1,7},{2,4},{3,5},{4,2},{5,3},{6,0},{7,1},{8,14},{9,15},{10,... | collective-permute-start | bytes 589832 | tf_op jit(solution)/shard_map/ppermute | solution.py:232
  52.3 18.8 %collective-permute-start.17 = (bf16[3,64,512]{2,1,0:T(8,128)(2,1)}, bf16[3,64,512]{2,1,0:T(8,128)(2,1)S(1)}, u32[]{:S(2)}, u32[]{:S(2)}) collective-permute-start(bf16[3,64,512]{2,1,0:T(8,128)(2,1)} %get-tuple-element.48), channel_id=1, source_target_pairs={{0,3},{1,2},{2,1},{3,0},{4,7},{5,6},{6,5},{7,4},{8,11},{9,10},{10,... | collective-permute-start | bytes 589832 | tf_op jit(solution)/shard_map/ppermute | solution.py:232
  54.0 20.9 %collective-permute-start.18 = (bf16[3,64,512]{2,1,0:T(8,128)(2,1)}, bf16[3,64,512]{2,1,0:T(8,128)(2,1)S(1)}, u32[]{:S(2)}, u32[]{:S(2)}) collective-permute-start(bf16[3,64,512]{2,1,0:T(8,128)(2,1)} %get-tuple-element.49), channel_id=1, source_target_pairs={{0,7},{1,6},{2,5},{3,4},{4,3},{5,2},{6,1},{7,0},{8,15},{9,14},{10,... | collective-permute-start | bytes 589832 | tf_op jit(solution)/shard_map/ppermute | solution.py:232
  63.3 23.3 %collective-permute-start.8 = (bf16[64,512]{1,0:T(8,128)(2,1)S(1)}, bf16[64,512]{1,0:T(8,128)(2,1)S(1)}, u32[]{:S(2)}, u32[]{:S(2)}) collective-permute-start(bf16[64,512]{1,0:T(8,128)(2,1)S(1)} %get-tuple-element.39), channel_id=1, source_target_pairs={{0,4},{1,5},{2,6},{3,7},{4,0},{5,1},{6,2},{7,3},{8,12},{9,13},{10,... | collective-permute-start | bytes 196616 | tf_op jit(solution)/shard_map/ppermute | solution.py:232
  64.0 23.9 %collective-permute-start.9 = (bf16[64,512]{1,0:T(8,128)(2,1)S(1)}, bf16[64,512]{1,0:T(8,128)(2,1)S(1)}, u32[]{:S(2)}, u32[]{:S(2)}) collective-permute-start(bf16[64,512]{1,0:T(8,128)(2,1)S(1)} %get-tuple-element.40), channel_id=1, source_target_pairs={{0,5},{1,4},{2,7},{3,6},{4,1},{5,0},{6,3},{7,2},{8,13},{9,12},{10,... | collective-permute-start | bytes 196616 | tf_op jit(solution)/shard_map/ppermute | solution.py:232
  70.0 18.9 %collective-permute-start.10 = (bf16[64,512]{1,0:T(8,128)(2,1)S(1)}, bf16[64,512]{1,0:T(8,128)(2,1)S(1)}, u32[]{:S(2)}, u32[]{:S(2)}) collective-permute-start(bf16[64,512]{1,0:T(8,128)(2,1)S(1)} %get-tuple-element.41), channel_id=1, source_target_pairs={{0,6},{1,7},{2,4},{3,5},{4,2},{5,3},{6,0},{7,1},{8,14},{9,15},{10,... | collective-permute-start | bytes 196616 | tf_op jit(solution)/shard_map/ppermute | solution.py:232
  71.1 18.3 %collective-permute-start.11 = (bf16[64,512]{1,0:T(8,128)(2,1)S(1)}, bf16[64,512]{1,0:T(8,128)(2,1)S(1)}, u32[]{:S(2)}, u32[]{:S(2)}) collective-permute-start(bf16[64,512]{1,0:T(8,128)(2,1)S(1)} %get-tuple-element.42), channel_id=1, source_target_pairs={{0,7},{1,6},{2,5},{3,4},{4,3},{5,2},{6,1},{7,0},{8,15},{9,14},{10,... | collective-permute-start | bytes 196616 | tf_op jit(solution)/shard_map/ppermute | solution.py:232
  78.1 12.0 %collective-permute-start.19 = (bf16[64,512]{1,0:T(8,128)(2,1)S(1)}, bf16[64,512]{1,0:T(8,128)(2,1)S(1)}, u32[]{:S(2)}, u32[]{:S(2)}) collective-permute-start(bf16[64,512]{1,0:T(8,128)(2,1)S(1)} %get-tuple-element.54), channel_id=1, source_target_pairs={{0,4},{1,5},{2,6},{3,7},{4,0},{5,1},{6,2},{7,3},{8,12},{9,13},{10,... | collective-permute-start | bytes 196616 | tf_op jit(solution)/shard_map/ppermute | solution.py:232
  86.6 8.6 %collective-permute-start.20 = (bf16[64,512]{1,0:T(8,128)(2,1)S(1)}, bf16[64,512]{1,0:T(8,128)(2,1)S(1)}, u32[]{:S(2)}, u32[]{:S(2)}) collective-permute-start(bf16[64,512]{1,0:T(8,128)(2,1)S(1)} %get-tuple-element.55), channel_id=1, source_target_pairs={{0,5},{1,4},{2,7},{3,6},{4,1},{5,0},{6,3},{7,2},{8,13},{9,12},{10,... | collective-permute-start | bytes 196616 | tf_op jit(solution)/shard_map/ppermute | solution.py:232
  87.9 13.1 %collective-permute-start.23 = (bf16[64,1024]{1,0:T(8,128)(2,1)S(1)}, bf16[64,1024]{1,0:T(8,128)(2,1)S(1)}, u32[]{:S(2)}, u32[]{:S(2)}) collective-permute-start(bf16[64,1024]{1,0:T(8,128)(2,1)S(1)} %get-tuple-element.58), channel_id=1, source_target_pairs={{0,2},{1,3},{2,0},{3,1},{4,6},{5,7},{6,4},{7,5},{8,10},{9,11},{10,... | collective-permute-start | bytes 393224 | tf_op jit(solution)/shard_map/ppermute | solution.py:232
  89.0 12.0 %collective-permute-start.24 = (bf16[64,1024]{1,0:T(8,128)(2,1)S(1)}, bf16[64,1024]{1,0:T(8,128)(2,1)S(1)}, u32[]{:S(2)}, u32[]{:S(2)}) collective-permute-start(bf16[64,1024]{1,0:T(8,128)(2,1)S(1)} %get-tuple-element.59), channel_id=1, source_target_pairs={{0,3},{1,2},{2,1},{3,0},{4,7},{5,6},{6,5},{7,4},{8,11},{9,10},{10,... | collective-permute-start | bytes 393224 | tf_op jit(solution)/shard_map/ppermute | solution.py:232
  89.3 11.6 %collective-permute-start.25 = (bf16[64,1024]{1,0:T(8,128)(2,1)S(1)}, bf16[64,1024]{1,0:T(8,128)(2,1)S(1)}, u32[]{:S(2)}, u32[]{:S(2)}) collective-permute-start(bf16[64,1024]{1,0:T(8,128)(2,1)S(1)} %get-tuple-element.60), channel_id=1, source_target_pairs={{0,1},{1,0},{2,3},{3,2},{4,5},{5,4},{6,7},{7,6},{8,9},{9,8},{10,11... | collective-permute-start | bytes 393224 | tf_op jit(solution)/shard_map/ppermute | solution.py:232
  90.0 9.5 %collective-permute-start.21 = (bf16[64,512]{1,0:T(8,128)(2,1)S(1)}, bf16[64,512]{1,0:T(8,128)(2,1)S(1)}, u32[]{:S(2)}, u32[]{:S(2)}) collective-permute-start(bf16[64,512]{1,0:T(8,128)(2,1)S(1)} %get-tuple-element.56), channel_id=1, source_target_pairs={{0,6},{1,7},{2,4},{3,5},{4,2},{5,3},{6,0},{7,1},{8,14},{9,15},{10,... | collective-permute-start | bytes 196616 | tf_op jit(solution)/shard_map/ppermute | solution.py:232
  95.2 5.7 %collective-permute-start.22 = (bf16[64,512]{1,0:T(8,128)(2,1)S(1)}, bf16[64,512]{1,0:T(8,128)(2,1)S(1)}, u32[]{:S(2)}, u32[]{:S(2)}) collective-permute-start(bf16[64,512]{1,0:T(8,128)(2,1)S(1)} %get-tuple-element.57), channel_id=1, source_target_pairs={{0,7},{1,6},{2,5},{3,4},{4,3},{5,2},{6,1},{7,0},{8,15},{9,14},{10,... | collective-permute-start | bytes 196616 | tf_op jit(solution)/shard_map/ppermute | solution.py:232
  (2 other events, 9.8 us)

commit v6 on v5

--- a/solution.py
+++ b/solution.py
@@ -35,20 +35,12 @@
 def own_columns(layer, dp_count, seq_count, width):
     shard_cols = layer.shape[1]
     assert shard_cols % width == 0
-    rounds = []
-    for owner in range(dp_count):
-        wanted = [
-            (dp, seq)
-            for seq in range(seq_count)
-            if seq * width // shard_cols == owner
-            for dp in range(dp_count)
-            if dp != owner
-        ]
-        for place, (dp, seq) in enumerate(wanted):
-            turn, source = divmod(place, seq_count)
-            while len(rounds) <= turn:
-                rounds.append([])
-            rounds[turn].append((owner * seq_count + source, dp * seq_count + seq))
+    rounds = [[] for _ in range(dp_count - 1)]
+    for seq in range(seq_count):
+        owner = seq * width // shard_cols
+        for turn, pairs in enumerate(rounds):
+            other = (owner + turn + 1) % dp_count
+            pairs.append((owner * seq_count + seq, other * seq_count + seq))
     first_col = lax.axis_index("seq") * width
     mine = lax.axis_index("dp") == first_col // shard_cols
     found = jnp.where(mine, layer, jnp.zeros_like(layer))
@@ -68,6 +60,15 @@
         (sample, first * HD, slice(place * HD, (place + count) * HD), count * HD)
         for sample, first, count, place in runs
     ]
+
+
+def cut_out(qkv, chunk, slot, width):
+    own = lax.bitwise_xor(lax.axis_index("seq"), slot) * width
+    runs = [
+        lax.dynamic_slice_in_dim(qkv[:, 0, sample], own + first, size, 2)
+        for sample, first, _, size in spans(chunk)
+    ]
+    return jnp.concatenate(runs, axis=2)
 
 
 def pack_kernel(chunk, slots, width, source, *rest):
@@ -250,9 +251,8 @@
     ]
     landed = []
     for chunk, slots in zip(chunks, orders, strict=True):
-        parts = []
-        for some in [slots[:1], slots[1:-1]] if chunk is chunks[0] else [slots[:-1]]:
-            parts += pack(qkv, chunk, some, width)
+        parts = [] if landed else [cut_out(qkv, chunk, slots[0], width)]
+        parts += pack(qkv, chunk, slots[len(parts) : -1], width)
         landed.append([swap(part, slot) for part, slot in zip(parts, slots[:-1], strict=True)])
     updated, first_moment, second_moment = adamw(master, moment_one, moment_two, grads)
     layer = own_columns(updated.astype(jnp.bfloat16), dp_count, seq_count, width)

time: 102 us -> 99.6 us (0.976)
  starting transfers between devices: 78.1 us -> 42.4 us
  waiting for transfers between devices: 4.9 us -> 38.2 us
  Pallas kernels: 15.6 us -> 13.9 us
  local copies, waits for them, and re-layouts: 1.91 us -> 3.33 us
    ppermute x25, starting transfers between devices: 74.8 us -> 35.4 us  [swap(): lax.ppermute(part, 'seq', [(place, place ^ slot) for place in range(lax.a...]
    ppermute x25, waiting for transfers between devices: 4.9 us -> 35.5 us  [swap(): lax.ppermute(part, 'seq', [(place, place ^ slot) for place in range(lax.a...]
    ppermute x1 -> x3, starting transfers between devices: 3.38 us -> 7.03 us  [own_columns(): found = found + lax.ppermute(layer, ('dp', 'seq'), pairs)]
    ppermute x1 -> x3, waiting for transfers between devices: 0.01 us -> 2.7 us  [own_columns(): found = found + lax.ppermute(layer, ('dp', 'seq'), pairs)]
    pallas_call x3 -> x2, Pallas kernels: 6.67 us -> 4.94 us  [pack(): pl.pallas_call(functools.partial(pack_kernel, chunk, slots, width), out_s...]
    slice x0 -> x2, local copies, waits for them, and re-layouts: none -> 1.4 us  [cut_out(): qkv[:, 0, sample]]
  transfers between devices with their start and end apart: 26 -> 28, of which waited for: 2 -> 10; matrix products, arithmetic and copies ran while one was open for 1% -> 1% of each run, Pallas kernels for 13% -> 13%
where the time goes in v6:
time: 99.6 us; the launch traced here: 99.3 us
  starting transfers between devices  42.4 us (43%)
  waiting for transfers between devices  38.2 us (38%)
  Pallas kernels  13.9 us (14%)
  local copies, waits for them, and re-layouts  3.33 us (3%)
    ppermute x25, waiting for transfers between devices, swap(): lax.ppermute(part, 'seq', [(place, place ^ slot) for place in range(lax.a...  35.5 us
    ppermute x25, starting transfers between devices, swap(): lax.ppermute(part, 'seq', [(place, place ^ slot) for place in range(lax.a...  35.4 us
    pallas_call x2, Pallas kernels, attend(): pl.pallas_call(functools.partial(attend_kernel, chunk, slots, width, fetc...  7.85 us
    ppermute x3, starting transfers between devices, own_columns(): found = found + lax.ppermute(layer, ('dp', 'seq'), pairs)  7.03 us
    pallas_call x2, Pallas kernels, pack(): pl.pallas_call(functools.partial(pack_kernel, chunk, slots, width), out_s...  4.94 us
    ppermute x3, waiting for transfers between devices, own_columns(): found = found + lax.ppermute(layer, ('dp', 'seq'), pairs)  2.7 us
  transfers between devices with their start and end apart: 28, of which 10 were waited for; matrix products, arithmetic and copies ran while one was open for 1% of the time, Pallas kernels for 13%

profile of v6, /device:TPU:0, one launch (start us, length us, event | category | flops | bytes accessed | tf_op | source)
XLA Modules:
  0.0 99.3 jit_solution(10960573260613606029)
XLA Ops:
  0.7 1.4 %slice-done = bf16[3,1,1,64,4096]{4,3,2,1,0:T(8,128)(2,1)S(1)} async-done(((bf16[3,1,2,64,4096]{4,3,2,1,0:T(8,128)(2,1)}), bf16[3,1,1,64,4096]{4,3,2,1,0:T(8,128)(2,1)S(1)}, s32[]{:S(2)}) %slice-start) | async-done | bytes 1572888 | tf_op jit(solution)/shard_map/slice | solution.py:68
  2.1 5.1 %collective-permute-start.3 = (bf16[3,64,512]{2,1,0:T(8,128)(2,1)S(1)}, bf16[3,64,512]{2,1,0:T(8,128)(2,1)S(1)}, u32[]{:S(2)}, u32[]{:S(2)}) collective-permute-start(bf16[3,64,512]{2,1,0:T(8,128)(2,1)S(1)} %dynamic-slice_bitcast_fusion), channel_id=1, source_target_pairs={{0,6},{1,7},{2,4},{3,5},{4,2},{5,3},{6,0},{7,1},{8,14},{9,15},{10,... | collective-permute-start | bytes 589832 | tf_op jit(solution)/shard_map/ppermute | solution.py:233
  7.2 2.4 %pack.2 = (bf16[3,64,512]{2,1,0:T(8,128)(2,1)}, bf16[3,64,512]{2,1,0:T(8,128)(2,1)}, bf16[3,64,512]{2,1,0:T(8,128)(2,1)}, bf16[3,64,512]{2,1,0:T(8,128)(2,1)}, b...) custom-call(bf16[3,1,2,64,4096]{4,3,2,1,0:T(8,128)(2,1)} %qkv.3), custom_call_target="tpu_custom_call" | custom-call | tf_op jit(solution)/shard_map/pack/pallas_call | solution.py:92
  11.5 4.5 %collective-permute-start.2 = (bf16[4,1024]{1,0:T(4,128)(2,1)S(1)}, bf16[4,1024]{1,0:T(4,128)(2,1)S(1)}, u32[]{:S(2)}, u32[]{:S(2)}) collective-permute-start(bf16[4,1024]{1,0:T(4,128)(2,1)S(1)} %get-tuple-element.62), channel_id=1, source_target_pairs={{0,24},{1,25},{10,2},{11,3},{20,12},{21,13},{30,22},{31,23}} | collective-permute-start | bytes 24584 | tf_op jit(solution)/shard_map/ppermute | solution.py:48
  16.0 1.3 %collective-permute-done.2 = bf16[4,1024]{1,0:T(4,128)(2,1)S(1)} collective-permute-done((bf16[4,1024]{1,0:T(4,128)(2,1)S(1)}, bf16[4,1024]{1,0:T(4,128)(2,1)S(1)}, u32[]{:S(2)}, u32[]{:S(2)}) %collective-permute-start.2) | collective-permute-done | bytes 8224 | tf_op jit(solution)/shard_map/ppermute | solution.py:48
  17.3 1.3 %collective-permute-start.1 = (bf16[4,1024]{1,0:T(4,128)(2,1)S(1)}, bf16[4,1024]{1,0:T(4,128)(2,1)S(1)}, u32[]{:S(2)}, u32[]{:S(2)}) collective-permute-start(bf16[4,1024]{1,0:T(4,128)(2,1)S(1)} %get-tuple-element.62), channel_id=1, source_target_pairs={{0,16},{1,17},{10,26},{11,27},{20,4},{21,5},{30,14},{31,15}} | collective-permute-start | bytes 24584 | tf_op jit(solution)/shard_map/ppermute | solution.py:48
  18.6 1.3 %collective-permute-done.1 = bf16[4,1024]{1,0:T(4,128)(2,1)S(1)} collective-permute-done((bf16[4,1024]{1,0:T(4,128)(2,1)S(1)}, bf16[4,1024]{1,0:T(4,128)(2,1)S(1)}, u32[]{:S(2)}, u32[]{:S(2)}) %collective-permute-start.1) | collective-permute-done | bytes 8224 | tf_op jit(solution)/shard_map/ppermute | solution.py:48
  20.0 1.3 %collective-permute-start = (bf16[4,1024]{1,0:T(4,128)(2,1)S(1)}, bf16[4,1024]{1,0:T(4,128)(2,1)S(1)}, u32[]{:S(2)}, u32[]{:S(2)}) collective-permute-start(bf16[4,1024]{1,0:T(4,128)(2,1)S(1)} %get-tuple-element.62), channel_id=1, source_target_pairs={{0,8},{1,9},{10,18},{11,19},{20,28},{21,29},{30,6},{31,7}} | collective-permute-start | bytes 24584 | tf_op jit(solution)/shard_map/ppermute | solution.py:48
  21.2 2.6 %pack.3 = (bf16[3,64,512]{2,1,0:T(8,128)(2,1)}, bf16[3,64,512]{2,1,0:T(8,128)(2,1)}, bf16[3,64,512]{2,1,0:T(8,128)(2,1)}, bf16[3,64,512]{2,1,0:T(8,128)(2,1)}, b...) custom-call(bf16[3,1,2,64,4096]{4,3,2,1,0:T(8,128)(2,1)} %qkv.3), custom_call_target="tpu_custom_call" | custom-call | tf_op jit(solution)/shard_map/pack/pallas_call | solution.py:92
  24.6 3.4 %collective-permute-start.9 = (bf16[3,64,512]{2,1,0:T(8,128)(2,1)S(1)}, bf16[3,64,512]{2,1,0:T(8,128)(2,1)S(1)}, u32[]{:S(2)}, u32[]{:S(2)}) collective-permute-start(bf16[3,64,512]{2,1,0:T(8,128)(2,1)S(1)} %copy-done.5), channel_id=1, source_target_pairs={{0,3},{1,2},{2,1},{3,0},{4,7},{5,6},{6,5},{7,4},{8,11},{9,10},{10,... | collective-permute-start | bytes 589832 | tf_op jit(solution)/shard_map/ppermute | solution.py:233
  28.7 8.8 %collective-permute-done.6.rest_3_ = bf16[3,64,512]{2,1,0:T(8,128)(2,1)S(1)} collective-permute-done((bf16[3,64,512]{2,1,0:T(8,128)(2,1)}, bf16[3,64,512]{2,1,0:T(8,128)(2,1)S(1)}, u32[]{:S(2)}, u32[]{:S(2)}) %collective-permute-start.6) | collective-permute-done | bytes 196640 | tf_op jit(solution)/shard_map/ppermute | solution.py:233
  37.5 10.7 %collective-permute-done.8.rest_5_ = bf16[3,64,512]{2,1,0:T(8,128)(2,1)S(1)} collective-permute-done((bf16[3,64,512]{2,1,0:T(8,128)(2,1)S(1)}, bf16[3,64,512]{2,1,0:T(8,128)(2,1)S(1)}, u32[]{:S(2)}, u32[]{:S(2)}) %collective-permute-start.8) | collective-permute-done | bytes 196640 | tf_op jit(solution)/shard_map/ppermute | solution.py:233
  48.2 1.8 %collective-permute-start.17 = (bf16[3,64,512]{2,1,0:T(8,128)(2,1)}, bf16[3,64,512]{2,1,0:T(8,128)(2,1)S(1)}, u32[]{:S(2)}, u32[]{:S(2)}) collective-permute-start(bf16[3,64,512]{2,1,0:T(8,128)(2,1)} %get-tuple-element.46), channel_id=1, source_target_pairs={{0,2},{1,3},{2,0},{3,1},{4,6},{5,7},{6,4},{7,5},{8,10},{9,11},{10,... | collective-permute-start | bytes 589832 | tf_op jit(solution)/shard_map/ppermute | solution.py:233
  50.1 1.1 %collective-permute-start.18 = (bf16[3,64,512]{2,1,0:T(8,128)(2,1)}, bf16[3,64,512]{2,1,0:T(8,128)(2,1)S(1)}, u32[]{:S(2)}, u32[]{:S(2)}) collective-permute-start(bf16[3,64,512]{2,1,0:T(8,128)(2,1)} %get-tuple-element.47), channel_id=1, source_target_pairs={{0,6},{1,7},{2,4},{3,5},{4,2},{5,3},{6,0},{7,1},{8,14},{9,15},{10,... | collective-permute-start | bytes 589832 | tf_op jit(solution)/shard_map/ppermute | solution.py:233
  51.2 3.3 %collective-permute-done.14.rest_0_ = bf16[3,64,512]{2,1,0:T(8,128)(2,1)S(1)} collective-permute-done((bf16[3,64,512]{2,1,0:T(8,128)(2,1)}, bf16[3,64,512]{2,1,0:T(8,128)(2,1)S(1)}, u32[]{:S(2)}, u32[]{:S(2)}) %collective-permute-start.14) | collective-permute-done | bytes 196640 | tf_op jit(solution)/shard_map/ppermute | solution.py:233
  55.3 1.9 %copy-done = bf16[3,1,2,64,4096]{4,3,2,1,0:T(8,128)(2,1)S(1)} copy-done((bf16[3,1,2,64,4096]{4,3,2,1,0:T(8,128)(2,1)S(1)}, bf16[3,1,2,64,4096]{4,3,2,1,0:T(8,128)(2,1)}, u32[]{:S(2)}) %copy-start) | copy-done | bytes 3145752
  57.2 4.7 %attend.2 = (bf16[64,512]{1,0:T(8,128)(2,1)S(1)}, bf16[64,512]{1,0:T(8,128)(2,1)S(1)}, bf16[64,512]{1,0:T(8,128)(2,1)S(1)}, bf16[64,512]{1,0:T(8,128)(2,1)S(1)},...) custom-call(bf16[4,512]{1,0:T(4,128)(2,1)S(1)} %dynamic-slice_add_fu, ...), custom_call_target="tpu_custom_call" | custom-call | flops 536870912 | bytes 2097152 | tf_op jit(solution)/shard_map/attend/pallas_call | solution.py:178
  61.9 2.5 %collective-permute-start.10 = (bf16[64,512]{1,0:T(8,128)(2,1)S(1)}, bf16[64,512]{1,0:T(8,128)(2,1)S(1)}, u32[]{:S(2)}, u32[]{:S(2)}) collective-permute-start(bf16[64,512]{1,0:T(8,128)(2,1)S(1)} %get-tuple-element.39), channel_id=1, source_target_pairs={{0,4},{1,5},{2,6},{3,7},{4,0},{5,1},{6,2},{7,3},{8,12},{9,13},{10,... | collective-permute-start | bytes 196616 | tf_op jit(solution)/shard_map/ppermute | solution.py:233
  64.4 5.2 %collective-permute-done.17.rest_3_ = bf16[3,64,512]{2,1,0:T(8,128)(2,1)S(1)} collective-permute-done((bf16[3,64,512]{2,1,0:T(8,128)(2,1)}, bf16[3,64,512]{2,1,0:T(8,128)(2,1)S(1)}, u32[]{:S(2)}, u32[]{:S(2)}) %collective-permute-start.17) | collective-permute-done | bytes 196640 | tf_op jit(solution)/shard_map/ppermute | solution.py:233
  69.7 1.1 %collective-permute-start.11 = (bf16[64,512]{1,0:T(8,128)(2,1)S(1)}, bf16[64,512]{1,0:T(8,128)(2,1)S(1)}, u32[]{:S(2)}, u32[]{:S(2)}) collective-permute-start(bf16[64,512]{1,0:T(8,128)(2,1)S(1)} %get-tuple-element.40), channel_id=1, source_target_pairs={{0,5},{1,4},{2,7},{3,6},{4,1},{5,0},{6,3},{7,2},{8,13},{9,12},{10,... | collective-permute-start | bytes 196616 | tf_op jit(solution)/shard_map/ppermute | solution.py:233
  70.7 2.0 %collective-permute-start.12 = (bf16[64,512]{1,0:T(8,128)(2,1)S(1)}, bf16[64,512]{1,0:T(8,128)(2,1)S(1)}, u32[]{:S(2)}, u32[]{:S(2)}) collective-permute-start(bf16[64,512]{1,0:T(8,128)(2,1)S(1)} %get-tuple-element.41), channel_id=1, source_target_pairs={{0,6},{1,7},{2,4},{3,5},{4,2},{5,3},{6,0},{7,1},{8,14},{9,15},{10,... | collective-permute-start | bytes 196616 | tf_op jit(solution)/shard_map/ppermute | solution.py:233
  72.7 1.8 %collective-permute-done.19.rest_5_ = bf16[3,64,512]{2,1,0:T(8,128)(2,1)S(1)} collective-permute-done((bf16[3,64,512]{2,1,0:T(8,128)(2,1)}, bf16[3,64,512]{2,1,0:T(8,128)(2,1)S(1)}, u32[]{:S(2)}, u32[]{:S(2)}) %collective-permute-start.19) | collective-permute-done | bytes 196640 | tf_op jit(solution)/shard_map/ppermute | solution.py:233
  74.5 2.1 %collective-permute-start.13 = (bf16[64,512]{1,0:T(8,128)(2,1)S(1)}, bf16[64,512]{1,0:T(8,128)(2,1)S(1)}, u32[]{:S(2)}, u32[]{:S(2)}) collective-permute-start(bf16[64,512]{1,0:T(8,128)(2,1)S(1)} %get-tuple-element.42), channel_id=1, source_target_pairs={{0,7},{1,6},{2,5},{3,4},{4,3},{5,2},{6,1},{7,0},{8,15},{9,14},{10,... | collective-permute-start | bytes 196616 | tf_op jit(solution)/shard_map/ppermute | solution.py:233
  76.6 3.1 %attend.3 = (bf16[64,1024]{1,0:T(8,128)(2,1)S(1)}, bf16[64,1024]{1,0:T(8,128)(2,1)S(1)}, bf16[64,1024]{1,0:T(8,128)(2,1)S(1)}, bf16[64,1024]{1,0:T(8,128)(2,1)S(...) custom-call(bf16[4,512]{1,0:T(4,128)(2,1)S(1)} %dynamic-slice_add_fu, ...), custom_call_target="tpu_custom_call" | custom-call | flops 536870912 | bytes 2097152 | tf_op jit(solution)/shard_map/attend/pallas_call | solution.py:178
  79.7 2.7 %collective-permute-start.21 = (bf16[64,512]{1,0:T(8,128)(2,1)S(1)}, bf16[64,512]{1,0:T(8,128)(2,1)S(1)}, u32[]{:S(2)}, u32[]{:S(2)}) collective-permute-start(bf16[64,512]{1,0:T(8,128)(2,1)S(1)} %get-tuple-element.54), channel_id=1, source_target_pairs={{0,4},{1,5},{2,6},{3,7},{4,0},{5,1},{6,2},{7,3},{8,12},{9,13},{10,... | collective-permute-start | bytes 196616 | tf_op jit(solution)/shard_map/ppermute | solution.py:233
  82.5 3.1 %collective-permute-start.22 = (bf16[64,512]{1,0:T(8,128)(2,1)S(1)}, bf16[64,512]{1,0:T(8,128)(2,1)S(1)}, u32[]{:S(2)}, u32[]{:S(2)}) collective-permute-start(bf16[64,512]{1,0:T(8,128)(2,1)S(1)} %get-tuple-element.55), channel_id=1, source_target_pairs={{0,5},{1,4},{2,7},{3,6},{4,1},{5,0},{6,3},{7,2},{8,13},{9,12},{10,... | collective-permute-start | bytes 196616 | tf_op jit(solution)/shard_map/ppermute | solution.py:233
  85.6 1.3 %collective-permute-start.25 = (bf16[64,1024]{1,0:T(8,128)(2,1)S(1)}, bf16[64,1024]{1,0:T(8,128)(2,1)S(1)}, u32[]{:S(2)}, u32[]{:S(2)}) collective-permute-start(bf16[64,1024]{1,0:T(8,128)(2,1)S(1)} %get-tuple-element.58), channel_id=1, source_target_pairs={{0,2},{1,3},{2,0},{3,1},{4,6},{5,7},{6,4},{7,5},{8,10},{9,11},{10,... | collective-permute-start | bytes 393224 | tf_op jit(solution)/shard_map/ppermute | solution.py:233
  87.8 2.7 %collective-permute-start.23 = (bf16[64,512]{1,0:T(8,128)(2,1)S(1)}, bf16[64,512]{1,0:T(8,128)(2,1)S(1)}, u32[]{:S(2)}, u32[]{:S(2)}) collective-permute-start(bf16[64,512]{1,0:T(8,128)(2,1)S(1)} %get-tuple-element.56), channel_id=1, source_target_pairs={{0,6},{1,7},{2,4},{3,5},{4,2},{5,3},{6,0},{7,1},{8,14},{9,15},{10,... | collective-permute-start | bytes 196616 | tf_op jit(solution)/shard_map/ppermute | solution.py:233
  90.5 1.0 collective-permute-done.22.rest_5_
  91.5 2.2 %collective-permute-start.24 = (bf16[64,512]{1,0:T(8,128)(2,1)S(1)}, bf16[64,512]{1,0:T(8,128)(2,1)S(1)}, u32[]{:S(2)}, u32[]{:S(2)}) collective-permute-start(bf16[64,512]{1,0:T(8,128)(2,1)S(1)} %get-tuple-element.57), channel_id=1, source_target_pairs={{0,7},{1,6},{2,5},{3,4},{4,3},{5,2},{6,1},{7,0},{8,15},{9,14},{10,... | collective-permute-start | bytes 196616 | tf_op jit(solution)/shard_map/ppermute | solution.py:233
  93.6 4.5 %collective-permute-done.23.rest_6_ = bf16[64,512]{1,0:T(8,128)(2,1)S(1)} collective-permute-done((bf16[64,512]{1,0:T(8,128)(2,1)S(1)}, bf16[64,512]{1,0:T(8,128)(2,1)S(1)}, u32[]{:S(2)}, u32[]{:S(2)}) %collective-permute-start.23) | collective-permute-done | bytes 65568 | tf_op jit(solution)/shard_map/ppermute | solution.py:233
  98.2 1.1 %unpack.1 = bf16[1,2,64,4096]{3,2,1,0:T(8,128)(2,1)} custom-call(bf16[64,512]{1,0:T(8,128)(2,1)S(1)} %collective-permute-done.10.rest_0_, bf16[64,512]{1,0:T(8,128)(2,1)S(1)} %collective-permute-done.11.rest_1_, bf16[64,512]{1,0:T(8,128)(2,1)S(1)} %collective-permute-done.12.rest_2_, bf16[64,512]{1,0:T(8,128)(2,1)S(1)} %collective-permute-done.13.rest_3_, ...), custom_call_target="tpu_custom_call" | custom-call | tf_op jit(solution)/shard_map/unpack/pallas_call | solution.py:217
  (50 shorter events, 5.2 us)
Async XLA Ops:
  2.1 8.8 %copy-start.1 = (f32[4,1024]{1,0:T(4,128)S(1)}, f32[4,1024]{1,0:T(4,128)}, u32[]{:S(2)}) copy-start(f32[4,1024]{1,0:T(4,128)} %param.6) | copy-start | bytes 49156
  2.1 22.4 %collective-permute-start.3 = (bf16[3,64,512]{2,1,0:T(8,128)(2,1)S(1)}, bf16[3,64,512]{2,1,0:T(8,128)(2,1)S(1)}, u32[]{:S(2)}, u32[]{:S(2)}) collective-permute-start(bf16[3,64,512]{2,1,0:T(8,128)(2,1)S(1)} %dynamic-slice_bitcast_fusion), channel_id=1, source_target_pairs={{0,6},{1,7},{2,4},{3,5},{4,2},{5,3},{6,0},{7,1},{8,14},{9,15},{10,... | collective-permute-start | bytes 589832 | tf_op jit(solution)/shard_map/ppermute | solution.py:233
  9.6 14.9 %collective-permute-start.4 = (bf16[3,64,512]{2,1,0:T(8,128)(2,1)}, bf16[3,64,512]{2,1,0:T(8,128)(2,1)S(1)}, u32[]{:S(2)}, u32[]{:S(2)}) collective-permute-start(bf16[3,64,512]{2,1,0:T(8,128)(2,1)} %get-tuple-element.33), channel_id=1, source_target_pairs={{0,1},{1,0},{2,3},{3,2},{4,5},{5,4},{6,7},{7,6},{8,9},{9,8},{10,11... | collective-permute-start | bytes 589832 | tf_op jit(solution)/shard_map/ppermute | solution.py:233
  9.7 18.2 %collective-permute-start.5 = (bf16[3,64,512]{2,1,0:T(8,128)(2,1)}, bf16[3,64,512]{2,1,0:T(8,128)(2,1)S(1)}, u32[]{:S(2)}, u32[]{:S(2)}) collective-permute-start(bf16[3,64,512]{2,1,0:T(8,128)(2,1)} %get-tuple-element.34), channel_id=1, source_target_pairs={{0,7},{1,6},{2,5},{3,4},{4,3},{5,2},{6,1},{7,0},{8,15},{9,14},{10,... | collective-permute-start | bytes 589832 | tf_op jit(solution)/shard_map/ppermute | solution.py:233
  9.8 27.7 %collective-permute-start.6 = (bf16[3,64,512]{2,1,0:T(8,128)(2,1)}, bf16[3,64,512]{2,1,0:T(8,128)(2,1)S(1)}, u32[]{:S(2)}, u32[]{:S(2)}) collective-permute-start(bf16[3,64,512]{2,1,0:T(8,128)(2,1)} %get-tuple-element.35), channel_id=1, source_target_pairs={{0,4},{1,5},{2,6},{3,7},{4,0},{5,1},{6,2},{7,3},{8,12},{9,13},{10,... | collective-permute-start | bytes 589832 | tf_op jit(solution)/shard_map/ppermute | solution.py:233
  11.5 12.3 %copy-start.7 = (bf16[3,64,512]{2,1,0:T(8,128)(2,1)S(1)}, bf16[3,64,512]{2,1,0:T(8,128)(2,1)}, u32[]{:S(2)}) copy-start(bf16[3,64,512]{2,1,0:T(8,128)(2,1)} %get-tuple-element.36) | copy-start | bytes 589828
  11.5 13.0 %copy-start.6 = (bf16[3,64,512]{2,1,0:T(8,128)(2,1)S(1)}, bf16[3,64,512]{2,1,0:T(8,128)(2,1)}, u32[]{:S(2)}) copy-start(bf16[3,64,512]{2,1,0:T(8,128)(2,1)} %get-tuple-element.37) | copy-start | bytes 589828
  11.5 13.1 %copy-start.5 = (bf16[3,64,512]{2,1,0:T(8,128)(2,1)S(1)}, bf16[3,64,512]{2,1,0:T(8,128)(2,1)}, u32[]{:S(2)}) copy-start(bf16[3,64,512]{2,1,0:T(8,128)(2,1)} %get-tuple-element.38) | copy-start | bytes 589828
  11.5 5.8 %collective-permute-start.2 = (bf16[4,1024]{1,0:T(4,128)(2,1)S(1)}, bf16[4,1024]{1,0:T(4,128)(2,1)S(1)}, u32[]{:S(2)}, u32[]{:S(2)}) collective-permute-start(bf16[4,1024]{1,0:T(4,128)(2,1)S(1)} %get-tuple-element.62), channel_id=1, source_target_pairs={{0,24},{1,25},{10,2},{11,3},{20,12},{21,13},{30,22},{31,23}} | collective-permute-start | bytes 24584 | tf_op jit(solution)/shard_map/ppermute | solution.py:48
  17.3 2.6 %collective-permute-start.1 = (bf16[4,1024]{1,0:T(4,128)(2,1)S(1)}, bf16[4,1024]{1,0:T(4,128)(2,1)S(1)}, u32[]{:S(2)}, u32[]{:S(2)}) collective-permute-start(bf16[4,1024]{1,0:T(4,128)(2,1)S(1)} %get-tuple-element.62), channel_id=1, source_target_pairs={{0,16},{1,17},{10,26},{11,27},{20,4},{21,5},{30,14},{31,15}} | collective-permute-start | bytes 24584 | tf_op jit(solution)/shard_map/ppermute | solution.py:48
  20.0 3.9 %collective-permute-start = (bf16[4,1024]{1,0:T(4,128)(2,1)S(1)}, bf16[4,1024]{1,0:T(4,128)(2,1)S(1)}, u32[]{:S(2)}, u32[]{:S(2)}) collective-permute-start(bf16[4,1024]{1,0:T(4,128)(2,1)S(1)} %get-tuple-element.62), channel_id=1, source_target_pairs={{0,8},{1,9},{10,18},{11,19},{20,28},{21,29},{30,6},{31,7}} | collective-permute-start | bytes 24584 | tf_op jit(solution)/shard_map/ppermute | solution.py:48
  23.8 13.7 %collective-permute-start.7 = (bf16[3,64,512]{2,1,0:T(8,128)(2,1)S(1)}, bf16[3,64,512]{2,1,0:T(8,128)(2,1)S(1)}, u32[]{:S(2)}, u32[]{:S(2)}) collective-permute-start(bf16[3,64,512]{2,1,0:T(8,128)(2,1)S(1)} %copy-done.7), channel_id=1, source_target_pairs={{0,2},{1,3},{2,0},{3,1},{4,6},{5,7},{6,4},{7,5},{8,10},{9,11},{10,... | collective-permute-start | bytes 589832 | tf_op jit(solution)/shard_map/ppermute | solution.py:233
  24.5 23.7 %collective-permute-start.8 = (bf16[3,64,512]{2,1,0:T(8,128)(2,1)S(1)}, bf16[3,64,512]{2,1,0:T(8,128)(2,1)S(1)}, u32[]{:S(2)}, u32[]{:S(2)}) collective-permute-start(bf16[3,64,512]{2,1,0:T(8,128)(2,1)S(1)} %copy-done.6), channel_id=1, source_target_pairs={{0,5},{1,4},{2,7},{3,6},{4,1},{5,0},{6,3},{7,2},{8,13},{9,12},{10,... | collective-permute-start | bytes 589832 | tf_op jit(solution)/shard_map/ppermute | solution.py:233
  24.6 25.5 %collective-permute-start.9 = (bf16[3,64,512]{2,1,0:T(8,128)(2,1)S(1)}, bf16[3,64,512]{2,1,0:T(8,128)(2,1)S(1)}, u32[]{:S(2)}, u32[]{:S(2)}) collective-permute-start(bf16[3,64,512]{2,1,0:T(8,128)(2,1)S(1)} %copy-done.5), channel_id=1, source_target_pairs={{0,3},{1,2},{2,1},{3,0},{4,7},{5,6},{6,5},{7,4},{8,11},{9,10},{10,... | collective-permute-start | bytes 589832 | tf_op jit(solution)/shard_map/ppermute | solution.py:233
  27.9 26.5 %collective-permute-start.14 = (bf16[3,64,512]{2,1,0:T(8,128)(2,1)}, bf16[3,64,512]{2,1,0:T(8,128)(2,1)S(1)}, u32[]{:S(2)}, u32[]{:S(2)}) collective-permute-start(bf16[3,64,512]{2,1,0:T(8,128)(2,1)} %get-tuple-element.43), channel_id=1, source_target_pairs={{0,4},{1,5},{2,6},{3,7},{4,0},{5,1},{6,2},{7,3},{8,12},{9,13},{10,... | collective-permute-start | bytes 589832 | tf_op jit(solution)/shard_map/ppermute | solution.py:233
  37.5 17.0 %collective-permute-start.15 = (bf16[3,64,512]{2,1,0:T(8,128)(2,1)}, bf16[3,64,512]{2,1,0:T(8,128)(2,1)S(1)}, u32[]{:S(2)}, u32[]{:S(2)}) collective-permute-start(bf16[3,64,512]{2,1,0:T(8,128)(2,1)} %get-tuple-element.44), channel_id=1, source_target_pairs={{0,1},{1,0},{2,3},{3,2},{4,5},{5,4},{6,7},{7,6},{8,9},{9,8},{10,11... | collective-permute-start | bytes 589832 | tf_op jit(solution)/shard_map/ppermute | solution.py:233
  37.5 24.4 %collective-permute-start.16 = (bf16[3,64,512]{2,1,0:T(8,128)(2,1)}, bf16[3,64,512]{2,1,0:T(8,128)(2,1)S(1)}, u32[]{:S(2)}, u32[]{:S(2)}) collective-permute-start(bf16[3,64,512]{2,1,0:T(8,128)(2,1)} %get-tuple-element.45), channel_id=1, source_target_pairs={{0,5},{1,4},{2,7},{3,6},{4,1},{5,0},{6,3},{7,2},{8,13},{9,12},{10,... | collective-permute-start | bytes 589832 | tf_op jit(solution)/shard_map/ppermute | solution.py:233
  48.2 21.4 %collective-permute-start.17 = (bf16[3,64,512]{2,1,0:T(8,128)(2,1)}, bf16[3,64,512]{2,1,0:T(8,128)(2,1)S(1)}, u32[]{:S(2)}, u32[]{:S(2)}) collective-permute-start(bf16[3,64,512]{2,1,0:T(8,128)(2,1)} %get-tuple-element.46), channel_id=1, source_target_pairs={{0,2},{1,3},{2,0},{3,1},{4,6},{5,7},{6,4},{7,5},{8,10},{9,11},{10,... | collective-permute-start | bytes 589832 | tf_op jit(solution)/shard_map/ppermute | solution.py:233
  50.1 20.7 %collective-permute-start.18 = (bf16[3,64,512]{2,1,0:T(8,128)(2,1)}, bf16[3,64,512]{2,1,0:T(8,128)(2,1)S(1)}, u32[]{:S(2)}, u32[]{:S(2)}) collective-permute-start(bf16[3,64,512]{2,1,0:T(8,128)(2,1)} %get-tuple-element.47), channel_id=1, source_target_pairs={{0,6},{1,7},{2,4},{3,5},{4,2},{5,3},{6,0},{7,1},{8,14},{9,15},{10,... | collective-permute-start | bytes 589832 | tf_op jit(solution)/shard_map/ppermute | solution.py:233
  54.5 20.0 %collective-permute-start.19 = (bf16[3,64,512]{2,1,0:T(8,128)(2,1)}, bf16[3,64,512]{2,1,0:T(8,128)(2,1)S(1)}, u32[]{:S(2)}, u32[]{:S(2)}) collective-permute-start(bf16[3,64,512]{2,1,0:T(8,128)(2,1)} %get-tuple-element.48), channel_id=1, source_target_pairs={{0,3},{1,2},{2,1},{3,0},{4,7},{5,6},{6,5},{7,4},{8,11},{9,10},{10,... | collective-permute-start | bytes 589832 | tf_op jit(solution)/shard_map/ppermute | solution.py:233
  54.5 22.1 %collective-permute-start.20 = (bf16[3,64,512]{2,1,0:T(8,128)(2,1)}, bf16[3,64,512]{2,1,0:T(8,128)(2,1)S(1)}, u32[]{:S(2)}, u32[]{:S(2)}) collective-permute-start(bf16[3,64,512]{2,1,0:T(8,128)(2,1)} %get-tuple-element.49), channel_id=1, source_target_pairs={{0,7},{1,6},{2,5},{3,4},{4,3},{5,2},{6,1},{7,0},{8,15},{9,14},{10,... | collective-permute-start | bytes 589832 | tf_op jit(solution)/shard_map/ppermute | solution.py:233
  61.9 20.6 %collective-permute-start.10 = (bf16[64,512]{1,0:T(8,128)(2,1)S(1)}, bf16[64,512]{1,0:T(8,128)(2,1)S(1)}, u32[]{:S(2)}, u32[]{:S(2)}) collective-permute-start(bf16[64,512]{1,0:T(8,128)(2,1)S(1)} %get-tuple-element.39), channel_id=1, source_target_pairs={{0,4},{1,5},{2,6},{3,7},{4,0},{5,1},{6,2},{7,3},{8,12},{9,13},{10,... | collective-permute-start | bytes 196616 | tf_op jit(solution)/shard_map/ppermute | solution.py:233
  69.7 15.9 %collective-permute-start.11 = (bf16[64,512]{1,0:T(8,128)(2,1)S(1)}, bf16[64,512]{1,0:T(8,128)(2,1)S(1)}, u32[]{:S(2)}, u32[]{:S(2)}) collective-permute-start(bf16[64,512]{1,0:T(8,128)(2,1)S(1)} %get-tuple-element.40), channel_id=1, source_target_pairs={{0,5},{1,4},{2,7},{3,6},{4,1},{5,0},{6,3},{7,2},{8,13},{9,12},{10,... | collective-permute-start | bytes 196616 | tf_op jit(solution)/shard_map/ppermute | solution.py:233
  70.7 16.2 %collective-permute-start.12 = (bf16[64,512]{1,0:T(8,128)(2,1)S(1)}, bf16[64,512]{1,0:T(8,128)(2,1)S(1)}, u32[]{:S(2)}, u32[]{:S(2)}) collective-permute-start(bf16[64,512]{1,0:T(8,128)(2,1)S(1)} %get-tuple-element.41), channel_id=1, source_target_pairs={{0,6},{1,7},{2,4},{3,5},{4,2},{5,3},{6,0},{7,1},{8,14},{9,15},{10,... | collective-permute-start | bytes 196616 | tf_op jit(solution)/shard_map/ppermute | solution.py:233
  74.5 12.6 %collective-permute-start.13 = (bf16[64,512]{1,0:T(8,128)(2,1)S(1)}, bf16[64,512]{1,0:T(8,128)(2,1)S(1)}, u32[]{:S(2)}, u32[]{:S(2)}) collective-permute-start(bf16[64,512]{1,0:T(8,128)(2,1)S(1)} %get-tuple-element.42), channel_id=1, source_target_pairs={{0,7},{1,6},{2,5},{3,4},{4,3},{5,2},{6,1},{7,0},{8,15},{9,14},{10,... | collective-permute-start | bytes 196616 | tf_op jit(solution)/shard_map/ppermute | solution.py:233
  79.7 8.0 %collective-permute-start.21 = (bf16[64,512]{1,0:T(8,128)(2,1)S(1)}, bf16[64,512]{1,0:T(8,128)(2,1)S(1)}, u32[]{:S(2)}, u32[]{:S(2)}) collective-permute-start(bf16[64,512]{1,0:T(8,128)(2,1)S(1)} %get-tuple-element.54), channel_id=1, source_target_pairs={{0,4},{1,5},{2,6},{3,7},{4,0},{5,1},{6,2},{7,3},{8,12},{9,13},{10,... | collective-permute-start | bytes 196616 | tf_op jit(solution)/shard_map/ppermute | solution.py:233
  82.5 9.0 %collective-permute-start.22 = (bf16[64,512]{1,0:T(8,128)(2,1)S(1)}, bf16[64,512]{1,0:T(8,128)(2,1)S(1)}, u32[]{:S(2)}, u32[]{:S(2)}) collective-permute-start(bf16[64,512]{1,0:T(8,128)(2,1)S(1)} %get-tuple-element.55), channel_id=1, source_target_pairs={{0,5},{1,4},{2,7},{3,6},{4,1},{5,0},{6,3},{7,2},{8,13},{9,12},{10,... | collective-permute-start | bytes 196616 | tf_op jit(solution)/shard_map/ppermute | solution.py:233
  85.6 12.6 %collective-permute-start.25 = (bf16[64,1024]{1,0:T(8,128)(2,1)S(1)}, bf16[64,1024]{1,0:T(8,128)(2,1)S(1)}, u32[]{:S(2)}, u32[]{:S(2)}) collective-permute-start(bf16[64,1024]{1,0:T(8,128)(2,1)S(1)} %get-tuple-element.58), channel_id=1, source_target_pairs={{0,2},{1,3},{2,0},{3,1},{4,6},{5,7},{6,4},{7,5},{8,10},{9,11},{10,... | collective-permute-start | bytes 393224 | tf_op jit(solution)/shard_map/ppermute | solution.py:233
  86.9 11.3 %collective-permute-start.26 = (bf16[64,1024]{1,0:T(8,128)(2,1)S(1)}, bf16[64,1024]{1,0:T(8,128)(2,1)S(1)}, u32[]{:S(2)}, u32[]{:S(2)}) collective-permute-start(bf16[64,1024]{1,0:T(8,128)(2,1)S(1)} %get-tuple-element.59), channel_id=1, source_target_pairs={{0,3},{1,2},{2,1},{3,0},{4,7},{5,6},{6,5},{7,4},{8,11},{9,10},{10,... | collective-permute-start | bytes 393224 | tf_op jit(solution)/shard_map/ppermute | solution.py:233
  87.1 11.1 %collective-permute-start.27 = (bf16[64,1024]{1,0:T(8,128)(2,1)S(1)}, bf16[64,1024]{1,0:T(8,128)(2,1)S(1)}, u32[]{:S(2)}, u32[]{:S(2)}) collective-permute-start(bf16[64,1024]{1,0:T(8,128)(2,1)S(1)} %get-tuple-element.60), channel_id=1, source_target_pairs={{0,1},{1,0},{2,3},{3,2},{4,5},{5,4},{6,7},{7,6},{8,9},{9,8},{10,11... | collective-permute-start | bytes 393224 | tf_op jit(solution)/shard_map/ppermute | solution.py:233
  87.8 10.4 %collective-permute-start.23 = (bf16[64,512]{1,0:T(8,128)(2,1)S(1)}, bf16[64,512]{1,0:T(8,128)(2,1)S(1)}, u32[]{:S(2)}, u32[]{:S(2)}) collective-permute-start(bf16[64,512]{1,0:T(8,128)(2,1)S(1)} %get-tuple-element.56), channel_id=1, source_target_pairs={{0,6},{1,7},{2,4},{3,5},{4,2},{5,3},{6,0},{7,1},{8,14},{9,15},{10,... | collective-permute-start | bytes 196616 | tf_op jit(solution)/shard_map/ppermute | solution.py:233
  91.5 6.7 %collective-permute-start.24 = (bf16[64,512]{1,0:T(8,128)(2,1)S(1)}, bf16[64,512]{1,0:T(8,128)(2,1)S(1)}, u32[]{:S(2)}, u32[]{:S(2)}) collective-permute-start(bf16[64,512]{1,0:T(8,128)(2,1)S(1)} %get-tuple-element.57), channel_id=1, source_target_pairs={{0,7},{1,6},{2,5},{3,4},{4,3},{5,2},{6,1},{7,0},{8,15},{9,14},{10,... | collective-permute-start | bytes 196616 | tf_op jit(solution)/shard_map/ppermute | solution.py:233
  (5 other events, 29.6 us)

commit v7 on v6

--- a/solution.py
+++ b/solution.py
@@ -107,9 +107,8 @@
     return (centred * lax.rsqrt(spread + 1e-06) * gain + bias).astype(jnp.bfloat16)
 
 
-def attend_kernel(chunk, slots, width, fetch, layer, qkv, *rest):
+def attend_kernel(chunk, slots, joined, width, fetch, layer, qkv, *rest):
     count = len(slots)
-    half = count // 2
     landed, rest = dict(zip(slots[:-1], rest[: count - 1], strict=True)), rest[count - 1 :]
     held, sems = rest[-2:]
     outs = rest[-2 - count : -2]
@@ -128,10 +127,10 @@
     landed[0] = held.at[0]
     for copy in copies:
         copy.start()
-    done = 0
-    for out, before in zip(outs, given):
-        done = before.shape[1]
-        out[:, :done] = before[...]
+    done = [0] * count
+    for slot, before in zip(joined, given):
+        done[slot] = before.shape[1]
+        outs[slot][:, : done[slot]] = before[...]
     if fetch:
         for copy in copies:
             copy.wait()
@@ -163,22 +162,21 @@
             result = result.astype(jnp.bfloat16)
             for turn, slot in enumerate(here):
                 part = result[turn * rows : (turn + 1) * rows]
-                if slot < half:
-                    outs[slot][:, done + place * HD : done + (place + 1) * HD] = part
-                else:
-                    outs[slot][:, cols] = part
-
-
-def attend(chunk, slots, width, fetch, layer, qkv, arrived, given):
+                start = done[slot] + place * HD
+                outs[slot][:, start : start + HD] = part
+
+
+def attend(chunk, slots, joined, width, fetch, layer, qkv, arrived, given):
     count = len(slots)
-    half = count // 2
     _, rows, cols = arrived[0].shape
     patches = count * rows
     before = given[0].shape[1] if given else 0
     outs = pl.pallas_call(
-        functools.partial(attend_kernel, chunk, slots, width, fetch),
-        out_shape=[jax.ShapeDtypeStruct((rows, before + cols), jnp.bfloat16)] * half
-        + [jax.ShapeDtypeStruct((rows, cols), jnp.bfloat16)] * half,
+        functools.partial(attend_kernel, chunk, slots, joined, width, fetch),
+        out_shape=[
+            jax.ShapeDtypeStruct((rows, cols + (before if slot in joined else 0)), jnp.bfloat16)
+            for slot in range(count)
+        ],
         in_specs=[VMEM, HBM]
         + [ANY if fetch else VMEM] * (count - 1)
         + [VMEM] * len(given),
@@ -195,7 +193,7 @@
         ),
         name="attend",
     )(layer, qkv, *arrived, *given)
-    return list(outs[:half]), list(outs[half:])
+    return list(outs)
 
 
 def unpack_kernel(places, width, *rest):
@@ -256,16 +254,17 @@
         landed.append([swap(part, slot) for part, slot in zip(parts, slots[:-1], strict=True)])
     updated, first_moment, second_moment = adamw(master, moment_one, moment_two, grads)
     layer = own_columns(updated.astype(jnp.bfloat16), dp_count, seq_count, width)
-    parts, places, near_out = [], [], []
+    joined, alone = [0] + near[:-1], near[-1]
+    made, outs = {}, []
     for turn, (chunk, slots) in enumerate(zip(chunks, orders, strict=True)):
-        near_out, far_out = attend(
-            chunk, slots, width, turn == 0, layer, qkv, landed[turn], near_out
-        )
-        parts += [swap(out, slot) for out, slot in zip(far_out, far, strict=True)]
-        places += [(chunk, slot) for slot in far]
-    for slot in near[1:] + near[:1] + [0]:
-        parts.append(swap(near_out[slot], slot))
-        places.append((pairs, slot))
+        given = [outs[slot] for slot in joined] if outs else []
+        outs = attend(chunk, slots, joined, width, turn == 0, layer, qkv, landed[turn], given)
+        made.update({(turn, slot): (out, chunk) for slot, out in enumerate(outs)})
+    made.update({(1, slot): (outs[slot], pairs) for slot in joined})
+    order = [(0, alone)] + [(turn, slot) for turn in range(2) for slot in far]
+    order += [(1, slot) for slot in near[1:] + near[:1] + [0]]
+    parts = [swap(made[key][0], key[1]) for key in order]
+    places = [(made[key][1], key[1]) for key in order]
     attended = unpack(parts, places, width, (1, *qkv.shape[2:]))
     return (attended, updated, first_moment, second_moment)
 

time: 99.6 us -> 98.2 us (0.986)
  starting transfers between devices: 42.4 us -> 36.1 us
  waiting for transfers between devices: 38.2 us -> 43 us
    ppermute x25 -> x26, starting transfers between devices: 35.4 us -> 29.1 us  [swap(): lax.ppermute(part, 'seq', [(place, place ^ slot) for place in range(lax.a...]
    ppermute x25 -> x26, waiting for transfers between devices: 35.5 us -> 40.3 us  [swap(): lax.ppermute(part, 'seq', [(place, place ^ slot) for place in range(lax.a...]
  transfers between devices with their start and end apart: 28 -> 29, of which waited for: 10 -> 10; matrix products, arithmetic and copies ran while one was open for 1% -> 1% of each run, Pallas kernels for 13% -> 13%
where the time goes in v7:
time: 98.2 us; the launch traced here: 97.8 us
  waiting for transfers between devices  43 us (44%)
  starting transfers between devices  36.1 us (37%)
  Pallas kernels  13.9 us (14%)
  local copies, waits for them, and re-layouts  3.33 us (3%)
    ppermute x26, waiting for transfers between devices, swap(): lax.ppermute(part, 'seq', [(place, place ^ slot) for place in range(lax.a...  40.3 us
    ppermute x26, starting transfers between devices, swap(): lax.ppermute(part, 'seq', [(place, place ^ slot) for place in range(lax.a...  29.1 us
    pallas_call x2, Pallas kernels, attend(): pl.pallas_call(functools.partial(attend_kernel, chunk, slots, joined, wid...  7.85 us
    ppermute x3, starting transfers between devices, own_columns(): found = found + lax.ppermute(layer, ('dp', 'seq'), pairs)  7.03 us
    pallas_call x2, Pallas kernels, pack(): pl.pallas_call(functools.partial(pack_kernel, chunk, slots, width), out_s...  4.96 us
    ppermute x3, waiting for transfers between devices, own_columns(): found = found + lax.ppermute(layer, ('dp', 'seq'), pairs)  2.7 us
  transfers between devices with their start and end apart: 29, of which 10 were waited for; matrix products, arithmetic and copies ran while one was open for 1% of the time, Pallas kernels for 13%

profile of v7, /device:TPU:0, one launch (start us, length us, event | category | flops | bytes accessed | tf_op | source)
XLA Modules:
  0.0 97.8 jit_solution(12487778585035408725)
XLA Ops:
  0.7 1.4 %slice-done = bf16[3,1,1,64,4096]{4,3,2,1,0:T(8,128)(2,1)S(1)} async-done(((bf16[3,1,2,64,4096]{4,3,2,1,0:T(8,128)(2,1)}), bf16[3,1,1,64,4096]{4,3,2,1,0:T(8,128)(2,1)S(1)}, s32[]{:S(2)}) %slice-start) | async-done | bytes 1572888 | tf_op jit(solution)/shard_map/slice | solution.py:68
  2.1 5.1 %collective-permute-start.3 = (bf16[3,64,512]{2,1,0:T(8,128)(2,1)S(1)}, bf16[3,64,512]{2,1,0:T(8,128)(2,1)S(1)}, u32[]{:S(2)}, u32[]{:S(2)}) collective-permute-start(bf16[3,64,512]{2,1,0:T(8,128)(2,1)S(1)} %dynamic-slice_bitcast_fusion), channel_id=1, source_target_pairs={{0,6},{1,7},{2,4},{3,5},{4,2},{5,3},{6,0},{7,1},{8,14},{9,15},{10,... | collective-permute-start | bytes 589832 | tf_op jit(solution)/shard_map/ppermute | solution.py:231
  7.2 2.4 %pack.2 = (bf16[3,64,512]{2,1,0:T(8,128)(2,1)}, bf16[3,64,512]{2,1,0:T(8,128)(2,1)}, bf16[3,64,512]{2,1,0:T(8,128)(2,1)}, bf16[3,64,512]{2,1,0:T(8,128)(2,1)}, b...) custom-call(bf16[3,1,2,64,4096]{4,3,2,1,0:T(8,128)(2,1)} %qkv.3), custom_call_target="tpu_custom_call" | custom-call | tf_op jit(solution)/shard_map/pack/pallas_call | solution.py:92
  11.5 4.5 %collective-permute-start.2 = (bf16[4,1024]{1,0:T(4,128)(2,1)S(1)}, bf16[4,1024]{1,0:T(4,128)(2,1)S(1)}, u32[]{:S(2)}, u32[]{:S(2)}) collective-permute-start(bf16[4,1024]{1,0:T(4,128)(2,1)S(1)} %get-tuple-element.62), channel_id=1, source_target_pairs={{0,24},{1,25},{10,2},{11,3},{20,12},{21,13},{30,22},{31,23}} | collective-permute-start | bytes 24584 | tf_op jit(solution)/shard_map/ppermute | solution.py:48
  16.0 1.3 %collective-permute-done.2 = bf16[4,1024]{1,0:T(4,128)(2,1)S(1)} collective-permute-done((bf16[4,1024]{1,0:T(4,128)(2,1)S(1)}, bf16[4,1024]{1,0:T(4,128)(2,1)S(1)}, u32[]{:S(2)}, u32[]{:S(2)}) %collective-permute-start.2) | collective-permute-done | bytes 8224 | tf_op jit(solution)/shard_map/ppermute | solution.py:48
  17.3 1.3 %collective-permute-start.1 = (bf16[4,1024]{1,0:T(4,128)(2,1)S(1)}, bf16[4,1024]{1,0:T(4,128)(2,1)S(1)}, u32[]{:S(2)}, u32[]{:S(2)}) collective-permute-start(bf16[4,1024]{1,0:T(4,128)(2,1)S(1)} %get-tuple-element.62), channel_id=1, source_target_pairs={{0,16},{1,17},{10,26},{11,27},{20,4},{21,5},{30,14},{31,15}} | collective-permute-start | bytes 24584 | tf_op jit(solution)/shard_map/ppermute | solution.py:48
  18.6 1.3 %collective-permute-done.1 = bf16[4,1024]{1,0:T(4,128)(2,1)S(1)} collective-permute-done((bf16[4,1024]{1,0:T(4,128)(2,1)S(1)}, bf16[4,1024]{1,0:T(4,128)(2,1)S(1)}, u32[]{:S(2)}, u32[]{:S(2)}) %collective-permute-start.1) | collective-permute-done | bytes 8224 | tf_op jit(solution)/shard_map/ppermute | solution.py:48
  20.0 1.3 %collective-permute-start = (bf16[4,1024]{1,0:T(4,128)(2,1)S(1)}, bf16[4,1024]{1,0:T(4,128)(2,1)S(1)}, u32[]{:S(2)}, u32[]{:S(2)}) collective-permute-start(bf16[4,1024]{1,0:T(4,128)(2,1)S(1)} %get-tuple-element.62), channel_id=1, source_target_pairs={{0,8},{1,9},{10,18},{11,19},{20,28},{21,29},{30,6},{31,7}} | collective-permute-start | bytes 24584 | tf_op jit(solution)/shard_map/ppermute | solution.py:48
  21.2 2.6 %pack.3 = (bf16[3,64,512]{2,1,0:T(8,128)(2,1)}, bf16[3,64,512]{2,1,0:T(8,128)(2,1)}, bf16[3,64,512]{2,1,0:T(8,128)(2,1)}, bf16[3,64,512]{2,1,0:T(8,128)(2,1)}, b...) custom-call(bf16[3,1,2,64,4096]{4,3,2,1,0:T(8,128)(2,1)} %qkv.3), custom_call_target="tpu_custom_call" | custom-call | tf_op jit(solution)/shard_map/pack/pallas_call | solution.py:92
  24.6 3.4 %collective-permute-start.9 = (bf16[3,64,512]{2,1,0:T(8,128)(2,1)S(1)}, bf16[3,64,512]{2,1,0:T(8,128)(2,1)S(1)}, u32[]{:S(2)}, u32[]{:S(2)}) collective-permute-start(bf16[3,64,512]{2,1,0:T(8,128)(2,1)S(1)} %copy-done.5), channel_id=1, source_target_pairs={{0,3},{1,2},{2,1},{3,0},{4,7},{5,6},{6,5},{7,4},{8,11},{9,10},{10,... | collective-permute-start | bytes 589832 | tf_op jit(solution)/shard_map/ppermute | solution.py:231
  28.7 8.8 %collective-permute-done.6.rest_3_ = bf16[3,64,512]{2,1,0:T(8,128)(2,1)S(1)} collective-permute-done((bf16[3,64,512]{2,1,0:T(8,128)(2,1)}, bf16[3,64,512]{2,1,0:T(8,128)(2,1)S(1)}, u32[]{:S(2)}, u32[]{:S(2)}) %collective-permute-start.6) | collective-permute-done | bytes 196640 | tf_op jit(solution)/shard_map/ppermute | solution.py:231
  37.5 10.7 %collective-permute-done.8.rest_5_ = bf16[3,64,512]{2,1,0:T(8,128)(2,1)S(1)} collective-permute-done((bf16[3,64,512]{2,1,0:T(8,128)(2,1)S(1)}, bf16[3,64,512]{2,1,0:T(8,128)(2,1)S(1)}, u32[]{:S(2)}, u32[]{:S(2)}) %collective-permute-start.8) | collective-permute-done | bytes 196640 | tf_op jit(solution)/shard_map/ppermute | solution.py:231
  48.2 1.8 %collective-permute-start.18 = (bf16[3,64,512]{2,1,0:T(8,128)(2,1)}, bf16[3,64,512]{2,1,0:T(8,128)(2,1)S(1)}, u32[]{:S(2)}, u32[]{:S(2)}) collective-permute-start(bf16[3,64,512]{2,1,0:T(8,128)(2,1)} %get-tuple-element.47), channel_id=1, source_target_pairs={{0,2},{1,3},{2,0},{3,1},{4,6},{5,7},{6,4},{7,5},{8,10},{9,11},{10,... | collective-permute-start | bytes 589832 | tf_op jit(solution)/shard_map/ppermute | solution.py:231
  50.1 1.1 %collective-permute-start.19 = (bf16[3,64,512]{2,1,0:T(8,128)(2,1)}, bf16[3,64,512]{2,1,0:T(8,128)(2,1)S(1)}, u32[]{:S(2)}, u32[]{:S(2)}) collective-permute-start(bf16[3,64,512]{2,1,0:T(8,128)(2,1)} %get-tuple-element.48), channel_id=1, source_target_pairs={{0,6},{1,7},{2,4},{3,5},{4,2},{5,3},{6,0},{7,1},{8,14},{9,15},{10,... | collective-permute-start | bytes 589832 | tf_op jit(solution)/shard_map/ppermute | solution.py:231
  51.2 3.3 %collective-permute-done.15.rest_0_ = bf16[3,64,512]{2,1,0:T(8,128)(2,1)S(1)} collective-permute-done((bf16[3,64,512]{2,1,0:T(8,128)(2,1)}, bf16[3,64,512]{2,1,0:T(8,128)(2,1)S(1)}, u32[]{:S(2)}, u32[]{:S(2)}) %collective-permute-start.15) | collective-permute-done | bytes 196640 | tf_op jit(solution)/shard_map/ppermute | solution.py:231
  55.3 1.9 %copy-done = bf16[3,1,2,64,4096]{4,3,2,1,0:T(8,128)(2,1)S(1)} copy-done((bf16[3,1,2,64,4096]{4,3,2,1,0:T(8,128)(2,1)S(1)}, bf16[3,1,2,64,4096]{4,3,2,1,0:T(8,128)(2,1)}, u32[]{:S(2)}) %copy-start) | copy-done | bytes 3145752
  57.2 4.7 %attend.2 = (bf16[64,512]{1,0:T(8,128)(2,1)S(1)}, bf16[64,512]{1,0:T(8,128)(2,1)S(1)}, bf16[64,512]{1,0:T(8,128)(2,1)S(1)}, bf16[64,512]{1,0:T(8,128)(2,1)S(1)},...) custom-call(bf16[4,512]{1,0:T(4,128)(2,1)S(1)} %dynamic-slice_add_fu, ...), custom_call_target="tpu_custom_call" | custom-call | flops 536870912 | bytes 2097152 | tf_op jit(solution)/shard_map/attend/pallas_call | solution.py:174
  61.9 1.0 %collective-permute-start.10 = (bf16[64,512]{1,0:T(8,128)(2,1)S(1)}, bf16[64,512]{1,0:T(8,128)(2,1)S(1)}, u32[]{:S(2)}, u32[]{:S(2)}) collective-permute-start(bf16[64,512]{1,0:T(8,128)(2,1)S(1)} %get-tuple-element.39), channel_id=1, source_target_pairs={{0,3},{1,2},{2,1},{3,0},{4,7},{5,6},{6,5},{7,4},{8,11},{9,10},{10,... | collective-permute-start | bytes 196616 | tf_op jit(solution)/shard_map/ppermute | solution.py:231
  63.0 6.7 %collective-permute-done.18.rest_3_ = bf16[3,64,512]{2,1,0:T(8,128)(2,1)S(1)} collective-permute-done((bf16[3,64,512]{2,1,0:T(8,128)(2,1)}, bf16[3,64,512]{2,1,0:T(8,128)(2,1)S(1)}, u32[]{:S(2)}, u32[]{:S(2)}) %collective-permute-start.18) | collective-permute-done | bytes 196640 | tf_op jit(solution)/shard_map/ppermute | solution.py:231
  70.5 1.9 %collective-permute-start.12 = (bf16[64,512]{1,0:T(8,128)(2,1)S(1)}, bf16[64,512]{1,0:T(8,128)(2,1)S(1)}, u32[]{:S(2)}, u32[]{:S(2)}) collective-permute-start(bf16[64,512]{1,0:T(8,128)(2,1)S(1)} %get-tuple-element.41), channel_id=1, source_target_pairs={{0,5},{1,4},{2,7},{3,6},{4,1},{5,0},{6,3},{7,2},{8,13},{9,12},{10,... | collective-permute-start | bytes 196616 | tf_op jit(solution)/shard_map/ppermute | solution.py:231
  72.4 2.2 %collective-permute-done.20.rest_5_ = bf16[3,64,512]{2,1,0:T(8,128)(2,1)S(1)} collective-permute-done((bf16[3,64,512]{2,1,0:T(8,128)(2,1)}, bf16[3,64,512]{2,1,0:T(8,128)(2,1)S(1)}, u32[]{:S(2)}, u32[]{:S(2)}) %collective-permute-start.20) | collective-permute-done | bytes 196640 | tf_op jit(solution)/shard_map/ppermute | solution.py:231
  74.6 2.5 %collective-permute-start.13 = (bf16[64,512]{1,0:T(8,128)(2,1)S(1)}, bf16[64,512]{1,0:T(8,128)(2,1)S(1)}, u32[]{:S(2)}, u32[]{:S(2)}) collective-permute-start(bf16[64,512]{1,0:T(8,128)(2,1)S(1)} %get-tuple-element.42), channel_id=1, source_target_pairs={{0,6},{1,7},{2,4},{3,5},{4,2},{5,3},{6,0},{7,1},{8,14},{9,15},{10,... | collective-permute-start | bytes 196616 | tf_op jit(solution)/shard_map/ppermute | solution.py:231
  77.7 3.1 %attend.3 = (bf16[64,1024]{1,0:T(8,128)(2,1)S(1)}, bf16[64,1024]{1,0:T(8,128)(2,1)S(1)}, bf16[64,1024]{1,0:T(8,128)(2,1)S(1)}, bf16[64,512]{1,0:T(8,128)(2,1)S(1...) custom-call(bf16[4,512]{1,0:T(4,128)(2,1)S(1)} %dynamic-slice_add_fu, ...), custom_call_target="tpu_custom_call" | custom-call | flops 536870912 | bytes 2097152 | tf_op jit(solution)/shard_map/attend/pallas_call | solution.py:174
  80.8 2.1 %collective-permute-start.22 = (bf16[64,512]{1,0:T(8,128)(2,1)S(1)}, bf16[64,512]{1,0:T(8,128)(2,1)S(1)}, u32[]{:S(2)}, u32[]{:S(2)}) collective-permute-start(bf16[64,512]{1,0:T(8,128)(2,1)S(1)} %get-tuple-element.54), channel_id=1, source_target_pairs={{0,4},{1,5},{2,6},{3,7},{4,0},{5,1},{6,2},{7,3},{8,12},{9,13},{10,... | collective-permute-start | bytes 196616 | tf_op jit(solution)/shard_map/ppermute | solution.py:231
  83.0 1.0 %collective-permute-start.23 = (bf16[64,512]{1,0:T(8,128)(2,1)S(1)}, bf16[64,512]{1,0:T(8,128)(2,1)S(1)}, u32[]{:S(2)}, u32[]{:S(2)}) collective-permute-start(bf16[64,512]{1,0:T(8,128)(2,1)S(1)} %get-tuple-element.55), channel_id=1, source_target_pairs={{0,5},{1,4},{2,7},{3,6},{4,1},{5,0},{6,3},{7,2},{8,13},{9,12},{10,... | collective-permute-start | bytes 196616 | tf_op jit(solution)/shard_map/ppermute | solution.py:231
  84.5 1.6 %collective-permute-start.28 = (bf16[64,1024]{1,0:T(8,128)(2,1)S(1)}, bf16[64,1024]{1,0:T(8,128)(2,1)S(1)}, u32[]{:S(2)}, u32[]{:S(2)}) collective-permute-start(bf16[64,1024]{1,0:T(8,128)(2,1)S(1)} %get-tuple-element.60), channel_id=1, source_target_pairs={{0,1},{1,0},{2,3},{3,2},{4,5},{5,4},{6,7},{7,6},{8,9},{9,8},{10,11... | collective-permute-start | bytes 393224 | tf_op jit(solution)/shard_map/ppermute | solution.py:231
  86.0 1.2 %collective-permute-start.24 = (bf16[64,512]{1,0:T(8,128)(2,1)S(1)}, bf16[64,512]{1,0:T(8,128)(2,1)S(1)}, u32[]{:S(2)}, u32[]{:S(2)}) collective-permute-start(bf16[64,512]{1,0:T(8,128)(2,1)S(1)} %get-tuple-element.56), channel_id=1, source_target_pairs={{0,6},{1,7},{2,4},{3,5},{4,2},{5,3},{6,0},{7,1},{8,14},{9,15},{10,... | collective-permute-start | bytes 196616 | tf_op jit(solution)/shard_map/ppermute | solution.py:231
  87.2 3.4 %collective-permute-done.22.rest_5_ = bf16[64,512]{1,0:T(8,128)(2,1)S(1)} collective-permute-done((bf16[64,512]{1,0:T(8,128)(2,1)S(1)}, bf16[64,512]{1,0:T(8,128)(2,1)S(1)}, u32[]{:S(2)}, u32[]{:S(2)}) %collective-permute-start.22) | collective-permute-done | bytes 65568 | tf_op jit(solution)/shard_map/ppermute | solution.py:231
  90.6 1.0 %collective-permute-start.25 = (bf16[64,512]{1,0:T(8,128)(2,1)S(1)}, bf16[64,512]{1,0:T(8,128)(2,1)S(1)}, u32[]{:S(2)}, u32[]{:S(2)}) collective-permute-start(bf16[64,512]{1,0:T(8,128)(2,1)S(1)} %get-tuple-element.57), channel_id=1, source_target_pairs={{0,7},{1,6},{2,5},{3,4},{4,3},{5,2},{6,1},{7,0},{8,15},{9,14},{10,... | collective-permute-start | bytes 196616 | tf_op jit(solution)/shard_map/ppermute | solution.py:231
  91.6 2.0 %collective-permute-done.24.rest_7_ = bf16[64,512]{1,0:T(8,128)(2,1)S(1)} collective-permute-done((bf16[64,512]{1,0:T(8,128)(2,1)S(1)}, bf16[64,512]{1,0:T(8,128)(2,1)S(1)}, u32[]{:S(2)}, u32[]{:S(2)}) %collective-permute-start.24) | collective-permute-done | bytes 65568 | tf_op jit(solution)/shard_map/ppermute | solution.py:231
  93.6 3.1 %collective-permute-done.25.rest_8_ = bf16[64,512]{1,0:T(8,128)(2,1)S(1)} collective-permute-done((bf16[64,512]{1,0:T(8,128)(2,1)S(1)}, bf16[64,512]{1,0:T(8,128)(2,1)S(1)}, u32[]{:S(2)}, u32[]{:S(2)}) %collective-permute-start.25) | collective-permute-done | bytes 65568 | tf_op jit(solution)/shard_map/ppermute | solution.py:231
  96.7 1.1 %unpack.1 = bf16[1,2,64,4096]{3,2,1,0:T(8,128)(2,1)} custom-call(bf16[64,512]{1,0:T(8,128)(2,1)S(1)} %collective-permute-done.10.rest_0_, bf16[64,512]{1,0:T(8,128)(2,1)S(1)} %collective-permute-done.11.rest_1_, bf16[64,512]{1,0:T(8,128)(2,1)S(1)} %collective-permute-done.12.rest_2_, bf16[64,512]{1,0:T(8,128)(2,1)S(1)} %collective-permute-done.13.rest_3_, ...), custom_call_target="tpu_custom_call" | custom-call | tf_op jit(solution)/shard_map/unpack/pallas_call | solution.py:215
  (52 shorter events, 6.2 us)
Async XLA Ops:
  2.1 22.4 %collective-permute-start.3 = (bf16[3,64,512]{2,1,0:T(8,128)(2,1)S(1)}, bf16[3,64,512]{2,1,0:T(8,128)(2,1)S(1)}, u32[]{:S(2)}, u32[]{:S(2)}) collective-permute-start(bf16[3,64,512]{2,1,0:T(8,128)(2,1)S(1)} %dynamic-slice_bitcast_fusion), channel_id=1, source_target_pairs={{0,6},{1,7},{2,4},{3,5},{4,2},{5,3},{6,0},{7,1},{8,14},{9,15},{10,... | collective-permute-start | bytes 589832 | tf_op jit(solution)/shard_map/ppermute | solution.py:231
  9.6 14.9 %collective-permute-start.4 = (bf16[3,64,512]{2,1,0:T(8,128)(2,1)}, bf16[3,64,512]{2,1,0:T(8,128)(2,1)S(1)}, u32[]{:S(2)}, u32[]{:S(2)}) collective-permute-start(bf16[3,64,512]{2,1,0:T(8,128)(2,1)} %get-tuple-element.33), channel_id=1, source_target_pairs={{0,1},{1,0},{2,3},{3,2},{4,5},{5,4},{6,7},{7,6},{8,9},{9,8},{10,11... | collective-permute-start | bytes 589832 | tf_op jit(solution)/shard_map/ppermute | solution.py:231
  9.7 18.3 %collective-permute-start.5 = (bf16[3,64,512]{2,1,0:T(8,128)(2,1)}, bf16[3,64,512]{2,1,0:T(8,128)(2,1)S(1)}, u32[]{:S(2)}, u32[]{:S(2)}) collective-permute-start(bf16[3,64,512]{2,1,0:T(8,128)(2,1)} %get-tuple-element.34), channel_id=1, source_target_pairs={{0,7},{1,6},{2,5},{3,4},{4,3},{5,2},{6,1},{7,0},{8,15},{9,14},{10,... | collective-permute-start | bytes 589832 | tf_op jit(solution)/shard_map/ppermute | solution.py:231
  9.8 27.7 %collective-permute-start.6 = (bf16[3,64,512]{2,1,0:T(8,128)(2,1)}, bf16[3,64,512]{2,1,0:T(8,128)(2,1)S(1)}, u32[]{:S(2)}, u32[]{:S(2)}) collective-permute-start(bf16[3,64,512]{2,1,0:T(8,128)(2,1)} %get-tuple-element.35), channel_id=1, source_target_pairs={{0,4},{1,5},{2,6},{3,7},{4,0},{5,1},{6,2},{7,3},{8,12},{9,13},{10,... | collective-permute-start | bytes 589832 | tf_op jit(solution)/shard_map/ppermute | solution.py:231
  11.5 12.4 %copy-start.7 = (bf16[3,64,512]{2,1,0:T(8,128)(2,1)S(1)}, bf16[3,64,512]{2,1,0:T(8,128)(2,1)}, u32[]{:S(2)}) copy-start(bf16[3,64,512]{2,1,0:T(8,128)(2,1)} %get-tuple-element.36) | copy-start | bytes 589828
  11.5 13.1 %copy-start.6 = (bf16[3,64,512]{2,1,0:T(8,128)(2,1)S(1)}, bf16[3,64,512]{2,1,0:T(8,128)(2,1)}, u32[]{:S(2)}) copy-start(bf16[3,64,512]{2,1,0:T(8,128)(2,1)} %get-tuple-element.37) | copy-start | bytes 589828
  11.5 13.1 %copy-start.5 = (bf16[3,64,512]{2,1,0:T(8,128)(2,1)S(1)}, bf16[3,64,512]{2,1,0:T(8,128)(2,1)}, u32[]{:S(2)}) copy-start(bf16[3,64,512]{2,1,0:T(8,128)(2,1)} %get-tuple-element.38) | copy-start | bytes 589828
  11.5 5.8 %collective-permute-start.2 = (bf16[4,1024]{1,0:T(4,128)(2,1)S(1)}, bf16[4,1024]{1,0:T(4,128)(2,1)S(1)}, u32[]{:S(2)}, u32[]{:S(2)}) collective-permute-start(bf16[4,1024]{1,0:T(4,128)(2,1)S(1)} %get-tuple-element.62), channel_id=1, source_target_pairs={{0,24},{1,25},{10,2},{11,3},{20,12},{21,13},{30,22},{31,23}} | collective-permute-start | bytes 24584 | tf_op jit(solution)/shard_map/ppermute | solution.py:48
  17.3 2.6 %collective-permute-start.1 = (bf16[4,1024]{1,0:T(4,128)(2,1)S(1)}, bf16[4,1024]{1,0:T(4,128)(2,1)S(1)}, u32[]{:S(2)}, u32[]{:S(2)}) collective-permute-start(bf16[4,1024]{1,0:T(4,128)(2,1)S(1)} %get-tuple-element.62), channel_id=1, source_target_pairs={{0,16},{1,17},{10,26},{11,27},{20,4},{21,5},{30,14},{31,15}} | collective-permute-start | bytes 24584 | tf_op jit(solution)/shard_map/ppermute | solution.py:48
  20.0 3.9 %collective-permute-start = (bf16[4,1024]{1,0:T(4,128)(2,1)S(1)}, bf16[4,1024]{1,0:T(4,128)(2,1)S(1)}, u32[]{:S(2)}, u32[]{:S(2)}) collective-permute-start(bf16[4,1024]{1,0:T(4,128)(2,1)S(1)} %get-tuple-element.62), channel_id=1, source_target_pairs={{0,8},{1,9},{10,18},{11,19},{20,28},{21,29},{30,6},{31,7}} | collective-permute-start | bytes 24584 | tf_op jit(solution)/shard_map/ppermute | solution.py:48
  23.8 13.7 %collective-permute-start.7 = (bf16[3,64,512]{2,1,0:T(8,128)(2,1)S(1)}, bf16[3,64,512]{2,1,0:T(8,128)(2,1)S(1)}, u32[]{:S(2)}, u32[]{:S(2)}) collective-permute-start(bf16[3,64,512]{2,1,0:T(8,128)(2,1)S(1)} %copy-done.7), channel_id=1, source_target_pairs={{0,2},{1,3},{2,0},{3,1},{4,6},{5,7},{6,4},{7,5},{8,10},{9,11},{10,... | collective-permute-start | bytes 589832 | tf_op jit(solution)/shard_map/ppermute | solution.py:231
  24.5 23.7 %collective-permute-start.8 = (bf16[3,64,512]{2,1,0:T(8,128)(2,1)S(1)}, bf16[3,64,512]{2,1,0:T(8,128)(2,1)S(1)}, u32[]{:S(2)}, u32[]{:S(2)}) collective-permute-start(bf16[3,64,512]{2,1,0:T(8,128)(2,1)S(1)} %copy-done.6), channel_id=1, source_target_pairs={{0,5},{1,4},{2,7},{3,6},{4,1},{5,0},{6,3},{7,2},{8,13},{9,12},{10,... | collective-permute-start | bytes 589832 | tf_op jit(solution)/shard_map/ppermute | solution.py:231
  24.6 25.5 %collective-permute-start.9 = (bf16[3,64,512]{2,1,0:T(8,128)(2,1)S(1)}, bf16[3,64,512]{2,1,0:T(8,128)(2,1)S(1)}, u32[]{:S(2)}, u32[]{:S(2)}) collective-permute-start(bf16[3,64,512]{2,1,0:T(8,128)(2,1)S(1)} %copy-done.5), channel_id=1, source_target_pairs={{0,3},{1,2},{2,1},{3,0},{4,7},{5,6},{6,5},{7,4},{8,11},{9,10},{10,... | collective-permute-start | bytes 589832 | tf_op jit(solution)/shard_map/ppermute | solution.py:231
  27.9 26.5 %collective-permute-start.15 = (bf16[3,64,512]{2,1,0:T(8,128)(2,1)}, bf16[3,64,512]{2,1,0:T(8,128)(2,1)S(1)}, u32[]{:S(2)}, u32[]{:S(2)}) collective-permute-start(bf16[3,64,512]{2,1,0:T(8,128)(2,1)} %get-tuple-element.44), channel_id=1, source_target_pairs={{0,4},{1,5},{2,6},{3,7},{4,0},{5,1},{6,2},{7,3},{8,12},{9,13},{10,... | collective-permute-start | bytes 589832 | tf_op jit(solution)/shard_map/ppermute | solution.py:231
  37.5 17.0 %collective-permute-start.16 = (bf16[3,64,512]{2,1,0:T(8,128)(2,1)}, bf16[3,64,512]{2,1,0:T(8,128)(2,1)S(1)}, u32[]{:S(2)}, u32[]{:S(2)}) collective-permute-start(bf16[3,64,512]{2,1,0:T(8,128)(2,1)} %get-tuple-element.45), channel_id=1, source_target_pairs={{0,1},{1,0},{2,3},{3,2},{4,5},{5,4},{6,7},{7,6},{8,9},{9,8},{10,11... | collective-permute-start | bytes 589832 | tf_op jit(solution)/shard_map/ppermute | solution.py:231
  37.5 24.4 %collective-permute-start.17 = (bf16[3,64,512]{2,1,0:T(8,128)(2,1)}, bf16[3,64,512]{2,1,0:T(8,128)(2,1)S(1)}, u32[]{:S(2)}, u32[]{:S(2)}) collective-permute-start(bf16[3,64,512]{2,1,0:T(8,128)(2,1)} %get-tuple-element.46), channel_id=1, source_target_pairs={{0,5},{1,4},{2,7},{3,6},{4,1},{5,0},{6,3},{7,2},{8,13},{9,12},{10,... | collective-permute-start | bytes 589832 | tf_op jit(solution)/shard_map/ppermute | solution.py:231
  48.2 21.5 %collective-permute-start.18 = (bf16[3,64,512]{2,1,0:T(8,128)(2,1)}, bf16[3,64,512]{2,1,0:T(8,128)(2,1)S(1)}, u32[]{:S(2)}, u32[]{:S(2)}) collective-permute-start(bf16[3,64,512]{2,1,0:T(8,128)(2,1)} %get-tuple-element.47), channel_id=1, source_target_pairs={{0,2},{1,3},{2,0},{3,1},{4,6},{5,7},{6,4},{7,5},{8,10},{9,11},{10,... | collective-permute-start | bytes 589832 | tf_op jit(solution)/shard_map/ppermute | solution.py:231
  50.1 20.5 %collective-permute-start.19 = (bf16[3,64,512]{2,1,0:T(8,128)(2,1)}, bf16[3,64,512]{2,1,0:T(8,128)(2,1)S(1)}, u32[]{:S(2)}, u32[]{:S(2)}) collective-permute-start(bf16[3,64,512]{2,1,0:T(8,128)(2,1)} %get-tuple-element.48), channel_id=1, source_target_pairs={{0,6},{1,7},{2,4},{3,5},{4,2},{5,3},{6,0},{7,1},{8,14},{9,15},{10,... | collective-permute-start | bytes 589832 | tf_op jit(solution)/shard_map/ppermute | solution.py:231
  54.5 20.1 %collective-permute-start.20 = (bf16[3,64,512]{2,1,0:T(8,128)(2,1)}, bf16[3,64,512]{2,1,0:T(8,128)(2,1)S(1)}, u32[]{:S(2)}, u32[]{:S(2)}) collective-permute-start(bf16[3,64,512]{2,1,0:T(8,128)(2,1)} %get-tuple-element.49), channel_id=1, source_target_pairs={{0,3},{1,2},{2,1},{3,0},{4,7},{5,6},{6,5},{7,4},{8,11},{9,10},{10,... | collective-permute-start | bytes 589832 | tf_op jit(solution)/shard_map/ppermute | solution.py:231
  54.5 22.6 %collective-permute-start.21 = (bf16[3,64,512]{2,1,0:T(8,128)(2,1)}, bf16[3,64,512]{2,1,0:T(8,128)(2,1)S(1)}, u32[]{:S(2)}, u32[]{:S(2)}) collective-permute-start(bf16[3,64,512]{2,1,0:T(8,128)(2,1)} %get-tuple-element.50), channel_id=1, source_target_pairs={{0,7},{1,6},{2,5},{3,4},{4,3},{5,2},{6,1},{7,0},{8,15},{9,14},{10,... | collective-permute-start | bytes 589832 | tf_op jit(solution)/shard_map/ppermute | solution.py:231
  61.9 18.9 %collective-permute-start.10 = (bf16[64,512]{1,0:T(8,128)(2,1)S(1)}, bf16[64,512]{1,0:T(8,128)(2,1)S(1)}, u32[]{:S(2)}, u32[]{:S(2)}) collective-permute-start(bf16[64,512]{1,0:T(8,128)(2,1)S(1)} %get-tuple-element.39), channel_id=1, source_target_pairs={{0,3},{1,2},{2,1},{3,0},{4,7},{5,6},{6,5},{7,4},{8,11},{9,10},{10,... | collective-permute-start | bytes 196616 | tf_op jit(solution)/shard_map/ppermute | solution.py:231
  69.7 13.3 %collective-permute-start.11 = (bf16[64,512]{1,0:T(8,128)(2,1)S(1)}, bf16[64,512]{1,0:T(8,128)(2,1)S(1)}, u32[]{:S(2)}, u32[]{:S(2)}) collective-permute-start(bf16[64,512]{1,0:T(8,128)(2,1)S(1)} %get-tuple-element.40), channel_id=1, source_target_pairs={{0,4},{1,5},{2,6},{3,7},{4,0},{5,1},{6,2},{7,3},{8,12},{9,13},{10,... | collective-permute-start | bytes 196616 | tf_op jit(solution)/shard_map/ppermute | solution.py:231
  70.5 13.4 %collective-permute-start.12 = (bf16[64,512]{1,0:T(8,128)(2,1)S(1)}, bf16[64,512]{1,0:T(8,128)(2,1)S(1)}, u32[]{:S(2)}, u32[]{:S(2)}) collective-permute-start(bf16[64,512]{1,0:T(8,128)(2,1)S(1)} %get-tuple-element.41), channel_id=1, source_target_pairs={{0,5},{1,4},{2,7},{3,6},{4,1},{5,0},{6,3},{7,2},{8,13},{9,12},{10,... | collective-permute-start | bytes 196616 | tf_op jit(solution)/shard_map/ppermute | solution.py:231
  74.6 9.9 %collective-permute-start.13 = (bf16[64,512]{1,0:T(8,128)(2,1)S(1)}, bf16[64,512]{1,0:T(8,128)(2,1)S(1)}, u32[]{:S(2)}, u32[]{:S(2)}) collective-permute-start(bf16[64,512]{1,0:T(8,128)(2,1)S(1)} %get-tuple-element.42), channel_id=1, source_target_pairs={{0,6},{1,7},{2,4},{3,5},{4,2},{5,3},{6,0},{7,1},{8,14},{9,15},{10,... | collective-permute-start | bytes 196616 | tf_op jit(solution)/shard_map/ppermute | solution.py:231
  77.1 9.0 %collective-permute-start.14 = (bf16[64,512]{1,0:T(8,128)(2,1)S(1)}, bf16[64,512]{1,0:T(8,128)(2,1)S(1)}, u32[]{:S(2)}, u32[]{:S(2)}) collective-permute-start(bf16[64,512]{1,0:T(8,128)(2,1)S(1)} %get-tuple-element.43), channel_id=1, source_target_pairs={{0,7},{1,6},{2,5},{3,4},{4,3},{5,2},{6,1},{7,0},{8,15},{9,14},{10,... | collective-permute-start | bytes 196616 | tf_op jit(solution)/shard_map/ppermute | solution.py:231
  80.8 9.8 %collective-permute-start.22 = (bf16[64,512]{1,0:T(8,128)(2,1)S(1)}, bf16[64,512]{1,0:T(8,128)(2,1)S(1)}, u32[]{:S(2)}, u32[]{:S(2)}) collective-permute-start(bf16[64,512]{1,0:T(8,128)(2,1)S(1)} %get-tuple-element.54), channel_id=1, source_target_pairs={{0,4},{1,5},{2,6},{3,7},{4,0},{5,1},{6,2},{7,3},{8,12},{9,13},{10,... | collective-permute-start | bytes 196616 | tf_op jit(solution)/shard_map/ppermute | solution.py:231
  83.0 8.6 %collective-permute-start.23 = (bf16[64,512]{1,0:T(8,128)(2,1)S(1)}, bf16[64,512]{1,0:T(8,128)(2,1)S(1)}, u32[]{:S(2)}, u32[]{:S(2)}) collective-permute-start(bf16[64,512]{1,0:T(8,128)(2,1)S(1)} %get-tuple-element.55), channel_id=1, source_target_pairs={{0,5},{1,4},{2,7},{3,6},{4,1},{5,0},{6,3},{7,2},{8,13},{9,12},{10,... | collective-permute-start | bytes 196616 | tf_op jit(solution)/shard_map/ppermute | solution.py:231
  84.0 12.8 %collective-permute-start.26 = (bf16[64,1024]{1,0:T(8,128)(2,1)S(1)}, bf16[64,1024]{1,0:T(8,128)(2,1)S(1)}, u32[]{:S(2)}, u32[]{:S(2)}) collective-permute-start(bf16[64,1024]{1,0:T(8,128)(2,1)S(1)} %get-tuple-element.58), channel_id=1, source_target_pairs={{0,2},{1,3},{2,0},{3,1},{4,6},{5,7},{6,4},{7,5},{8,10},{9,11},{10,... | collective-permute-start | bytes 393224 | tf_op jit(solution)/shard_map/ppermute | solution.py:231
  84.5 12.3 %collective-permute-start.28 = (bf16[64,1024]{1,0:T(8,128)(2,1)S(1)}, bf16[64,1024]{1,0:T(8,128)(2,1)S(1)}, u32[]{:S(2)}, u32[]{:S(2)}) collective-permute-start(bf16[64,1024]{1,0:T(8,128)(2,1)S(1)} %get-tuple-element.60), channel_id=1, source_target_pairs={{0,1},{1,0},{2,3},{3,2},{4,5},{5,4},{6,7},{7,6},{8,9},{9,8},{10,11... | collective-permute-start | bytes 393224 | tf_op jit(solution)/shard_map/ppermute | solution.py:231
  86.0 7.6 %collective-permute-start.24 = (bf16[64,512]{1,0:T(8,128)(2,1)S(1)}, bf16[64,512]{1,0:T(8,128)(2,1)S(1)}, u32[]{:S(2)}, u32[]{:S(2)}) collective-permute-start(bf16[64,512]{1,0:T(8,128)(2,1)S(1)} %get-tuple-element.56), channel_id=1, source_target_pairs={{0,6},{1,7},{2,4},{3,5},{4,2},{5,3},{6,0},{7,1},{8,14},{9,15},{10,... | collective-permute-start | bytes 196616 | tf_op jit(solution)/shard_map/ppermute | solution.py:231
  90.6 6.1 %collective-permute-start.25 = (bf16[64,512]{1,0:T(8,128)(2,1)S(1)}, bf16[64,512]{1,0:T(8,128)(2,1)S(1)}, u32[]{:S(2)}, u32[]{:S(2)}) collective-permute-start(bf16[64,512]{1,0:T(8,128)(2,1)S(1)} %get-tuple-element.57), channel_id=1, source_target_pairs={{0,7},{1,6},{2,5},{3,4},{4,3},{5,2},{6,1},{7,0},{8,15},{9,14},{10,... | collective-permute-start | bytes 196616 | tf_op jit(solution)/shard_map/ppermute | solution.py:231
  91.6 5.1 %collective-permute-start.27 = (bf16[64,512]{1,0:T(8,128)(2,1)S(1)}, bf16[64,512]{1,0:T(8,128)(2,1)S(1)}, u32[]{:S(2)}, u32[]{:S(2)}) collective-permute-start(bf16[64,512]{1,0:T(8,128)(2,1)S(1)} %get-tuple-element.59), channel_id=1, source_target_pairs={{0,3},{1,2},{2,1},{3,0},{4,7},{5,6},{6,5},{7,4},{8,11},{9,10},{10,... | collective-permute-start | bytes 196616 | tf_op jit(solution)/shard_map/ppermute | solution.py:231
  (6 other events, 38.3 us)

commit v8 on v7

--- a/solution.py
+++ b/solution.py
@@ -78,8 +78,10 @@
     for out, slot in zip(outs, slots, strict=True):
         for sample, first, cols, size in spans(chunk):
             start = pl.multiple_of(lax.bitwise_xor(me, slot) * width + first, HD)
-            part = source.at[:, 0, sample, :, pl.ds(start, size)]
-            copies.append(pltpu.make_async_copy(part, out.at[:, :, cols], sems.at[len(copies)]))
+            for which in range(3):
+                part = source.at[which, 0, sample, :, pl.ds(start, size)]
+                there = out.at[which, :, cols]
+                copies.append(pltpu.make_async_copy(part, there, sems.at[len(copies)]))
     for copy in copies:
         copy.start()
     for copy in copies:
@@ -88,7 +90,7 @@
 
 def pack(qkv, chunk, slots, width):
     shape = jax.ShapeDtypeStruct((3, qkv.shape[3], len(chunk) * HD), qkv.dtype)
-    count = len(slots) * len(spans(chunk))
+    count = 3 * len(slots) * len(spans(chunk))
     return pl.pallas_call(
         functools.partial(pack_kernel, chunk, slots, width),
         out_shape=[shape] * len(slots),

time: 98.2 us -> 98.3 us (level)
  waiting for transfers between devices: 43 us -> 36.5 us
  starting transfers between devices: 36.1 us -> 42.5 us
    ppermute x26, waiting for transfers between devices: 40.3 us -> 33.8 us  [swap(): lax.ppermute(part, 'seq', [(place, place ^ slot) for place in range(lax.a...]
    ppermute x26, starting transfers between devices: 29.1 us -> 35.5 us  [swap(): lax.ppermute(part, 'seq', [(place, place ^ slot) for place in range(lax.a...]
where the time goes in v8:
time: 98.3 us; the launch traced here: 97.8 us
  starting transfers between devices  42.5 us (43%)
  waiting for transfers between devices  36.5 us (37%)
  Pallas kernels  14 us (14%)
  local copies, waits for them, and re-layouts  3.33 us (3%)
    ppermute x26, starting transfers between devices, swap(): lax.ppermute(part, 'seq', [(place, place ^ slot) for place in range(lax.a...  35.5 us
    ppermute x26, waiting for transfers between devices, swap(): lax.ppermute(part, 'seq', [(place, place ^ slot) for place in range(lax.a...  33.8 us
    pallas_call x2, Pallas kernels, attend(): pl.pallas_call(functools.partial(attend_kernel, chunk, slots, joined, wid...  7.85 us
    ppermute x3, starting transfers between devices, own_columns(): found = found + lax.ppermute(layer, ('dp', 'seq'), pairs)  7.03 us
    pallas_call x2, Pallas kernels, pack(): pl.pallas_call(functools.partial(pack_kernel, chunk, slots, width), out_s...  5.05 us
    ppermute x3, waiting for transfers between devices, own_columns(): found = found + lax.ppermute(layer, ('dp', 'seq'), pairs)  2.7 us
  transfers between devices with their start and end apart: 29, of which 10 were waited for; matrix products, arithmetic and copies ran while one was open for 1% of the time, Pallas kernels for 13%

profile of v8, /device:TPU:0, one launch (start us, length us, event | category | flops | bytes accessed | tf_op | source)
XLA Modules:
  0.0 97.8 jit_solution(5793167440771932464)
XLA Ops:
  0.7 1.4 %slice-done = bf16[3,1,1,64,4096]{4,3,2,1,0:T(8,128)(2,1)S(1)} async-done(((bf16[3,1,2,64,4096]{4,3,2,1,0:T(8,128)(2,1)}), bf16[3,1,1,64,4096]{4,3,2,1,0:T(8,128)(2,1)S(1)}, s32[]{:S(2)}) %slice-start) | async-done | bytes 1572888 | tf_op jit(solution)/shard_map/slice | solution.py:68
  2.1 5.1 %collective-permute-start.3 = (bf16[3,64,512]{2,1,0:T(8,128)(2,1)S(1)}, bf16[3,64,512]{2,1,0:T(8,128)(2,1)S(1)}, u32[]{:S(2)}, u32[]{:S(2)}) collective-permute-start(bf16[3,64,512]{2,1,0:T(8,128)(2,1)S(1)} %dynamic-slice_bitcast_fusion), channel_id=1, source_target_pairs={{0,6},{1,7},{2,4},{3,5},{4,2},{5,3},{6,0},{7,1},{8,14},{9,15},{10,... | collective-permute-start | bytes 589832 | tf_op jit(solution)/shard_map/ppermute | solution.py:233
  7.2 2.4 %pack.2 = (bf16[3,64,512]{2,1,0:T(8,128)(2,1)}, bf16[3,64,512]{2,1,0:T(8,128)(2,1)}, bf16[3,64,512]{2,1,0:T(8,128)(2,1)}, bf16[3,64,512]{2,1,0:T(8,128)(2,1)}, b...) custom-call(bf16[3,1,2,64,4096]{4,3,2,1,0:T(8,128)(2,1)} %qkv.3), custom_call_target="tpu_custom_call" | custom-call | tf_op jit(solution)/shard_map/pack/pallas_call | solution.py:94
  11.5 4.5 %collective-permute-start.2 = (bf16[4,1024]{1,0:T(4,128)(2,1)S(1)}, bf16[4,1024]{1,0:T(4,128)(2,1)S(1)}, u32[]{:S(2)}, u32[]{:S(2)}) collective-permute-start(bf16[4,1024]{1,0:T(4,128)(2,1)S(1)} %get-tuple-element.62), channel_id=1, source_target_pairs={{0,24},{1,25},{10,2},{11,3},{20,12},{21,13},{30,22},{31,23}} | collective-permute-start | bytes 24584 | tf_op jit(solution)/shard_map/ppermute | solution.py:48
  16.0 1.3 %collective-permute-done.2 = bf16[4,1024]{1,0:T(4,128)(2,1)S(1)} collective-permute-done((bf16[4,1024]{1,0:T(4,128)(2,1)S(1)}, bf16[4,1024]{1,0:T(4,128)(2,1)S(1)}, u32[]{:S(2)}, u32[]{:S(2)}) %collective-permute-start.2) | collective-permute-done | bytes 8224 | tf_op jit(solution)/shard_map/ppermute | solution.py:48
  17.4 1.3 %collective-permute-start.1 = (bf16[4,1024]{1,0:T(4,128)(2,1)S(1)}, bf16[4,1024]{1,0:T(4,128)(2,1)S(1)}, u32[]{:S(2)}, u32[]{:S(2)}) collective-permute-start(bf16[4,1024]{1,0:T(4,128)(2,1)S(1)} %get-tuple-element.62), channel_id=1, source_target_pairs={{0,16},{1,17},{10,26},{11,27},{20,4},{21,5},{30,14},{31,15}} | collective-permute-start | bytes 24584 | tf_op jit(solution)/shard_map/ppermute | solution.py:48
  18.6 1.3 %collective-permute-done.1 = bf16[4,1024]{1,0:T(4,128)(2,1)S(1)} collective-permute-done((bf16[4,1024]{1,0:T(4,128)(2,1)S(1)}, bf16[4,1024]{1,0:T(4,128)(2,1)S(1)}, u32[]{:S(2)}, u32[]{:S(2)}) %collective-permute-start.1) | collective-permute-done | bytes 8224 | tf_op jit(solution)/shard_map/ppermute | solution.py:48
  20.0 1.3 %collective-permute-start = (bf16[4,1024]{1,0:T(4,128)(2,1)S(1)}, bf16[4,1024]{1,0:T(4,128)(2,1)S(1)}, u32[]{:S(2)}, u32[]{:S(2)}) collective-permute-start(bf16[4,1024]{1,0:T(4,128)(2,1)S(1)} %get-tuple-element.62), channel_id=1, source_target_pairs={{0,8},{1,9},{10,18},{11,19},{20,28},{21,29},{30,6},{31,7}} | collective-permute-start | bytes 24584 | tf_op jit(solution)/shard_map/ppermute | solution.py:48
  21.3 2.6 %pack.3 = (bf16[3,64,512]{2,1,0:T(8,128)(2,1)}, bf16[3,64,512]{2,1,0:T(8,128)(2,1)}, bf16[3,64,512]{2,1,0:T(8,128)(2,1)}, bf16[3,64,512]{2,1,0:T(8,128)(2,1)}, b...) custom-call(bf16[3,1,2,64,4096]{4,3,2,1,0:T(8,128)(2,1)} %qkv.3), custom_call_target="tpu_custom_call" | custom-call | tf_op jit(solution)/shard_map/pack/pallas_call | solution.py:94
  24.7 3.4 %collective-permute-start.9 = (bf16[3,64,512]{2,1,0:T(8,128)(2,1)S(1)}, bf16[3,64,512]{2,1,0:T(8,128)(2,1)S(1)}, u32[]{:S(2)}, u32[]{:S(2)}) collective-permute-start(bf16[3,64,512]{2,1,0:T(8,128)(2,1)S(1)} %copy-done.5), channel_id=1, source_target_pairs={{0,3},{1,2},{2,1},{3,0},{4,7},{5,6},{6,5},{7,4},{8,11},{9,10},{10,... | collective-permute-start | bytes 589832 | tf_op jit(solution)/shard_map/ppermute | solution.py:233
  28.7 8.7 %collective-permute-done.6.rest_3_ = bf16[3,64,512]{2,1,0:T(8,128)(2,1)S(1)} collective-permute-done((bf16[3,64,512]{2,1,0:T(8,128)(2,1)}, bf16[3,64,512]{2,1,0:T(8,128)(2,1)S(1)}, u32[]{:S(2)}, u32[]{:S(2)}) %collective-permute-start.6) | collective-permute-done | bytes 196640 | tf_op jit(solution)/shard_map/ppermute | solution.py:233
  37.4 4.4 %collective-permute-done.8.rest_5_ = bf16[3,64,512]{2,1,0:T(8,128)(2,1)S(1)} collective-permute-done((bf16[3,64,512]{2,1,0:T(8,128)(2,1)S(1)}, bf16[3,64,512]{2,1,0:T(8,128)(2,1)S(1)}, u32[]{:S(2)}, u32[]{:S(2)}) %collective-permute-start.8) | collective-permute-done | bytes 196640 | tf_op jit(solution)/shard_map/ppermute | solution.py:233
  41.8 8.2 %collective-permute-start.18 = (bf16[3,64,512]{2,1,0:T(8,128)(2,1)}, bf16[3,64,512]{2,1,0:T(8,128)(2,1)S(1)}, u32[]{:S(2)}, u32[]{:S(2)}) collective-permute-start(bf16[3,64,512]{2,1,0:T(8,128)(2,1)} %get-tuple-element.47), channel_id=1, source_target_pairs={{0,2},{1,3},{2,0},{3,1},{4,6},{5,7},{6,4},{7,5},{8,10},{9,11},{10,... | collective-permute-start | bytes 589832 | tf_op jit(solution)/shard_map/ppermute | solution.py:233
  50.1 1.1 %collective-permute-start.19 = (bf16[3,64,512]{2,1,0:T(8,128)(2,1)}, bf16[3,64,512]{2,1,0:T(8,128)(2,1)S(1)}, u32[]{:S(2)}, u32[]{:S(2)}) collective-permute-start(bf16[3,64,512]{2,1,0:T(8,128)(2,1)} %get-tuple-element.48), channel_id=1, source_target_pairs={{0,6},{1,7},{2,4},{3,5},{4,2},{5,3},{6,0},{7,1},{8,14},{9,15},{10,... | collective-permute-start | bytes 589832 | tf_op jit(solution)/shard_map/ppermute | solution.py:233
  51.2 3.3 %collective-permute-done.15.rest_0_ = bf16[3,64,512]{2,1,0:T(8,128)(2,1)S(1)} collective-permute-done((bf16[3,64,512]{2,1,0:T(8,128)(2,1)}, bf16[3,64,512]{2,1,0:T(8,128)(2,1)S(1)}, u32[]{:S(2)}, u32[]{:S(2)}) %collective-permute-start.15) | collective-permute-done | bytes 196640 | tf_op jit(solution)/shard_map/ppermute | solution.py:233
  55.3 1.9 %copy-done = bf16[3,1,2,64,4096]{4,3,2,1,0:T(8,128)(2,1)S(1)} copy-done((bf16[3,1,2,64,4096]{4,3,2,1,0:T(8,128)(2,1)S(1)}, bf16[3,1,2,64,4096]{4,3,2,1,0:T(8,128)(2,1)}, u32[]{:S(2)}) %copy-start) | copy-done | bytes 3145752
  57.2 4.7 %attend.2 = (bf16[64,512]{1,0:T(8,128)(2,1)S(1)}, bf16[64,512]{1,0:T(8,128)(2,1)S(1)}, bf16[64,512]{1,0:T(8,128)(2,1)S(1)}, bf16[64,512]{1,0:T(8,128)(2,1)S(1)},...) custom-call(bf16[4,512]{1,0:T(4,128)(2,1)S(1)} %dynamic-slice_add_fu, ...), custom_call_target="tpu_custom_call" | custom-call | flops 536870912 | bytes 2097152 | tf_op jit(solution)/shard_map/attend/pallas_call | solution.py:176
  61.9 1.0 %collective-permute-start.10 = (bf16[64,512]{1,0:T(8,128)(2,1)S(1)}, bf16[64,512]{1,0:T(8,128)(2,1)S(1)}, u32[]{:S(2)}, u32[]{:S(2)}) collective-permute-start(bf16[64,512]{1,0:T(8,128)(2,1)S(1)} %get-tuple-element.39), channel_id=1, source_target_pairs={{0,3},{1,2},{2,1},{3,0},{4,7},{5,6},{6,5},{7,4},{8,11},{9,10},{10,... | collective-permute-start | bytes 196616 | tf_op jit(solution)/shard_map/ppermute | solution.py:233
  63.0 6.7 %collective-permute-done.18.rest_3_ = bf16[3,64,512]{2,1,0:T(8,128)(2,1)S(1)} collective-permute-done((bf16[3,64,512]{2,1,0:T(8,128)(2,1)}, bf16[3,64,512]{2,1,0:T(8,128)(2,1)S(1)}, u32[]{:S(2)}, u32[]{:S(2)}) %collective-permute-start.18) | collective-permute-done | bytes 196640 | tf_op jit(solution)/shard_map/ppermute | solution.py:233
  70.5 1.9 %collective-permute-start.12 = (bf16[64,512]{1,0:T(8,128)(2,1)S(1)}, bf16[64,512]{1,0:T(8,128)(2,1)S(1)}, u32[]{:S(2)}, u32[]{:S(2)}) collective-permute-start(bf16[64,512]{1,0:T(8,128)(2,1)S(1)} %get-tuple-element.41), channel_id=1, source_target_pairs={{0,5},{1,4},{2,7},{3,6},{4,1},{5,0},{6,3},{7,2},{8,13},{9,12},{10,... | collective-permute-start | bytes 196616 | tf_op jit(solution)/shard_map/ppermute | solution.py:233
  72.4 2.2 %collective-permute-done.20.rest_5_ = bf16[3,64,512]{2,1,0:T(8,128)(2,1)S(1)} collective-permute-done((bf16[3,64,512]{2,1,0:T(8,128)(2,1)}, bf16[3,64,512]{2,1,0:T(8,128)(2,1)S(1)}, u32[]{:S(2)}, u32[]{:S(2)}) %collective-permute-start.20) | collective-permute-done | bytes 196640 | tf_op jit(solution)/shard_map/ppermute | solution.py:233
  74.6 2.5 %collective-permute-start.13 = (bf16[64,512]{1,0:T(8,128)(2,1)S(1)}, bf16[64,512]{1,0:T(8,128)(2,1)S(1)}, u32[]{:S(2)}, u32[]{:S(2)}) collective-permute-start(bf16[64,512]{1,0:T(8,128)(2,1)S(1)} %get-tuple-element.42), channel_id=1, source_target_pairs={{0,6},{1,7},{2,4},{3,5},{4,2},{5,3},{6,0},{7,1},{8,14},{9,15},{10,... | collective-permute-start | bytes 196616 | tf_op jit(solution)/shard_map/ppermute | solution.py:233
  77.7 3.1 %attend.3 = (bf16[64,1024]{1,0:T(8,128)(2,1)S(1)}, bf16[64,1024]{1,0:T(8,128)(2,1)S(1)}, bf16[64,1024]{1,0:T(8,128)(2,1)S(1)}, bf16[64,512]{1,0:T(8,128)(2,1)S(1...) custom-call(bf16[4,512]{1,0:T(4,128)(2,1)S(1)} %dynamic-slice_add_fu, ...), custom_call_target="tpu_custom_call" | custom-call | flops 536870912 | bytes 2097152 | tf_op jit(solution)/shard_map/attend/pallas_call | solution.py:176
  80.8 2.2 %collective-permute-start.22 = (bf16[64,512]{1,0:T(8,128)(2,1)S(1)}, bf16[64,512]{1,0:T(8,128)(2,1)S(1)}, u32[]{:S(2)}, u32[]{:S(2)}) collective-permute-start(bf16[64,512]{1,0:T(8,128)(2,1)S(1)} %get-tuple-element.54), channel_id=1, source_target_pairs={{0,4},{1,5},{2,6},{3,7},{4,0},{5,1},{6,2},{7,3},{8,12},{9,13},{10,... | collective-permute-start | bytes 196616 | tf_op jit(solution)/shard_map/ppermute | solution.py:233
  83.0 1.0 %collective-permute-start.23 = (bf16[64,512]{1,0:T(8,128)(2,1)S(1)}, bf16[64,512]{1,0:T(8,128)(2,1)S(1)}, u32[]{:S(2)}, u32[]{:S(2)}) collective-permute-start(bf16[64,512]{1,0:T(8,128)(2,1)S(1)} %get-tuple-element.55), channel_id=1, source_target_pairs={{0,5},{1,4},{2,7},{3,6},{4,1},{5,0},{6,3},{7,2},{8,13},{9,12},{10,... | collective-permute-start | bytes 196616 | tf_op jit(solution)/shard_map/ppermute | solution.py:233
  84.5 1.6 %collective-permute-start.28 = (bf16[64,1024]{1,0:T(8,128)(2,1)S(1)}, bf16[64,1024]{1,0:T(8,128)(2,1)S(1)}, u32[]{:S(2)}, u32[]{:S(2)}) collective-permute-start(bf16[64,1024]{1,0:T(8,128)(2,1)S(1)} %get-tuple-element.60), channel_id=1, source_target_pairs={{0,1},{1,0},{2,3},{3,2},{4,5},{5,4},{6,7},{7,6},{8,9},{9,8},{10,11... | collective-permute-start | bytes 393224 | tf_op jit(solution)/shard_map/ppermute | solution.py:233
  86.0 1.2 %collective-permute-start.24 = (bf16[64,512]{1,0:T(8,128)(2,1)S(1)}, bf16[64,512]{1,0:T(8,128)(2,1)S(1)}, u32[]{:S(2)}, u32[]{:S(2)}) collective-permute-start(bf16[64,512]{1,0:T(8,128)(2,1)S(1)} %get-tuple-element.56), channel_id=1, source_target_pairs={{0,6},{1,7},{2,4},{3,5},{4,2},{5,3},{6,0},{7,1},{8,14},{9,15},{10,... | collective-permute-start | bytes 196616 | tf_op jit(solution)/shard_map/ppermute | solution.py:233
  87.2 3.4 %collective-permute-done.22.rest_5_ = bf16[64,512]{1,0:T(8,128)(2,1)S(1)} collective-permute-done((bf16[64,512]{1,0:T(8,128)(2,1)S(1)}, bf16[64,512]{1,0:T(8,128)(2,1)S(1)}, u32[]{:S(2)}, u32[]{:S(2)}) %collective-permute-start.22) | collective-permute-done | bytes 65568 | tf_op jit(solution)/shard_map/ppermute | solution.py:233
  90.6 1.0 %collective-permute-start.25 = (bf16[64,512]{1,0:T(8,128)(2,1)S(1)}, bf16[64,512]{1,0:T(8,128)(2,1)S(1)}, u32[]{:S(2)}, u32[]{:S(2)}) collective-permute-start(bf16[64,512]{1,0:T(8,128)(2,1)S(1)} %get-tuple-element.57), channel_id=1, source_target_pairs={{0,7},{1,6},{2,5},{3,4},{4,3},{5,2},{6,1},{7,0},{8,15},{9,14},{10,... | collective-permute-start | bytes 196616 | tf_op jit(solution)/shard_map/ppermute | solution.py:233
  91.6 2.0 %collective-permute-done.24.rest_7_ = bf16[64,512]{1,0:T(8,128)(2,1)S(1)} collective-permute-done((bf16[64,512]{1,0:T(8,128)(2,1)S(1)}, bf16[64,512]{1,0:T(8,128)(2,1)S(1)}, u32[]{:S(2)}, u32[]{:S(2)}) %collective-permute-start.24) | collective-permute-done | bytes 65568 | tf_op jit(solution)/shard_map/ppermute | solution.py:233
  93.6 3.1 %collective-permute-done.25.rest_8_ = bf16[64,512]{1,0:T(8,128)(2,1)S(1)} collective-permute-done((bf16[64,512]{1,0:T(8,128)(2,1)S(1)}, bf16[64,512]{1,0:T(8,128)(2,1)S(1)}, u32[]{:S(2)}, u32[]{:S(2)}) %collective-permute-start.25) | collective-permute-done | bytes 65568 | tf_op jit(solution)/shard_map/ppermute | solution.py:233
  96.7 1.1 %unpack.1 = bf16[1,2,64,4096]{3,2,1,0:T(8,128)(2,1)} custom-call(bf16[64,512]{1,0:T(8,128)(2,1)S(1)} %collective-permute-done.10.rest_0_, bf16[64,512]{1,0:T(8,128)(2,1)S(1)} %collective-permute-done.11.rest_1_, bf16[64,512]{1,0:T(8,128)(2,1)S(1)} %collective-permute-done.12.rest_2_, bf16[64,512]{1,0:T(8,128)(2,1)S(1)} %collective-permute-done.13.rest_3_, ...), custom_call_target="tpu_custom_call" | custom-call | tf_op jit(solution)/shard_map/unpack/pallas_call | solution.py:217
  (52 shorter events, 6.1 us)
Async XLA Ops:
  2.1 22.5 %collective-permute-start.3 = (bf16[3,64,512]{2,1,0:T(8,128)(2,1)S(1)}, bf16[3,64,512]{2,1,0:T(8,128)(2,1)S(1)}, u32[]{:S(2)}, u32[]{:S(2)}) collective-permute-start(bf16[3,64,512]{2,1,0:T(8,128)(2,1)S(1)} %dynamic-slice_bitcast_fusion), channel_id=1, source_target_pairs={{0,6},{1,7},{2,4},{3,5},{4,2},{5,3},{6,0},{7,1},{8,14},{9,15},{10,... | collective-permute-start | bytes 589832 | tf_op jit(solution)/shard_map/ppermute | solution.py:233
  9.7 15.0 %collective-permute-start.4 = (bf16[3,64,512]{2,1,0:T(8,128)(2,1)}, bf16[3,64,512]{2,1,0:T(8,128)(2,1)S(1)}, u32[]{:S(2)}, u32[]{:S(2)}) collective-permute-start(bf16[3,64,512]{2,1,0:T(8,128)(2,1)} %get-tuple-element.33), channel_id=1, source_target_pairs={{0,1},{1,0},{2,3},{3,2},{4,5},{5,4},{6,7},{7,6},{8,9},{9,8},{10,11... | collective-permute-start | bytes 589832 | tf_op jit(solution)/shard_map/ppermute | solution.py:233
  9.7 18.3 %collective-permute-start.5 = (bf16[3,64,512]{2,1,0:T(8,128)(2,1)}, bf16[3,64,512]{2,1,0:T(8,128)(2,1)S(1)}, u32[]{:S(2)}, u32[]{:S(2)}) collective-permute-start(bf16[3,64,512]{2,1,0:T(8,128)(2,1)} %get-tuple-element.34), channel_id=1, source_target_pairs={{0,7},{1,6},{2,5},{3,4},{4,3},{5,2},{6,1},{7,0},{8,15},{9,14},{10,... | collective-permute-start | bytes 589832 | tf_op jit(solution)/shard_map/ppermute | solution.py:233
  9.9 27.5 %collective-permute-start.6 = (bf16[3,64,512]{2,1,0:T(8,128)(2,1)}, bf16[3,64,512]{2,1,0:T(8,128)(2,1)S(1)}, u32[]{:S(2)}, u32[]{:S(2)}) collective-permute-start(bf16[3,64,512]{2,1,0:T(8,128)(2,1)} %get-tuple-element.35), channel_id=1, source_target_pairs={{0,4},{1,5},{2,6},{3,7},{4,0},{5,1},{6,2},{7,3},{8,12},{9,13},{10,... | collective-permute-start | bytes 589832 | tf_op jit(solution)/shard_map/ppermute | solution.py:233
  11.5 12.4 %copy-start.7 = (bf16[3,64,512]{2,1,0:T(8,128)(2,1)S(1)}, bf16[3,64,512]{2,1,0:T(8,128)(2,1)}, u32[]{:S(2)}) copy-start(bf16[3,64,512]{2,1,0:T(8,128)(2,1)} %get-tuple-element.36) | copy-start | bytes 589828
  11.5 13.1 %copy-start.6 = (bf16[3,64,512]{2,1,0:T(8,128)(2,1)S(1)}, bf16[3,64,512]{2,1,0:T(8,128)(2,1)}, u32[]{:S(2)}) copy-start(bf16[3,64,512]{2,1,0:T(8,128)(2,1)} %get-tuple-element.37) | copy-start | bytes 589828
  11.5 13.1 %copy-start.5 = (bf16[3,64,512]{2,1,0:T(8,128)(2,1)S(1)}, bf16[3,64,512]{2,1,0:T(8,128)(2,1)}, u32[]{:S(2)}) copy-start(bf16[3,64,512]{2,1,0:T(8,128)(2,1)} %get-tuple-element.38) | copy-start | bytes 589828
  11.5 5.8 %collective-permute-start.2 = (bf16[4,1024]{1,0:T(4,128)(2,1)S(1)}, bf16[4,1024]{1,0:T(4,128)(2,1)S(1)}, u32[]{:S(2)}, u32[]{:S(2)}) collective-permute-start(bf16[4,1024]{1,0:T(4,128)(2,1)S(1)} %get-tuple-element.62), channel_id=1, source_target_pairs={{0,24},{1,25},{10,2},{11,3},{20,12},{21,13},{30,22},{31,23}} | collective-permute-start | bytes 24584 | tf_op jit(solution)/shard_map/ppermute | solution.py:48
  17.4 2.6 %collective-permute-start.1 = (bf16[4,1024]{1,0:T(4,128)(2,1)S(1)}, bf16[4,1024]{1,0:T(4,128)(2,1)S(1)}, u32[]{:S(2)}, u32[]{:S(2)}) collective-permute-start(bf16[4,1024]{1,0:T(4,128)(2,1)S(1)} %get-tuple-element.62), channel_id=1, source_target_pairs={{0,16},{1,17},{10,26},{11,27},{20,4},{21,5},{30,14},{31,15}} | collective-permute-start | bytes 24584 | tf_op jit(solution)/shard_map/ppermute | solution.py:48
  20.0 3.9 %collective-permute-start = (bf16[4,1024]{1,0:T(4,128)(2,1)S(1)}, bf16[4,1024]{1,0:T(4,128)(2,1)S(1)}, u32[]{:S(2)}, u32[]{:S(2)}) collective-permute-start(bf16[4,1024]{1,0:T(4,128)(2,1)S(1)} %get-tuple-element.62), channel_id=1, source_target_pairs={{0,8},{1,9},{10,18},{11,19},{20,28},{21,29},{30,6},{31,7}} | collective-permute-start | bytes 24584 | tf_op jit(solution)/shard_map/ppermute | solution.py:48
  23.9 13.5 %collective-permute-start.7 = (bf16[3,64,512]{2,1,0:T(8,128)(2,1)S(1)}, bf16[3,64,512]{2,1,0:T(8,128)(2,1)S(1)}, u32[]{:S(2)}, u32[]{:S(2)}) collective-permute-start(bf16[3,64,512]{2,1,0:T(8,128)(2,1)S(1)} %copy-done.7), channel_id=1, source_target_pairs={{0,2},{1,3},{2,0},{3,1},{4,6},{5,7},{6,4},{7,5},{8,10},{9,11},{10,... | collective-permute-start | bytes 589832 | tf_op jit(solution)/shard_map/ppermute | solution.py:233
  24.6 17.2 %collective-permute-start.8 = (bf16[3,64,512]{2,1,0:T(8,128)(2,1)S(1)}, bf16[3,64,512]{2,1,0:T(8,128)(2,1)S(1)}, u32[]{:S(2)}, u32[]{:S(2)}) collective-permute-start(bf16[3,64,512]{2,1,0:T(8,128)(2,1)S(1)} %copy-done.6), channel_id=1, source_target_pairs={{0,5},{1,4},{2,7},{3,6},{4,1},{5,0},{6,3},{7,2},{8,13},{9,12},{10,... | collective-permute-start | bytes 589832 | tf_op jit(solution)/shard_map/ppermute | solution.py:233
  24.7 25.4 %collective-permute-start.9 = (bf16[3,64,512]{2,1,0:T(8,128)(2,1)S(1)}, bf16[3,64,512]{2,1,0:T(8,128)(2,1)S(1)}, u32[]{:S(2)}, u32[]{:S(2)}) collective-permute-start(bf16[3,64,512]{2,1,0:T(8,128)(2,1)S(1)} %copy-done.5), channel_id=1, source_target_pairs={{0,3},{1,2},{2,1},{3,0},{4,7},{5,6},{6,5},{7,4},{8,11},{9,10},{10,... | collective-permute-start | bytes 589832 | tf_op jit(solution)/shard_map/ppermute | solution.py:233
  28.0 26.4 %collective-permute-start.15 = (bf16[3,64,512]{2,1,0:T(8,128)(2,1)}, bf16[3,64,512]{2,1,0:T(8,128)(2,1)S(1)}, u32[]{:S(2)}, u32[]{:S(2)}) collective-permute-start(bf16[3,64,512]{2,1,0:T(8,128)(2,1)} %get-tuple-element.44), channel_id=1, source_target_pairs={{0,4},{1,5},{2,6},{3,7},{4,0},{5,1},{6,2},{7,3},{8,12},{9,13},{10,... | collective-permute-start | bytes 589832 | tf_op jit(solution)/shard_map/ppermute | solution.py:233
  37.4 17.1 %collective-permute-start.16 = (bf16[3,64,512]{2,1,0:T(8,128)(2,1)}, bf16[3,64,512]{2,1,0:T(8,128)(2,1)S(1)}, u32[]{:S(2)}, u32[]{:S(2)}) collective-permute-start(bf16[3,64,512]{2,1,0:T(8,128)(2,1)} %get-tuple-element.45), channel_id=1, source_target_pairs={{0,1},{1,0},{2,3},{3,2},{4,5},{5,4},{6,7},{7,6},{8,9},{9,8},{10,11... | collective-permute-start | bytes 589832 | tf_op jit(solution)/shard_map/ppermute | solution.py:233
  37.4 24.5 %collective-permute-start.17 = (bf16[3,64,512]{2,1,0:T(8,128)(2,1)}, bf16[3,64,512]{2,1,0:T(8,128)(2,1)S(1)}, u32[]{:S(2)}, u32[]{:S(2)}) collective-permute-start(bf16[3,64,512]{2,1,0:T(8,128)(2,1)} %get-tuple-element.46), channel_id=1, source_target_pairs={{0,5},{1,4},{2,7},{3,6},{4,1},{5,0},{6,3},{7,2},{8,13},{9,12},{10,... | collective-permute-start | bytes 589832 | tf_op jit(solution)/shard_map/ppermute | solution.py:233
  41.8 27.9 %collective-permute-start.18 = (bf16[3,64,512]{2,1,0:T(8,128)(2,1)}, bf16[3,64,512]{2,1,0:T(8,128)(2,1)S(1)}, u32[]{:S(2)}, u32[]{:S(2)}) collective-permute-start(bf16[3,64,512]{2,1,0:T(8,128)(2,1)} %get-tuple-element.47), channel_id=1, source_target_pairs={{0,2},{1,3},{2,0},{3,1},{4,6},{5,7},{6,4},{7,5},{8,10},{9,11},{10,... | collective-permute-start | bytes 589832 | tf_op jit(solution)/shard_map/ppermute | solution.py:233
  50.1 20.5 %collective-permute-start.19 = (bf16[3,64,512]{2,1,0:T(8,128)(2,1)}, bf16[3,64,512]{2,1,0:T(8,128)(2,1)S(1)}, u32[]{:S(2)}, u32[]{:S(2)}) collective-permute-start(bf16[3,64,512]{2,1,0:T(8,128)(2,1)} %get-tuple-element.48), channel_id=1, source_target_pairs={{0,6},{1,7},{2,4},{3,5},{4,2},{5,3},{6,0},{7,1},{8,14},{9,15},{10,... | collective-permute-start | bytes 589832 | tf_op jit(solution)/shard_map/ppermute | solution.py:233
  54.5 20.1 %collective-permute-start.20 = (bf16[3,64,512]{2,1,0:T(8,128)(2,1)}, bf16[3,64,512]{2,1,0:T(8,128)(2,1)S(1)}, u32[]{:S(2)}, u32[]{:S(2)}) collective-permute-start(bf16[3,64,512]{2,1,0:T(8,128)(2,1)} %get-tuple-element.49), channel_id=1, source_target_pairs={{0,3},{1,2},{2,1},{3,0},{4,7},{5,6},{6,5},{7,4},{8,11},{9,10},{10,... | collective-permute-start | bytes 589832 | tf_op jit(solution)/shard_map/ppermute | solution.py:233
  54.5 22.6 %collective-permute-start.21 = (bf16[3,64,512]{2,1,0:T(8,128)(2,1)}, bf16[3,64,512]{2,1,0:T(8,128)(2,1)S(1)}, u32[]{:S(2)}, u32[]{:S(2)}) collective-permute-start(bf16[3,64,512]{2,1,0:T(8,128)(2,1)} %get-tuple-element.50), channel_id=1, source_target_pairs={{0,7},{1,6},{2,5},{3,4},{4,3},{5,2},{6,1},{7,0},{8,15},{9,14},{10,... | collective-permute-start | bytes 589832 | tf_op jit(solution)/shard_map/ppermute | solution.py:233
  61.9 18.9 %collective-permute-start.10 = (bf16[64,512]{1,0:T(8,128)(2,1)S(1)}, bf16[64,512]{1,0:T(8,128)(2,1)S(1)}, u32[]{:S(2)}, u32[]{:S(2)}) collective-permute-start(bf16[64,512]{1,0:T(8,128)(2,1)S(1)} %get-tuple-element.39), channel_id=1, source_target_pairs={{0,3},{1,2},{2,1},{3,0},{4,7},{5,6},{6,5},{7,4},{8,11},{9,10},{10,... | collective-permute-start | bytes 196616 | tf_op jit(solution)/shard_map/ppermute | solution.py:233
  69.7 13.3 %collective-permute-start.11 = (bf16[64,512]{1,0:T(8,128)(2,1)S(1)}, bf16[64,512]{1,0:T(8,128)(2,1)S(1)}, u32[]{:S(2)}, u32[]{:S(2)}) collective-permute-start(bf16[64,512]{1,0:T(8,128)(2,1)S(1)} %get-tuple-element.40), channel_id=1, source_target_pairs={{0,4},{1,5},{2,6},{3,7},{4,0},{5,1},{6,2},{7,3},{8,12},{9,13},{10,... | collective-permute-start | bytes 196616 | tf_op jit(solution)/shard_map/ppermute | solution.py:233
  70.5 13.4 %collective-permute-start.12 = (bf16[64,512]{1,0:T(8,128)(2,1)S(1)}, bf16[64,512]{1,0:T(8,128)(2,1)S(1)}, u32[]{:S(2)}, u32[]{:S(2)}) collective-permute-start(bf16[64,512]{1,0:T(8,128)(2,1)S(1)} %get-tuple-element.41), channel_id=1, source_target_pairs={{0,5},{1,4},{2,7},{3,6},{4,1},{5,0},{6,3},{7,2},{8,13},{9,12},{10,... | collective-permute-start | bytes 196616 | tf_op jit(solution)/shard_map/ppermute | solution.py:233
  74.6 9.9 %collective-permute-start.13 = (bf16[64,512]{1,0:T(8,128)(2,1)S(1)}, bf16[64,512]{1,0:T(8,128)(2,1)S(1)}, u32[]{:S(2)}, u32[]{:S(2)}) collective-permute-start(bf16[64,512]{1,0:T(8,128)(2,1)S(1)} %get-tuple-element.42), channel_id=1, source_target_pairs={{0,6},{1,7},{2,4},{3,5},{4,2},{5,3},{6,0},{7,1},{8,14},{9,15},{10,... | collective-permute-start | bytes 196616 | tf_op jit(solution)/shard_map/ppermute | solution.py:233
  77.1 9.0 %collective-permute-start.14 = (bf16[64,512]{1,0:T(8,128)(2,1)S(1)}, bf16[64,512]{1,0:T(8,128)(2,1)S(1)}, u32[]{:S(2)}, u32[]{:S(2)}) collective-permute-start(bf16[64,512]{1,0:T(8,128)(2,1)S(1)} %get-tuple-element.43), channel_id=1, source_target_pairs={{0,7},{1,6},{2,5},{3,4},{4,3},{5,2},{6,1},{7,0},{8,15},{9,14},{10,... | collective-permute-start | bytes 196616 | tf_op jit(solution)/shard_map/ppermute | solution.py:233
  80.8 9.8 %collective-permute-start.22 = (bf16[64,512]{1,0:T(8,128)(2,1)S(1)}, bf16[64,512]{1,0:T(8,128)(2,1)S(1)}, u32[]{:S(2)}, u32[]{:S(2)}) collective-permute-start(bf16[64,512]{1,0:T(8,128)(2,1)S(1)} %get-tuple-element.54), channel_id=1, source_target_pairs={{0,4},{1,5},{2,6},{3,7},{4,0},{5,1},{6,2},{7,3},{8,12},{9,13},{10,... | collective-permute-start | bytes 196616 | tf_op jit(solution)/shard_map/ppermute | solution.py:233
  83.0 8.6 %collective-permute-start.23 = (bf16[64,512]{1,0:T(8,128)(2,1)S(1)}, bf16[64,512]{1,0:T(8,128)(2,1)S(1)}, u32[]{:S(2)}, u32[]{:S(2)}) collective-permute-start(bf16[64,512]{1,0:T(8,128)(2,1)S(1)} %get-tuple-element.55), channel_id=1, source_target_pairs={{0,5},{1,4},{2,7},{3,6},{4,1},{5,0},{6,3},{7,2},{8,13},{9,12},{10,... | collective-permute-start | bytes 196616 | tf_op jit(solution)/shard_map/ppermute | solution.py:233
  84.0 12.8 %collective-permute-start.26 = (bf16[64,1024]{1,0:T(8,128)(2,1)S(1)}, bf16[64,1024]{1,0:T(8,128)(2,1)S(1)}, u32[]{:S(2)}, u32[]{:S(2)}) collective-permute-start(bf16[64,1024]{1,0:T(8,128)(2,1)S(1)} %get-tuple-element.58), channel_id=1, source_target_pairs={{0,2},{1,3},{2,0},{3,1},{4,6},{5,7},{6,4},{7,5},{8,10},{9,11},{10,... | collective-permute-start | bytes 393224 | tf_op jit(solution)/shard_map/ppermute | solution.py:233
  84.5 12.2 %collective-permute-start.28 = (bf16[64,1024]{1,0:T(8,128)(2,1)S(1)}, bf16[64,1024]{1,0:T(8,128)(2,1)S(1)}, u32[]{:S(2)}, u32[]{:S(2)}) collective-permute-start(bf16[64,1024]{1,0:T(8,128)(2,1)S(1)} %get-tuple-element.60), channel_id=1, source_target_pairs={{0,1},{1,0},{2,3},{3,2},{4,5},{5,4},{6,7},{7,6},{8,9},{9,8},{10,11... | collective-permute-start | bytes 393224 | tf_op jit(solution)/shard_map/ppermute | solution.py:233
  86.0 7.6 %collective-permute-start.24 = (bf16[64,512]{1,0:T(8,128)(2,1)S(1)}, bf16[64,512]{1,0:T(8,128)(2,1)S(1)}, u32[]{:S(2)}, u32[]{:S(2)}) collective-permute-start(bf16[64,512]{1,0:T(8,128)(2,1)S(1)} %get-tuple-element.56), channel_id=1, source_target_pairs={{0,6},{1,7},{2,4},{3,5},{4,2},{5,3},{6,0},{7,1},{8,14},{9,15},{10,... | collective-permute-start | bytes 196616 | tf_op jit(solution)/shard_map/ppermute | solution.py:233
  90.6 6.1 %collective-permute-start.25 = (bf16[64,512]{1,0:T(8,128)(2,1)S(1)}, bf16[64,512]{1,0:T(8,128)(2,1)S(1)}, u32[]{:S(2)}, u32[]{:S(2)}) collective-permute-start(bf16[64,512]{1,0:T(8,128)(2,1)S(1)} %get-tuple-element.57), channel_id=1, source_target_pairs={{0,7},{1,6},{2,5},{3,4},{4,3},{5,2},{6,1},{7,0},{8,15},{9,14},{10,... | collective-permute-start | bytes 196616 | tf_op jit(solution)/shard_map/ppermute | solution.py:233
  91.6 5.1 %collective-permute-start.27 = (bf16[64,512]{1,0:T(8,128)(2,1)S(1)}, bf16[64,512]{1,0:T(8,128)(2,1)S(1)}, u32[]{:S(2)}, u32[]{:S(2)}) collective-permute-start(bf16[64,512]{1,0:T(8,128)(2,1)S(1)} %get-tuple-element.59), channel_id=1, source_target_pairs={{0,3},{1,2},{2,1},{3,0},{4,7},{5,6},{6,5},{7,4},{8,11},{9,10},{10,... | collective-permute-start | bytes 196616 | tf_op jit(solution)/shard_map/ppermute | solution.py:233
  (6 other events, 38.5 us)

commit v9 on v8

--- a/solution.py
+++ b/solution.py
@@ -260,7 +260,7 @@
     made, outs = {}, []
     for turn, (chunk, slots) in enumerate(zip(chunks, orders, strict=True)):
         given = [outs[slot] for slot in joined] if outs else []
-        outs = attend(chunk, slots, joined, width, turn == 0, layer, qkv, landed[turn], given)
+        outs = attend(chunk, slots, joined, width, False, layer, qkv, landed[turn], given)
         made.update({(turn, slot): (out, chunk) for slot, out in enumerate(outs)})
     made.update({(1, slot): (outs[slot], pairs) for slot in joined})
     order = [(0, alone)] + [(turn, slot) for turn in range(2) for slot in far]

time: 98.3 us -> 98.3 us (level)
  waiting for transfers between devices: 36.5 us -> 38.1 us
  Pallas kernels: 14 us -> 12.4 us
    pallas_call x2, Pallas kernels: 7.85 us -> 6.2 us  [attend(): pl.pallas_call(functools.partial(attend_kernel, chunk, slots, joined, wid...]
    ppermute x26, waiting for transfers between devices: 33.8 us -> 35.4 us  [swap(): lax.ppermute(part, 'seq', [(place, place ^ slot) for place in range(lax.a...]
  transfers between devices with their start and end apart: 29 -> 29, of which waited for: 10 -> 10; matrix products, arithmetic and copies ran while one was open for 1% -> 1% of each run, Pallas kernels for 13% -> 12%
where the time goes in v9:
time: 98.3 us; the launch traced here: 97.8 us
  starting transfers between devices  42.5 us (43%)
  waiting for transfers between devices  38.1 us (39%)
  Pallas kernels  12.4 us (13%)
  local copies, waits for them, and re-layouts  3.33 us (3%)
    ppermute x26, starting transfers between devices, swap(): lax.ppermute(part, 'seq', [(place, place ^ slot) for place in range(lax.a...  35.5 us
    ppermute x26, waiting for transfers between devices, swap(): lax.ppermute(part, 'seq', [(place, place ^ slot) for place in range(lax.a...  35.4 us
    ppermute x3, starting transfers between devices, own_columns(): found = found + lax.ppermute(layer, ('dp', 'seq'), pairs)  7.03 us
    pallas_call x2, Pallas kernels, attend(): pl.pallas_call(functools.partial(attend_kernel, chunk, slots, joined, wid...  6.2 us
    pallas_call x2, Pallas kernels, pack(): pl.pallas_call(functools.partial(pack_kernel, chunk, slots, width), out_s...  5.05 us
    ppermute x3, waiting for transfers between devices, own_columns(): found = found + lax.ppermute(layer, ('dp', 'seq'), pairs)  2.7 us
  transfers between devices with their start and end apart: 29, of which 10 were waited for; matrix products, arithmetic and copies ran while one was open for 1% of the time, Pallas kernels for 12%

profile of v9, /device:TPU:0, one launch (start us, length us, event | category | flops | bytes accessed | tf_op | source)
XLA Modules:
  0.0 97.8 jit_solution(13079084475577881621)
XLA Ops:
  0.7 1.4 %slice-done = bf16[3,1,1,64,4096]{4,3,2,1,0:T(8,128)(2,1)S(1)} async-done(((bf16[3,1,2,64,4096]{4,3,2,1,0:T(8,128)(2,1)}), bf16[3,1,1,64,4096]{4,3,2,1,0:T(8,128)(2,1)S(1)}, s32[]{:S(2)}) %slice-start) | async-done | bytes 1572888 | tf_op jit(solution)/shard_map/slice | solution.py:68
  2.1 5.1 %collective-permute-start.3 = (bf16[3,64,512]{2,1,0:T(8,128)(2,1)S(1)}, bf16[3,64,512]{2,1,0:T(8,128)(2,1)S(1)}, u32[]{:S(2)}, u32[]{:S(2)}) collective-permute-start(bf16[3,64,512]{2,1,0:T(8,128)(2,1)S(1)} %dynamic-slice_bitcast_fusion), channel_id=1, source_target_pairs={{0,6},{1,7},{2,4},{3,5},{4,2},{5,3},{6,0},{7,1},{8,14},{9,15},{10,... | collective-permute-start | bytes 589832 | tf_op jit(solution)/shard_map/ppermute | solution.py:233
  7.2 2.4 %pack.2 = (bf16[3,64,512]{2,1,0:T(8,128)(2,1)}, bf16[3,64,512]{2,1,0:T(8,128)(2,1)}, bf16[3,64,512]{2,1,0:T(8,128)(2,1)}, bf16[3,64,512]{2,1,0:T(8,128)(2,1)}, b...) custom-call(bf16[3,1,2,64,4096]{4,3,2,1,0:T(8,128)(2,1)} %qkv.3), custom_call_target="tpu_custom_call" | custom-call | tf_op jit(solution)/shard_map/pack/pallas_call | solution.py:94
  11.5 4.5 %collective-permute-start.2 = (bf16[4,1024]{1,0:T(4,128)(2,1)S(1)}, bf16[4,1024]{1,0:T(4,128)(2,1)S(1)}, u32[]{:S(2)}, u32[]{:S(2)}) collective-permute-start(bf16[4,1024]{1,0:T(4,128)(2,1)S(1)} %get-tuple-element.62), channel_id=1, source_target_pairs={{0,24},{1,25},{10,2},{11,3},{20,12},{21,13},{30,22},{31,23}} | collective-permute-start | bytes 24584 | tf_op jit(solution)/shard_map/ppermute | solution.py:48
  16.0 1.3 %collective-permute-done.2 = bf16[4,1024]{1,0:T(4,128)(2,1)S(1)} collective-permute-done((bf16[4,1024]{1,0:T(4,128)(2,1)S(1)}, bf16[4,1024]{1,0:T(4,128)(2,1)S(1)}, u32[]{:S(2)}, u32[]{:S(2)}) %collective-permute-start.2) | collective-permute-done | bytes 8224 | tf_op jit(solution)/shard_map/ppermute | solution.py:48
  17.4 1.3 %collective-permute-start.1 = (bf16[4,1024]{1,0:T(4,128)(2,1)S(1)}, bf16[4,1024]{1,0:T(4,128)(2,1)S(1)}, u32[]{:S(2)}, u32[]{:S(2)}) collective-permute-start(bf16[4,1024]{1,0:T(4,128)(2,1)S(1)} %get-tuple-element.62), channel_id=1, source_target_pairs={{0,16},{1,17},{10,26},{11,27},{20,4},{21,5},{30,14},{31,15}} | collective-permute-start | bytes 24584 | tf_op jit(solution)/shard_map/ppermute | solution.py:48
  18.6 1.3 %collective-permute-done.1 = bf16[4,1024]{1,0:T(4,128)(2,1)S(1)} collective-permute-done((bf16[4,1024]{1,0:T(4,128)(2,1)S(1)}, bf16[4,1024]{1,0:T(4,128)(2,1)S(1)}, u32[]{:S(2)}, u32[]{:S(2)}) %collective-permute-start.1) | collective-permute-done | bytes 8224 | tf_op jit(solution)/shard_map/ppermute | solution.py:48
  20.0 1.3 %collective-permute-start = (bf16[4,1024]{1,0:T(4,128)(2,1)S(1)}, bf16[4,1024]{1,0:T(4,128)(2,1)S(1)}, u32[]{:S(2)}, u32[]{:S(2)}) collective-permute-start(bf16[4,1024]{1,0:T(4,128)(2,1)S(1)} %get-tuple-element.62), channel_id=1, source_target_pairs={{0,8},{1,9},{10,18},{11,19},{20,28},{21,29},{30,6},{31,7}} | collective-permute-start | bytes 24584 | tf_op jit(solution)/shard_map/ppermute | solution.py:48
  21.3 2.6 %pack.3 = (bf16[3,64,512]{2,1,0:T(8,128)(2,1)}, bf16[3,64,512]{2,1,0:T(8,128)(2,1)}, bf16[3,64,512]{2,1,0:T(8,128)(2,1)}, bf16[3,64,512]{2,1,0:T(8,128)(2,1)}, b...) custom-call(bf16[3,1,2,64,4096]{4,3,2,1,0:T(8,128)(2,1)} %qkv.3), custom_call_target="tpu_custom_call" | custom-call | tf_op jit(solution)/shard_map/pack/pallas_call | solution.py:94
  24.7 3.4 %collective-permute-start.9 = (bf16[3,64,512]{2,1,0:T(8,128)(2,1)S(1)}, bf16[3,64,512]{2,1,0:T(8,128)(2,1)S(1)}, u32[]{:S(2)}, u32[]{:S(2)}) collective-permute-start(bf16[3,64,512]{2,1,0:T(8,128)(2,1)S(1)} %copy-done.5), channel_id=1, source_target_pairs={{0,3},{1,2},{2,1},{3,0},{4,7},{5,6},{6,5},{7,4},{8,11},{9,10},{10,... | collective-permute-start | bytes 589832 | tf_op jit(solution)/shard_map/ppermute | solution.py:233
  28.7 8.7 %collective-permute-done.6.rest_3_ = bf16[3,64,512]{2,1,0:T(8,128)(2,1)S(1)} collective-permute-done((bf16[3,64,512]{2,1,0:T(8,128)(2,1)}, bf16[3,64,512]{2,1,0:T(8,128)(2,1)S(1)}, u32[]{:S(2)}, u32[]{:S(2)}) %collective-permute-start.6) | collective-permute-done | bytes 196640 | tf_op jit(solution)/shard_map/ppermute | solution.py:233
  37.4 4.4 %collective-permute-done.8.rest_5_ = bf16[3,64,512]{2,1,0:T(8,128)(2,1)S(1)} collective-permute-done((bf16[3,64,512]{2,1,0:T(8,128)(2,1)S(1)}, bf16[3,64,512]{2,1,0:T(8,128)(2,1)S(1)}, u32[]{:S(2)}, u32[]{:S(2)}) %collective-permute-start.8) | collective-permute-done | bytes 196640 | tf_op jit(solution)/shard_map/ppermute | solution.py:233
  41.8 8.2 %collective-permute-start.18 = (bf16[3,64,512]{2,1,0:T(8,128)(2,1)}, bf16[3,64,512]{2,1,0:T(8,128)(2,1)S(1)}, u32[]{:S(2)}, u32[]{:S(2)}) collective-permute-start(bf16[3,64,512]{2,1,0:T(8,128)(2,1)} %get-tuple-element.47), channel_id=1, source_target_pairs={{0,2},{1,3},{2,0},{3,1},{4,6},{5,7},{6,4},{7,5},{8,10},{9,11},{10,... | collective-permute-start | bytes 589832 | tf_op jit(solution)/shard_map/ppermute | solution.py:233
  50.1 1.1 %collective-permute-start.19 = (bf16[3,64,512]{2,1,0:T(8,128)(2,1)}, bf16[3,64,512]{2,1,0:T(8,128)(2,1)S(1)}, u32[]{:S(2)}, u32[]{:S(2)}) collective-permute-start(bf16[3,64,512]{2,1,0:T(8,128)(2,1)} %get-tuple-element.48), channel_id=1, source_target_pairs={{0,6},{1,7},{2,4},{3,5},{4,2},{5,3},{6,0},{7,1},{8,14},{9,15},{10,... | collective-permute-start | bytes 589832 | tf_op jit(solution)/shard_map/ppermute | solution.py:233
  51.2 3.3 %collective-permute-done.15.rest_0_ = bf16[3,64,512]{2,1,0:T(8,128)(2,1)S(1)} collective-permute-done((bf16[3,64,512]{2,1,0:T(8,128)(2,1)}, bf16[3,64,512]{2,1,0:T(8,128)(2,1)S(1)}, u32[]{:S(2)}, u32[]{:S(2)}) %collective-permute-start.15) | collective-permute-done | bytes 196640 | tf_op jit(solution)/shard_map/ppermute | solution.py:233
  55.3 1.9 %copy-done = bf16[3,1,2,64,4096]{4,3,2,1,0:T(8,128)(2,1)S(1)} copy-done((bf16[3,1,2,64,4096]{4,3,2,1,0:T(8,128)(2,1)S(1)}, bf16[3,1,2,64,4096]{4,3,2,1,0:T(8,128)(2,1)}, u32[]{:S(2)}) %copy-start) | copy-done | bytes 3145752
  57.2 3.1 %attend.2 = (bf16[64,512]{1,0:T(8,128)(2,1)S(1)}, bf16[64,512]{1,0:T(8,128)(2,1)S(1)}, bf16[64,512]{1,0:T(8,128)(2,1)S(1)}, bf16[64,512]{1,0:T(8,128)(2,1)S(1)},...) custom-call(bf16[4,512]{1,0:T(4,128)(2,1)S(1)} %dynamic-slice_add_fu, ...), custom_call_target="tpu_custom_call" | custom-call | flops 536870912 | bytes 2097152 | tf_op jit(solution)/shard_map/attend/pallas_call | solution.py:176
  60.3 1.0 %collective-permute-start.10 = (bf16[64,512]{1,0:T(8,128)(2,1)S(1)}, bf16[64,512]{1,0:T(8,128)(2,1)S(1)}, u32[]{:S(2)}, u32[]{:S(2)}) collective-permute-start(bf16[64,512]{1,0:T(8,128)(2,1)S(1)} %get-tuple-element.39), channel_id=1, source_target_pairs={{0,3},{1,2},{2,1},{3,0},{4,7},{5,6},{6,5},{7,4},{8,11},{9,10},{10,... | collective-permute-start | bytes 196616 | tf_op jit(solution)/shard_map/ppermute | solution.py:233
  61.3 8.4 %collective-permute-done.18.rest_3_ = bf16[3,64,512]{2,1,0:T(8,128)(2,1)S(1)} collective-permute-done((bf16[3,64,512]{2,1,0:T(8,128)(2,1)}, bf16[3,64,512]{2,1,0:T(8,128)(2,1)S(1)}, u32[]{:S(2)}, u32[]{:S(2)}) %collective-permute-start.18) | collective-permute-done | bytes 196640 | tf_op jit(solution)/shard_map/ppermute | solution.py:233
  70.5 1.9 %collective-permute-start.12 = (bf16[64,512]{1,0:T(8,128)(2,1)S(1)}, bf16[64,512]{1,0:T(8,128)(2,1)S(1)}, u32[]{:S(2)}, u32[]{:S(2)}) collective-permute-start(bf16[64,512]{1,0:T(8,128)(2,1)S(1)} %get-tuple-element.41), channel_id=1, source_target_pairs={{0,5},{1,4},{2,7},{3,6},{4,1},{5,0},{6,3},{7,2},{8,13},{9,12},{10,... | collective-permute-start | bytes 196616 | tf_op jit(solution)/shard_map/ppermute | solution.py:233
  72.4 2.2 %collective-permute-done.20.rest_5_ = bf16[3,64,512]{2,1,0:T(8,128)(2,1)S(1)} collective-permute-done((bf16[3,64,512]{2,1,0:T(8,128)(2,1)}, bf16[3,64,512]{2,1,0:T(8,128)(2,1)S(1)}, u32[]{:S(2)}, u32[]{:S(2)}) %collective-permute-start.20) | collective-permute-done | bytes 196640 | tf_op jit(solution)/shard_map/ppermute | solution.py:233
  74.6 2.5 %collective-permute-start.13 = (bf16[64,512]{1,0:T(8,128)(2,1)S(1)}, bf16[64,512]{1,0:T(8,128)(2,1)S(1)}, u32[]{:S(2)}, u32[]{:S(2)}) collective-permute-start(bf16[64,512]{1,0:T(8,128)(2,1)S(1)} %get-tuple-element.42), channel_id=1, source_target_pairs={{0,6},{1,7},{2,4},{3,5},{4,2},{5,3},{6,0},{7,1},{8,14},{9,15},{10,... | collective-permute-start | bytes 196616 | tf_op jit(solution)/shard_map/ppermute | solution.py:233
  77.7 3.1 %attend.3 = (bf16[64,1024]{1,0:T(8,128)(2,1)S(1)}, bf16[64,1024]{1,0:T(8,128)(2,1)S(1)}, bf16[64,1024]{1,0:T(8,128)(2,1)S(1)}, bf16[64,512]{1,0:T(8,128)(2,1)S(1...) custom-call(bf16[4,512]{1,0:T(4,128)(2,1)S(1)} %dynamic-slice_add_fu, ...), custom_call_target="tpu_custom_call" | custom-call | flops 536870912 | bytes 2097152 | tf_op jit(solution)/shard_map/attend/pallas_call | solution.py:176
  80.8 2.2 %collective-permute-start.22 = (bf16[64,512]{1,0:T(8,128)(2,1)S(1)}, bf16[64,512]{1,0:T(8,128)(2,1)S(1)}, u32[]{:S(2)}, u32[]{:S(2)}) collective-permute-start(bf16[64,512]{1,0:T(8,128)(2,1)S(1)} %get-tuple-element.54), channel_id=1, source_target_pairs={{0,4},{1,5},{2,6},{3,7},{4,0},{5,1},{6,2},{7,3},{8,12},{9,13},{10,... | collective-permute-start | bytes 196616 | tf_op jit(solution)/shard_map/ppermute | solution.py:233
  83.0 1.0 %collective-permute-start.23 = (bf16[64,512]{1,0:T(8,128)(2,1)S(1)}, bf16[64,512]{1,0:T(8,128)(2,1)S(1)}, u32[]{:S(2)}, u32[]{:S(2)}) collective-permute-start(bf16[64,512]{1,0:T(8,128)(2,1)S(1)} %get-tuple-element.55), channel_id=1, source_target_pairs={{0,5},{1,4},{2,7},{3,6},{4,1},{5,0},{6,3},{7,2},{8,13},{9,12},{10,... | collective-permute-start | bytes 196616 | tf_op jit(solution)/shard_map/ppermute | solution.py:233
  84.5 1.6 %collective-permute-start.28 = (bf16[64,1024]{1,0:T(8,128)(2,1)S(1)}, bf16[64,1024]{1,0:T(8,128)(2,1)S(1)}, u32[]{:S(2)}, u32[]{:S(2)}) collective-permute-start(bf16[64,1024]{1,0:T(8,128)(2,1)S(1)} %get-tuple-element.60), channel_id=1, source_target_pairs={{0,1},{1,0},{2,3},{3,2},{4,5},{5,4},{6,7},{7,6},{8,9},{9,8},{10,11... | collective-permute-start | bytes 393224 | tf_op jit(solution)/shard_map/ppermute | solution.py:233
  86.0 1.2 %collective-permute-start.24 = (bf16[64,512]{1,0:T(8,128)(2,1)S(1)}, bf16[64,512]{1,0:T(8,128)(2,1)S(1)}, u32[]{:S(2)}, u32[]{:S(2)}) collective-permute-start(bf16[64,512]{1,0:T(8,128)(2,1)S(1)} %get-tuple-element.56), channel_id=1, source_target_pairs={{0,6},{1,7},{2,4},{3,5},{4,2},{5,3},{6,0},{7,1},{8,14},{9,15},{10,... | collective-permute-start | bytes 196616 | tf_op jit(solution)/shard_map/ppermute | solution.py:233
  87.2 3.4 %collective-permute-done.22.rest_5_ = bf16[64,512]{1,0:T(8,128)(2,1)S(1)} collective-permute-done((bf16[64,512]{1,0:T(8,128)(2,1)S(1)}, bf16[64,512]{1,0:T(8,128)(2,1)S(1)}, u32[]{:S(2)}, u32[]{:S(2)}) %collective-permute-start.22) | collective-permute-done | bytes 65568 | tf_op jit(solution)/shard_map/ppermute | solution.py:233
  90.6 1.0 %collective-permute-start.25 = (bf16[64,512]{1,0:T(8,128)(2,1)S(1)}, bf16[64,512]{1,0:T(8,128)(2,1)S(1)}, u32[]{:S(2)}, u32[]{:S(2)}) collective-permute-start(bf16[64,512]{1,0:T(8,128)(2,1)S(1)} %get-tuple-element.57), channel_id=1, source_target_pairs={{0,7},{1,6},{2,5},{3,4},{4,3},{5,2},{6,1},{7,0},{8,15},{9,14},{10,... | collective-permute-start | bytes 196616 | tf_op jit(solution)/shard_map/ppermute | solution.py:233
  91.6 2.0 %collective-permute-done.24.rest_7_ = bf16[64,512]{1,0:T(8,128)(2,1)S(1)} collective-permute-done((bf16[64,512]{1,0:T(8,128)(2,1)S(1)}, bf16[64,512]{1,0:T(8,128)(2,1)S(1)}, u32[]{:S(2)}, u32[]{:S(2)}) %collective-permute-start.24) | collective-permute-done | bytes 65568 | tf_op jit(solution)/shard_map/ppermute | solution.py:233
  93.6 3.1 %collective-permute-done.25.rest_8_ = bf16[64,512]{1,0:T(8,128)(2,1)S(1)} collective-permute-done((bf16[64,512]{1,0:T(8,128)(2,1)S(1)}, bf16[64,512]{1,0:T(8,128)(2,1)S(1)}, u32[]{:S(2)}, u32[]{:S(2)}) %collective-permute-start.25) | collective-permute-done | bytes 65568 | tf_op jit(solution)/shard_map/ppermute | solution.py:233
  96.7 1.1 %unpack.1 = bf16[1,2,64,4096]{3,2,1,0:T(8,128)(2,1)} custom-call(bf16[64,512]{1,0:T(8,128)(2,1)S(1)} %collective-permute-done.10.rest_0_, bf16[64,512]{1,0:T(8,128)(2,1)S(1)} %collective-permute-done.11.rest_1_, bf16[64,512]{1,0:T(8,128)(2,1)S(1)} %collective-permute-done.12.rest_2_, bf16[64,512]{1,0:T(8,128)(2,1)S(1)} %collective-permute-done.13.rest_3_, ...), custom_call_target="tpu_custom_call" | custom-call | tf_op jit(solution)/shard_map/unpack/pallas_call | solution.py:217
  (52 shorter events, 6.1 us)
Async XLA Ops:
  2.1 22.5 %collective-permute-start.3 = (bf16[3,64,512]{2,1,0:T(8,128)(2,1)S(1)}, bf16[3,64,512]{2,1,0:T(8,128)(2,1)S(1)}, u32[]{:S(2)}, u32[]{:S(2)}) collective-permute-start(bf16[3,64,512]{2,1,0:T(8,128)(2,1)S(1)} %dynamic-slice_bitcast_fusion), channel_id=1, source_target_pairs={{0,6},{1,7},{2,4},{3,5},{4,2},{5,3},{6,0},{7,1},{8,14},{9,15},{10,... | collective-permute-start | bytes 589832 | tf_op jit(solution)/shard_map/ppermute | solution.py:233
  9.7 15.0 %collective-permute-start.4 = (bf16[3,64,512]{2,1,0:T(8,128)(2,1)}, bf16[3,64,512]{2,1,0:T(8,128)(2,1)S(1)}, u32[]{:S(2)}, u32[]{:S(2)}) collective-permute-start(bf16[3,64,512]{2,1,0:T(8,128)(2,1)} %get-tuple-element.33), channel_id=1, source_target_pairs={{0,1},{1,0},{2,3},{3,2},{4,5},{5,4},{6,7},{7,6},{8,9},{9,8},{10,11... | collective-permute-start | bytes 589832 | tf_op jit(solution)/shard_map/ppermute | solution.py:233
  9.7 18.3 %collective-permute-start.5 = (bf16[3,64,512]{2,1,0:T(8,128)(2,1)}, bf16[3,64,512]{2,1,0:T(8,128)(2,1)S(1)}, u32[]{:S(2)}, u32[]{:S(2)}) collective-permute-start(bf16[3,64,512]{2,1,0:T(8,128)(2,1)} %get-tuple-element.34), channel_id=1, source_target_pairs={{0,7},{1,6},{2,5},{3,4},{4,3},{5,2},{6,1},{7,0},{8,15},{9,14},{10,... | collective-permute-start | bytes 589832 | tf_op jit(solution)/shard_map/ppermute | solution.py:233
  9.9 27.5 %collective-permute-start.6 = (bf16[3,64,512]{2,1,0:T(8,128)(2,1)}, bf16[3,64,512]{2,1,0:T(8,128)(2,1)S(1)}, u32[]{:S(2)}, u32[]{:S(2)}) collective-permute-start(bf16[3,64,512]{2,1,0:T(8,128)(2,1)} %get-tuple-element.35), channel_id=1, source_target_pairs={{0,4},{1,5},{2,6},{3,7},{4,0},{5,1},{6,2},{7,3},{8,12},{9,13},{10,... | collective-permute-start | bytes 589832 | tf_op jit(solution)/shard_map/ppermute | solution.py:233
  11.5 12.4 %copy-start.7 = (bf16[3,64,512]{2,1,0:T(8,128)(2,1)S(1)}, bf16[3,64,512]{2,1,0:T(8,128)(2,1)}, u32[]{:S(2)}) copy-start(bf16[3,64,512]{2,1,0:T(8,128)(2,1)} %get-tuple-element.36) | copy-start | bytes 589828
  11.5 13.1 %copy-start.6 = (bf16[3,64,512]{2,1,0:T(8,128)(2,1)S(1)}, bf16[3,64,512]{2,1,0:T(8,128)(2,1)}, u32[]{:S(2)}) copy-start(bf16[3,64,512]{2,1,0:T(8,128)(2,1)} %get-tuple-element.37) | copy-start | bytes 589828
  11.5 13.1 %copy-start.5 = (bf16[3,64,512]{2,1,0:T(8,128)(2,1)S(1)}, bf16[3,64,512]{2,1,0:T(8,128)(2,1)}, u32[]{:S(2)}) copy-start(bf16[3,64,512]{2,1,0:T(8,128)(2,1)} %get-tuple-element.38) | copy-start | bytes 589828
  11.5 5.8 %collective-permute-start.2 = (bf16[4,1024]{1,0:T(4,128)(2,1)S(1)}, bf16[4,1024]{1,0:T(4,128)(2,1)S(1)}, u32[]{:S(2)}, u32[]{:S(2)}) collective-permute-start(bf16[4,1024]{1,0:T(4,128)(2,1)S(1)} %get-tuple-element.62), channel_id=1, source_target_pairs={{0,24},{1,25},{10,2},{11,3},{20,12},{21,13},{30,22},{31,23}} | collective-permute-start | bytes 24584 | tf_op jit(solution)/shard_map/ppermute | solution.py:48
  17.4 2.6 %collective-permute-start.1 = (bf16[4,1024]{1,0:T(4,128)(2,1)S(1)}, bf16[4,1024]{1,0:T(4,128)(2,1)S(1)}, u32[]{:S(2)}, u32[]{:S(2)}) collective-permute-start(bf16[4,1024]{1,0:T(4,128)(2,1)S(1)} %get-tuple-element.62), channel_id=1, source_target_pairs={{0,16},{1,17},{10,26},{11,27},{20,4},{21,5},{30,14},{31,15}} | collective-permute-start | bytes 24584 | tf_op jit(solution)/shard_map/ppermute | solution.py:48
  20.0 3.9 %collective-permute-start = (bf16[4,1024]{1,0:T(4,128)(2,1)S(1)}, bf16[4,1024]{1,0:T(4,128)(2,1)S(1)}, u32[]{:S(2)}, u32[]{:S(2)}) collective-permute-start(bf16[4,1024]{1,0:T(4,128)(2,1)S(1)} %get-tuple-element.62), channel_id=1, source_target_pairs={{0,8},{1,9},{10,18},{11,19},{20,28},{21,29},{30,6},{31,7}} | collective-permute-start | bytes 24584 | tf_op jit(solution)/shard_map/ppermute | solution.py:48
  23.9 13.5 %collective-permute-start.7 = (bf16[3,64,512]{2,1,0:T(8,128)(2,1)S(1)}, bf16[3,64,512]{2,1,0:T(8,128)(2,1)S(1)}, u32[]{:S(2)}, u32[]{:S(2)}) collective-permute-start(bf16[3,64,512]{2,1,0:T(8,128)(2,1)S(1)} %copy-done.7), channel_id=1, source_target_pairs={{0,2},{1,3},{2,0},{3,1},{4,6},{5,7},{6,4},{7,5},{8,10},{9,11},{10,... | collective-permute-start | bytes 589832 | tf_op jit(solution)/shard_map/ppermute | solution.py:233
  24.6 17.2 %collective-permute-start.8 = (bf16[3,64,512]{2,1,0:T(8,128)(2,1)S(1)}, bf16[3,64,512]{2,1,0:T(8,128)(2,1)S(1)}, u32[]{:S(2)}, u32[]{:S(2)}) collective-permute-start(bf16[3,64,512]{2,1,0:T(8,128)(2,1)S(1)} %copy-done.6), channel_id=1, source_target_pairs={{0,5},{1,4},{2,7},{3,6},{4,1},{5,0},{6,3},{7,2},{8,13},{9,12},{10,... | collective-permute-start | bytes 589832 | tf_op jit(solution)/shard_map/ppermute | solution.py:233
  24.7 25.4 %collective-permute-start.9 = (bf16[3,64,512]{2,1,0:T(8,128)(2,1)S(1)}, bf16[3,64,512]{2,1,0:T(8,128)(2,1)S(1)}, u32[]{:S(2)}, u32[]{:S(2)}) collective-permute-start(bf16[3,64,512]{2,1,0:T(8,128)(2,1)S(1)} %copy-done.5), channel_id=1, source_target_pairs={{0,3},{1,2},{2,1},{3,0},{4,7},{5,6},{6,5},{7,4},{8,11},{9,10},{10,... | collective-permute-start | bytes 589832 | tf_op jit(solution)/shard_map/ppermute | solution.py:233
  28.0 26.4 %collective-permute-start.15 = (bf16[3,64,512]{2,1,0:T(8,128)(2,1)}, bf16[3,64,512]{2,1,0:T(8,128)(2,1)S(1)}, u32[]{:S(2)}, u32[]{:S(2)}) collective-permute-start(bf16[3,64,512]{2,1,0:T(8,128)(2,1)} %get-tuple-element.44), channel_id=1, source_target_pairs={{0,4},{1,5},{2,6},{3,7},{4,0},{5,1},{6,2},{7,3},{8,12},{9,13},{10,... | collective-permute-start | bytes 589832 | tf_op jit(solution)/shard_map/ppermute | solution.py:233
  37.4 17.1 %collective-permute-start.16 = (bf16[3,64,512]{2,1,0:T(8,128)(2,1)}, bf16[3,64,512]{2,1,0:T(8,128)(2,1)S(1)}, u32[]{:S(2)}, u32[]{:S(2)}) collective-permute-start(bf16[3,64,512]{2,1,0:T(8,128)(2,1)} %get-tuple-element.45), channel_id=1, source_target_pairs={{0,1},{1,0},{2,3},{3,2},{4,5},{5,4},{6,7},{7,6},{8,9},{9,8},{10,11... | collective-permute-start | bytes 589832 | tf_op jit(solution)/shard_map/ppermute | solution.py:233
  37.4 22.8 %collective-permute-start.17 = (bf16[3,64,512]{2,1,0:T(8,128)(2,1)}, bf16[3,64,512]{2,1,0:T(8,128)(2,1)S(1)}, u32[]{:S(2)}, u32[]{:S(2)}) collective-permute-start(bf16[3,64,512]{2,1,0:T(8,128)(2,1)} %get-tuple-element.46), channel_id=1, source_target_pairs={{0,5},{1,4},{2,7},{3,6},{4,1},{5,0},{6,3},{7,2},{8,13},{9,12},{10,... | collective-permute-start | bytes 589832 | tf_op jit(solution)/shard_map/ppermute | solution.py:233
  41.8 27.9 %collective-permute-start.18 = (bf16[3,64,512]{2,1,0:T(8,128)(2,1)}, bf16[3,64,512]{2,1,0:T(8,128)(2,1)S(1)}, u32[]{:S(2)}, u32[]{:S(2)}) collective-permute-start(bf16[3,64,512]{2,1,0:T(8,128)(2,1)} %get-tuple-element.47), channel_id=1, source_target_pairs={{0,2},{1,3},{2,0},{3,1},{4,6},{5,7},{6,4},{7,5},{8,10},{9,11},{10,... | collective-permute-start | bytes 589832 | tf_op jit(solution)/shard_map/ppermute | solution.py:233
  50.1 20.5 %collective-permute-start.19 = (bf16[3,64,512]{2,1,0:T(8,128)(2,1)}, bf16[3,64,512]{2,1,0:T(8,128)(2,1)S(1)}, u32[]{:S(2)}, u32[]{:S(2)}) collective-permute-start(bf16[3,64,512]{2,1,0:T(8,128)(2,1)} %get-tuple-element.48), channel_id=1, source_target_pairs={{0,6},{1,7},{2,4},{3,5},{4,2},{5,3},{6,0},{7,1},{8,14},{9,15},{10,... | collective-permute-start | bytes 589832 | tf_op jit(solution)/shard_map/ppermute | solution.py:233
  54.5 20.1 %collective-permute-start.20 = (bf16[3,64,512]{2,1,0:T(8,128)(2,1)}, bf16[3,64,512]{2,1,0:T(8,128)(2,1)S(1)}, u32[]{:S(2)}, u32[]{:S(2)}) collective-permute-start(bf16[3,64,512]{2,1,0:T(8,128)(2,1)} %get-tuple-element.49), channel_id=1, source_target_pairs={{0,3},{1,2},{2,1},{3,0},{4,7},{5,6},{6,5},{7,4},{8,11},{9,10},{10,... | collective-permute-start | bytes 589832 | tf_op jit(solution)/shard_map/ppermute | solution.py:233
  54.5 22.6 %collective-permute-start.21 = (bf16[3,64,512]{2,1,0:T(8,128)(2,1)}, bf16[3,64,512]{2,1,0:T(8,128)(2,1)S(1)}, u32[]{:S(2)}, u32[]{:S(2)}) collective-permute-start(bf16[3,64,512]{2,1,0:T(8,128)(2,1)} %get-tuple-element.50), channel_id=1, source_target_pairs={{0,7},{1,6},{2,5},{3,4},{4,3},{5,2},{6,1},{7,0},{8,15},{9,14},{10,... | collective-permute-start | bytes 589832 | tf_op jit(solution)/shard_map/ppermute | solution.py:233
  60.3 20.5 %collective-permute-start.10 = (bf16[64,512]{1,0:T(8,128)(2,1)S(1)}, bf16[64,512]{1,0:T(8,128)(2,1)S(1)}, u32[]{:S(2)}, u32[]{:S(2)}) collective-permute-start(bf16[64,512]{1,0:T(8,128)(2,1)S(1)} %get-tuple-element.39), channel_id=1, source_target_pairs={{0,3},{1,2},{2,1},{3,0},{4,7},{5,6},{6,5},{7,4},{8,11},{9,10},{10,... | collective-permute-start | bytes 196616 | tf_op jit(solution)/shard_map/ppermute | solution.py:233
  69.7 13.3 %collective-permute-start.11 = (bf16[64,512]{1,0:T(8,128)(2,1)S(1)}, bf16[64,512]{1,0:T(8,128)(2,1)S(1)}, u32[]{:S(2)}, u32[]{:S(2)}) collective-permute-start(bf16[64,512]{1,0:T(8,128)(2,1)S(1)} %get-tuple-element.40), channel_id=1, source_target_pairs={{0,4},{1,5},{2,6},{3,7},{4,0},{5,1},{6,2},{7,3},{8,12},{9,13},{10,... | collective-permute-start | bytes 196616 | tf_op jit(solution)/shard_map/ppermute | solution.py:233
  70.5 13.4 %collective-permute-start.12 = (bf16[64,512]{1,0:T(8,128)(2,1)S(1)}, bf16[64,512]{1,0:T(8,128)(2,1)S(1)}, u32[]{:S(2)}, u32[]{:S(2)}) collective-permute-start(bf16[64,512]{1,0:T(8,128)(2,1)S(1)} %get-tuple-element.41), channel_id=1, source_target_pairs={{0,5},{1,4},{2,7},{3,6},{4,1},{5,0},{6,3},{7,2},{8,13},{9,12},{10,... | collective-permute-start | bytes 196616 | tf_op jit(solution)/shard_map/ppermute | solution.py:233
  74.6 9.9 %collective-permute-start.13 = (bf16[64,512]{1,0:T(8,128)(2,1)S(1)}, bf16[64,512]{1,0:T(8,128)(2,1)S(1)}, u32[]{:S(2)}, u32[]{:S(2)}) collective-permute-start(bf16[64,512]{1,0:T(8,128)(2,1)S(1)} %get-tuple-element.42), channel_id=1, source_target_pairs={{0,6},{1,7},{2,4},{3,5},{4,2},{5,3},{6,0},{7,1},{8,14},{9,15},{10,... | collective-permute-start | bytes 196616 | tf_op jit(solution)/shard_map/ppermute | solution.py:233
  77.1 9.0 %collective-permute-start.14 = (bf16[64,512]{1,0:T(8,128)(2,1)S(1)}, bf16[64,512]{1,0:T(8,128)(2,1)S(1)}, u32[]{:S(2)}, u32[]{:S(2)}) collective-permute-start(bf16[64,512]{1,0:T(8,128)(2,1)S(1)} %get-tuple-element.43), channel_id=1, source_target_pairs={{0,7},{1,6},{2,5},{3,4},{4,3},{5,2},{6,1},{7,0},{8,15},{9,14},{10,... | collective-permute-start | bytes 196616 | tf_op jit(solution)/shard_map/ppermute | solution.py:233
  80.8 9.8 %collective-permute-start.22 = (bf16[64,512]{1,0:T(8,128)(2,1)S(1)}, bf16[64,512]{1,0:T(8,128)(2,1)S(1)}, u32[]{:S(2)}, u32[]{:S(2)}) collective-permute-start(bf16[64,512]{1,0:T(8,128)(2,1)S(1)} %get-tuple-element.54), channel_id=1, source_target_pairs={{0,4},{1,5},{2,6},{3,7},{4,0},{5,1},{6,2},{7,3},{8,12},{9,13},{10,... | collective-permute-start | bytes 196616 | tf_op jit(solution)/shard_map/ppermute | solution.py:233
  83.0 8.6 %collective-permute-start.23 = (bf16[64,512]{1,0:T(8,128)(2,1)S(1)}, bf16[64,512]{1,0:T(8,128)(2,1)S(1)}, u32[]{:S(2)}, u32[]{:S(2)}) collective-permute-start(bf16[64,512]{1,0:T(8,128)(2,1)S(1)} %get-tuple-element.55), channel_id=1, source_target_pairs={{0,5},{1,4},{2,7},{3,6},{4,1},{5,0},{6,3},{7,2},{8,13},{9,12},{10,... | collective-permute-start | bytes 196616 | tf_op jit(solution)/shard_map/ppermute | solution.py:233
  84.0 12.8 %collective-permute-start.26 = (bf16[64,1024]{1,0:T(8,128)(2,1)S(1)}, bf16[64,1024]{1,0:T(8,128)(2,1)S(1)}, u32[]{:S(2)}, u32[]{:S(2)}) collective-permute-start(bf16[64,1024]{1,0:T(8,128)(2,1)S(1)} %get-tuple-element.58), channel_id=1, source_target_pairs={{0,2},{1,3},{2,0},{3,1},{4,6},{5,7},{6,4},{7,5},{8,10},{9,11},{10,... | collective-permute-start | bytes 393224 | tf_op jit(solution)/shard_map/ppermute | solution.py:233
  84.5 12.2 %collective-permute-start.28 = (bf16[64,1024]{1,0:T(8,128)(2,1)S(1)}, bf16[64,1024]{1,0:T(8,128)(2,1)S(1)}, u32[]{:S(2)}, u32[]{:S(2)}) collective-permute-start(bf16[64,1024]{1,0:T(8,128)(2,1)S(1)} %get-tuple-element.60), channel_id=1, source_target_pairs={{0,1},{1,0},{2,3},{3,2},{4,5},{5,4},{6,7},{7,6},{8,9},{9,8},{10,11... | collective-permute-start | bytes 393224 | tf_op jit(solution)/shard_map/ppermute | solution.py:233
  86.0 7.6 %collective-permute-start.24 = (bf16[64,512]{1,0:T(8,128)(2,1)S(1)}, bf16[64,512]{1,0:T(8,128)(2,1)S(1)}, u32[]{:S(2)}, u32[]{:S(2)}) collective-permute-start(bf16[64,512]{1,0:T(8,128)(2,1)S(1)} %get-tuple-element.56), channel_id=1, source_target_pairs={{0,6},{1,7},{2,4},{3,5},{4,2},{5,3},{6,0},{7,1},{8,14},{9,15},{10,... | collective-permute-start | bytes 196616 | tf_op jit(solution)/shard_map/ppermute | solution.py:233
  90.6 6.1 %collective-permute-start.25 = (bf16[64,512]{1,0:T(8,128)(2,1)S(1)}, bf16[64,512]{1,0:T(8,128)(2,1)S(1)}, u32[]{:S(2)}, u32[]{:S(2)}) collective-permute-start(bf16[64,512]{1,0:T(8,128)(2,1)S(1)} %get-tuple-element.57), channel_id=1, source_target_pairs={{0,7},{1,6},{2,5},{3,4},{4,3},{5,2},{6,1},{7,0},{8,15},{9,14},{10,... | collective-permute-start | bytes 196616 | tf_op jit(solution)/shard_map/ppermute | solution.py:233
  91.6 5.1 %collective-permute-start.27 = (bf16[64,512]{1,0:T(8,128)(2,1)S(1)}, bf16[64,512]{1,0:T(8,128)(2,1)S(1)}, u32[]{:S(2)}, u32[]{:S(2)}) collective-permute-start(bf16[64,512]{1,0:T(8,128)(2,1)S(1)} %get-tuple-element.59), channel_id=1, source_target_pairs={{0,3},{1,2},{2,1},{3,0},{4,7},{5,6},{6,5},{7,4},{8,11},{9,10},{10,... | collective-permute-start | bytes 196616 | tf_op jit(solution)/shard_map/ppermute | solution.py:233
  (6 other events, 38.5 us)
